TPU v7x, 512 devices: a whole 4x4x16 slice. The times are simulated.
512 devices in a mesh: dp: 8 (over y, core), shard: 64 (over z, x).
Axes of the slice: x: 4, y: 4, z: 16, core: 2. Of those that a mesh axis runs over, the one named last changes fastest.
Arguments:
- candidates: bfloat16 [114688, 1024], P(('dp', 'shard')), may hold values from -6 to 6
- cotangent: bfloat16 [114688, 1024], P(('dp', 'shard')), may hold values from -6 to 6
- history: bfloat16 [65536, 1024], P(('dp', 'shard')), may hold values from -6 to 6
- request_blocks: int32 [1024, 8], P(('dp', 'shard')), may hold values from 0 to 7, each once within a row
- request_length: int32 [1024], P(('dp', 'shard')), may hold values from 1 to 8
- candidate_request: int32 [114688], P(('dp', 'shard')), may hold values from 0 to 1
- in_weight: bfloat16 [1024, 1024], replicated, may hold values from -0.1875 to 0.1875
- out_weight: bfloat16 [512, 1024], replicated, may hold values from -0.25 to 0.25
Outputs:
- layer_out: bfloat16 [114688, 1024], P(('dp', 'shard'))
- grad_out_weight: float32 [512, 1024], P('shard')
- grad_history: bfloat16 [65536, 1024], P(('dp', 'shard'))
Inputs may be any that keep to these rules, and one draw needn't show every extreme that they name: `request_blocks`: each row holds every block number of the window once.
All inputs are finite; a program needn't handle non-finite values.
Results may differ from a plain program's by a relative error of at most 0.0084.
Values may be sent and summed in bfloat16 or wider, within the bound.
No kernel may reach another device: no remote copies, remote signals or barrier semaphores. Data moves between devices by JAX's collectives and lax.ppermute only.
A program may use at most 64 MiB of HBM per device.

v0:
```python
import math

import jax
import jax.numpy as jnp
from jax import lax
from jax.sharding import PartitionSpec as P

HEADS = 4
BLK = 128
SPAN = 8


def shifted(block, axis, distance):
    devices = range(lax.axis_size(axis))
    route = [((i - distance) % len(devices), i) for i in devices]
    return lax.ppermute(block, axis, route)


def layer_norm(values):
    average = jnp.mean(values, axis=-1, keepdims=True)
    centered = values - average
    inv_scale = lax.rsqrt(jnp.mean(centered * centered, axis=-1, keepdims=True) + 1e-05)
    return (centered * inv_scale, inv_scale)


def usage_mask(request_blocks, request_length, candidate_request):
    count_blocks = request_blocks.shape[1]
    positions = jnp.arange(count_blocks, dtype=jnp.int32)
    matches = request_blocks[:, :, None] == positions[None, None, :]
    in_length = positions[None, :] < request_length[:, None]
    used_blocks = jnp.sum(
        jnp.where(matches & in_length[:, :, None], jnp.float32(1.0), jnp.float32(0.0)), axis=1
    )
    request_ids = jnp.arange(request_blocks.shape[0], dtype=jnp.int32)
    membership = jnp.where(
        candidate_request[:, None] == request_ids[None, :], jnp.float32(1.0), jnp.float32(0.0)
    )
    return jnp.dot(membership, used_blocks, precision=lax.Precision.HIGHEST)


def score_block(cand_rows, cot_rows, window, usage, in_weight, out_weight):
    cand_count = cand_rows.shape[0]
    inner_width = out_weight.shape[0]
    head_size = inner_width // HEADS
    row_count = window.shape[0]
    grad_scale = 1.0 / math.sqrt(head_size)
    normed_in, _ = layer_norm(cand_rows.astype(jnp.float32))
    projected = jnp.dot(
        normed_in.astype(jnp.bfloat16), in_weight, preferred_element_type=jnp.float32
    )
    queries = projected[:, :inner_width].astype(jnp.bfloat16).reshape(cand_count, HEADS, head_size)
    gating = jax.nn.silu(projected[:, inner_width:])
    key_rows = window[:, :inner_width].reshape(row_count, HEADS, head_size)
    value_rows = window[:, inner_width:].reshape(row_count, HEADS, head_size)
    usage_rows = jnp.repeat(usage, BLK, axis=1)
    scores = (
        jnp.einsum("chd,rhd->hcr", queries, key_rows, preferred_element_type=jnp.float32)
        * grad_scale
    )
    weights = (jax.nn.silu(scores) * usage_rows[None]).astype(jnp.bfloat16)
    attended = jnp.einsum(
        "hcr,rhd->chd", weights, value_rows, preferred_element_type=jnp.float32
    ).reshape(cand_count, inner_width)
    normed, inv_scale = layer_norm(attended)
    gated_out = (normed * gating).astype(jnp.bfloat16)
    result = (
        cand_rows.astype(jnp.float32)
        + jnp.dot(gated_out, out_weight, preferred_element_type=jnp.float32)
    ).astype(jnp.bfloat16)
    zed_grad = lax.dot_general(
        cot_rows, out_weight, (((1,), (1,)), ((), ())), preferred_element_type=jnp.float32
    )
    pre_grad = zed_grad * gating
    attn_grad = inv_scale * (
        pre_grad
        - jnp.mean(pre_grad, axis=-1, keepdims=True)
        - normed * jnp.mean(pre_grad * normed, axis=-1, keepdims=True)
    )
    attn_grad = attn_grad.astype(jnp.bfloat16).reshape(cand_count, HEADS, head_size)
    value_grad = jnp.einsum("hcr,chd->rhd", weights, attn_grad, preferred_element_type=jnp.float32)
    weight_grad = jnp.einsum(
        "chd,rhd->hcr", attn_grad, value_rows, preferred_element_type=jnp.float32
    )
    sigmoid = jax.nn.sigmoid(scores)
    score_grad = (
        weight_grad * usage_rows[None] * (sigmoid * (1.0 + scores * (1.0 - sigmoid))) * grad_scale
    ).astype(jnp.bfloat16)
    key_grad = jnp.einsum("hcr,chd->rhd", score_grad, queries, preferred_element_type=jnp.float32)
    contribution = jnp.concatenate(
        [key_grad.reshape(row_count, inner_width), value_grad.reshape(row_count, inner_width)],
        axis=1,
    ).astype(jnp.bfloat16)
    return (result, gated_out, contribution)


def on_device(
    candidates,
    cotangent,
    history,
    request_blocks,
    request_length,
    candidate_request,
    in_weight,
    out_weight,
):
    owned_rows = history.shape[0]
    pieces = [history]
    for offset in range(1, SPAN):
        pieces.append(shifted(history, "shard", -offset))
    window = jnp.concatenate(pieces, axis=0)
    usage = usage_mask(request_blocks, request_length, candidate_request)
    layer_out, gated_out, contribution = score_block(
        candidates, cotangent, window, usage, in_weight, out_weight
    )
    total_cands = candidates.shape[0] * lax.axis_size("dp") * lax.axis_size("shard")
    grad_scale = 1.0 / math.sqrt(total_cands)
    full_grad = (
        lax.dot_general(
            gated_out, cotangent, (((0,), (0,)), ((), ())), preferred_element_type=jnp.float32
        )
        * grad_scale
    )
    summed = lax.psum(full_grad, "dp")
    grad_rows = lax.psum_scatter(summed, "shard", scatter_dimension=0, tiled=True)
    accumulated = contribution[:owned_rows].astype(jnp.float32)
    for offset in range(1, SPAN):
        returned = shifted(
            contribution[offset * owned_rows : (offset + 1) * owned_rows], "shard", offset
        )
        accumulated = accumulated + returned.astype(jnp.float32)
    return (layer_out, grad_rows, accumulated.astype(jnp.bfloat16))


def solution(mesh):
    in_specs = (
        P(("dp", "shard"), None),
        P(("dp", "shard"), None),
        P(("dp", "shard"), None),
        P(("dp", "shard"), None),
        P(("dp", "shard")),
        P(("dp", "shard")),
        P(),
        P(),
    )
    out_specs = (P(("dp", "shard"), None), P("shard", None), P(("dp", "shard"), None))
    return jax.shard_map(
        on_device, mesh=mesh, in_specs=in_specs, out_specs=out_specs, check_vma=False
    )
```

profile of v0, /device:TPU:1, one launch (start us, length us, event | category | flops | bytes accessed | tf_op | source)
XLA Modules:
  0.0 814.8 jit_solution(10639494365713643479)
XLA Ops:
  8.5 14.1 %collective-permute-start = (bf16[128,1024]{0,1:T(8,128)(2,1)S(1)}, bf16[128,1024]{0,1:T(8,128)(2,1)S(1)}, u32[]{:S(2)}, u32[]{:S(2)}) collective-permute-start(bf16[128,1024]{0,1:T(8,128)(2,1)S(1)} %copy.42), channel_id=1, source_target_pairs={{1,0},{2,1},{3,2},{4,3},{5,4},{6,5},{7,6},{8,7},{9,8},{10,9},{11,1... | collective-permute-start | bytes 786440 | tf_op jit(solution)/shard_map/ppermute | solution.py:16
  22.6 2.4 collective-permute-start.1
  25.1 3.0 collective-permute-start.2
  28.0 2.6 collective-permute-start.3
  30.7 4.4 collective-permute-start.4
  41.0 5.2 collective-permute-start.5
  46.4 1.9 collective-permute-start.6
  50.1 17.6 %collective-permute-done.4 = bf16[128,1024]{0,1:T(8,128)(2,1)S(1)} collective-permute-done((bf16[128,1024]{0,1:T(8,128)(2,1)S(1)}, bf16[128,1024]{0,1:T(8,128)(2,1)S(1)}, u32[]{:S(2)}, u32[]{:S(2)}) %collective-permute-start.4) | collective-permute-done | bytes 262176 | tf_op jit(solution)/shard_map/ppermute | solution.py:16
  67.9 5.7 collective-permute-done.5
  73.6 8.3 %collective-permute-done.6 = bf16[128,1024]{0,1:T(8,128)(2,1)S(1)} collective-permute-done((bf16[128,1024]{0,1:T(8,128)(2,1)S(1)}, bf16[128,1024]{0,1:T(8,128)(2,1)S(1)}, u32[]{:S(2)}, u32[]{:S(2)}) %collective-permute-start.6) | collective-permute-done | bytes 262176 | tf_op jit(solution)/shard_map/ppermute | solution.py:16
  82.3 3.2 multiply_convert_fusion.1
  87.7 1.9 convolution_multiply_fusion
  89.7 2.3 fusion.44
  95.2 5.9 fusion.1
  101.1 2.3 copy.52
  105.0 1.9 collective-permute-start.10
  106.9 1.9 collective-permute-start.11
  110.8 4.9 collective-permute-start.13
  117.6 7.0 collective-permute-start.8
  124.6 2.1 collective-permute-start.9
  128.0 9.5 %collective-permute-done.13 = bf16[128,1024]{1,0:T(8,128)(2,1)S(1)} collective-permute-done((bf16[128,1024]{1,0:T(8,128)(2,1)S(1)}, bf16[128,1024]{1,0:T(8,128)(2,1)S(1)}, u32[]{:S(2)}, u32[]{:S(2)}) %collective-permute-start.13) | collective-permute-done | bytes 262176 | tf_op jit(solution)/shard_map/ppermute | solution.py:16
  137.5 7.3 collective-permute-done.7
  145.8 629.0 %reduce-scatter.2.cloned.1.call-done = f32[8,1024]{1,0:T(8,128)} async-done(((f32[512,1024]{1,0:T(8,128)}), f32[8,1024]{1,0:T(8,128)}) %reduce-scatter.2.cloned.1.call-update) | async-done | bytes 32784 | tf_op jit(solution)/shard_map/reduce_scatter | solution.py:124
  774.9 33.1 %psum.8 = f32[8,1024]{1,0:T(8,128)} all-reduce(f32[8,1024]{1,0:T(8,128)} %reduce-scatter.2.cloned.1.call-done), channel_id=1, replica_groups=mesh['dp'=8,'shard'=64] {'dp'}, use_global_device_ids=true, to_apply=%region_5.6 | all-reduce | flops 8192 | bytes 65536 | tf_op jit(solution)/shard_map/psum | solution.py:123
  (74 shorter events, 22.7 us)
Async XLA Ops:
  7.2 31.2 %copy-start = (bf16[1024,1024]{1,0:T(8,128)(2,1)S(1)}, bf16[1024,1024]{1,0:T(8,128)(2,1)}, u32[]{:S(2)}) copy-start(bf16[1024,1024]{1,0:T(8,128)(2,1)} %param.14) | copy-start | bytes 6291460
  7.2 767.7 %reduce-scatter.2.cloned.1.call-start = ((), (), s32[]{:S(2)}) async-start(), calls=%async_computation.1 | async-start | bytes 2129920 | tf_op jit(solution)/shard_map/reduce_scatter | solution.py:124
  8.5 32.5 %collective-permute-start = (bf16[128,1024]{0,1:T(8,128)(2,1)S(1)}, bf16[128,1024]{0,1:T(8,128)(2,1)S(1)}, u32[]{:S(2)}, u32[]{:S(2)}) collective-permute-start(bf16[128,1024]{0,1:T(8,128)(2,1)S(1)} %copy.42), channel_id=1, source_target_pairs={{1,0},{2,1},{3,2},{4,3},{5,4},{6,5},{7,6},{8,7},{9,8},{10,9},{11,1... | collective-permute-start | bytes 786440 | tf_op jit(solution)/shard_map/ppermute | solution.py:16
  22.6 23.7 %collective-permute-start.1 = (bf16[128,1024]{0,1:T(8,128)(2,1)S(1)}, bf16[128,1024]{0,1:T(8,128)(2,1)S(1)}, u32[]{:S(2)}, u32[]{:S(2)}) collective-permute-start(bf16[128,1024]{0,1:T(8,128)(2,1)S(1)} %copy.42), channel_id=1, source_target_pairs={{2,0},{3,1},{4,2},{5,3},{6,4},{7,5},{8,6},{9,7},{10,8},{11,9},{12,... | collective-permute-start | bytes 786440 | tf_op jit(solution)/shard_map/ppermute | solution.py:16
  25.1 23.3 %collective-permute-start.2 = (bf16[128,1024]{0,1:T(8,128)(2,1)S(1)}, bf16[128,1024]{0,1:T(8,128)(2,1)S(1)}, u32[]{:S(2)}, u32[]{:S(2)}) collective-permute-start(bf16[128,1024]{0,1:T(8,128)(2,1)S(1)} %copy.42), channel_id=1, source_target_pairs={{3,0},{4,1},{5,2},{6,3},{7,4},{8,5},{9,6},{10,7},{11,8},{12,9},{13... | collective-permute-start | bytes 786440 | tf_op jit(solution)/shard_map/ppermute | solution.py:16
  28.0 22.0 %collective-permute-start.3 = (bf16[128,1024]{0,1:T(8,128)(2,1)S(1)}, bf16[128,1024]{0,1:T(8,128)(2,1)S(1)}, u32[]{:S(2)}, u32[]{:S(2)}) collective-permute-start(bf16[128,1024]{0,1:T(8,128)(2,1)S(1)} %copy.42), channel_id=1, source_target_pairs={{4,0},{5,1},{6,2},{7,3},{8,4},{9,5},{10,6},{11,7},{12,8},{13,9},{1... | collective-permute-start | bytes 786440 | tf_op jit(solution)/shard_map/ppermute | solution.py:16
  30.7 37.1 %collective-permute-start.4 = (bf16[128,1024]{0,1:T(8,128)(2,1)S(1)}, bf16[128,1024]{0,1:T(8,128)(2,1)S(1)}, u32[]{:S(2)}, u32[]{:S(2)}) collective-permute-start(bf16[128,1024]{0,1:T(8,128)(2,1)S(1)} %copy.42), channel_id=1, source_target_pairs={{5,0},{6,1},{7,2},{8,3},{9,4},{10,5},{11,6},{12,7},{13,8},{14,9},{... | collective-permute-start | bytes 786440 | tf_op jit(solution)/shard_map/ppermute | solution.py:16
  40.1 47.6 %copy-start.13 = (f32[224,1024]{1,0:T(8,128)}, f32[224,1024]{1,0:T(8,128)S(1)}, u32[]{:S(2)}) copy-start(f32[224,1024]{1,0:T(8,128)S(1)} %fusion.7) | copy-start | bytes 2752516
  41.0 41.2 %copy-start.8 = (f32[28,8,8,128]{3,1,2,0:T(8,128)}, f32[28,8,8,128]{3,1,2,0:T(8,128)S(1)}, u32[]{:S(2)}) copy-start(f32[28,8,8,128]{3,1,2,0:T(8,128)S(1)} %copy.93) | copy-start | bytes 2752516
  41.0 32.5 %collective-permute-start.5 = (bf16[128,1024]{0,1:T(8,128)(2,1)S(1)}, bf16[128,1024]{0,1:T(8,128)(2,1)S(1)}, u32[]{:S(2)}, u32[]{:S(2)}) collective-permute-start(bf16[128,1024]{0,1:T(8,128)(2,1)S(1)} %copy.42), channel_id=1, source_target_pairs={{6,0},{7,1},{8,2},{9,3},{10,4},{11,5},{12,6},{13,7},{14,8},{15,9},... | collective-permute-start | bytes 786440 | tf_op jit(solution)/shard_map/ppermute | solution.py:16
  46.4 35.6 %collective-permute-start.6 = (bf16[128,1024]{0,1:T(8,128)(2,1)S(1)}, bf16[128,1024]{0,1:T(8,128)(2,1)S(1)}, u32[]{:S(2)}, u32[]{:S(2)}) collective-permute-start(bf16[128,1024]{0,1:T(8,128)(2,1)S(1)} %copy.42), channel_id=1, source_target_pairs={{7,0},{8,1},{9,2},{10,3},{11,4},{12,5},{13,6},{14,7},{15,8},{16,9}... | collective-permute-start | bytes 786440 | tf_op jit(solution)/shard_map/ppermute | solution.py:16
  87.4 4.5 copy-start.5
  103.4 23.3 %copy-start.6 = (f32[4,128,224]{1,2,0:T(8,128)S(1)}, f32[4,128,224]{1,2,0:T(8,128)}, u32[]{:S(2)}) copy-start(f32[4,128,224]{1,2,0:T(8,128)} %copy-done.5) | copy-start | bytes 1376260
  103.4 23.4 %copy-start.7 = (bf16[224,1024]{1,0:T(8,128)(2,1)S(1)}, bf16[224,1024]{1,0:T(8,128)(2,1)}, u32[]{:S(2)}) copy-start(bf16[224,1024]{1,0:T(8,128)(2,1)} %param.8) | copy-start | bytes 1376260
  103.4 23.4 %copy-start.11 = (bf16[512,1024]{1,0:T(8,128)(2,1)S(1)}, bf16[512,1024]{1,0:T(8,128)(2,1)}, u32[]{:S(2)}) copy-start(bf16[512,1024]{1,0:T(8,128)(2,1)} %param.15) | copy-start | bytes 3145732
  103.4 23.4 %copy-start.14 = (f32[224,1024]{1,0:T(8,128)S(1)}, f32[224,1024]{1,0:T(8,128)}, u32[]{:S(2)}) copy-start(f32[224,1024]{1,0:T(8,128)} %copy-done.13) | copy-start | bytes 2752516
  105.0 12.6 %collective-permute-start.10 = (bf16[128,1024]{1,0:T(8,128)(2,1)S(1)}, bf16[128,1024]{1,0:T(8,128)(2,1)S(1)}, u32[]{:S(2)}, u32[]{:S(2)}) collective-permute-start(bf16[128,1024]{1,0:T(8,128)(2,1)S(1)} %get-tuple-element.8), channel_id=1, source_target_pairs={{60,0},{61,1},{62,2},{63,3},{0,4},{1,5},{2,6},{3,7},{4,8},{5,9},{6... | collective-permute-start | bytes 786440 | tf_op jit(solution)/shard_map/ppermute | solution.py:16
  106.9 17.7 %collective-permute-start.11 = (bf16[128,1024]{1,0:T(8,128)(2,1)S(1)}, bf16[128,1024]{1,0:T(8,128)(2,1)S(1)}, u32[]{:S(2)}, u32[]{:S(2)}) collective-permute-start(bf16[128,1024]{1,0:T(8,128)(2,1)S(1)} %get-tuple-element.9), channel_id=1, source_target_pairs={{59,0},{60,1},{61,2},{62,3},{63,4},{0,5},{1,6},{2,7},{3,8},{4,9},{... | collective-permute-start | bytes 786440 | tf_op jit(solution)/shard_map/ppermute | solution.py:16
  108.9 19.2 %collective-permute-start.12 = (bf16[128,1024]{1,0:T(8,128)(2,1)S(1)}, bf16[128,1024]{1,0:T(8,128)(2,1)S(1)}, u32[]{:S(2)}, u32[]{:S(2)}) collective-permute-start(bf16[128,1024]{1,0:T(8,128)(2,1)S(1)} %get-tuple-element.11), channel_id=1, source_target_pairs={{58,0},{59,1},{60,2},{61,3},{62,4},{63,5},{0,6},{1,7},{2,8},{3,9},... | collective-permute-start | bytes 786440 | tf_op jit(solution)/shard_map/ppermute | solution.py:16
  110.8 26.7 %collective-permute-start.13 = (bf16[128,1024]{1,0:T(8,128)(2,1)S(1)}, bf16[128,1024]{1,0:T(8,128)(2,1)S(1)}, u32[]{:S(2)}, u32[]{:S(2)}) collective-permute-start(bf16[128,1024]{1,0:T(8,128)(2,1)S(1)} %get-tuple-element.10), channel_id=1, source_target_pairs={{57,0},{58,1},{59,2},{60,3},{61,4},{62,5},{63,6},{0,7},{1,8},{2,9}... | collective-permute-start | bytes 786440 | tf_op jit(solution)/shard_map/ppermute | solution.py:16
  115.7 29.1 %collective-permute-start.7 = (bf16[128,1024]{1,0:T(8,128)(2,1)S(1)}, bf16[128,1024]{1,0:T(8,128)(2,1)S(1)}, u32[]{:S(2)}, u32[]{:S(2)}) collective-permute-start(bf16[128,1024]{1,0:T(8,128)(2,1)S(1)} %get-tuple-element.5), channel_id=1, source_target_pairs={{63,0},{0,1},{1,2},{2,3},{3,4},{4,5},{5,6},{6,7},{7,8},{8,9},{9,10... | collective-permute-start | bytes 786440 | tf_op jit(solution)/shard_map/ppermute | solution.py:16
  117.6 27.2 %collective-permute-start.8 = (bf16[128,1024]{1,0:T(8,128)(2,1)S(1)}, bf16[128,1024]{1,0:T(8,128)(2,1)S(1)}, u32[]{:S(2)}, u32[]{:S(2)}) collective-permute-start(bf16[128,1024]{1,0:T(8,128)(2,1)S(1)} %get-tuple-element.6), channel_id=1, source_target_pairs={{62,0},{63,1},{0,2},{1,3},{2,4},{3,5},{4,6},{5,7},{6,8},{7,9},{8,1... | collective-permute-start | bytes 786440 | tf_op jit(solution)/shard_map/ppermute | solution.py:16
  124.6 20.2 %copy-start.1 = (bf16[1024,512]{1,0:T(8,128)(2,1)S(1)}, bf16[1024,512]{1,0:T(8,128)(2,1)}, u32[]{:S(2)}) copy-start(bf16[1024,512]{1,0:T(8,128)(2,1)} %copy.52) | copy-start | bytes 3145732
  124.6 20.2 %collective-permute-start.9 = (bf16[128,1024]{1,0:T(8,128)(2,1)S(1)}, bf16[128,1024]{1,0:T(8,128)(2,1)S(1)}, u32[]{:S(2)}, u32[]{:S(2)}) collective-permute-start(bf16[128,1024]{1,0:T(8,128)(2,1)S(1)} %get-tuple-element.7), channel_id=1, source_target_pairs={{61,0},{62,1},{63,2},{0,3},{1,4},{2,5},{3,6},{4,7},{5,8},{6,9},{7,... | collective-permute-start | bytes 786440 | tf_op jit(solution)/shard_map/ppermute | solution.py:16
  (6 other events, 14.3 us)
Sparse Core Ops, SparseCore 0:
  89.8 685.0 reduce-scatter.1
where the time goes:
time: 817 us; the launch traced here: 815 us
  waiting for transfers between devices  679 us (83%)
  starting transfers between devices  55.4 us (7%)
  blocking collectives  33.1 us (4%)
  matrix products  18.9 us (2%)
  between operations  14.5 us (2%)
    reduce_scatter x1, waiting for transfers between devices, on_device(): lax.psum_scatter(summed, 'shard', scatter_dimension=0, tiled=True)  629 us
    ppermute x14, starting transfers between devices, shifted(): return lax.ppermute(block, axis, route)  55.4 us
    ppermute x14, waiting for transfers between devices, shifted(): return lax.ppermute(block, axis, route)  50 us
    psum x1, blocking collectives, on_device(): summed = lax.psum(full_grad, 'dp')  33.1 us
  transfers between devices with their start and end apart: 15, of which 7 were waited for; matrix products, arithmetic and copies ran while one was open for 3% of the time, Pallas kernels for 0%

commit v1 on v0

--- a/solution.py
+++ b/solution.py
@@ -3,17 +3,48 @@
 import jax
 import jax.numpy as jnp
 from jax import lax
-from jax.sharding import PartitionSpec as P
+from jax.sharding import Mesh, PartitionSpec as P
 
 HEADS = 4
 BLK = 128
 SPAN = 8
 
 
+SHARD = ("z", "x")
+
+
 def shifted(block, axis, distance):
     devices = range(lax.axis_size(axis))
     route = [((i - distance) % len(devices), i) for i in devices]
     return lax.ppermute(block, axis, route)
+
+
+def exchanged(chunks, axis):
+    return lax.all_to_all(chunks, axis, 0, 0, tiled=True)
+
+
+def summed_over(chunks, axis, kind):
+    arrived = exchanged(chunks.astype(kind), axis)
+    return jnp.sum(arrived.astype(jnp.float32), axis=0)
+
+
+def spread_over(block, axis):
+    size = lax.axis_size(axis)
+    return exchanged(jnp.broadcast_to(block[None], (size,) + block.shape), axis)
+
+
+def summed_rows(full_grad):
+    ys, cores, zs, xs = (lax.axis_size(name) for name in ("y", "core", "z", "x"))
+    rows, cols = full_grad.shape
+    piece = (rows // (zs * xs), cols // (ys * cores))
+    chunks = full_grad.reshape(zs, xs, piece[0], cores, ys, piece[1])
+    chunks = chunks.transpose(3, 4, 1, 0, 2, 5)
+    part = summed_over(chunks, "core", jnp.bfloat16)
+    part = summed_over(part, "y", jnp.bfloat16)
+    part = summed_over(part, "x", jnp.float32)
+    part = summed_over(part, "z", jnp.float32)
+    wide = spread_over(spread_over(part, "y"), "core")
+    return wide.transpose(2, 0, 1, 3).reshape(piece[0], cols)
 
 
 def layer_norm(values):
@@ -106,13 +137,13 @@
     owned_rows = history.shape[0]
     pieces = [history]
     for offset in range(1, SPAN):
-        pieces.append(shifted(history, "shard", -offset))
+        pieces.append(shifted(history, SHARD, -offset))
     window = jnp.concatenate(pieces, axis=0)
     usage = usage_mask(request_blocks, request_length, candidate_request)
     layer_out, gated_out, contribution = score_block(
         candidates, cotangent, window, usage, in_weight, out_weight
     )
-    total_cands = candidates.shape[0] * lax.axis_size("dp") * lax.axis_size("shard")
+    total_cands = candidates.shape[0] * lax.axis_size(("y", "core", "z", "x"))
     grad_scale = 1.0 / math.sqrt(total_cands)
     full_grad = (
         lax.dot_general(
@@ -120,29 +151,23 @@
         )
         * grad_scale
     )
-    summed = lax.psum(full_grad, "dp")
-    grad_rows = lax.psum_scatter(summed, "shard", scatter_dimension=0, tiled=True)
+    grad_rows = summed_rows(full_grad)
     accumulated = contribution[:owned_rows].astype(jnp.float32)
     for offset in range(1, SPAN):
         returned = shifted(
-            contribution[offset * owned_rows : (offset + 1) * owned_rows], "shard", offset
+            contribution[offset * owned_rows : (offset + 1) * owned_rows], SHARD, offset
         )
         accumulated = accumulated + returned.astype(jnp.float32)
     return (layer_out, grad_rows, accumulated.astype(jnp.bfloat16))
 
 
 def solution(mesh):
-    in_specs = (
-        P(("dp", "shard"), None),
-        P(("dp", "shard"), None),
-        P(("dp", "shard"), None),
-        P(("dp", "shard"), None),
-        P(("dp", "shard")),
-        P(("dp", "shard")),
-        P(),
-        P(),
+    inner = Mesh(mesh.devices.reshape(4, 2, 16, 4), ("y", "core", "z", "x"))
+    rows = P(("y", "core", "z", "x"))
+    return jax.shard_map(
+        on_device,
+        mesh=inner,
+        in_specs=(rows, rows, rows, rows, rows, rows, P(), P()),
+        out_specs=(rows, P(SHARD), rows),
+        check_vma=False,
     )
-    out_specs = (P(("dp", "shard"), None), P("shard", None), P(("dp", "shard"), None))
-    return jax.shard_map(
-        on_device, mesh=mesh, in_specs=in_specs, out_specs=out_specs, check_vma=False
-    )

time: 817 us -> 183 us (0.22)
  the two profiles are of different devices: /device:TPU:1 before, /device:TPU:7 now
where the time goes in v1:
time: 183 us; the launch traced here: 182 us
  starting transfers between devices  98 us (54%)
  waiting for transfers between devices  24.9 us (14%)
  matrix products  19.3 us (11%)
  blocking collectives  14.8 us (8%)
  other arithmetic  12.7 us (7%)
  local copies, waits for them, and re-layouts  11.1 us (6%)
    ppermute x14, starting transfers between devices, shifted(): return lax.ppermute(block, axis, route)  68.3 us
    all_to_all x4, starting transfers between devices, exchanged(): return lax.all_to_all(chunks, axis, 0, 0, tiled=True)  29.8 us
    all_to_all x2, blocking collectives, exchanged(): return lax.all_to_all(chunks, axis, 0, 0, tiled=True)  14.8 us
    all_to_all x4, waiting for transfers between devices, exchanged(): return lax.all_to_all(chunks, axis, 0, 0, tiled=True)  12.9 us
    ppermute x14, waiting for transfers between devices, shifted(): return lax.ppermute(block, axis, route)  12 us
    dot_general x1, matrix products, score_block(): jnp.einsum('hcr,chd->rhd', score_grad, queries, preferred_element_type=jn...  5.63 us
  transfers between devices with their start and end apart: 18, of which 5 were waited for; matrix products, arithmetic and copies ran while one was open for 17% of the time, Pallas kernels for 0%

profile of v1, /device:TPU:7, one launch (start us, length us, event | category | flops | bytes accessed | tf_op | source)
XLA Modules:
  0.0 182.0 jit_solution(869324925091200408)
XLA Ops:
  6.9 12.9 %collective-permute-start.2 = (bf16[128,1024]{0,1:T(8,128)(2,1)S(1)}, bf16[128,1024]{0,1:T(8,128)(2,1)S(1)}, u32[]{:S(2)}, u32[]{:S(2)}) collective-permute-start(bf16[128,1024]{0,1:T(8,128)(2,1)S(1)} %copy.110), channel_id=1, source_target_pairs={{3,0},{4,1},{5,2},{6,3},{7,4},{8,5},{9,6},{10,7},{11,8},{12,9},{13... | collective-permute-start | bytes 786440 | tf_op jit(solution)/shard_map/ppermute | solution.py:19
  19.8 2.6 %collective-permute-start.3 = (bf16[128,1024]{0,1:T(8,128)(2,1)S(1)}, bf16[128,1024]{0,1:T(8,128)(2,1)S(1)}, u32[]{:S(2)}, u32[]{:S(2)}) collective-permute-start(bf16[128,1024]{0,1:T(8,128)(2,1)S(1)} %copy.110), channel_id=1, source_target_pairs={{4,0},{5,1},{6,2},{7,3},{8,4},{9,5},{10,6},{11,7},{12,8},{13,9},{1... | collective-permute-start | bytes 786440 | tf_op jit(solution)/shard_map/ppermute | solution.py:19
  30.8 5.7 %collective-permute-start.5 = (bf16[128,1024]{0,1:T(8,128)(2,1)S(1)}, bf16[128,1024]{0,1:T(8,128)(2,1)S(1)}, u32[]{:S(2)}, u32[]{:S(2)}) collective-permute-start(bf16[128,1024]{0,1:T(8,128)(2,1)S(1)} %copy.110), channel_id=1, source_target_pairs={{6,0},{7,1},{8,2},{9,3},{10,4},{11,5},{12,6},{13,7},{14,8},{15,9},... | collective-permute-start | bytes 786440 | tf_op jit(solution)/shard_map/ppermute | solution.py:19
  36.6 4.9 %collective-permute-start.6 = (bf16[128,1024]{0,1:T(8,128)(2,1)S(1)}, bf16[128,1024]{0,1:T(8,128)(2,1)S(1)}, u32[]{:S(2)}, u32[]{:S(2)}) collective-permute-start(bf16[128,1024]{0,1:T(8,128)(2,1)S(1)} %copy.110), channel_id=1, source_target_pairs={{7,0},{8,1},{9,2},{10,3},{11,4},{12,5},{13,6},{14,7},{15,8},{16,9}... | collective-permute-start | bytes 786440 | tf_op jit(solution)/shard_map/ppermute | solution.py:19
  42.3 3.7 %collective-permute-done.5 = bf16[128,1024]{0,1:T(8,128)(2,1)S(1)} collective-permute-done((bf16[128,1024]{0,1:T(8,128)(2,1)S(1)}, bf16[128,1024]{0,1:T(8,128)(2,1)S(1)}, u32[]{:S(2)}, u32[]{:S(2)}) %collective-permute-start.5) | collective-permute-done | bytes 262176 | tf_op jit(solution)/shard_map/ppermute | solution.py:19
  46.1 7.9 %collective-permute-done.6 = bf16[128,1024]{0,1:T(8,128)(2,1)S(1)} collective-permute-done((bf16[128,1024]{0,1:T(8,128)(2,1)S(1)}, bf16[128,1024]{0,1:T(8,128)(2,1)S(1)}, u32[]{:S(2)}, u32[]{:S(2)}) %collective-permute-start.6) | collective-permute-done | bytes 262176 | tf_op jit(solution)/shard_map/ppermute | solution.py:19
  54.3 3.2 %multiply_convert_fusion.1 = (bf16[4,224,1024]{2,1,0:T(8,128)(2,1)S(1)}, f32[4,224,1024]{2,1,0:T(8,128)}) fusion(f32[224,1024]{1,0:T(8,128)S(1)} %bitcast.90, bf16[1024,4,128]{0,2,1:T(8,128)(2,1)S(1)} %bitcast.89, f32[224,1024]{1,0:T(8,128)S(1)} %fusion.7), kind=kOutput, calls=%fused_computation.15 | convolution fusion | flops 241303552 | bytes 7700480 | tf_op jit(solution)/shard_map/chd,rhd->hcr/dot_general | solution.py:88
  61.1 6.4 %all_to_all.30 = bf16[2,4,4,16,8,128]{5,4,1,2,3,0:T(8,128)(2,1)S(1)} all-to-all(bf16[2,4,4,16,8,128]{5,4,1,2,3,0:T(8,128)(2,1)S(1)} %bitcast.83), channel_id=1, replica_groups=mesh['y'=4,'core'=2,'z'=16,'x'=4] {'core'}, dimensions={0} | all-to-all | bytes 2097152 | tf_op jit(solution)/shard_map/all_to_all | solution.py:23
  70.7 4.2 %all-to-all-start.1 = ((bf16[4,4,16,8,128]{4,3,1,2,0:T(8,128)(2,1)}), bf16[4,4,16,8,128]{4,3,1,2,0:T(8,128)(2,1)}, u32[]{:S(2)}, u32[]{:S(2)}) async-start(bf16[4,4,16,8,128]{4,3,1,2,0:T(8,128)(2,1)} %copy.118), calls=%async_computation.1 | async-start | bytes 1048576 | tf_op jit(solution)/shard_map/all_to_all | solution.py:23
  76.3 5.6 %fusion.1 = bf16[4,128,1024]{2,1,0:T(8,128)(2,1)} fusion(f32[4,224,1024]{2,1,0:T(8,128)} %get-tuple-element.15, bf16[1024,4,128]{0,2,1:T(8,128)(2,1)S(1)} %bitcast.85, f32[224,1024]{1,0:T(8,128)} %bitcast.91, bf16[28,4,8,128]{3,2,1,0:T(8,128)(2,1)S(1)} %fusion.21, f32[224,1024]{1,0:T(8,128)} %copy-done.10), kind=kOutput, calls=%fused_computation.20 | convolution fusion | flops 481296384 | bytes 7143424 | tf_op jit(solution)/shard_map/hcr,chd->rhd/dot_general | solution.py:119
  81.9 3.0 %convolution_convert_fusion = bf16[4,128,1024]{2,1,0:T(8,128)(2,1)} fusion(bf16[4,224,1024]{2,1,0:T(8,128)(2,1)} %copy-done.1, bf16[28,4,8,128]{3,2,1,0:T(8,128)(2,1)S(1)} %fusion.21), kind=kOutput, calls=%fused_computation.19 | convolution fusion | flops 235405312 | bytes 3112960 | tf_op jit(solution)/shard_map/hcr,chd->rhd/dot_general | solution.py:111
  91.2 6.0 %collective-permute-start.10 = (bf16[128,1024]{1,0:T(8,128)(2,1)}, bf16[128,1024]{1,0:T(8,128)(2,1)}, u32[]{:S(2)}, u32[]{:S(2)}) collective-permute-start(bf16[128,1024]{1,0:T(8,128)(2,1)} %get-tuple-element.8), channel_id=1, source_target_pairs={{60,0},{61,1},{62,2},{63,3},{0,4},{1,5},{2,6},{3,7},{4,8},{5,9},{6... | collective-permute-start | bytes 786440 | tf_op jit(solution)/shard_map/ppermute | solution.py:19
  97.1 9.5 %collective-permute-start.11 = (bf16[128,1024]{1,0:T(8,128)(2,1)}, bf16[128,1024]{1,0:T(8,128)(2,1)}, u32[]{:S(2)}, u32[]{:S(2)}) collective-permute-start(bf16[128,1024]{1,0:T(8,128)(2,1)} %get-tuple-element.9), channel_id=1, source_target_pairs={{59,0},{60,1},{61,2},{62,3},{63,4},{0,5},{1,6},{2,7},{3,8},{4,9},{... | collective-permute-start | bytes 786440 | tf_op jit(solution)/shard_map/ppermute | solution.py:19
  108.5 11.9 %all-to-all-start.2 = ((f32[4,16,8,128]{3,2,1,0:T(8,128)}), f32[4,16,8,128]{3,2,1,0:T(8,128)S(1)}, u32[]{:S(2)}, u32[]{:S(2)}) async-start(f32[4,16,8,128]{3,2,1,0:T(8,128)} %copy.120), calls=%async_computation.2 | async-start | bytes 524288 | tf_op jit(solution)/shard_map/all_to_all | solution.py:23
  120.4 3.6 %collective-permute-start.12 = (bf16[128,1024]{1,0:T(8,128)(2,1)}, bf16[128,1024]{1,0:T(8,128)(2,1)}, u32[]{:S(2)}, u32[]{:S(2)}) collective-permute-start(bf16[128,1024]{1,0:T(8,128)(2,1)} %get-tuple-element.11), channel_id=1, source_target_pairs={{58,0},{59,1},{60,2},{61,3},{62,4},{63,5},{0,6},{1,7},{2,8},{3,9},... | collective-permute-start | bytes 786440 | tf_op jit(solution)/shard_map/ppermute | solution.py:19
  124.1 4.4 %collective-permute-start.13 = (bf16[128,1024]{1,0:T(8,128)(2,1)}, bf16[128,1024]{1,0:T(8,128)(2,1)}, u32[]{:S(2)}, u32[]{:S(2)}) collective-permute-start(bf16[128,1024]{1,0:T(8,128)(2,1)} %get-tuple-element.10), channel_id=1, source_target_pairs={{57,0},{58,1},{59,2},{60,3},{61,4},{62,5},{63,6},{0,7},{1,8},{2,9}... | collective-permute-start | bytes 786440 | tf_op jit(solution)/shard_map/ppermute | solution.py:19
  128.5 5.1 %collective-permute-start.7 = (bf16[128,1024]{1,0:T(8,128)(2,1)}, bf16[128,1024]{1,0:T(8,128)(2,1)}, u32[]{:S(2)}, u32[]{:S(2)}) collective-permute-start(bf16[128,1024]{1,0:T(8,128)(2,1)} %get-tuple-element.5), channel_id=1, source_target_pairs={{63,0},{0,1},{1,2},{2,3},{3,4},{4,5},{5,6},{6,7},{7,8},{8,9},{9,10... | collective-permute-start | bytes 786440 | tf_op jit(solution)/shard_map/ppermute | solution.py:19
  134.3 10.2 %all-to-all-start.3 = ((f32[16,8,128]{2,1,0:T(8,128)}), f32[16,8,128]{2,1,0:T(8,128)S(1)}, u32[]{:S(2)}, u32[]{:S(2)}) async-start(f32[16,8,128]{2,1,0:T(8,128)} %reduce_sum.109), calls=%async_computation.3 | async-start | bytes 131072 | tf_op jit(solution)/shard_map/all_to_all | solution.py:23
  144.5 2.7 %collective-permute-start.8 = (bf16[128,1024]{1,0:T(8,128)(2,1)}, bf16[128,1024]{1,0:T(8,128)(2,1)S(1)}, u32[]{:S(2)}, u32[]{:S(2)}) collective-permute-start(bf16[128,1024]{1,0:T(8,128)(2,1)} %get-tuple-element.6), channel_id=1, source_target_pairs={{62,0},{63,1},{0,2},{1,3},{2,4},{3,5},{4,6},{5,7},{6,8},{7,9},{8,1... | collective-permute-start | bytes 786440 | tf_op jit(solution)/shard_map/ppermute | solution.py:19
  147.2 3.4 %collective-permute-start.9 = (bf16[128,1024]{1,0:T(8,128)(2,1)}, bf16[128,1024]{1,0:T(8,128)(2,1)}, u32[]{:S(2)}, u32[]{:S(2)}) collective-permute-start(bf16[128,1024]{1,0:T(8,128)(2,1)} %get-tuple-element.7), channel_id=1, source_target_pairs={{61,0},{62,1},{63,2},{0,3},{1,4},{2,5},{3,6},{4,7},{5,8},{6,9},{7,... | collective-permute-start | bytes 786440 | tf_op jit(solution)/shard_map/ppermute | solution.py:19
  150.6 2.9 %fusion.2 = bf16[224,1024]{1,0:T(8,128)(2,1)} fusion(bf16[512,1024]{1,0:T(8,128)(2,1)} %param.15, bf16[224,1024]{1,0:T(8,128)(2,1)} %param.8, f32[224]{0:T(256)S(1)} %add_rsqrt_fusion, f32[224]{0:T(256)S(1)} %broadcast_multiply_fusion.2, f32[224,1024]{1,0:T(8,128)} %copy-done.10, f32[4,128,224]{1,2,0:T(8,128)} %copy-done.4), kind=kOutput, calls=%fused_computation.24 | convolution fusion | flops 236486656 | bytes 2885376 | tf_op jit(solution)/shard_map/dot_general | solution.py:99
  153.5 11.2 %all-to-all-done.3 = f32[16,8,128]{2,1,0:T(8,128)S(1)} async-done(((f32[16,8,128]{2,1,0:T(8,128)}), f32[16,8,128]{2,1,0:T(8,128)S(1)}, u32[]{:S(2)}, u32[]{:S(2)}) %all-to-all-start.3) | async-done | bytes 65568 | tf_op jit(solution)/shard_map/all_to_all | solution.py:23
  165.3 3.4 %all-to-all-start.4 = ((f32[4,8,128]{2,1,0:T(8,128)}), f32[4,8,128]{2,1,0:T(8,128)S(1)}, u32[]{:S(2)}, u32[]{:S(2)}) async-start(f32[4,8,128]{2,1,0:T(8,128)} %broadcast_in_dim.27), calls=%async_computation.4 | async-start | bytes 32768 | tf_op jit(solution)/shard_map/all_to_all | solution.py:23
  173.0 8.4 %all_to_all.31 = f32[2,4,8,128]{3,2,1,0:T(8,128)S(1)} all-to-all(f32[2,4,8,128]{3,2,1,0:T(8,128)S(1)} %broadcast_in_dim.28), channel_id=1, replica_groups=mesh['y'=4,'core'=2,'z'=16,'x'=4] {'core'}, dimensions={0} | all-to-all | bytes 65536 | tf_op jit(solution)/shard_map/all_to_all | solution.py:23
  (82 shorter events, 38.0 us)
Async XLA Ops:
  0.6 27.5 %copy-start = (bf16[1024,1024]{1,0:T(8,128)(2,1)S(1)}, bf16[1024,1024]{1,0:T(8,128)(2,1)}, u32[]{:S(2)}) copy-start(bf16[1024,1024]{1,0:T(8,128)(2,1)} %param.14) | copy-start | bytes 6291460
  1.9 28.9 %collective-permute-start = (bf16[128,1024]{0,1:T(8,128)(2,1)S(1)}, bf16[128,1024]{0,1:T(8,128)(2,1)S(1)}, u32[]{:S(2)}, u32[]{:S(2)}) collective-permute-start(bf16[128,1024]{0,1:T(8,128)(2,1)S(1)} %copy.110), channel_id=1, source_target_pairs={{1,0},{2,1},{3,2},{4,3},{5,4},{6,5},{7,6},{8,7},{9,8},{10,9},{11,1... | collective-permute-start | bytes 786440 | tf_op jit(solution)/shard_map/ppermute | solution.py:19
  4.4 32.2 %collective-permute-start.1 = (bf16[128,1024]{0,1:T(8,128)(2,1)S(1)}, bf16[128,1024]{0,1:T(8,128)(2,1)S(1)}, u32[]{:S(2)}, u32[]{:S(2)}) collective-permute-start(bf16[128,1024]{0,1:T(8,128)(2,1)S(1)} %copy.110), channel_id=1, source_target_pairs={{2,0},{3,1},{4,2},{5,3},{6,4},{7,5},{8,6},{9,7},{10,8},{11,9},{12,... | collective-permute-start | bytes 786440 | tf_op jit(solution)/shard_map/ppermute | solution.py:19
  6.9 34.8 %collective-permute-start.2 = (bf16[128,1024]{0,1:T(8,128)(2,1)S(1)}, bf16[128,1024]{0,1:T(8,128)(2,1)S(1)}, u32[]{:S(2)}, u32[]{:S(2)}) collective-permute-start(bf16[128,1024]{0,1:T(8,128)(2,1)S(1)} %copy.110), channel_id=1, source_target_pairs={{3,0},{4,1},{5,2},{6,3},{7,4},{8,5},{9,6},{10,7},{11,8},{12,9},{13... | collective-permute-start | bytes 786440 | tf_op jit(solution)/shard_map/ppermute | solution.py:19
  19.8 22.0 %collective-permute-start.3 = (bf16[128,1024]{0,1:T(8,128)(2,1)S(1)}, bf16[128,1024]{0,1:T(8,128)(2,1)S(1)}, u32[]{:S(2)}, u32[]{:S(2)}) collective-permute-start(bf16[128,1024]{0,1:T(8,128)(2,1)S(1)} %copy.110), channel_id=1, source_target_pairs={{4,0},{5,1},{6,2},{7,3},{8,4},{9,5},{10,6},{11,7},{12,8},{13,9},{1... | collective-permute-start | bytes 786440 | tf_op jit(solution)/shard_map/ppermute | solution.py:19
  22.4 19.8 %collective-permute-start.4 = (bf16[128,1024]{0,1:T(8,128)(2,1)S(1)}, bf16[128,1024]{0,1:T(8,128)(2,1)S(1)}, u32[]{:S(2)}, u32[]{:S(2)}) collective-permute-start(bf16[128,1024]{0,1:T(8,128)(2,1)S(1)} %copy.110), channel_id=1, source_target_pairs={{5,0},{6,1},{7,2},{8,3},{9,4},{10,5},{11,6},{12,7},{13,8},{14,9},{... | collective-permute-start | bytes 786440 | tf_op jit(solution)/shard_map/ppermute | solution.py:19
  27.3 2.6 %copy-start.6 = (s32[224]{0:T(256)S(1)}, s32[224]{0:T(256)}, u32[]{:S(2)}) copy-start(s32[224]{0:T(256)} %param.13) | copy-start | bytes 2692
  29.8 29.6 %copy-start.10 = (f32[224,1024]{1,0:T(8,128)}, f32[224,1024]{1,0:T(8,128)S(1)}, u32[]{:S(2)}) copy-start(f32[224,1024]{1,0:T(8,128)S(1)} %fusion.7) | copy-start | bytes 2752516
  30.8 23.5 %copy-start.5 = (f32[28,8,8,128]{3,1,2,0:T(8,128)}, f32[28,8,8,128]{3,1,2,0:T(8,128)S(1)}, u32[]{:S(2)}) copy-start(f32[28,8,8,128]{3,1,2,0:T(8,128)S(1)} %copy.170) | copy-start | bytes 2752516
  30.8 15.2 %collective-permute-start.5 = (bf16[128,1024]{0,1:T(8,128)(2,1)S(1)}, bf16[128,1024]{0,1:T(8,128)(2,1)S(1)}, u32[]{:S(2)}, u32[]{:S(2)}) collective-permute-start(bf16[128,1024]{0,1:T(8,128)(2,1)S(1)} %copy.110), channel_id=1, source_target_pairs={{6,0},{7,1},{8,2},{9,3},{10,4},{11,5},{12,6},{13,7},{14,8},{15,9},... | collective-permute-start | bytes 786440 | tf_op jit(solution)/shard_map/ppermute | solution.py:19
  36.6 17.4 %collective-permute-start.6 = (bf16[128,1024]{0,1:T(8,128)(2,1)S(1)}, bf16[128,1024]{0,1:T(8,128)(2,1)S(1)}, u32[]{:S(2)}, u32[]{:S(2)}) collective-permute-start(bf16[128,1024]{0,1:T(8,128)(2,1)S(1)} %copy.110), channel_id=1, source_target_pairs={{7,0},{8,1},{9,2},{10,3},{11,4},{12,5},{13,6},{14,7},{15,8},{16,9}... | collective-permute-start | bytes 786440 | tf_op jit(solution)/shard_map/ppermute | solution.py:19
  54.3 3.2 %copy-start.2 = (bf16[1024,512]{0,1:T(8,128)(2,1)}, bf16[1024,512]{0,1:T(8,128)(2,1)S(1)}, u32[]{:S(2)}) copy-start(bf16[1024,512]{0,1:T(8,128)(2,1)S(1)} %get-tuple-element.13) | copy-start | bytes 3145732
  68.7 7.6 %copy-start.3 = (bf16[1024,512]{0,1:T(8,128)(2,1)S(1)}, bf16[1024,512]{0,1:T(8,128)(2,1)}, u32[]{:S(2)}) copy-start(bf16[1024,512]{0,1:T(8,128)(2,1)} %copy-done.2) | copy-start | bytes 3145732
  70.7 35.9 %all-to-all-start.1 = ((bf16[4,4,16,8,128]{4,3,1,2,0:T(8,128)(2,1)}), bf16[4,4,16,8,128]{4,3,1,2,0:T(8,128)(2,1)}, u32[]{:S(2)}, u32[]{:S(2)}) async-start(bf16[4,4,16,8,128]{4,3,1,2,0:T(8,128)(2,1)} %copy.118), calls=%async_computation.1 | async-start | bytes 1048576 | tf_op jit(solution)/shard_map/all_to_all | solution.py:23
  91.2 53.4 %collective-permute-start.10 = (bf16[128,1024]{1,0:T(8,128)(2,1)}, bf16[128,1024]{1,0:T(8,128)(2,1)}, u32[]{:S(2)}, u32[]{:S(2)}) collective-permute-start(bf16[128,1024]{1,0:T(8,128)(2,1)} %get-tuple-element.8), channel_id=1, source_target_pairs={{60,0},{61,1},{62,2},{63,3},{0,4},{1,5},{2,6},{3,7},{4,8},{5,9},{6... | collective-permute-start | bytes 786440 | tf_op jit(solution)/shard_map/ppermute | solution.py:19
  97.1 50.1 %collective-permute-start.11 = (bf16[128,1024]{1,0:T(8,128)(2,1)}, bf16[128,1024]{1,0:T(8,128)(2,1)}, u32[]{:S(2)}, u32[]{:S(2)}) collective-permute-start(bf16[128,1024]{1,0:T(8,128)(2,1)} %get-tuple-element.9), channel_id=1, source_target_pairs={{59,0},{60,1},{61,2},{62,3},{63,4},{0,5},{1,6},{2,7},{3,8},{4,9},{... | collective-permute-start | bytes 786440 | tf_op jit(solution)/shard_map/ppermute | solution.py:19
  108.5 25.1 %all-to-all-start.2 = ((f32[4,16,8,128]{3,2,1,0:T(8,128)}), f32[4,16,8,128]{3,2,1,0:T(8,128)S(1)}, u32[]{:S(2)}, u32[]{:S(2)}) async-start(f32[4,16,8,128]{3,2,1,0:T(8,128)} %copy.120), calls=%async_computation.2 | async-start | bytes 524288 | tf_op jit(solution)/shard_map/all_to_all | solution.py:23
  120.4 48.3 %collective-permute-start.12 = (bf16[128,1024]{1,0:T(8,128)(2,1)}, bf16[128,1024]{1,0:T(8,128)(2,1)}, u32[]{:S(2)}, u32[]{:S(2)}) collective-permute-start(bf16[128,1024]{1,0:T(8,128)(2,1)} %get-tuple-element.11), channel_id=1, source_target_pairs={{58,0},{59,1},{60,2},{61,3},{62,4},{63,5},{0,6},{1,7},{2,8},{3,9},... | collective-permute-start | bytes 786440 | tf_op jit(solution)/shard_map/ppermute | solution.py:19
  124.1 44.7 %collective-permute-start.13 = (bf16[128,1024]{1,0:T(8,128)(2,1)}, bf16[128,1024]{1,0:T(8,128)(2,1)}, u32[]{:S(2)}, u32[]{:S(2)}) collective-permute-start(bf16[128,1024]{1,0:T(8,128)(2,1)} %get-tuple-element.10), channel_id=1, source_target_pairs={{57,0},{58,1},{59,2},{60,3},{61,4},{62,5},{63,6},{0,7},{1,8},{2,9}... | collective-permute-start | bytes 786440 | tf_op jit(solution)/shard_map/ppermute | solution.py:19
  128.5 40.3 %collective-permute-start.7 = (bf16[128,1024]{1,0:T(8,128)(2,1)}, bf16[128,1024]{1,0:T(8,128)(2,1)}, u32[]{:S(2)}, u32[]{:S(2)}) collective-permute-start(bf16[128,1024]{1,0:T(8,128)(2,1)} %get-tuple-element.5), channel_id=1, source_target_pairs={{63,0},{0,1},{1,2},{2,3},{3,4},{4,5},{5,6},{6,7},{7,8},{8,9},{9,10... | collective-permute-start | bytes 786440 | tf_op jit(solution)/shard_map/ppermute | solution.py:19
  134.3 30.4 %all-to-all-start.3 = ((f32[16,8,128]{2,1,0:T(8,128)}), f32[16,8,128]{2,1,0:T(8,128)S(1)}, u32[]{:S(2)}, u32[]{:S(2)}) async-start(f32[16,8,128]{2,1,0:T(8,128)} %reduce_sum.109), calls=%async_computation.3 | async-start | bytes 131072 | tf_op jit(solution)/shard_map/all_to_all | solution.py:23
  144.5 24.2 %collective-permute-start.8 = (bf16[128,1024]{1,0:T(8,128)(2,1)}, bf16[128,1024]{1,0:T(8,128)(2,1)S(1)}, u32[]{:S(2)}, u32[]{:S(2)}) collective-permute-start(bf16[128,1024]{1,0:T(8,128)(2,1)} %get-tuple-element.6), channel_id=1, source_target_pairs={{62,0},{63,1},{0,2},{1,3},{2,4},{3,5},{4,6},{5,7},{6,8},{7,9},{8,1... | collective-permute-start | bytes 786440 | tf_op jit(solution)/shard_map/ppermute | solution.py:19
  147.2 21.6 %collective-permute-start.9 = (bf16[128,1024]{1,0:T(8,128)(2,1)}, bf16[128,1024]{1,0:T(8,128)(2,1)}, u32[]{:S(2)}, u32[]{:S(2)}) collective-permute-start(bf16[128,1024]{1,0:T(8,128)(2,1)} %get-tuple-element.7), channel_id=1, source_target_pairs={{61,0},{62,1},{63,2},{0,3},{1,4},{2,5},{3,6},{4,7},{5,8},{6,9},{7,... | collective-permute-start | bytes 786440 | tf_op jit(solution)/shard_map/ppermute | solution.py:19
  165.3 7.7 %all-to-all-start.4 = ((f32[4,8,128]{2,1,0:T(8,128)}), f32[4,8,128]{2,1,0:T(8,128)S(1)}, u32[]{:S(2)}, u32[]{:S(2)}) async-start(f32[4,8,128]{2,1,0:T(8,128)} %broadcast_in_dim.27), calls=%async_computation.4 | async-start | bytes 32768 | tf_op jit(solution)/shard_map/all_to_all | solution.py:23
  (5 other events, 8.2 us)

commit v2 on v1

v2 whole, which is shorter than its diff:
```python
import math

import jax
import jax.numpy as jnp
from jax import lax
from jax.experimental import pallas as pl
from jax.experimental.pallas import tpu as pltpu
from jax.sharding import Mesh, PartitionSpec as P

HEADS = 4
SPAN = 8
BF16 = jnp.bfloat16
F32 = jnp.float32
ALL = ("y", "core", "zh", "zl", "x")
DEPTH = ("zh", "zl")
NT = (((1,), (1,)), ((), ()))
TN = (((0,), (0,)), ((), ()))


def on_core(kernel, outs, *operands):
    return pl.pallas_call(
        kernel,
        out_shape=outs,
        in_specs=[pl.BlockSpec(memory_space=pltpu.VMEM)] * len(operands),
        out_specs=jax.tree.map(lambda _: pl.BlockSpec(memory_space=pltpu.VMEM), outs),
        compiler_params=pltpu.CompilerParams(vmem_limit_bytes=40 * 1024 * 1024),
    )(*operands)


def shaped(shape, kind):
    return jax.ShapeDtypeStruct(shape, kind)


def sigmoid(values):
    return 0.5 + 0.5 * jnp.tanh(0.5 * values)


def served(ring, group):
    return {0: range(group, HEADS), 1: range(0, HEADS), 2: range(0, group)}[ring]


def prepare_kernel(cand_ref, cot_ref, in_ref, out_ref, bundle_ref):
    rows = cand_ref[...].astype(F32)
    centered = rows - jnp.mean(rows, axis=-1, keepdims=True)
    inv_scale = lax.rsqrt(jnp.mean(centered * centered, axis=-1, keepdims=True) + 1e-05)
    normed = (centered * inv_scale).astype(BF16)
    projected = jnp.dot(normed, in_ref[...], preferred_element_type=F32).T
    zed_grad = lax.dot_general(out_ref[...], cot_ref[...], NT, preferred_element_type=F32)
    inner = out_ref.shape[0]
    size = inner // HEADS
    for head in range(HEADS):
        part = slice(head * size, (head + 1) * size)
        gate_in = projected[inner + head * size : inner + (head + 1) * size]
        gating = gate_in * sigmoid(gate_in)
        bundle_ref[head, 0:size] = projected[part].astype(BF16)
        bundle_ref[head, size : 2 * size] = gating.astype(BF16)
        bundle_ref[head, 2 * size : 3 * size] = (zed_grad[part] * gating).astype(BF16)


def attend(ring, blocks_ref, bundle_ref, usage_ref, weight_ref, slope_ref, group):
    size = bundle_ref.shape[1] // 3
    span = served(ring, group)
    if len(span) == 0:
        return None
    first, count, tall = span[0], len(span), blocks_ref.shape[1]
    keys = blocks_ref[first : first + count, :, 0:size].reshape(count * tall, size)
    values = blocks_ref[first : first + count, :, size:].reshape(count * tall, size)
    scale = 1.0 / math.sqrt(size)
    scores = jnp.dot(keys, bundle_ref[group, 0:size], preferred_element_type=F32) * scale
    part = sigmoid(scores)
    weights = scores * part
    slopes = (part + weights * (1.0 - part)) * scale
    usage = usage_ref[group].astype(F32)
    kept = []
    for place, block in enumerate(span):
        position = HEADS * ring + block - group
        mask = usage[position : position + 1]
        lines = slice(place * tall, (place + 1) * tall)
        kept.append((weights[lines] * mask).astype(BF16))
        weight_ref[group, block] = kept[-1]
        slope_ref[group, block] = (slopes[lines] * mask).astype(BF16)
    return lax.dot_general(
        values, jnp.concatenate(kept, axis=0), TN, preferred_element_type=F32
    )


def early_kernel(*refs):
    ring0, ring1, bundle, usage, w0, s0, w1, s1, attended_ref = refs
    for group in range(HEADS):
        attended_ref[group] = attend(0, ring0, bundle, usage, w0, s0, group) + attend(
            1, ring1, bundle, usage, w1, s1, group
        )


def late_kernel(ring2, bundle, usage, before, w2, s2, attended_ref, stats_ref):
    size = bundle.shape[1] // 3
    for group in range(HEADS):
        attended = before[group]
        more = attend(2, ring2, bundle, usage, w2, s2, group)
        if more is not None:
            attended = attended + more
        attended_ref[group] = attended
        dy = bundle[group, 2 * size :].astype(F32)
        mean = jnp.mean(attended, axis=0, keepdims=True)
        centered = attended - mean
        stats_ref[4 * group : 4 * group + 1] = mean
        stats_ref[4 * group + 1 : 4 * group + 2] = jnp.sum(centered * centered, axis=0, keepdims=True)
        stats_ref[4 * group + 2 : 4 * group + 3] = jnp.sum(dy, axis=0, keepdims=True)
        stats_ref[4 * group + 3 : 4 * group + 4] = jnp.sum(dy * centered, axis=0, keepdims=True)


def norm_kernel(total_cands, attended, bundle, stats, cots, gated_ref, grad_ref, out_grad_ref):
    size = bundle.shape[1] // 3
    width = HEADS * size
    total = None
    for group in range(HEADS):
        head_stats = [stats[head, 4 * group : 4 * group + 4] for head in range(HEADS)]
        mean = sum(one[0:1] for one in head_stats) * (1.0 / HEADS)
        apart = [one[0:1] - mean for one in head_stats]
        spread = sum(one[1:2] + size * off * off for one, off in zip(head_stats, apart))
        inv_scale = lax.rsqrt(spread * (1.0 / width) + 1e-05)
        mean_dy = sum(one[2:3] for one in head_stats) * (1.0 / width)
        mixed = sum(one[3:4] + off * one[2:3] for one, off in zip(head_stats, apart))
        mean_mixed = mixed * inv_scale * (1.0 / width)
        normed = (attended[group] - mean) * inv_scale
        gated = (normed * bundle[group, size : 2 * size].astype(F32)).astype(BF16)
        dy = bundle[group, 2 * size :].astype(F32)
        gated_ref[group] = gated
        grad_ref[group] = (inv_scale * (dy - mean_dy - normed * mean_mixed)).astype(BF16)
        part = jnp.dot(gated, cots[group], preferred_element_type=F32)
        total = part if total is None else total + part
    total = (total * (1.0 / math.sqrt(total_cands))).astype(BF16)
    half = total.shape[1] // 2
    out_grad_ref[0] = total[:, :half]
    out_grad_ref[1] = total[:, half:]


def back_kernel(ring, blocks_ref, bundle, grads, weights, slopes, sum_ref):
    size = bundle.shape[1] // 3
    count, tall = sum_ref.shape[0], blocks_ref.shape[1]
    keys = [None] * count
    values = [None] * count
    for group in range(HEADS):
        span = served(ring, group)
        if len(span) == 0:
            continue
        first, many = span[0], len(span)
        grad = grads[group]
        value_rows = blocks_ref[first : first + many, :, size:].reshape(many * tall, size)
        weight_grad = jnp.dot(value_rows, grad, preferred_element_type=F32)
        for place, block in enumerate(span):
            lines = slice(place * tall, (place + 1) * tall)
            score_grad = (weight_grad[lines] * slopes[group, block].astype(F32)).astype(BF16)
            key = lax.dot_general(score_grad, bundle[group, 0:size], NT, preferred_element_type=F32)
            value = lax.dot_general(weights[group, block], grad, NT, preferred_element_type=F32)
            keys[block] = key if keys[block] is None else keys[block] + key
            values[block] = value if values[block] is None else values[block] + value
    for block in range(count):
        sum_ref[block, :, 0:size] = keys[block].astype(sum_ref.dtype)
        sum_ref[block, :, size:] = values[block].astype(sum_ref.dtype)


def out_kernel(cand_ref, gated_ref, out_ref, result_ref):
    heads, size, count = gated_ref.shape
    gated = gated_ref[...].reshape(heads * size, count)
    product = lax.dot_general(gated, out_ref[...], TN, preferred_element_type=F32)
    result_ref[...] = (cand_ref[...].astype(F32) + product).astype(BF16)


def moved(block, distance):
    size = lax.axis_size(DEPTH)
    return lax.ppermute(block, DEPTH, [((i + distance) % size, i) for i in range(size)])


def exchanged(chunks, axis):
    return lax.all_to_all(chunks, axis, 0, 0, tiled=True)


def spread_over(block, axis):
    size = lax.axis_size(axis)
    return exchanged(jnp.broadcast_to(block[None], (size,) + block.shape), axis)


def summed(parts):
    return jnp.sum(parts.astype(F32), axis=0)


def used_blocks(request_blocks, request_length, candidate_request):
    positions = jnp.arange(request_blocks.shape[1], dtype=jnp.int32)
    matches = request_blocks[:, :, None] == positions[None, None, :]
    in_length = positions[None, :] < request_length[:, None]
    used = jnp.sum(jnp.where(matches & in_length[:, :, None], 1.0, 0.0), axis=1)
    ids = jnp.arange(request_blocks.shape[0], dtype=jnp.int32)
    member = jnp.where(candidate_request[None, :] == ids[:, None], 1.0, 0.0)
    return jnp.sum(used[:, :, None] * member[:, None, :], axis=0)


def summed_rows(out_grad):
    rows, half = out_grad.shape[1:]
    zh, zl, xs = (lax.axis_size(name) for name in ("zh", "zl", "x"))
    own = rows // (zl * xs)
    part = summed(exchanged(out_grad, "core")).astype(BF16)
    part = summed(exchanged(part.reshape(zl, xs, own, half), "zl")).astype(BF16)
    part = exchanged(jnp.broadcast_to(part[None], (zh, xs, own, half)).reshape(zh * xs, own, half), ("zh", "x"))
    part = lax.dynamic_index_in_dim(part.reshape(zh, xs, own, half), lax.axis_index("zh"), axis=1, keepdims=False)
    part = summed(spread_over(summed(part), "y"))
    return spread_over(part, "core").transpose(1, 0, 2).reshape(own, 2 * half)


def on_device(
    candidates,
    cotangent,
    history,
    request_blocks,
    request_length,
    candidate_request,
    in_weight,
    out_weight,
):
    tall, wide = history.shape
    inner = wide // 2
    size = inner // HEADS
    count = candidates.shape[0]
    total_cands = count * lax.axis_size(ALL)

    usage = used_blocks(request_blocks, request_length, candidate_request)
    usage = lax.all_gather(usage.astype(BF16), "x")
    cots = lax.all_gather(cotangent, "x")

    by_head = history.reshape(tall, 2, HEADS, size).transpose(2, 0, 1, 3).reshape(HEADS, tall, 2 * size)
    ring0 = exchanged(by_head, "x")
    ring1 = moved(ring0, 1)
    ring2 = moved(ring1[: HEADS - 1], 1)

    bundle = on_core(
        prepare_kernel,
        shaped((HEADS, 3 * size, count), BF16),
        candidates,
        cotangent,
        in_weight,
        out_weight,
    )
    bundle = exchanged(bundle, "x")

    pairs = shaped((HEADS, HEADS, tall, count), BF16)
    late_pairs = shaped((HEADS, HEADS - 1, tall, count), BF16)
    attended_shape = shaped((HEADS, size, count), F32)
    w0, s0, w1, s1, before = on_core(
        early_kernel, (pairs, pairs, pairs, pairs, attended_shape), ring0, ring1, bundle, usage
    )
    w2, s2, attended, stats = on_core(
        late_kernel,
        (late_pairs, late_pairs, attended_shape, shaped((4 * HEADS, count), F32)),
        ring2,
        bundle,
        usage,
        before,
    )
    stats = spread_over(stats, "x")

    head_shape = shaped((HEADS, size, count), BF16)
    gated, grads, out_grad = on_core(
        lambda *refs: norm_kernel(total_cands, *refs),
        (head_shape, head_shape, shaped((2, size, out_weight.shape[1] // 2), BF16)),
        attended,
        bundle,
        stats,
        cots,
    )
    grad_rows = summed_rows(out_grad)

    def back(ring, blocks, weights, slopes, kind):
        return on_core(
            lambda *refs: back_kernel(ring, *refs),
            shaped((blocks.shape[0], tall, 2 * size), kind),
            blocks,
            bundle,
            grads,
            weights,
            slopes,
        )

    back2 = moved(back(2, ring2, w2, s2, BF16), -1)
    back1 = back(1, ring1, w1, s1, F32)
    back0 = back(0, ring0, w0, s0, F32)
    back1 = back1 + jnp.pad(back2, ((0, 1), (0, 0), (0, 0))).astype(F32)
    back1 = moved(back1.astype(BF16), -1)
    own = exchanged((back0 + back1.astype(F32)).astype(BF16), "x")
    grad_history = own.reshape(HEADS, tall, 2, size).transpose(1, 2, 0, 3).reshape(tall, wide)

    gated = exchanged(gated, "x")
    layer_out = on_core(
        out_kernel, shaped(candidates.shape, BF16), candidates, gated, out_weight
    )
    return (layer_out, grad_rows, grad_history)


def solution(mesh):
    inner = Mesh(mesh.devices.reshape(4, 2, 4, 4, 4), ALL)
    rows = P(ALL)
    return jax.shard_map(
        on_device,
        mesh=inner,
        in_specs=(rows, rows, rows, rows, rows, rows, P(), P()),
        out_specs=(rows, P(("zh", "zl", "x")), rows),
        check_vma=False,
    )
```

time: 183 us -> 171 us (0.934)
  the two profiles are of different devices: /device:TPU:7 before, /device:TPU:1 now
where the time goes in v2:
time: 171 us; the launch traced here: 169 us
  starting transfers between devices  54 us (32%)
  blocking collectives  37.9 us (22%)
  local copies, waits for them, and re-layouts  26.7 us (16%)
  waiting for transfers between devices  24.4 us (14%)
  between operations  14.4 us (8%)
  Pallas kernels  9.3 us (5%)
  other arithmetic  2.71 us (2%)
    all_to_all x7, starting transfers between devices, exchanged(): return lax.all_to_all(chunks, axis, 0, 0, tiled=True)  30.8 us
    all_to_all x3, blocking collectives, exchanged(): return lax.all_to_all(chunks, axis, 0, 0, tiled=True)  28.2 us
    ppermute x4, starting transfers between devices, moved(): lax.ppermute(block, DEPTH, [((i + distance) % size, i) for i in range(siz...  23.2 us
    all_to_all x7, waiting for transfers between devices, exchanged(): return lax.all_to_all(chunks, axis, 0, 0, tiled=True)  20.5 us
    unnamed x47, local copies, waits for them, and re-layouts  18.5 us
    all_gather x1, blocking collectives, on_device(): usage = lax.all_gather(usage.astype(BF16), 'x')  9.68 us
    pallas_call x8, Pallas kernels, on_core(): pl.pallas_call(kernel, out_shape=outs, in_specs=[pl.BlockSpec(memory_spac...  9.3 us
  transfers between devices with their start and end apart: 12, of which 6 were waited for; matrix products, arithmetic and copies ran while one was open for 6% of the time, Pallas kernels for 5%

profile of v2, /device:TPU:1, one launch (start us, length us, event | category | flops | bytes accessed | tf_op | source)
XLA Modules:
  0.0 169.3 jit_solution(1508193124797965261)
XLA Ops:
  10.1 4.8 %all-to-all-start = ((bf16[4,128,256]{2,1,0:T(8,128)(2,1)}), bf16[4,128,256]{2,1,0:T(8,128)(2,1)S(1)}, u32[]{:S(2)}, u32[]{:S(2)}) async-start(bf16[4,128,256]{2,1,0:T(8,128)(2,1)} %reshape.85), calls=%async_computation | async-start | bytes 524288 | tf_op jit(solution)/shard_map/all_to_all | solution.py:176
  15.0 1.6 copy-done.1
  18.9 1.6 all-to-all-done.refs_0_
  20.5 4.2 %all-to-all-start.1 = ((bf16[4,384,224]{1,2,0:T(8,128)(2,1)}), bf16[4,384,224]{1,2,0:T(8,128)(2,1)}, u32[]{:S(2)}, u32[]{:S(2)}) async-start(bf16[4,384,224]{1,2,0:T(8,128)(2,1)} %copy.25), calls=%async_computation.1 | async-start | bytes 1376256 | tf_op jit(solution)/shard_map/all_to_all | solution.py:176
  24.7 11.2 %collective-permute-start = (bf16[4,128,256]{2,1,0:T(8,128)(2,1)S(1)}, bf16[4,128,256]{2,1,0:T(8,128)(2,1)S(1)}, u32[]{:S(2)}, u32[]{:S(2)}) collective-permute-start(bf16[4,128,256]{2,1,0:T(8,128)(2,1)S(1)} %all-to-all-done.refs_0_), channel_id=1, source_target_pairs={{4,0},{8,4},{12,8},{16,12},{20,16},{24,20},{28,24},{32,28},{36,32}... | collective-permute-start | bytes 786440 | tf_op jit(solution)/shard_map/ppermute | solution.py:172
  35.9 3.2 %collective-permute-done.refs_1_.refs_0_ = bf16[4,128,256]{2,1,0:T(8,128)(2,1)S(1)} collective-permute-done((bf16[4,128,256]{2,1,0:T(8,128)(2,1)S(1)}, bf16[4,128,256]{2,1,0:T(8,128)(2,1)S(1)}, u32[]{:S(2)}, u32[]{:S(2)}) %collective-permute-start) | collective-permute-done | bytes 262176 | tf_op jit(solution)/shard_map/ppermute | solution.py:172
  39.2 5.6 %collective-permute-start.1 = (bf16[3,128,256]{2,1,0:T(8,128)(2,1)S(1)}, bf16[3,128,256]{2,1,0:T(8,128)(2,1)S(1)}, u32[]{:S(2)}, u32[]{:S(2)}) collective-permute-start(bf16[3,128,256]{2,1,0:T(8,128)(2,1)S(1)} %slice.4), channel_id=1, source_target_pairs={{4,0},{8,4},{12,8},{16,12},{20,16},{24,20},{28,24},{32,28},{36,32}... | collective-permute-start | bytes 589832 | tf_op jit(solution)/shard_map/ppermute | solution.py:172
  45.0 9.7 %all-gather = bf16[32,224]{1,0:T(8,128)(2,1)S(1)} all-gather(bf16[8,224]{1,0:T(8,128)(2,1)S(1)} %multiply_reduce_fusion), channel_id=2, replica_groups=mesh['y'=4,'core'=2,'zh'=4,'zl'=4,'x'=4] {'x'}, dimensions={0}, use_global_device_ids=true | all-gather | bytes 17920 | tf_op jit(solution)/shard_map/all_gather | solution.py:227
  54.7 1.4 copy.27.refs_2_.bundle.refs_1_
  56.0 2.3 %shard_map.104 = (bf16[4,4,128,224]{3,2,1,0:T(8,128)(2,1)S(1)}, bf16[4,4,128,224]{3,2,1,0:T(8,128)(2,1)S(1)}, bf16[4,4,128,224]{3,2,1,0:T(8,128)(2,1)S(1)}, bf16...) custom-call(bf16[4,128,256]{2,1,0:T(8,128)(2,1)S(1)} %all-to-all-done.refs_0_, ...), custom_call_target="tpu_custom_call" | custom-call | tf_op jit(solution)/shard_map/pallas_call | solution.py:21
  65.8 7.9 %all_to_all.50.refs_2_ = f32[4,16,224]{2,1,0:T(8,128)S(1)} all-to-all(f32[4,16,224]{2,1,0:T(8,128)S(1)} %broadcast_in_dim.28), channel_id=1, replica_groups=mesh['y'=4,'core'=2,'zh'=4,'zl'=4,'x'=4] {'x'}, dimensions={0} | all-to-all | bytes 114688 | tf_op jit(solution)/shard_map/all_to_all | solution.py:176
  73.8 1.5 copy-done.5
  76.8 10.6 %all_to_all.51 = bf16[2,128,512]{2,1,0:T(8,128)(2,1)S(1)} all-to-all(bf16[2,128,512]{2,1,0:T(8,128)(2,1)S(1)} %get-tuple-element.19), channel_id=1, replica_groups=mesh['y'=4,'core'=2,'zh'=4,'zl'=4,'x'=4] {'core'}, dimensions={0} | all-to-all | bytes 524288 | tf_op jit(solution)/shard_map/all_to_all | solution.py:176
  88.2 3.3 %all-to-all-start.5 = ((bf16[4,4,8,512]{3,2,1,0:T(8,128)(2,1)}), bf16[4,4,8,512]{3,2,1,0:T(8,128)(2,1)S(1)}, u32[]{:S(2)}, u32[]{:S(2)}) async-start(bf16[4,4,8,512]{3,2,1,0:T(8,128)(2,1)} %bitcast.3), calls=%async_computation.5 | async-start | bytes 262144 | tf_op jit(solution)/shard_map/all_to_all | solution.py:176
  95.0 3.3 %collective-permute-start.2 = (bf16[3,128,256]{2,1,0:T(8,128)(2,1)}, bf16[3,128,256]{2,1,0:T(8,128)(2,1)}, u32[]{:S(2)}, u32[]{:S(2)}) collective-permute-start(bf16[3,128,256]{2,1,0:T(8,128)(2,1)} %shard_map.110), channel_id=1, source_target_pairs={{60,0},{0,4},{4,8},{8,12},{12,16},{16,20},{20,24},{24,28},{28,32},... | collective-permute-start | bytes 589832 | tf_op jit(solution)/shard_map/ppermute | solution.py:172
  102.6 3.4 %all-to-all-start.3 = ((bf16[4,128,224]{1,2,0:T(8,128)(2,1)}), bf16[4,128,224]{1,2,0:T(8,128)(2,1)S(1)}, u32[]{:S(2)}, u32[]{:S(2)}) async-start(bf16[4,128,224]{1,2,0:T(8,128)(2,1)} %copy.29), calls=%async_computation.3 | async-start | bytes 458752 | tf_op jit(solution)/shard_map/all_to_all | solution.py:176
  107.0 3.1 %collective-permute-start.3 = (bf16[4,128,256]{2,1,0:T(8,128)(2,1)S(1)}, bf16[4,128,256]{2,1,0:T(8,128)(2,1)S(1)}, u32[]{:S(2)}, u32[]{:S(2)}) collective-permute-start(bf16[4,128,256]{2,1,0:T(8,128)(2,1)S(1)} %add_convert_fusion.1), channel_id=1, source_target_pairs={{60,0},{0,4},{4,8},{8,12},{12,16},{16,20},{20,24},{24,28},{28,32},... | collective-permute-start | bytes 786440 | tf_op jit(solution)/shard_map/ppermute | solution.py:172
  112.0 7.1 %all-to-all-start.6 = ((bf16[16,8,512]{2,1,0:T(8,128)(2,1)}), bf16[16,8,512]{2,1,0:T(8,128)(2,1)S(1)}, u32[]{:S(2)}, u32[]{:S(2)}) async-start(bf16[16,8,512]{2,1,0:T(8,128)(2,1)} %bitcast.4), calls=%async_computation.6 | async-start | bytes 262144 | tf_op jit(solution)/shard_map/all_to_all | solution.py:176
  123.4 10.3 %all-to-all-done.6 = bf16[16,8,512]{2,1,0:T(8,128)(2,1)S(1)} async-done(((bf16[16,8,512]{2,1,0:T(8,128)(2,1)}), bf16[16,8,512]{2,1,0:T(8,128)(2,1)S(1)}, u32[]{:S(2)}, u32[]{:S(2)}) %all-to-all-start.6) | async-done | bytes 131104 | tf_op jit(solution)/shard_map/all_to_all | solution.py:176
  133.7 3.7 %all-to-all-start.9 = ((bf16[4,128,256]{2,1,0:T(8,128)(2,1)}), bf16[4,128,256]{2,1,0:T(8,128)(2,1)S(1)}, u32[]{:S(2)}, u32[]{:S(2)}) async-start(bf16[4,128,256]{2,1,0:T(8,128)(2,1)} %add_convert_fusion), calls=%async_computation.9 | async-start | bytes 524288 | tf_op jit(solution)/shard_map/all_to_all | solution.py:176
  137.4 5.5 %all-to-all-done.9 = bf16[4,128,256]{2,1,0:T(8,128)(2,1)S(1)} async-done(((bf16[4,128,256]{2,1,0:T(8,128)(2,1)}), bf16[4,128,256]{2,1,0:T(8,128)(2,1)S(1)}, u32[]{:S(2)}, u32[]{:S(2)}) %all-to-all-start.9) | async-done | bytes 262176 | tf_op jit(solution)/shard_map/all_to_all | solution.py:176
  143.5 4.2 %all-to-all-start.7 = ((f32[4,8,512]{2,1,0:T(8,128)}), f32[4,8,512]{2,1,0:T(8,128)S(1)}, u32[]{:S(2)}, u32[]{:S(2)}) async-start(f32[4,8,512]{2,1,0:T(8,128)} %broadcast_in_dim.30), calls=%async_computation.7 | async-start | bytes 131072 | tf_op jit(solution)/shard_map/all_to_all | solution.py:176
  150.4 1.8 %all-to-all-done.7 = f32[4,8,512]{2,1,0:T(8,128)S(1)} async-done(((f32[4,8,512]{2,1,0:T(8,128)}), f32[4,8,512]{2,1,0:T(8,128)S(1)}, u32[]{:S(2)}, u32[]{:S(2)}) %all-to-all-start.7) | async-done | bytes 65568 | tf_op jit(solution)/shard_map/all_to_all | solution.py:176
  152.2 9.6 %all_to_all.52 = f32[2,8,512]{2,1,0:T(8,128)S(1)} all-to-all(f32[2,8,512]{2,1,0:T(8,128)S(1)} %broadcast_in_dim.31), channel_id=1, replica_groups=mesh['y'=4,'core'=2,'zh'=4,'zl'=4,'x'=4] {'core'}, dimensions={0} | all-to-all | bytes 65536 | tf_op jit(solution)/shard_map/all_to_all | solution.py:176
  (85 shorter events, 33.9 us)
Async XLA Ops:
  7.2 7.8 %copy-start.2 = (bf16[224,1024]{1,0:T(8,128)(2,1)S(1)}, bf16[224,1024]{1,0:T(8,128)(2,1)}, u32[]{:S(2)}) copy-start(bf16[224,1024]{1,0:T(8,128)(2,1)} %cot_ref.1) | copy-start | bytes 1376260
  7.2 7.8 %copy-start = (bf16[512,1024]{1,0:T(8,128)(2,1)S(1)}, bf16[512,1024]{1,0:T(8,128)(2,1)}, u32[]{:S(2)}) copy-start(bf16[512,1024]{1,0:T(8,128)(2,1)} %out_ref.3) | copy-start | bytes 3145732
  7.2 7.8 %copy-start.3 = (bf16[224,1024]{1,0:T(8,128)(2,1)S(1)}, bf16[224,1024]{1,0:T(8,128)(2,1)}, u32[]{:S(2)}) copy-start(bf16[224,1024]{1,0:T(8,128)(2,1)} %cand_ref.3) | copy-start | bytes 1376260
  7.2 66.6 %all-gather.4.cloned.1.call-start = ((), (), s32[]{:S(2)}) async-start(), calls=%async_computation.10 | async-start | bytes 2293760 | tf_op jit(solution)/shard_map/all_gather | solution.py:228
  10.1 10.4 %all-to-all-start = ((bf16[4,128,256]{2,1,0:T(8,128)(2,1)}), bf16[4,128,256]{2,1,0:T(8,128)(2,1)S(1)}, u32[]{:S(2)}, u32[]{:S(2)}) async-start(bf16[4,128,256]{2,1,0:T(8,128)(2,1)} %reshape.85), calls=%async_computation | async-start | bytes 524288 | tf_op jit(solution)/shard_map/all_to_all | solution.py:176
  15.0 1.6 copy-start.1
  17.8 18.1 %copy-start.22 = (s32[2]{0:T(128)S(1)}, s32[2]{0:T(128)}, u32[]{:S(2)}) copy-start(s32[2]{0:T(128)} %param.12) | copy-start | bytes 28
  17.8 18.2 %copy-start.20 = (s32[224]{0:T(256)S(1)}, s32[224]{0:T(256)}, u32[]{:S(2)}) copy-start(s32[224]{0:T(256)} %param.13) | copy-start | bytes 2692
  17.8 27.0 %copy-start.21 = (s32[2,8]{1,0:T(2,128)S(1)}, s32[2,8]{1,0:T(2,128)}, u32[]{:S(2)}) copy-start(s32[2,8]{1,0:T(2,128)} %param.11) | copy-start | bytes 196
  20.5 34.2 %all-to-all-start.1 = ((bf16[4,384,224]{1,2,0:T(8,128)(2,1)}), bf16[4,384,224]{1,2,0:T(8,128)(2,1)}, u32[]{:S(2)}, u32[]{:S(2)}) async-start(bf16[4,384,224]{1,2,0:T(8,128)(2,1)} %copy.25), calls=%async_computation.1 | async-start | bytes 1376256 | tf_op jit(solution)/shard_map/all_to_all | solution.py:176
  24.7 14.5 %collective-permute-start = (bf16[4,128,256]{2,1,0:T(8,128)(2,1)S(1)}, bf16[4,128,256]{2,1,0:T(8,128)(2,1)S(1)}, u32[]{:S(2)}, u32[]{:S(2)}) collective-permute-start(bf16[4,128,256]{2,1,0:T(8,128)(2,1)S(1)} %all-to-all-done.refs_0_), channel_id=1, source_target_pairs={{4,0},{8,4},{12,8},{16,12},{20,16},{24,20},{28,24},{32,28},{36,32}... | collective-permute-start | bytes 786440 | tf_op jit(solution)/shard_map/ppermute | solution.py:172
  39.2 23.1 %collective-permute-start.1 = (bf16[3,128,256]{2,1,0:T(8,128)(2,1)S(1)}, bf16[3,128,256]{2,1,0:T(8,128)(2,1)S(1)}, u32[]{:S(2)}, u32[]{:S(2)}) collective-permute-start(bf16[3,128,256]{2,1,0:T(8,128)(2,1)S(1)} %slice.4), channel_id=1, source_target_pairs={{4,0},{8,4},{12,8},{16,12},{20,16},{24,20},{28,24},{32,28},{36,32}... | collective-permute-start | bytes 589832 | tf_op jit(solution)/shard_map/ppermute | solution.py:172
  73.8 1.5 copy-start.5
  88.2 14.4 %all-to-all-start.5 = ((bf16[4,4,8,512]{3,2,1,0:T(8,128)(2,1)}), bf16[4,4,8,512]{3,2,1,0:T(8,128)(2,1)S(1)}, u32[]{:S(2)}, u32[]{:S(2)}) async-start(bf16[4,4,8,512]{3,2,1,0:T(8,128)(2,1)} %bitcast.3), calls=%async_computation.5 | async-start | bytes 262144 | tf_op jit(solution)/shard_map/all_to_all | solution.py:176
  95.0 11.0 %collective-permute-start.2 = (bf16[3,128,256]{2,1,0:T(8,128)(2,1)}, bf16[3,128,256]{2,1,0:T(8,128)(2,1)}, u32[]{:S(2)}, u32[]{:S(2)}) collective-permute-start(bf16[3,128,256]{2,1,0:T(8,128)(2,1)} %shard_map.110), channel_id=1, source_target_pairs={{60,0},{0,4},{4,8},{8,12},{12,16},{16,20},{20,24},{24,28},{28,32},... | collective-permute-start | bytes 589832 | tf_op jit(solution)/shard_map/ppermute | solution.py:172
  99.2 1.2 copy-start.11
  100.4 1.2 copy-start.13
  102.6 8.7 %all-to-all-start.3 = ((bf16[4,128,224]{1,2,0:T(8,128)(2,1)}), bf16[4,128,224]{1,2,0:T(8,128)(2,1)S(1)}, u32[]{:S(2)}, u32[]{:S(2)}) async-start(bf16[4,128,224]{1,2,0:T(8,128)(2,1)} %copy.29), calls=%async_computation.3 | async-start | bytes 458752 | tf_op jit(solution)/shard_map/all_to_all | solution.py:176
  107.0 15.6 %collective-permute-start.3 = (bf16[4,128,256]{2,1,0:T(8,128)(2,1)S(1)}, bf16[4,128,256]{2,1,0:T(8,128)(2,1)S(1)}, u32[]{:S(2)}, u32[]{:S(2)}) collective-permute-start(bf16[4,128,256]{2,1,0:T(8,128)(2,1)S(1)} %add_convert_fusion.1), channel_id=1, source_target_pairs={{60,0},{0,4},{4,8},{8,12},{12,16},{16,20},{20,24},{24,28},{28,32},... | collective-permute-start | bytes 786440 | tf_op jit(solution)/shard_map/ppermute | solution.py:172
  112.0 21.7 %all-to-all-start.6 = ((bf16[16,8,512]{2,1,0:T(8,128)(2,1)}), bf16[16,8,512]{2,1,0:T(8,128)(2,1)S(1)}, u32[]{:S(2)}, u32[]{:S(2)}) async-start(bf16[16,8,512]{2,1,0:T(8,128)(2,1)} %bitcast.4), calls=%async_computation.6 | async-start | bytes 262144 | tf_op jit(solution)/shard_map/all_to_all | solution.py:176
  119.1 1.2 copy-start.7
  122.6 25.3 %copy-start.4 = (bf16[224,1024]{1,0:T(8,128)(2,1)S(1)}, bf16[224,1024]{1,0:T(8,128)(2,1)}, u32[]{:S(2)}) copy-start(bf16[224,1024]{1,0:T(8,128)(2,1)} %cand_ref.3) | copy-start | bytes 1376260
  133.7 9.2 %all-to-all-start.9 = ((bf16[4,128,256]{2,1,0:T(8,128)(2,1)}), bf16[4,128,256]{2,1,0:T(8,128)(2,1)S(1)}, u32[]{:S(2)}, u32[]{:S(2)}) async-start(bf16[4,128,256]{2,1,0:T(8,128)(2,1)} %add_convert_fusion), calls=%async_computation.9 | async-start | bytes 524288 | tf_op jit(solution)/shard_map/all_to_all | solution.py:176
  143.5 8.7 %all-to-all-start.7 = ((f32[4,8,512]{2,1,0:T(8,128)}), f32[4,8,512]{2,1,0:T(8,128)S(1)}, u32[]{:S(2)}, u32[]{:S(2)}) async-start(f32[4,8,512]{2,1,0:T(8,128)} %broadcast_in_dim.30), calls=%async_computation.7 | async-start | bytes 131072 | tf_op jit(solution)/shard_map/all_to_all | solution.py:176
  (11 other events, 11.1 us)
Sparse Core Ops, SparseCore 0:
  10.1 44.4 all-gather.3

commit v3 on v2

v3 whole, which is shorter than its diff:
```python
import math

import jax
import jax.numpy as jnp
from jax import lax
from jax.experimental import pallas as pl
from jax.experimental.pallas import tpu as pltpu
from jax.sharding import Mesh, PartitionSpec as P

HEADS = 4
SPAN = 8
BF16 = jnp.bfloat16
F32 = jnp.float32
ALL = ("y", "core", "zh", "zl", "x")
DEPTH = ("zh", "zl")
NT = (((1,), (1,)), ((), ()))
TN = (((0,), (0,)), ((), ()))


def on_core(kernel, outs, *operands, scalars=()):
    spaces = [pltpu.SMEM] * len(scalars) + [pltpu.VMEM] * len(operands)
    return pl.pallas_call(
        kernel,
        out_shape=outs,
        in_specs=[pl.BlockSpec(memory_space=space) for space in spaces],
        out_specs=jax.tree.map(lambda _: pl.BlockSpec(memory_space=pltpu.VMEM), outs),
        compiler_params=pltpu.CompilerParams(vmem_limit_bytes=12 * 1024 * 1024),
    )(*scalars, *operands)


def shaped(shape, kind):
    return jax.ShapeDtypeStruct(shape, kind)


def sigmoid(values):
    return 0.5 + 0.5 * jnp.tanh(0.5 * values)


def served(ring, group):
    return {0: range(group, HEADS), 1: range(0, HEADS), 2: range(0, group)}[ring]


def split_kernel(history_ref, chunks_ref):
    heads, _, both = chunks_ref.shape
    size = both // 2
    for head in range(heads):
        chunks_ref[head, :, :size] = history_ref[:, head * size : (head + 1) * size]
        chunks_ref[head, :, size:] = history_ref[:, (heads + head) * size : (heads + head + 1) * size]


def prepare_kernel(cand_ref, cot_ref, in_ref, out_ref, usage_ref, bundle_ref):
    rows = cand_ref[...].astype(F32)
    centered = rows - jnp.mean(rows, axis=-1, keepdims=True)
    inv_scale = lax.rsqrt(jnp.mean(centered * centered, axis=-1, keepdims=True) + 1e-05)
    normed = (centered * inv_scale).astype(BF16)
    projected = jnp.dot(normed, in_ref[...], preferred_element_type=F32).T
    zed_grad = lax.dot_general(out_ref[...], cot_ref[...], NT, preferred_element_type=F32)
    inner, count = out_ref.shape[0], cand_ref.shape[0]
    size = inner // HEADS
    bundle_ref[:, : 3 * size, count:] = jnp.zeros(
        (HEADS, 3 * size, bundle_ref.shape[2] - count), BF16
    )
    for head in range(HEADS):
        part = slice(head * size, (head + 1) * size)
        gate_in = projected[inner + head * size : inner + (head + 1) * size]
        gating = gate_in * sigmoid(gate_in)
        bundle_ref[head, 0:size, :count] = projected[part].astype(BF16)
        bundle_ref[head, size : 2 * size, :count] = gating.astype(BF16)
        bundle_ref[head, 2 * size : 3 * size, :count] = (zed_grad[part] * gating).astype(BF16)
        bundle_ref[head, 3 * size :] = usage_ref[...]


def scored(ring, blocks_ref, bundle_ref, group):
    span = served(ring, group)
    tall, size = blocks_ref.shape[1], blocks_ref.shape[2] // 2
    rows = blocks_ref[span[0] : span[-1] + 1].reshape(len(span) * tall, 2 * size)
    scores = jnp.dot(rows[:, :size], bundle_ref[group, 0:size], preferred_element_type=F32)
    scores = scores * (1.0 / math.sqrt(size))
    usage = bundle_ref[group, 3 * size :].astype(F32)
    parts = []
    for place, block in enumerate(span):
        position = HEADS * ring + block - group
        parts.append((scores[place * tall : (place + 1) * tall], usage[position : position + 1]))
    return rows[:, size:], parts


def attend(ring, blocks_ref, bundle_ref, group):
    values, parts = scored(ring, blocks_ref, bundle_ref, group)
    weights = [(scores * sigmoid(scores) * usage).astype(BF16) for scores, usage in parts]
    return lax.dot_general(
        values, jnp.concatenate(weights, axis=0), TN, preferred_element_type=F32
    )


def early_kernel(ring0, ring1, bundle, attended_ref):
    for group in range(HEADS):
        attended_ref[group] = attend(0, ring0, bundle, group) + attend(1, ring1, bundle, group)


def late_kernel(ring2, bundle, before, attended_ref, stats_ref):
    size = before.shape[1]
    for group in range(HEADS):
        attended = before[group]
        if len(served(2, group)) > 0:
            attended = attended + attend(2, ring2, bundle, group)
        attended_ref[group] = attended
        dy = bundle[group, 2 * size : 3 * size].astype(F32)
        mean = jnp.mean(attended, axis=0, keepdims=True)
        centered = attended - mean
        stats_ref[4 * group : 4 * group + 1] = mean
        stats_ref[4 * group + 1 : 4 * group + 2] = jnp.sum(centered * centered, axis=0, keepdims=True)
        stats_ref[4 * group + 2 : 4 * group + 3] = jnp.sum(dy, axis=0, keepdims=True)
        stats_ref[4 * group + 3 : 4 * group + 4] = jnp.sum(dy * centered, axis=0, keepdims=True)


def norm_kernel(total_cands, attended, bundle, stats, cots_ref, gated_ref, grad_ref, out_grad_ref, cots, arrival):
    copy = pltpu.make_async_copy(cots_ref, cots, arrival)
    copy.start()
    size = attended.shape[1]
    count = cots.shape[1]
    width = HEADS * size
    total = None
    for group in range(HEADS):
        head_stats = [stats[head, 4 * group : 4 * group + 4] for head in range(HEADS)]
        mean = sum(one[0:1] for one in head_stats) * (1.0 / HEADS)
        apart = [one[0:1] - mean for one in head_stats]
        spread = sum(one[1:2] + size * off * off for one, off in zip(head_stats, apart))
        inv_scale = lax.rsqrt(spread * (1.0 / width) + 1e-05)
        mean_dy = sum(one[2:3] for one in head_stats) * (1.0 / width)
        mixed = sum(one[3:4] + off * one[2:3] for one, off in zip(head_stats, apart))
        mean_mixed = mixed * inv_scale * (1.0 / width)
        normed = (attended[group] - mean) * inv_scale
        gated = (normed * bundle[group, size : 2 * size].astype(F32)).astype(BF16)
        dy = bundle[group, 2 * size : 3 * size].astype(F32)
        gated_ref[group] = gated
        grad_ref[group] = (inv_scale * (dy - mean_dy - normed * mean_mixed)).astype(BF16)
    copy.wait()
    for group in range(HEADS):
        part = jnp.dot(gated_ref[group, :, :count], cots[group], preferred_element_type=F32)
        total = part if total is None else total + part
    total = (total * (1.0 / math.sqrt(total_cands))).astype(BF16)
    halves, rows_of, lines, columns = out_grad_ref.shape
    for half in range(halves):
        for row in range(rows_of):
            out_grad_ref[half, row] = total[
                row * lines : (row + 1) * lines, half * columns : (half + 1) * columns
            ]


def back(ring, blocks_ref, bundle, grads, sum_ref):
    tall, size = blocks_ref.shape[1], blocks_ref.shape[2] // 2
    scale = 1.0 / math.sqrt(size)
    keys, values = {}, {}
    for group in range(HEADS):
        span = served(ring, group)
        if len(span) == 0:
            continue
        grad = grads[group]
        value_rows, parts = scored(ring, blocks_ref, bundle, group)
        weight_grad = jnp.dot(value_rows, grad, preferred_element_type=F32)
        for place, block in enumerate(span):
            scores, usage = parts[place]
            part = sigmoid(scores)
            weights = scores * part
            slopes = (part + weights * (1.0 - part)) * (usage * scale)
            lines = weight_grad[place * tall : (place + 1) * tall]
            key = lax.dot_general(
                (lines * slopes).astype(BF16), bundle[group, 0:size], NT, preferred_element_type=F32
            )
            value = lax.dot_general(
                (weights * usage).astype(BF16), grad, NT, preferred_element_type=F32
            )
            keys[block] = keys[block] + key if block in keys else key
            values[block] = values[block] + value if block in values else value
    for block in keys:
        sum_ref[block, :, 0:size] = keys[block].astype(sum_ref.dtype)
        sum_ref[block, :, size:] = values[block].astype(sum_ref.dtype)


def far_back_kernel(ring1, ring2, bundle, grads, back1, back2):
    back(2, ring2, bundle, grads, back2)
    back(1, ring1, bundle, grads, back1)


def near_back_kernel(ring0, bundle, grads, back0):
    back(0, ring0, bundle, grads, back0)


def parcel_kernel(place_ref, gated_ref, back0, back1, back2, *parcel_refs):
    size = gated_ref.shape[1]
    for step, parcel in enumerate(parcel_refs):
        target = lax.rem(place_ref[0] + step, HEADS)
        parcel[0:size] = gated_ref[target]
        total = back0[target] + back1[target].astype(F32)
        last = jnp.minimum(target, back2.shape[0] - 1)
        more = back2[last].astype(F32)
        parcel[size:] = (total + jnp.where(last == target, more, 0.0)).astype(BF16)


def join_kernel(place_ref, cand_ref, out_ref, *refs):
    *parcels, result_ref, grad_ref = refs
    inner, count = out_ref.shape[0], cand_ref.shape[0]
    size = inner // HEADS
    product = None
    for step, parcel in enumerate(parcels):
        head = lax.rem(place_ref[0] + HEADS - step, HEADS)
        rows = pl.ds(pl.multiple_of(head * size, size), size)
        part = lax.dot_general(parcel[0:size, :count], out_ref[rows], TN, preferred_element_type=F32)
        product = part if product is None else product + part
        grad_ref[:, rows] = parcel[size:, 0:size]
        grad_ref[:, pl.ds(pl.multiple_of(inner + head * size, size), size)] = parcel[size:, size:]
    result_ref[...] = (cand_ref[...].astype(F32) + product).astype(BF16)


def moved(block, distance):
    size = lax.axis_size(DEPTH)
    return lax.ppermute(block, DEPTH, [((i + distance) % size, i) for i in range(size)])


def exchanged(chunks, axis):
    return lax.all_to_all(chunks, axis, 0, 0, tiled=True)


def spread_over(block, axis):
    size = lax.axis_size(axis)
    return exchanged(jnp.broadcast_to(block[None], (size,) + block.shape), axis)


def summed(parts):
    return jnp.sum(parts.astype(F32), axis=0)


def used_blocks(request_blocks, request_length, candidate_request):
    positions = jnp.arange(request_blocks.shape[1], dtype=jnp.int32)
    matches = request_blocks[:, :, None] == positions[None, None, :]
    in_length = positions[None, :] < request_length[:, None]
    used = jnp.sum(jnp.where(matches & in_length[:, :, None], 1.0, 0.0), axis=1)
    ids = jnp.arange(request_blocks.shape[0], dtype=jnp.int32)
    member = jnp.where(candidate_request[None, :] == ids[:, None], 1.0, 0.0)
    return jnp.sum(used[:, :, None] * member[:, None, :], axis=0)


def on_device(
    candidates,
    cotangent,
    history,
    request_blocks,
    request_length,
    candidate_request,
    in_weight,
    out_weight,
):
    tall, wide = history.shape
    inner = wide // 2
    size = inner // HEADS
    count = candidates.shape[0]
    lanes = 2 * size
    total_cands = count * lax.axis_size(ALL)
    barrier = lax.optimization_barrier
    place = lax.axis_index("x").reshape(1).astype(jnp.int32)

    cots = lax.all_gather(cotangent, "x")
    ring_shape = shaped((HEADS, tall, 2 * size), BF16)
    ring0 = exchanged(on_core(split_kernel, ring_shape, history), "x")

    owners = jnp.pad(candidate_request, (0, lanes - count), constant_values=-1)
    usage = used_blocks(request_blocks, request_length, owners).astype(BF16)
    usage = jnp.pad(usage, ((0, 16 - usage.shape[0]), (0, 0)))
    ring2 = moved(ring0[: HEADS - 1], 2)
    ring1 = moved(ring0, 1)
    bundle = on_core(
        prepare_kernel,
        shaped((HEADS, 3 * size + 16, lanes), BF16),
        candidates,
        cotangent,
        in_weight,
        out_weight,
        usage,
    )
    bundle = exchanged(bundle, "x")

    attended_shape = shaped((HEADS, size, lanes), F32)
    before = on_core(early_kernel, attended_shape, ring0, ring1, bundle)
    ring2, cots = barrier((ring2, cots))
    attended, stats = on_core(
        late_kernel, (attended_shape, shaped((4 * HEADS, lanes), F32)), ring2, bundle, before
    )
    stats = spread_over(stats, "x")
    head_shape = shaped((HEADS, size, lanes), BF16)
    cores, zh, zl, xs = (lax.axis_size(name) for name in ("core", "zh", "zl", "x"))
    own, half = size // (zl * xs), out_weight.shape[1] // cores
    gated, grads, out_grad = pl.pallas_call(
        lambda *refs: norm_kernel(total_cands, *refs),
        out_shape=(head_shape, head_shape, shaped((cores, zl, size // zl, half), BF16)),
        in_specs=[pl.BlockSpec(memory_space=pltpu.VMEM)] * 3 + [pl.BlockSpec(memory_space=pltpu.HBM)],
        out_specs=(pl.BlockSpec(memory_space=pltpu.VMEM),) * 3,
        scratch_shapes=[pltpu.VMEM(cots.shape, BF16), pltpu.SemaphoreType.DMA],
        compiler_params=pltpu.CompilerParams(vmem_limit_bytes=12 * 1024 * 1024),
    )(attended, bundle, stats, cots)

    back1, back2 = on_core(
        far_back_kernel, (shaped(ring1.shape, BF16), shaped(ring2.shape, BF16)), ring1, ring2, bundle, grads
    )
    out_grad, back1, back2 = barrier((out_grad, back1, back2))
    back2 = moved(back2, -2)
    back1 = moved(back1, -1)
    part = exchanged(out_grad.reshape(cores * zl, size // zl, half), ("core", "zl"))
    part = summed(part).astype(BF16)
    part, grads = barrier((part, grads))
    back0 = on_core(near_back_kernel, shaped(ring0.shape, F32), ring0, bundle, grads)
    part = jnp.broadcast_to(part.reshape(1, xs, own, half), (zh, xs, own, half))
    part = exchanged(part.reshape(zh * xs, own, half), ("zh", "x")).reshape(zh, xs, own, half)
    part = lax.dynamic_index_in_dim(part, lax.axis_index("zh"), axis=1, keepdims=False)
    part, back0, back1, back2 = barrier((summed(part), back0, back1, back2))
    part = spread_over(part, ("y", "core")).reshape(-1, cores, own, half)
    grad_rows = summed(part).transpose(1, 0, 2).reshape(own, cores * half)

    parcels = on_core(
        parcel_kernel, [shaped((2 * size, lanes), BF16)] * HEADS, gated, back0, back1, back2, scalars=(place,)
    )
    arrived = [
        lax.ppermute(parcel, "x", [(i, (i + step) % HEADS) for i in range(HEADS)]) if step else parcel
        for step, parcel in enumerate(parcels)
    ]
    layer_out, grad_history = on_core(
        join_kernel,
        (shaped(candidates.shape, BF16), shaped(history.shape, BF16)),
        candidates,
        out_weight,
        *arrived,
        scalars=(place,),
    )
    return (layer_out, grad_rows, grad_history)


def solution(mesh):
    inner = Mesh(mesh.devices.reshape(4, 2, 4, 4, 4), ALL)
    rows = P(ALL)
    return jax.shard_map(
        on_device,
        mesh=inner,
        in_specs=(rows, rows, rows, rows, rows, rows, P(), P()),
        out_specs=(rows, P(("zh", "zl", "x")), rows),
        check_vma=False,
    )
```

time: 171 us -> 154 us (0.901)
  local copies, waits for them, and re-layouts: 26.7 us -> 8.43 us
  waiting for transfers between devices: 24.4 us -> 30.2 us
  blocking collectives: 37.9 us -> 33 us
  Pallas kernels: 9.3 us -> 13.1 us
  starting transfers between devices: 54 us -> 50.4 us
    all_to_all x7 -> x3, waiting for transfers between devices: 20.5 us -> 8.73 us  [exchanged(): return lax.all_to_all(chunks, axis, 0, 0, tiled=True)]
    unnamed x47 -> x18, local copies, waits for them, and re-layouts: 18.5 us -> 7.04 us
    ppermute x0 -> x3, starting transfers between devices: none -> 10.1 us  [on_device(): lax.ppermute(parcel, 'x', [(i, (i + step) % HEADS) for i in range(HEADS)])]
    ppermute x4, waiting for transfers between devices: 3.21 us -> 13.2 us  [moved(): lax.ppermute(block, DEPTH, [((i + distance) % size, i) for i in range(siz...]
    all_gather x1 -> x0, blocking collectives: 9.68 us -> none  [on_device(): usage = lax.all_gather(usage.astype(BF16), 'x')]
    all_to_all x7 -> x3, starting transfers between devices: 30.8 us -> 21.9 us  [exchanged(): return lax.all_to_all(chunks, axis, 0, 0, tiled=True)]
    all_gather x1, waiting for transfers between devices: 0.01 us -> 7.54 us  [on_device(): cots = lax.all_gather(cotangent, 'x')]
    ppermute x4, starting transfers between devices: 23.2 us -> 18.3 us  [moved(): lax.ppermute(block, DEPTH, [((i + distance) % size, i) for i in range(siz...]
  transfers between devices with their start and end apart: 12 -> 11, of which waited for: 6 -> 5; matrix products, arithmetic and copies ran while one was open for 6% -> 2% of each run, Pallas kernels for 5% -> 4%
where the time goes in v3:
time: 154 us; the launch traced here: 152 us
  starting transfers between devices  50.4 us (33%)
  blocking collectives  33 us (21%)
  waiting for transfers between devices  30.2 us (20%)
  between operations  14.2 us (9%)
  Pallas kernels  13.1 us (9%)
  local copies, waits for them, and re-layouts  8.43 us (5%)
  other arithmetic  2.24 us (1%)
    all_to_all x3, blocking collectives, exchanged(): return lax.all_to_all(chunks, axis, 0, 0, tiled=True)  33 us
    all_to_all x3, starting transfers between devices, exchanged(): return lax.all_to_all(chunks, axis, 0, 0, tiled=True)  21.9 us
    ppermute x4, starting transfers between devices, moved(): lax.ppermute(block, DEPTH, [((i + distance) % size, i) for i in range(siz...  18.3 us
    ppermute x4, waiting for transfers between devices, moved(): lax.ppermute(block, DEPTH, [((i + distance) % size, i) for i in range(siz...  13.2 us
    pallas_call x8, Pallas kernels, on_core(): pl.pallas_call(kernel, out_shape=outs, in_specs=[pl.BlockSpec(memory_spac...  12.2 us
    ppermute x3, starting transfers between devices, on_device(): lax.ppermute(parcel, 'x', [(i, (i + step) % HEADS) for i in range(HEADS)])  10.1 us
    all_to_all x3, waiting for transfers between devices, exchanged(): return lax.all_to_all(chunks, axis, 0, 0, tiled=True)  8.73 us
    all_gather x1, waiting for transfers between devices, on_device(): cots = lax.all_gather(cotangent, 'x')  7.54 us
  transfers between devices with their start and end apart: 11, of which 5 were waited for; matrix products, arithmetic and copies ran while one was open for 2% of the time, Pallas kernels for 4%

profile of v3, /device:TPU:1, one launch (start us, length us, event | category | flops | bytes accessed | tf_op | source)
XLA Modules:
  0.0 151.5 jit_solution(15635719784389401171)
XLA Ops:
  9.6 4.8 %all-to-all-start = ((bf16[4,128,256]{2,1,0:T(8,128)(2,1)}), bf16[4,128,256]{2,1,0:T(8,128)(2,1)S(1)}, u32[]{:S(2)}, u32[]{:S(2)}) async-start(bf16[4,128,256]{2,1,0:T(8,128)(2,1)} %shard_map.103), calls=%async_computation | async-start | bytes 524288 | tf_op jit(solution)/shard_map/all_to_all | solution.py:221
  16.7 1.6 %copy-done.1 = bf16[1024,1024]{1,0:T(8,128)(2,1)S(1)} copy-done((bf16[1024,1024]{1,0:T(8,128)(2,1)S(1)}, bf16[1024,1024]{1,0:T(8,128)(2,1)}, u32[]{:S(2)}) %copy-start.1) | copy-done | bytes 2097176
  20.4 2.2 %shard_map.104 = bf16[4,400,256]{2,1,0:T(8,128)(2,1)} custom-call(bf16[224,1024]{1,0:T(8,128)(2,1)S(1)} %copy-done.3, bf16[224,1024]{1,0:T(8,128)(2,1)S(1)} %copy-done.2, bf16[1024,1024]{1,0:T(8,128)(2,1)S(1)} %copy-done.1, bf16[512,1024]{1,0:T(8,128)(2,1)S(1)} %copy-done, bf16[16,256]{1,0:T(8,128)(2,1)S(1)} %pad.9.usage_ref), custom_call_target="tpu_custom_call" | custom-call | tf_op jit(solution)/shard_map/pallas_call | solution.py:22
  22.5 4.2 %all-to-all-start.1 = ((bf16[4,400,256]{2,1,0:T(8,128)(2,1)}), bf16[4,400,256]{2,1,0:T(8,128)(2,1)S(1)}, u32[]{:S(2)}, u32[]{:S(2)}) async-start(bf16[4,400,256]{2,1,0:T(8,128)(2,1)} %shard_map.104), calls=%async_computation.1 | async-start | bytes 1638400 | tf_op jit(solution)/shard_map/all_to_all | solution.py:221
  26.8 11.1 %collective-permute-start.1 = (bf16[4,128,256]{2,1,0:T(8,128)(2,1)S(1)}, bf16[4,128,256]{2,1,0:T(8,128)(2,1)S(1)}, u32[]{:S(2)}, u32[]{:S(2)}) collective-permute-start(bf16[4,128,256]{2,1,0:T(8,128)(2,1)S(1)} %all-to-all-done.ring0), channel_id=1, source_target_pairs={{4,0},{8,4},{12,8},{16,12},{20,16},{24,20},{28,24},{32,28},{36,32}... | collective-permute-start | bytes 786440 | tf_op jit(solution)/shard_map/ppermute | solution.py:217
  37.9 3.1 %collective-permute-start = (bf16[3,128,256]{2,1,0:T(8,128)(2,1)S(1)}, bf16[3,128,256]{2,1,0:T(8,128)(2,1)S(1)}, u32[]{:S(2)}, u32[]{:S(2)}) collective-permute-start(bf16[3,128,256]{2,1,0:T(8,128)(2,1)S(1)} %slice.4), channel_id=1, source_target_pairs={{8,0},{12,4},{16,8},{20,12},{24,16},{28,20},{32,24},{36,28},{40,32... | collective-permute-start | bytes 589832 | tf_op jit(solution)/shard_map/ppermute | solution.py:217
  42.0 1.7 %shard_map.105.before = f32[4,128,256]{2,1,0:T(8,128)S(1)} custom-call(bf16[4,128,256]{2,1,0:T(8,128)(2,1)S(1)} %all-to-all-done.ring0, bf16[4,128,256]{2,1,0:T(8,128)(2,1)S(1)} %collective-permute-done.1.ring1, bf16[4,400,256]{2,1,0:T(8,128)(2,1)S(1)} %all-to-all-done.1.bundle.refs_1_), custom_call_target="tpu_custom_call" | custom-call | tf_op jit(solution)/shard_map/pallas_call | solution.py:22
  43.6 5.0 %collective-permute-done.ring2 = bf16[3,128,256]{2,1,0:T(8,128)(2,1)S(1)} collective-permute-done((bf16[3,128,256]{2,1,0:T(8,128)(2,1)S(1)}, bf16[3,128,256]{2,1,0:T(8,128)(2,1)S(1)}, u32[]{:S(2)}, u32[]{:S(2)}) %collective-permute-start) | collective-permute-done | bytes 196640 | tf_op jit(solution)/shard_map/ppermute | solution.py:217
  48.6 7.5 %all-gather.3.cloned.1.call-done = bf16[896,1024]{1,0:T(8,128)(2,1)} async-done(((bf16[224,1024]{1,0:T(8,128)(2,1)}), bf16[896,1024]{1,0:T(8,128)(2,1)}) %all-gather.3.cloned.1.call-update) | async-done | bytes 1835024 | tf_op jit(solution)/shard_map/all_gather | solution.py:262
  57.0 7.2 %all_to_all.30.refs_2_ = f32[4,16,256]{2,1,0:T(8,128)S(1)} all-to-all(f32[4,16,256]{2,1,0:T(8,128)S(1)} %broadcast_in_dim.48), channel_id=1, replica_groups=mesh['y'=4,'core'=2,'zh'=4,'zl'=4,'x'=4] {'x'}, dimensions={0} | all-to-all | bytes 131072 | tf_op jit(solution)/shard_map/all_to_all | solution.py:221
  64.1 1.5 copy-done.5
  66.5 3.0 %shard_map.108 = (bf16[4,128,256]{2,1,0:T(8,128)(2,1)}, bf16[3,128,256]{2,1,0:T(8,128)(2,1)}) custom-call(bf16[4,128,256]{2,1,0:T(8,128)(2,1)S(1)} %collective-permute-done.1.ring1, bf16[3,128,256]{2,1,0:T(8,128)(2,1)S(1)} %collective-permute-done.ring2, bf16[4,400,256]{2,1,0:T(8,128)(2,1)S(1)} %all-to-all-done.1.bundle.refs_1_, ...), custom_call_target="tpu_custom_call" | custom-call | tf_op jit(solution)/shard_map/pallas_call | solution.py:22
  69.5 14.8 %all_to_all.31 = bf16[8,32,512]{2,1,0:T(8,128)(2,1)S(1)} all-to-all(bf16[8,32,512]{2,1,0:T(8,128)(2,1)S(1)} %bitcast.11), channel_id=1, replica_groups=mesh['y'=4,'core'=2,'zh'=4,'zl'=4,'x'=4] {'core','zl'}, dimensions={0} | all-to-all | bytes 524288 | tf_op jit(solution)/shard_map/all_to_all | solution.py:221
  85.0 12.8 %all-to-all-start.4 = ((bf16[16,8,512]{2,1,0:T(8,128)(2,1)}), bf16[16,8,512]{2,1,0:T(8,128)(2,1)S(1)}, u32[]{:S(2)}, u32[]{:S(2)}) async-start(bf16[16,8,512]{2,1,0:T(8,128)(2,1)} %bitcast.4), calls=%async_computation.4 | async-start | bytes 262144 | tf_op jit(solution)/shard_map/all_to_all | solution.py:221
  97.8 1.9 %collective-permute-start.2 = (bf16[4,128,256]{2,1,0:T(8,128)(2,1)}, bf16[4,128,256]{2,1,0:T(8,128)(2,1)}, u32[]{:S(2)}, u32[]{:S(2)}) collective-permute-start(bf16[4,128,256]{2,1,0:T(8,128)(2,1)} %get-tuple-element.39), channel_id=1, source_target_pairs={{60,0},{0,4},{4,8},{8,12},{12,16},{16,20},{20,24},{24,28},{28,32},... | collective-permute-start | bytes 786440 | tf_op jit(solution)/shard_map/ppermute | solution.py:217
  99.7 2.2 %collective-permute-start.3 = (bf16[3,128,256]{2,1,0:T(8,128)(2,1)}, bf16[3,128,256]{2,1,0:T(8,128)(2,1)}, u32[]{:S(2)}, u32[]{:S(2)}) collective-permute-start(bf16[3,128,256]{2,1,0:T(8,128)(2,1)} %get-tuple-element.40), channel_id=1, source_target_pairs={{56,0},{60,4},{0,8},{4,12},{8,16},{12,20},{16,24},{20,28},{24,32},... | collective-permute-start | bytes 589832 | tf_op jit(solution)/shard_map/ppermute | solution.py:217
  102.0 1.3 shard_map.109.back0
  103.3 8.7 %all-to-all-done.4 = bf16[16,8,512]{2,1,0:T(8,128)(2,1)S(1)} async-done(((bf16[16,8,512]{2,1,0:T(8,128)(2,1)}), bf16[16,8,512]{2,1,0:T(8,128)(2,1)S(1)}, u32[]{:S(2)}, u32[]{:S(2)}) %all-to-all-start.4) | async-done | bytes 131104 | tf_op jit(solution)/shard_map/all_to_all | solution.py:221
  112.0 7.3 %collective-permute-done.3.back2 = bf16[3,128,256]{2,1,0:T(8,128)(2,1)} collective-permute-done((bf16[3,128,256]{2,1,0:T(8,128)(2,1)}, bf16[3,128,256]{2,1,0:T(8,128)(2,1)}, u32[]{:S(2)}, u32[]{:S(2)}) %collective-permute-start.3) | collective-permute-done | bytes 196640 | tf_op jit(solution)/shard_map/ppermute | solution.py:217
  121.3 2.7 %collective-permute-start.4 = (bf16[256,256]{1,0:T(8,128)(2,1)S(1)}, bf16[256,256]{1,0:T(8,128)(2,1)S(1)}, u32[]{:S(2)}, u32[]{:S(2)}) collective-permute-start(bf16[256,256]{1,0:T(8,128)(2,1)S(1)} %get-tuple-element.45), channel_id=1, source_target_pairs={{0,1},{1,2},{2,3},{3,0},{4,5},{5,6},{6,7},{7,4},{8,9},{9,10},{10,1... | collective-permute-start | bytes 393224 | tf_op jit(solution)/shard_map/ppermute | solution.py:322
  124.0 4.3 %collective-permute-start.5 = (bf16[256,256]{1,0:T(8,128)(2,1)S(1)}, bf16[256,256]{1,0:T(8,128)(2,1)S(1)}, u32[]{:S(2)}, u32[]{:S(2)}) collective-permute-start(bf16[256,256]{1,0:T(8,128)(2,1)S(1)} %get-tuple-element.46), channel_id=1, source_target_pairs={{0,2},{1,3},{2,0},{3,1},{4,6},{5,7},{6,4},{7,5},{8,10},{9,11},{10,... | collective-permute-start | bytes 393224 | tf_op jit(solution)/shard_map/ppermute | solution.py:322
  128.3 3.1 %collective-permute-start.6 = (bf16[256,256]{1,0:T(8,128)(2,1)S(1)}, bf16[256,256]{1,0:T(8,128)(2,1)S(1)}, u32[]{:S(2)}, u32[]{:S(2)}) collective-permute-start(bf16[256,256]{1,0:T(8,128)(2,1)S(1)} %get-tuple-element.47), channel_id=1, source_target_pairs={{0,3},{1,0},{2,1},{3,2},{4,7},{5,4},{6,5},{7,6},{8,11},{9,8},{10,9... | collective-permute-start | bytes 393224 | tf_op jit(solution)/shard_map/ppermute | solution.py:322
  131.5 11.0 %all_to_all.32 = f32[8,8,512]{2,1,0:T(8,128)S(1)} all-to-all(f32[8,8,512]{2,1,0:T(8,128)S(1)} %broadcast_in_dim.51), channel_id=1, replica_groups=mesh['y'=4,'core'=2,'zh'=4,'zl'=4,'x'=4] {'y','core'}, dimensions={0} | all-to-all | bytes 262144 | tf_op jit(solution)/shard_map/all_to_all | solution.py:221
  143.2 1.5 shard_map.111
  (42 shorter events, 12.7 us)
Async XLA Ops:
  7.2 9.6 %copy-start = (bf16[512,1024]{1,0:T(8,128)(2,1)S(1)}, bf16[512,1024]{1,0:T(8,128)(2,1)}, u32[]{:S(2)}) copy-start(bf16[512,1024]{1,0:T(8,128)(2,1)} %out_ref.3) | copy-start | bytes 3145732
  7.2 49.0 %all-gather.3.cloned.1.call-start = ((), (), s32[]{:S(2)}) async-start(), calls=%async_computation.6 | async-start | bytes 2293760 | tf_op jit(solution)/shard_map/all_gather | solution.py:262
  7.9 1.0 copy-start.6
  9.6 12.9 %all-to-all-start = ((bf16[4,128,256]{2,1,0:T(8,128)(2,1)}), bf16[4,128,256]{2,1,0:T(8,128)(2,1)S(1)}, u32[]{:S(2)}, u32[]{:S(2)}) async-start(bf16[4,128,256]{2,1,0:T(8,128)(2,1)} %shard_map.103), calls=%async_computation | async-start | bytes 524288 | tf_op jit(solution)/shard_map/all_to_all | solution.py:221
  16.7 1.6 %copy-start.1 = (bf16[1024,1024]{1,0:T(8,128)(2,1)S(1)}, bf16[1024,1024]{1,0:T(8,128)(2,1)}, u32[]{:S(2)}) copy-start(bf16[1024,1024]{1,0:T(8,128)(2,1)} %in_ref.1) | copy-start | bytes 6291460
  18.3 1.0 copy-start.2
  19.3 1.0 copy-start.3
  22.5 19.4 %all-to-all-start.1 = ((bf16[4,400,256]{2,1,0:T(8,128)(2,1)}), bf16[4,400,256]{2,1,0:T(8,128)(2,1)S(1)}, u32[]{:S(2)}, u32[]{:S(2)}) async-start(bf16[4,400,256]{2,1,0:T(8,128)(2,1)} %shard_map.104), calls=%async_computation.1 | async-start | bytes 1638400 | tf_op jit(solution)/shard_map/all_to_all | solution.py:221
  26.8 15.2 %collective-permute-start.1 = (bf16[4,128,256]{2,1,0:T(8,128)(2,1)S(1)}, bf16[4,128,256]{2,1,0:T(8,128)(2,1)S(1)}, u32[]{:S(2)}, u32[]{:S(2)}) collective-permute-start(bf16[4,128,256]{2,1,0:T(8,128)(2,1)S(1)} %all-to-all-done.ring0), channel_id=1, source_target_pairs={{4,0},{8,4},{12,8},{16,12},{20,16},{24,20},{28,24},{32,28},{36,32}... | collective-permute-start | bytes 786440 | tf_op jit(solution)/shard_map/ppermute | solution.py:217
  37.9 10.7 %collective-permute-start = (bf16[3,128,256]{2,1,0:T(8,128)(2,1)S(1)}, bf16[3,128,256]{2,1,0:T(8,128)(2,1)S(1)}, u32[]{:S(2)}, u32[]{:S(2)}) collective-permute-start(bf16[3,128,256]{2,1,0:T(8,128)(2,1)S(1)} %slice.4), channel_id=1, source_target_pairs={{8,0},{12,4},{16,8},{20,12},{24,16},{28,20},{32,24},{36,28},{40,32... | collective-permute-start | bytes 589832 | tf_op jit(solution)/shard_map/ppermute | solution.py:217
  64.1 1.5 copy-start.5
  66.5 3.0 %copy-start.7 = (bf16[4,128,256]{2,1,0:T(8,128)(2,1)}, bf16[4,128,256]{2,1,0:T(8,128)(2,1)S(1)}, u32[]{:S(2)}) copy-start(bf16[4,128,256]{2,1,0:T(8,128)(2,1)S(1)} %get-tuple-element.31.gated_ref) | copy-start | bytes 786436
  84.3 58.9 %copy-start.4 = (bf16[224,1024]{1,0:T(8,128)(2,1)S(1)}, bf16[224,1024]{1,0:T(8,128)(2,1)}, u32[]{:S(2)}) copy-start(bf16[224,1024]{1,0:T(8,128)(2,1)} %cand_ref.3) | copy-start | bytes 1376260
  85.0 27.0 %all-to-all-start.4 = ((bf16[16,8,512]{2,1,0:T(8,128)(2,1)}), bf16[16,8,512]{2,1,0:T(8,128)(2,1)S(1)}, u32[]{:S(2)}, u32[]{:S(2)}) async-start(bf16[16,8,512]{2,1,0:T(8,128)(2,1)} %bitcast.4), calls=%async_computation.4 | async-start | bytes 262144 | tf_op jit(solution)/shard_map/all_to_all | solution.py:221
  97.8 21.5 %collective-permute-start.2 = (bf16[4,128,256]{2,1,0:T(8,128)(2,1)}, bf16[4,128,256]{2,1,0:T(8,128)(2,1)}, u32[]{:S(2)}, u32[]{:S(2)}) collective-permute-start(bf16[4,128,256]{2,1,0:T(8,128)(2,1)} %get-tuple-element.39), channel_id=1, source_target_pairs={{60,0},{0,4},{4,8},{8,12},{12,16},{16,20},{20,24},{24,28},{28,32},... | collective-permute-start | bytes 786440 | tf_op jit(solution)/shard_map/ppermute | solution.py:217
  99.7 19.5 %collective-permute-start.3 = (bf16[3,128,256]{2,1,0:T(8,128)(2,1)}, bf16[3,128,256]{2,1,0:T(8,128)(2,1)}, u32[]{:S(2)}, u32[]{:S(2)}) collective-permute-start(bf16[3,128,256]{2,1,0:T(8,128)(2,1)} %get-tuple-element.40), channel_id=1, source_target_pairs={{56,0},{60,4},{0,8},{4,12},{8,16},{12,20},{16,24},{20,28},{24,32},... | collective-permute-start | bytes 589832 | tf_op jit(solution)/shard_map/ppermute | solution.py:217
  119.3 1.0 copy-start.8
  121.3 21.8 %collective-permute-start.4 = (bf16[256,256]{1,0:T(8,128)(2,1)S(1)}, bf16[256,256]{1,0:T(8,128)(2,1)S(1)}, u32[]{:S(2)}, u32[]{:S(2)}) collective-permute-start(bf16[256,256]{1,0:T(8,128)(2,1)S(1)} %get-tuple-element.45), channel_id=1, source_target_pairs={{0,1},{1,2},{2,3},{3,0},{4,5},{5,6},{6,7},{7,4},{8,9},{9,10},{10,1... | collective-permute-start | bytes 393224 | tf_op jit(solution)/shard_map/ppermute | solution.py:322
  124.0 19.1 %collective-permute-start.5 = (bf16[256,256]{1,0:T(8,128)(2,1)S(1)}, bf16[256,256]{1,0:T(8,128)(2,1)S(1)}, u32[]{:S(2)}, u32[]{:S(2)}) collective-permute-start(bf16[256,256]{1,0:T(8,128)(2,1)S(1)} %get-tuple-element.46), channel_id=1, source_target_pairs={{0,2},{1,3},{2,0},{3,1},{4,6},{5,7},{6,4},{7,5},{8,10},{9,11},{10,... | collective-permute-start | bytes 393224 | tf_op jit(solution)/shard_map/ppermute | solution.py:322
  128.3 14.8 %collective-permute-start.6 = (bf16[256,256]{1,0:T(8,128)(2,1)S(1)}, bf16[256,256]{1,0:T(8,128)(2,1)S(1)}, u32[]{:S(2)}, u32[]{:S(2)}) collective-permute-start(bf16[256,256]{1,0:T(8,128)(2,1)S(1)} %get-tuple-element.47), channel_id=1, source_target_pairs={{0,3},{1,0},{2,1},{3,2},{4,7},{5,4},{6,5},{7,6},{8,11},{9,8},{10,9... | collective-permute-start | bytes 393224 | tf_op jit(solution)/shard_map/ppermute | solution.py:322
Sparse Core Ops, SparseCore 0:
  10.1 46.0 all-gather.2

commit v4 on v3

--- a/solution.py
+++ b/solution.py
@@ -48,7 +48,21 @@
         chunks_ref[head, :, size:] = history_ref[:, (heads + head) * size : (heads + head + 1) * size]
 
 
-def prepare_kernel(cand_ref, cot_ref, in_ref, out_ref, usage_ref, bundle_ref):
+def used_blocks(blocks_ref, length_ref, owner_ref):
+    requests, width = blocks_ref.shape
+    owners = owner_ref[...]
+    positions = lax.broadcasted_iota(jnp.int32, (16, owners.shape[1]), 0)
+    usage = jnp.zeros(positions.shape, F32)
+    for request in range(requests):
+        used = jnp.zeros(positions.shape, F32)
+        for entry in range(width):
+            block = jnp.where(entry < length_ref[request], blocks_ref[request, entry], -1)
+            used = used + jnp.where(positions == block, 1.0, 0.0)
+        usage = usage + jnp.where(owners == request, used, 0.0)
+    return usage
+
+
+def prepare_kernel(blocks_ref, length_ref, owner_ref, cand_ref, cot_ref, in_ref, out_ref, bundle_ref):
     rows = cand_ref[...].astype(F32)
     centered = rows - jnp.mean(rows, axis=-1, keepdims=True)
     inv_scale = lax.rsqrt(jnp.mean(centered * centered, axis=-1, keepdims=True) + 1e-05)
@@ -57,8 +71,9 @@
     zed_grad = lax.dot_general(out_ref[...], cot_ref[...], NT, preferred_element_type=F32)
     inner, count = out_ref.shape[0], cand_ref.shape[0]
     size = inner // HEADS
-    bundle_ref[:, : 3 * size, count:] = jnp.zeros(
-        (HEADS, 3 * size, bundle_ref.shape[2] - count), BF16
+    usage = used_blocks(blocks_ref, length_ref, owner_ref).astype(BF16)
+    bundle_ref[:, :, count:] = jnp.zeros(
+        (HEADS, bundle_ref.shape[1], bundle_ref.shape[2] - count), BF16
     )
     for head in range(HEADS):
         part = slice(head * size, (head + 1) * size)
@@ -67,7 +82,7 @@
         bundle_ref[head, 0:size, :count] = projected[part].astype(BF16)
         bundle_ref[head, size : 2 * size, :count] = gating.astype(BF16)
         bundle_ref[head, 2 * size : 3 * size, :count] = (zed_grad[part] * gating).astype(BF16)
-        bundle_ref[head, 3 * size :] = usage_ref[...]
+        bundle_ref[head, 3 * size :, :count] = usage
 
 
 def scored(ring, blocks_ref, bundle_ref, group):
@@ -113,13 +128,9 @@
         stats_ref[4 * group + 3 : 4 * group + 4] = jnp.sum(dy * centered, axis=0, keepdims=True)
 
 
-def norm_kernel(total_cands, attended, bundle, stats, cots_ref, gated_ref, grad_ref, out_grad_ref, cots, arrival):
-    copy = pltpu.make_async_copy(cots_ref, cots, arrival)
-    copy.start()
+def norm_kernel(attended, bundle, stats, gated_ref, grad_ref):
     size = attended.shape[1]
-    count = cots.shape[1]
     width = HEADS * size
-    total = None
     for group in range(HEADS):
         head_stats = [stats[head, 4 * group : 4 * group + 4] for head in range(HEADS)]
         mean = sum(one[0:1] for one in head_stats) * (1.0 / HEADS)
@@ -130,13 +141,16 @@
         mixed = sum(one[3:4] + off * one[2:3] for one, off in zip(head_stats, apart))
         mean_mixed = mixed * inv_scale * (1.0 / width)
         normed = (attended[group] - mean) * inv_scale
-        gated = (normed * bundle[group, size : 2 * size].astype(F32)).astype(BF16)
         dy = bundle[group, 2 * size : 3 * size].astype(F32)
-        gated_ref[group] = gated
+        gated_ref[group] = (normed * bundle[group, size : 2 * size].astype(F32)).astype(BF16)
         grad_ref[group] = (inv_scale * (dy - mean_dy - normed * mean_mixed)).astype(BF16)
-    copy.wait()
-    for group in range(HEADS):
-        part = jnp.dot(gated_ref[group, :, :count], cots[group], preferred_element_type=F32)
+
+
+def out_grad_kernel(total_cands, gated, cots, out_grad_ref):
+    count = cots.shape[1]
+    total = None
+    for group in range(HEADS):
+        part = jnp.dot(gated[group, :, :count], cots[group], preferred_element_type=F32)
         total = part if total is None else total + part
     total = (total * (1.0 / math.sqrt(total_cands))).astype(BF16)
     halves, rows_of, lines, columns = out_grad_ref.shape
@@ -230,16 +244,6 @@
     return jnp.sum(parts.astype(F32), axis=0)
 
 
-def used_blocks(request_blocks, request_length, candidate_request):
-    positions = jnp.arange(request_blocks.shape[1], dtype=jnp.int32)
-    matches = request_blocks[:, :, None] == positions[None, None, :]
-    in_length = positions[None, :] < request_length[:, None]
-    used = jnp.sum(jnp.where(matches & in_length[:, :, None], 1.0, 0.0), axis=1)
-    ids = jnp.arange(request_blocks.shape[0], dtype=jnp.int32)
-    member = jnp.where(candidate_request[None, :] == ids[:, None], 1.0, 0.0)
-    return jnp.sum(used[:, :, None] * member[:, None, :], axis=0)
-
-
 def on_device(
     candidates,
     cotangent,
@@ -263,25 +267,22 @@
     ring_shape = shaped((HEADS, tall, 2 * size), BF16)
     ring0 = exchanged(on_core(split_kernel, ring_shape, history), "x")
 
-    owners = jnp.pad(candidate_request, (0, lanes - count), constant_values=-1)
-    usage = used_blocks(request_blocks, request_length, owners).astype(BF16)
-    usage = jnp.pad(usage, ((0, 16 - usage.shape[0]), (0, 0)))
     ring2 = moved(ring0[: HEADS - 1], 2)
     ring1 = moved(ring0, 1)
     bundle = on_core(
         prepare_kernel,
         shaped((HEADS, 3 * size + 16, lanes), BF16),
+        candidate_request.reshape(1, count),
         candidates,
         cotangent,
         in_weight,
         out_weight,
-        usage,
+        scalars=(request_blocks, request_length),
     )
     bundle = exchanged(bundle, "x")
 
     attended_shape = shaped((HEADS, size, lanes), F32)
     before = on_core(early_kernel, attended_shape, ring0, ring1, bundle)
-    ring2, cots = barrier((ring2, cots))
     attended, stats = on_core(
         late_kernel, (attended_shape, shaped((4 * HEADS, lanes), F32)), ring2, bundle, before
     )
@@ -289,31 +290,25 @@
     head_shape = shaped((HEADS, size, lanes), BF16)
     cores, zh, zl, xs = (lax.axis_size(name) for name in ("core", "zh", "zl", "x"))
     own, half = size // (zl * xs), out_weight.shape[1] // cores
-    gated, grads, out_grad = pl.pallas_call(
-        lambda *refs: norm_kernel(total_cands, *refs),
-        out_shape=(head_shape, head_shape, shaped((cores, zl, size // zl, half), BF16)),
-        in_specs=[pl.BlockSpec(memory_space=pltpu.VMEM)] * 3 + [pl.BlockSpec(memory_space=pltpu.HBM)],
-        out_specs=(pl.BlockSpec(memory_space=pltpu.VMEM),) * 3,
-        scratch_shapes=[pltpu.VMEM(cots.shape, BF16), pltpu.SemaphoreType.DMA],
-        compiler_params=pltpu.CompilerParams(vmem_limit_bytes=12 * 1024 * 1024),
-    )(attended, bundle, stats, cots)
-
+    gated, grads = on_core(norm_kernel, (head_shape, head_shape), attended, bundle, stats)
     back1, back2 = on_core(
         far_back_kernel, (shaped(ring1.shape, BF16), shaped(ring2.shape, BF16)), ring1, ring2, bundle, grads
     )
-    out_grad, back1, back2 = barrier((out_grad, back1, back2))
     back2 = moved(back2, -2)
     back1 = moved(back1, -1)
+    out_grad = on_core(
+        lambda *refs: out_grad_kernel(total_cands, *refs),
+        shaped((cores, zl, size // zl, half), BF16),
+        gated,
+        cots,
+    )
+    out_grad, late_grads = barrier((out_grad, grads))
     part = exchanged(out_grad.reshape(cores * zl, size // zl, half), ("core", "zl"))
-    part = summed(part).astype(BF16)
-    part, grads = barrier((part, grads))
-    back0 = on_core(near_back_kernel, shaped(ring0.shape, F32), ring0, bundle, grads)
+    back0 = on_core(near_back_kernel, shaped(ring0.shape, F32), ring0, bundle, late_grads)
+    part, back0, back1, back2 = barrier((summed(part).astype(BF16), back0, back1, back2))
     part = jnp.broadcast_to(part.reshape(1, xs, own, half), (zh, xs, own, half))
     part = exchanged(part.reshape(zh * xs, own, half), ("zh", "x")).reshape(zh, xs, own, half)
     part = lax.dynamic_index_in_dim(part, lax.axis_index("zh"), axis=1, keepdims=False)
-    part, back0, back1, back2 = barrier((summed(part), back0, back1, back2))
-    part = spread_over(part, ("y", "core")).reshape(-1, cores, own, half)
-    grad_rows = summed(part).transpose(1, 0, 2).reshape(own, cores * half)
 
     parcels = on_core(
         parcel_kernel, [shaped((2 * size, lanes), BF16)] * HEADS, gated, back0, back1, back2, scalars=(place,)
@@ -322,6 +317,10 @@
         lax.ppermute(parcel, "x", [(i, (i + step) % HEADS) for i in range(HEADS)]) if step else parcel
         for step, parcel in enumerate(parcels)
     ]
+    part, arrived = barrier((summed(part), arrived))
+    part = spread_over(part, ("y", "core")).reshape(-1, cores, own, half)
+    grad_rows = summed(part).transpose(1, 0, 2).reshape(own, cores * half)
+
     layer_out, grad_history = on_core(
         join_kernel,
         (shaped(candidates.shape, BF16), shaped(history.shape, BF16)),

time: 154 us -> 141 us (0.916)
  the two profiles are of different devices: /device:TPU:1 before, /device:TPU:32 now
where the time goes in v4:
time: 141 us; the launch traced here: 140 us
  starting transfers between devices  60.6 us (43%)
  waiting for transfers between devices  28.5 us (20%)
  Pallas kernels  14.2 us (10%)
  between operations  14.2 us (10%)
  local copies, waits for them, and re-layouts  10.5 us (7%)
  blocking collectives  9.95 us (7%)
  other arithmetic  1.62 us (1%)
    all_to_all x5, starting transfers between devices, exchanged(): return lax.all_to_all(chunks, axis, 0, 0, tiled=True)  27.8 us
    ppermute x4, starting transfers between devices, moved(): lax.ppermute(block, DEPTH, [((i + distance) % size, i) for i in range(siz...  20.9 us
    ppermute x4, waiting for transfers between devices, moved(): lax.ppermute(block, DEPTH, [((i + distance) % size, i) for i in range(siz...  16.2 us
    pallas_call x10, Pallas kernels, on_core(): pl.pallas_call(kernel, out_shape=outs, in_specs=[pl.BlockSpec(memory_spac...  14.2 us
    ppermute x3, starting transfers between devices, on_device(): lax.ppermute(parcel, 'x', [(i, (i + step) % HEADS) for i in range(HEADS)])  11.8 us
    all_to_all x5, waiting for transfers between devices, exchanged(): return lax.all_to_all(chunks, axis, 0, 0, tiled=True)  11.3 us
    all_to_all x1, blocking collectives, exchanged(): return lax.all_to_all(chunks, axis, 0, 0, tiled=True)  9.95 us
    unnamed x24, local copies, waits for them, and re-layouts  9.11 us
  transfers between devices with their start and end apart: 13, of which 6 were waited for; matrix products, arithmetic and copies ran while one was open for 1% of the time, Pallas kernels for 9%

profile of v4, /device:TPU:32, one launch (start us, length us, event | category | flops | bytes accessed | tf_op | source)
XLA Modules:
  0.0 139.6 jit_solution(13387295677299985682)
XLA Ops:
  9.6 4.3 %all-to-all-start = ((bf16[4,128,256]{2,1,0:T(8,128)(2,1)}), bf16[4,128,256]{2,1,0:T(8,128)(2,1)S(1)}, u32[]{:S(2)}, u32[]{:S(2)}) async-start(bf16[4,128,256]{2,1,0:T(8,128)(2,1)} %shard_map.103), calls=%async_computation | async-start | bytes 524288 | tf_op jit(solution)/shard_map/all_to_all | solution.py:235
  13.9 1.6 %copy-done.1 = bf16[1024,1024]{1,0:T(8,128)(2,1)S(1)} copy-done((bf16[1024,1024]{1,0:T(8,128)(2,1)S(1)}, bf16[1024,1024]{1,0:T(8,128)(2,1)}, u32[]{:S(2)}) %copy-start.1) | copy-done | bytes 2097176
  19.6 2.7 %shard_map.104 = bf16[4,400,256]{2,1,0:T(8,128)(2,1)} custom-call(s32[2,8]{1,0:T(2,128)S(1)} %copy-done.9, s32[2]{0:T(128)S(1)} %copy-done.11, s32[1,224]{1,0:T(1,128)S(1)} %bitcast.12, bf16[224,1024]{1,0:T(8,128)(2,1)S(1)} %copy-done.3, bf16[224,1024]{1,0:T(8,128)(2,1)S(1)} %copy-done.2, bf16[1024,1024]{1,0:T(8,128)(2,1)S(1)} %copy-done.1, ...), custom_call_target="tpu_custom_call" | custom-call | tf_op jit(solution)/shard_map/pallas_call | solution.py:22
  22.3 4.8 %all-to-all-start.1 = ((bf16[4,400,256]{2,1,0:T(8,128)(2,1)}), bf16[4,400,256]{2,1,0:T(8,128)(2,1)S(1)}, u32[]{:S(2)}, u32[]{:S(2)}) async-start(bf16[4,400,256]{2,1,0:T(8,128)(2,1)} %shard_map.104), calls=%async_computation.1 | async-start | bytes 1638400 | tf_op jit(solution)/shard_map/all_to_all | solution.py:235
  27.1 6.5 %collective-permute-start.1 = (bf16[4,128,256]{2,1,0:T(8,128)(2,1)S(1)}, bf16[4,128,256]{2,1,0:T(8,128)(2,1)S(1)}, u32[]{:S(2)}, u32[]{:S(2)}) collective-permute-start(bf16[4,128,256]{2,1,0:T(8,128)(2,1)S(1)} %all-to-all-done.ring0), channel_id=1, source_target_pairs={{4,0},{8,4},{12,8},{16,12},{20,16},{24,20},{28,24},{32,28},{36,32}... | collective-permute-start | bytes 786440 | tf_op jit(solution)/shard_map/ppermute | solution.py:231
  33.6 7.4 %collective-permute-start = (bf16[3,128,256]{2,1,0:T(8,128)(2,1)S(1)}, bf16[3,128,256]{2,1,0:T(8,128)(2,1)S(1)}, u32[]{:S(2)}, u32[]{:S(2)}) collective-permute-start(bf16[3,128,256]{2,1,0:T(8,128)(2,1)S(1)} %slice.4), channel_id=1, source_target_pairs={{8,0},{12,4},{16,8},{20,12},{24,16},{28,20},{32,24},{36,28},{40,32... | collective-permute-start | bytes 589832 | tf_op jit(solution)/shard_map/ppermute | solution.py:231
  41.0 3.5 %all-to-all-done.1.bundle = bf16[4,400,256]{2,1,0:T(8,128)(2,1)S(1)} async-done(((bf16[4,400,256]{2,1,0:T(8,128)(2,1)}), bf16[4,400,256]{2,1,0:T(8,128)(2,1)S(1)}, u32[]{:S(2)}, u32[]{:S(2)}) %all-to-all-start.1) | async-done | bytes 819232 | tf_op jit(solution)/shard_map/all_to_all | solution.py:235
  44.5 1.7 %shard_map.105.before = f32[4,128,256]{2,1,0:T(8,128)S(1)} custom-call(bf16[4,128,256]{2,1,0:T(8,128)(2,1)S(1)} %all-to-all-done.ring0, bf16[4,128,256]{2,1,0:T(8,128)(2,1)S(1)} %collective-permute-done.1.ring1, bf16[4,400,256]{2,1,0:T(8,128)(2,1)S(1)} %all-to-all-done.1.bundle), custom_call_target="tpu_custom_call" | custom-call | tf_op jit(solution)/shard_map/pallas_call | solution.py:22
  46.2 2.1 %collective-permute-done.ring2 = bf16[3,128,256]{2,1,0:T(8,128)(2,1)S(1)} collective-permute-done((bf16[3,128,256]{2,1,0:T(8,128)(2,1)S(1)}, bf16[3,128,256]{2,1,0:T(8,128)(2,1)S(1)}, u32[]{:S(2)}, u32[]{:S(2)}) %collective-permute-start) | collective-permute-done | bytes 196640 | tf_op jit(solution)/shard_map/ppermute | solution.py:231
  49.1 9.9 %all_to_all.30.stats = f32[4,16,256]{2,1,0:T(8,128)S(1)} all-to-all(f32[4,16,256]{2,1,0:T(8,128)S(1)} %broadcast_in_dim.8), channel_id=1, replica_groups=mesh['y'=4,'core'=2,'zh'=4,'zl'=4,'x'=4] {'x'}, dimensions={0} | all-to-all | bytes 131072 | tf_op jit(solution)/shard_map/all_to_all | solution.py:235
  59.3 1.6 %copy-done.5 = bf16[896,1024]{1,0:T(8,128)(2,1)S(1)} copy-done((bf16[896,1024]{1,0:T(8,128)(2,1)S(1)}, bf16[896,1024]{1,0:T(8,128)(2,1)}, u32[]{:S(2)}) %copy-start.5) | copy-done | bytes 1835032
  62.1 7.4 %all-to-all-start.3 = ((bf16[8,32,512]{2,1,0:T(8,128)(2,1)}), bf16[8,32,512]{2,1,0:T(8,128)(2,1)}, u32[]{:S(2)}, u32[]{:S(2)}) async-start(bf16[8,32,512]{2,1,0:T(8,128)(2,1)} %bitcast.3), calls=%async_computation.3 | async-start | bytes 524288 | tf_op jit(solution)/shard_map/all_to_all | solution.py:235
  69.5 3.0 %shard_map.110 = (bf16[4,128,256]{2,1,0:T(8,128)(2,1)}, bf16[3,128,256]{2,1,0:T(8,128)(2,1)}) custom-call(bf16[4,128,256]{2,1,0:T(8,128)(2,1)S(1)} %collective-permute-done.1.ring1, bf16[3,128,256]{2,1,0:T(8,128)(2,1)S(1)} %collective-permute-done.ring2, bf16[4,400,256]{2,1,0:T(8,128)(2,1)S(1)} %all-to-all-done.1.bundle, ...), custom_call_target="tpu_custom_call" | custom-call | tf_op jit(solution)/shard_map/pallas_call | solution.py:22
  72.5 3.4 %collective-permute-start.2 = (bf16[4,128,256]{2,1,0:T(8,128)(2,1)}, bf16[4,128,256]{2,1,0:T(8,128)(2,1)}, u32[]{:S(2)}, u32[]{:S(2)}) collective-permute-start(bf16[4,128,256]{2,1,0:T(8,128)(2,1)} %get-tuple-element.32), channel_id=1, source_target_pairs={{60,0},{0,4},{4,8},{8,12},{12,16},{16,20},{20,24},{24,28},{28,32},... | collective-permute-start | bytes 786440 | tf_op jit(solution)/shard_map/ppermute | solution.py:231
  75.8 3.7 %collective-permute-start.3 = (bf16[3,128,256]{2,1,0:T(8,128)(2,1)}, bf16[3,128,256]{2,1,0:T(8,128)(2,1)}, u32[]{:S(2)}, u32[]{:S(2)}) collective-permute-start(bf16[3,128,256]{2,1,0:T(8,128)(2,1)} %get-tuple-element.33), channel_id=1, source_target_pairs={{56,0},{60,4},{0,8},{4,12},{8,16},{12,20},{16,24},{20,28},{24,32},... | collective-permute-start | bytes 589832 | tf_op jit(solution)/shard_map/ppermute | solution.py:231
  82.8 14.1 %collective-permute-done.3.back2 = bf16[3,128,256]{2,1,0:T(8,128)(2,1)} collective-permute-done((bf16[3,128,256]{2,1,0:T(8,128)(2,1)}, bf16[3,128,256]{2,1,0:T(8,128)(2,1)}, u32[]{:S(2)}, u32[]{:S(2)}) %collective-permute-start.3) | collective-permute-done | bytes 196640 | tf_op jit(solution)/shard_map/ppermute | solution.py:231
  97.5 6.7 %all-to-all-start.4 = ((bf16[16,8,512]{2,1,0:T(8,128)(2,1)}), bf16[16,8,512]{2,1,0:T(8,128)(2,1)S(1)}, u32[]{:S(2)}, u32[]{:S(2)}) async-start(bf16[16,8,512]{2,1,0:T(8,128)(2,1)} %bitcast.5), calls=%async_computation.4 | async-start | bytes 262144 | tf_op jit(solution)/shard_map/all_to_all | solution.py:235
  105.4 3.8 %collective-permute-start.4 = (bf16[256,256]{1,0:T(8,128)(2,1)S(1)}, bf16[256,256]{1,0:T(8,128)(2,1)S(1)}, u32[]{:S(2)}, u32[]{:S(2)}) collective-permute-start(bf16[256,256]{1,0:T(8,128)(2,1)S(1)} %get-tuple-element.39), channel_id=1, source_target_pairs={{0,1},{1,2},{2,3},{3,0},{4,5},{5,6},{6,7},{7,4},{8,9},{9,10},{10,1... | collective-permute-start | bytes 393224 | tf_op jit(solution)/shard_map/ppermute | solution.py:317
  109.2 4.6 %collective-permute-start.5 = (bf16[256,256]{1,0:T(8,128)(2,1)S(1)}, bf16[256,256]{1,0:T(8,128)(2,1)S(1)}, u32[]{:S(2)}, u32[]{:S(2)}) collective-permute-start(bf16[256,256]{1,0:T(8,128)(2,1)S(1)} %get-tuple-element.40), channel_id=1, source_target_pairs={{0,2},{1,3},{2,0},{3,1},{4,6},{5,7},{6,4},{7,5},{8,10},{9,11},{10,... | collective-permute-start | bytes 393224 | tf_op jit(solution)/shard_map/ppermute | solution.py:317
  113.8 3.4 %collective-permute-start.6 = (bf16[256,256]{1,0:T(8,128)(2,1)S(1)}, bf16[256,256]{1,0:T(8,128)(2,1)S(1)}, u32[]{:S(2)}, u32[]{:S(2)}) collective-permute-start(bf16[256,256]{1,0:T(8,128)(2,1)S(1)} %get-tuple-element.41), channel_id=1, source_target_pairs={{0,3},{1,0},{2,1},{3,2},{4,7},{5,4},{6,5},{7,6},{8,11},{9,8},{10,9... | collective-permute-start | bytes 393224 | tf_op jit(solution)/shard_map/ppermute | solution.py:317
  117.2 3.1 %all-to-all-done.4 = bf16[16,8,512]{2,1,0:T(8,128)(2,1)S(1)} async-done(((bf16[16,8,512]{2,1,0:T(8,128)(2,1)}), bf16[16,8,512]{2,1,0:T(8,128)(2,1)S(1)}, u32[]{:S(2)}, u32[]{:S(2)}) %all-to-all-start.4) | async-done | bytes 131104 | tf_op jit(solution)/shard_map/all_to_all | solution.py:235
  121.4 4.6 %all-to-all-start.5 = ((f32[8,8,512]{2,1,0:T(8,128)}), f32[8,8,512]{2,1,0:T(8,128)S(1)}, u32[]{:S(2)}, u32[]{:S(2)}) async-start(f32[8,8,512]{2,1,0:T(8,128)} %broadcast_in_dim.22), calls=%async_computation.5 | async-start | bytes 262144 | tf_op jit(solution)/shard_map/all_to_all | solution.py:235
  126.0 1.5 %shard_map.112 = (bf16[224,1024]{1,0:T(8,128)(2,1)}, bf16[128,1024]{1,0:T(8,128)(2,1)}) custom-call(s32[1]{0:T(128)} %bitcast.place_ref, bf16[224,1024]{1,0:T(8,128)(2,1)S(1)} %copy-done.4, bf16[512,1024]{1,0:T(8,128)(2,1)S(1)} %copy-done, bf16[256,256]{1,0:T(8,128)(2,1)S(1)} %get-tuple-element.42.refs_0_, ...), custom_call_target="tpu_custom_call" | custom-call | tf_op jit(solution)/shard_map/pallas_call | solution.py:22
  127.5 4.6 %all-to-all-done.5 = f32[8,8,512]{2,1,0:T(8,128)S(1)} async-done(((f32[8,8,512]{2,1,0:T(8,128)}), f32[8,8,512]{2,1,0:T(8,128)S(1)}, u32[]{:S(2)}, u32[]{:S(2)}) %all-to-all-start.5) | async-done | bytes 131104 | tf_op jit(solution)/shard_map/all_to_all | solution.py:235
  (45 shorter events, 15.3 us)
Async XLA Ops:
  7.2 6.7 %copy-start = (bf16[512,1024]{1,0:T(8,128)(2,1)S(1)}, bf16[512,1024]{1,0:T(8,128)(2,1)}, u32[]{:S(2)}) copy-start(bf16[512,1024]{1,0:T(8,128)(2,1)} %out_ref.3) | copy-start | bytes 3145732
  7.2 52.1 %all-gather.3.cloned.1.call-start = ((), (), s32[]{:S(2)}) async-start(), calls=%async_computation.6 | async-start | bytes 2293760 | tf_op jit(solution)/shard_map/all_gather | solution.py:266
  7.9 1.0 copy-start.8
  9.6 12.7 %all-to-all-start = ((bf16[4,128,256]{2,1,0:T(8,128)(2,1)}), bf16[4,128,256]{2,1,0:T(8,128)(2,1)S(1)}, u32[]{:S(2)}, u32[]{:S(2)}) async-start(bf16[4,128,256]{2,1,0:T(8,128)(2,1)} %shard_map.103), calls=%async_computation | async-start | bytes 524288 | tf_op jit(solution)/shard_map/all_to_all | solution.py:235
  13.9 1.6 %copy-start.1 = (bf16[1024,1024]{1,0:T(8,128)(2,1)S(1)}, bf16[1024,1024]{1,0:T(8,128)(2,1)}, u32[]{:S(2)}) copy-start(bf16[1024,1024]{1,0:T(8,128)(2,1)} %in_ref.1) | copy-start | bytes 6291460
  15.5 1.0 copy-start.2
  16.5 1.0 copy-start.3
  17.5 0.7 copy-start.9
  18.2 0.7 copy-start.10
  22.3 22.2 %all-to-all-start.1 = ((bf16[4,400,256]{2,1,0:T(8,128)(2,1)}), bf16[4,400,256]{2,1,0:T(8,128)(2,1)S(1)}, u32[]{:S(2)}, u32[]{:S(2)}) async-start(bf16[4,400,256]{2,1,0:T(8,128)(2,1)} %shard_map.104), calls=%async_computation.1 | async-start | bytes 1638400 | tf_op jit(solution)/shard_map/all_to_all | solution.py:235
  27.1 13.9 %collective-permute-start.1 = (bf16[4,128,256]{2,1,0:T(8,128)(2,1)S(1)}, bf16[4,128,256]{2,1,0:T(8,128)(2,1)S(1)}, u32[]{:S(2)}, u32[]{:S(2)}) collective-permute-start(bf16[4,128,256]{2,1,0:T(8,128)(2,1)S(1)} %all-to-all-done.ring0), channel_id=1, source_target_pairs={{4,0},{8,4},{12,8},{16,12},{20,16},{24,20},{28,24},{32,28},{36,32}... | collective-permute-start | bytes 786440 | tf_op jit(solution)/shard_map/ppermute | solution.py:231
  33.6 14.7 %collective-permute-start = (bf16[3,128,256]{2,1,0:T(8,128)(2,1)S(1)}, bf16[3,128,256]{2,1,0:T(8,128)(2,1)S(1)}, u32[]{:S(2)}, u32[]{:S(2)}) collective-permute-start(bf16[3,128,256]{2,1,0:T(8,128)(2,1)S(1)} %slice.4), channel_id=1, source_target_pairs={{8,0},{12,4},{16,8},{20,12},{24,16},{28,20},{32,24},{36,28},{40,32... | collective-permute-start | bytes 589832 | tf_op jit(solution)/shard_map/ppermute | solution.py:231
  59.3 13.2 %copy-start.6 = (bf16[4,128,256]{2,1,0:T(8,128)(2,1)}, bf16[4,128,256]{2,1,0:T(8,128)(2,1)S(1)}, u32[]{:S(2)}) copy-start(bf16[4,128,256]{2,1,0:T(8,128)(2,1)S(1)} %get-tuple-element.31.grads) | copy-start | bytes 786436
  59.3 1.6 %copy-start.5 = (bf16[896,1024]{1,0:T(8,128)(2,1)S(1)}, bf16[896,1024]{1,0:T(8,128)(2,1)}, u32[]{:S(2)}) copy-start(bf16[896,1024]{1,0:T(8,128)(2,1)} %all-gather.3.cloned.1.call-done) | copy-start | bytes 5505028
  62.1 19.7 %all-to-all-start.3 = ((bf16[8,32,512]{2,1,0:T(8,128)(2,1)}), bf16[8,32,512]{2,1,0:T(8,128)(2,1)}, u32[]{:S(2)}, u32[]{:S(2)}) async-start(bf16[8,32,512]{2,1,0:T(8,128)(2,1)} %bitcast.3), calls=%async_computation.3 | async-start | bytes 524288 | tf_op jit(solution)/shard_map/all_to_all | solution.py:235
  72.5 24.4 %collective-permute-start.2 = (bf16[4,128,256]{2,1,0:T(8,128)(2,1)}, bf16[4,128,256]{2,1,0:T(8,128)(2,1)}, u32[]{:S(2)}, u32[]{:S(2)}) collective-permute-start(bf16[4,128,256]{2,1,0:T(8,128)(2,1)} %get-tuple-element.32), channel_id=1, source_target_pairs={{60,0},{0,4},{4,8},{8,12},{12,16},{16,20},{20,24},{24,28},{28,32},... | collective-permute-start | bytes 786440 | tf_op jit(solution)/shard_map/ppermute | solution.py:231
  75.8 50.1 %copy-start.4 = (bf16[224,1024]{1,0:T(8,128)(2,1)S(1)}, bf16[224,1024]{1,0:T(8,128)(2,1)}, u32[]{:S(2)}) copy-start(bf16[224,1024]{1,0:T(8,128)(2,1)} %cand_ref.3) | copy-start | bytes 1376260
  75.8 21.0 %collective-permute-start.3 = (bf16[3,128,256]{2,1,0:T(8,128)(2,1)}, bf16[3,128,256]{2,1,0:T(8,128)(2,1)}, u32[]{:S(2)}, u32[]{:S(2)}) collective-permute-start(bf16[3,128,256]{2,1,0:T(8,128)(2,1)} %get-tuple-element.33), channel_id=1, source_target_pairs={{56,0},{60,4},{0,8},{4,12},{8,16},{12,20},{16,24},{20,28},{24,32},... | collective-permute-start | bytes 589832 | tf_op jit(solution)/shard_map/ppermute | solution.py:231
  79.6 1.0 copy-start.7
  97.5 22.8 %all-to-all-start.4 = ((bf16[16,8,512]{2,1,0:T(8,128)(2,1)}), bf16[16,8,512]{2,1,0:T(8,128)(2,1)S(1)}, u32[]{:S(2)}, u32[]{:S(2)}) async-start(bf16[16,8,512]{2,1,0:T(8,128)(2,1)} %bitcast.5), calls=%async_computation.4 | async-start | bytes 262144 | tf_op jit(solution)/shard_map/all_to_all | solution.py:235
  105.4 14.9 %collective-permute-start.4 = (bf16[256,256]{1,0:T(8,128)(2,1)S(1)}, bf16[256,256]{1,0:T(8,128)(2,1)S(1)}, u32[]{:S(2)}, u32[]{:S(2)}) collective-permute-start(bf16[256,256]{1,0:T(8,128)(2,1)S(1)} %get-tuple-element.39), channel_id=1, source_target_pairs={{0,1},{1,2},{2,3},{3,0},{4,5},{5,6},{6,7},{7,4},{8,9},{9,10},{10,1... | collective-permute-start | bytes 393224 | tf_op jit(solution)/shard_map/ppermute | solution.py:317
  109.2 11.1 %collective-permute-start.5 = (bf16[256,256]{1,0:T(8,128)(2,1)S(1)}, bf16[256,256]{1,0:T(8,128)(2,1)S(1)}, u32[]{:S(2)}, u32[]{:S(2)}) collective-permute-start(bf16[256,256]{1,0:T(8,128)(2,1)S(1)} %get-tuple-element.40), channel_id=1, source_target_pairs={{0,2},{1,3},{2,0},{3,1},{4,6},{5,7},{6,4},{7,5},{8,10},{9,11},{10,... | collective-permute-start | bytes 393224 | tf_op jit(solution)/shard_map/ppermute | solution.py:317
  113.8 6.9 %collective-permute-start.6 = (bf16[256,256]{1,0:T(8,128)(2,1)S(1)}, bf16[256,256]{1,0:T(8,128)(2,1)S(1)}, u32[]{:S(2)}, u32[]{:S(2)}) collective-permute-start(bf16[256,256]{1,0:T(8,128)(2,1)S(1)} %get-tuple-element.41), channel_id=1, source_target_pairs={{0,3},{1,0},{2,1},{3,2},{4,7},{5,4},{6,5},{7,6},{8,11},{9,8},{10,9... | collective-permute-start | bytes 393224 | tf_op jit(solution)/shard_map/ppermute | solution.py:317
  121.4 10.7 %all-to-all-start.5 = ((f32[8,8,512]{2,1,0:T(8,128)}), f32[8,8,512]{2,1,0:T(8,128)S(1)}, u32[]{:S(2)}, u32[]{:S(2)}) async-start(f32[8,8,512]{2,1,0:T(8,128)} %broadcast_in_dim.22), calls=%async_computation.5 | async-start | bytes 262144 | tf_op jit(solution)/shard_map/all_to_all | solution.py:235
  (1 other events, 0.7 us)
Sparse Core Ops, SparseCore 0:
  10.1 44.2 all-gather.2

commit v5 on v4

--- a/solution.py
+++ b/solution.py
@@ -25,6 +25,32 @@
         in_specs=[pl.BlockSpec(memory_space=space) for space in spaces],
         out_specs=jax.tree.map(lambda _: pl.BlockSpec(memory_space=pltpu.VMEM), outs),
         compiler_params=pltpu.CompilerParams(vmem_limit_bytes=12 * 1024 * 1024),
+    )(*scalars, *operands)
+
+
+def on_fetched(kernel, outs, *operands, scalars=()):
+    many = len(scalars) + len(operands)
+    first = len(jax.tree.leaves(outs)) + many
+
+    def body(*refs):
+        places, arrivals = refs[first : first + many], refs[first + many]
+        copies = [
+            pltpu.make_async_copy(source, place, arrivals.at[i])
+            for i, (source, place) in enumerate(zip(refs[:many], places))
+        ]
+        for copy in copies:
+            copy.start()
+        kernel(*zip(places, [copy.wait for copy in copies]), *refs[many:first])
+
+    return pl.pallas_call(
+        body,
+        out_shape=outs,
+        in_specs=[pl.BlockSpec(memory_space=pl.ANY)] * many,
+        out_specs=jax.tree.map(lambda _: pl.BlockSpec(memory_space=pltpu.VMEM), outs),
+        scratch_shapes=[pltpu.SMEM(one.shape, one.dtype) for one in scalars]
+        + [pltpu.VMEM(one.shape, one.dtype) for one in operands]
+        + [pltpu.SemaphoreType.DMA((many,))],
+        compiler_params=pltpu.CompilerParams(vmem_limit_bytes=56 * 1024 * 1024),
     )(*scalars, *operands)
 
 
@@ -62,19 +88,27 @@
     return usage
 
 
-def prepare_kernel(blocks_ref, length_ref, owner_ref, cand_ref, cot_ref, in_ref, out_ref, bundle_ref):
+def prepare_kernel(blocks, lengths, owners, cands, cots, in_weight, out_weight, bundle_ref):
+    (cand_ref, cand_here), (cot_ref, cot_here) = cands, cots
+    (in_ref, in_here), (out_ref, out_here) = in_weight, out_weight
+    inner, count = out_ref.shape[0], cand_ref.shape[0]
+    size = inner // HEADS
+    bundle_ref[:, :, count:] = jnp.zeros(
+        (HEADS, bundle_ref.shape[1], bundle_ref.shape[2] - count), BF16
+    )
+    for _, here in (blocks, lengths, owners):
+        here()
+    usage = used_blocks(blocks[0], lengths[0], owners[0]).astype(BF16)
+    cand_here()
     rows = cand_ref[...].astype(F32)
     centered = rows - jnp.mean(rows, axis=-1, keepdims=True)
     inv_scale = lax.rsqrt(jnp.mean(centered * centered, axis=-1, keepdims=True) + 1e-05)
     normed = (centered * inv_scale).astype(BF16)
+    cot_here()
+    out_here()
+    zed_grad = lax.dot_general(out_ref[...], cot_ref[...], NT, preferred_element_type=F32)
+    in_here()
     projected = jnp.dot(normed, in_ref[...], preferred_element_type=F32).T
-    zed_grad = lax.dot_general(out_ref[...], cot_ref[...], NT, preferred_element_type=F32)
-    inner, count = out_ref.shape[0], cand_ref.shape[0]
-    size = inner // HEADS
-    usage = used_blocks(blocks_ref, length_ref, owner_ref).astype(BF16)
-    bundle_ref[:, :, count:] = jnp.zeros(
-        (HEADS, bundle_ref.shape[1], bundle_ref.shape[2] - count), BF16
-    )
     for head in range(HEADS):
         part = slice(head * size, (head + 1) * size)
         gate_in = projected[inner + head * size : inner + (head + 1) * size]
@@ -146,9 +180,12 @@
         grad_ref[group] = (inv_scale * (dy - mean_dy - normed * mean_mixed)).astype(BF16)
 
 
-def out_grad_kernel(total_cands, gated, cots, out_grad_ref):
+def out_grad_kernel(total_cands, gates, cot_rows, out_grad_ref):
+    (gated, gated_here), (cots, cots_here) = gates, cot_rows
     count = cots.shape[1]
     total = None
+    gated_here()
+    cots_here()
     for group in range(HEADS):
         part = jnp.dot(gated[group, :, :count], cots[group], preferred_element_type=F32)
         total = part if total is None else total + part
@@ -191,24 +228,50 @@
         sum_ref[block, :, size:] = values[block].astype(sum_ref.dtype)
 
 
-def far_back_kernel(ring1, ring2, bundle, grads, back1, back2):
-    back(2, ring2, bundle, grads, back2)
-    back(1, ring1, bundle, grads, back1)
-
-
-def near_back_kernel(ring0, bundle, grads, back0):
-    back(0, ring0, bundle, grads, back0)
-
-
-def parcel_kernel(place_ref, gated_ref, back0, back1, back2, *parcel_refs):
+def back2_kernel(ring2, bundle, grads, sum_ref):
+    back(2, ring2, bundle, grads, sum_ref)
+
+
+def back1_kernel(ring1, bundle, grads, arrived, sum_ref, total):
+    back(1, ring1, bundle, grads, total)
+    count = arrived.shape[0]
+    sum_ref[:count] = (total[:count] + arrived[...].astype(F32)).astype(BF16)
+    sum_ref[count:] = total[count:].astype(BF16)
+
+
+def back0_kernel(ring0, bundle, grads, sum_ref):
+    back(0, ring0, bundle, grads, sum_ref)
+
+
+def fold_kernel(parts, folded_ref):
+    total = jnp.sum(parts[...].astype(F32), axis=0).astype(BF16)
+    lines = folded_ref.shape[2]
+    for row in range(folded_ref.shape[1]):
+        for copy in range(folded_ref.shape[0]):
+            folded_ref[copy, row] = total[row * lines : (row + 1) * lines]
+
+
+def pick_kernel(place_ref, parts, spread_ref):
+    total = jnp.zeros(spread_ref.shape[1:], F32)
+    for source in range(parts.shape[0]):
+        total = total + parts[source, place_ref[0]].astype(F32)
+    for peer in range(spread_ref.shape[0]):
+        spread_ref[peer] = total
+
+
+def last_kernel(parts, rows_ref):
+    cores = parts.shape[1]
+    half = rows_ref.shape[1] // cores
+    for core in range(cores):
+        rows_ref[:, core * half : (core + 1) * half] = jnp.sum(parts[:, core], axis=0)
+
+
+def parcel_kernel(place_ref, gated_ref, back0, back1, *parcel_refs):
     size = gated_ref.shape[1]
     for step, parcel in enumerate(parcel_refs):
         target = lax.rem(place_ref[0] + step, HEADS)
         parcel[0:size] = gated_ref[target]
-        total = back0[target] + back1[target].astype(F32)
-        last = jnp.minimum(target, back2.shape[0] - 1)
-        more = back2[last].astype(F32)
-        parcel[size:] = (total + jnp.where(last == target, more, 0.0)).astype(BF16)
+        parcel[size:] = (back0[target] + back1[target].astype(F32)).astype(BF16)
 
 
 def join_kernel(place_ref, cand_ref, out_ref, *refs):
@@ -269,7 +332,7 @@
 
     ring2 = moved(ring0[: HEADS - 1], 2)
     ring1 = moved(ring0, 1)
-    bundle = on_core(
+    bundle = on_fetched(
         prepare_kernel,
         shaped((HEADS, 3 * size + 16, lanes), BF16),
         candidate_request.reshape(1, count),
@@ -291,12 +354,8 @@
     cores, zh, zl, xs = (lax.axis_size(name) for name in ("core", "zh", "zl", "x"))
     own, half = size // (zl * xs), out_weight.shape[1] // cores
     gated, grads = on_core(norm_kernel, (head_shape, head_shape), attended, bundle, stats)
-    back1, back2 = on_core(
-        far_back_kernel, (shaped(ring1.shape, BF16), shaped(ring2.shape, BF16)), ring1, ring2, bundle, grads
-    )
-    back2 = moved(back2, -2)
-    back1 = moved(back1, -1)
-    out_grad = on_core(
+    back2 = moved(on_core(back2_kernel, shaped(ring2.shape, BF16), ring2, bundle, grads), -1)
+    out_grad = on_fetched(
         lambda *refs: out_grad_kernel(total_cands, *refs),
         shaped((cores, zl, size // zl, half), BF16),
         gated,
@@ -304,22 +363,32 @@
     )
     out_grad, late_grads = barrier((out_grad, grads))
     part = exchanged(out_grad.reshape(cores * zl, size // zl, half), ("core", "zl"))
-    back0 = on_core(near_back_kernel, shaped(ring0.shape, F32), ring0, bundle, late_grads)
-    part, back0, back1, back2 = barrier((summed(part).astype(BF16), back0, back1, back2))
-    part = jnp.broadcast_to(part.reshape(1, xs, own, half), (zh, xs, own, half))
+    back1 = pl.pallas_call(
+        back1_kernel,
+        out_shape=shaped(ring1.shape, BF16),
+        in_specs=[pl.BlockSpec(memory_space=pltpu.VMEM)] * 4,
+        out_specs=pl.BlockSpec(memory_space=pltpu.VMEM),
+        scratch_shapes=[pltpu.VMEM(ring1.shape, F32)],
+        compiler_params=pltpu.CompilerParams(vmem_limit_bytes=12 * 1024 * 1024),
+    )(ring1, bundle, late_grads, back2)
+    part, back1 = barrier((part, back1))
+    back1 = moved(back1, -1)
+    part = on_core(fold_kernel, shaped((zh, xs, own, half), BF16), part)
+    back0 = on_core(back0_kernel, shaped(ring0.shape, F32), ring0, bundle, late_grads)
     part = exchanged(part.reshape(zh * xs, own, half), ("zh", "x")).reshape(zh, xs, own, half)
-    part = lax.dynamic_index_in_dim(part, lax.axis_index("zh"), axis=1, keepdims=False)
+    depth = lax.axis_index("zh").reshape(1).astype(jnp.int32)
+    peers = lax.axis_size("y") * cores
+    part = on_core(pick_kernel, shaped((peers, own, half), F32), part, scalars=(depth,))
 
     parcels = on_core(
-        parcel_kernel, [shaped((2 * size, lanes), BF16)] * HEADS, gated, back0, back1, back2, scalars=(place,)
+        parcel_kernel, [shaped((2 * size, lanes), BF16)] * HEADS, gated, back0, back1, scalars=(place,)
     )
     arrived = [
         lax.ppermute(parcel, "x", [(i, (i + step) % HEADS) for i in range(HEADS)]) if step else parcel
         for step, parcel in enumerate(parcels)
     ]
-    part, arrived = barrier((summed(part), arrived))
-    part = spread_over(part, ("y", "core")).reshape(-1, cores, own, half)
-    grad_rows = summed(part).transpose(1, 0, 2).reshape(own, cores * half)
+    part = exchanged(part, ("y", "core")).reshape(-1, cores, own, half)
+    grad_rows = on_core(last_kernel, shaped((own, cores * half), F32), part)
 
     layer_out, grad_history = on_core(
         join_kernel,

time: 141 us -> 139 us (0.986)
  the two profiles are of different devices: /device:TPU:32 before, /device:TPU:1 now
where the time goes in v5:
time: 139 us; the launch traced here: 138 us
  starting transfers between devices  61.7 us (44%)
  waiting for transfers between devices  32.9 us (24%)
  Pallas kernels  18.4 us (13%)
  between operations  14.2 us (10%)
  blocking collectives  8.4 us (6%)
  local copies, waits for them, and re-layouts  2.38 us (2%)
    all_to_all x5, starting transfers between devices, exchanged(): return lax.all_to_all(chunks, axis, 0, 0, tiled=True)  30.5 us
    ppermute x4, waiting for transfers between devices, moved(): lax.ppermute(block, DEPTH, [((i + distance) % size, i) for i in range(siz...  27.9 us
    ppermute x4, starting transfers between devices, moved(): lax.ppermute(block, DEPTH, [((i + distance) % size, i) for i in range(siz...  20.6 us
    ppermute x3, starting transfers between devices, on_device(): lax.ppermute(parcel, 'x', [(i, (i + step) % HEADS) for i in range(HEADS)])  10.5 us
    pallas_call x11, Pallas kernels, on_core(): pl.pallas_call(kernel, out_shape=outs, in_specs=[pl.BlockSpec(memory_spac...  9.03 us
    all_to_all x1, blocking collectives, exchanged(): return lax.all_to_all(chunks, axis, 0, 0, tiled=True)  8.4 us
    pallas_call x2, Pallas kernels, on_fetched(): pl.pallas_call(body, out_shape=outs, in_specs=[pl.BlockSpec(memory_space=...  7.61 us
    all_to_all x5, waiting for transfers between devices, exchanged(): return lax.all_to_all(chunks, axis, 0, 0, tiled=True)  4.39 us
  transfers between devices with their start and end apart: 13, of which 6 were waited for; matrix products, arithmetic and copies ran while one was open for 0% of the time, Pallas kernels for 10%

profile of v5, /device:TPU:1, one launch (start us, length us, event | category | flops | bytes accessed | tf_op | source)
XLA Modules:
  0.0 138.0 jit_solution(16551701273062788390)
XLA Ops:
  7.9 0.9 copy-done.5
  9.6 4.8 %all-to-all-start = ((bf16[4,128,256]{2,1,0:T(8,128)(2,1)}), bf16[4,128,256]{2,1,0:T(8,128)(2,1)S(1)}, u32[]{:S(2)}, u32[]{:S(2)}) async-start(bf16[4,128,256]{2,1,0:T(8,128)(2,1)} %shard_map.103), calls=%async_computation | async-start | bytes 524288 | tf_op jit(solution)/shard_map/all_to_all | solution.py:298
  14.4 4.9 %shard_map.104 = bf16[4,400,256]{2,1,0:T(8,128)(2,1)} custom-call(s32[2,8]{1,0:T(2,128)} %refs_0_.1, s32[2]{0:T(128)} %refs_1_.1, s32[1,224]{1,0:T(1,128)} %bitcast.12, bf16[224,1024]{1,0:T(8,128)(2,1)} %cand_ref.1, bf16[224,1024]{1,0:T(8,128)(2,1)} %refs_4_.1, bf16[1024,1024]{1,0:T(8,128)(2,1)} %refs_5_.1, bf16[512,1024]{1,0:T(8,128)(2,1)} %out_ref.1), custom_call_target="tpu_custom_call" | custom-call | tf_op jit(solution)/shard_map/pallas_call | solution.py:45
  20.0 3.6 %all-to-all-start.1 = ((bf16[4,400,256]{2,1,0:T(8,128)(2,1)}), bf16[4,400,256]{2,1,0:T(8,128)(2,1)S(1)}, u32[]{:S(2)}, u32[]{:S(2)}) async-start(bf16[4,400,256]{2,1,0:T(8,128)(2,1)} %shard_map.104), calls=%async_computation.1 | async-start | bytes 1638400 | tf_op jit(solution)/shard_map/all_to_all | solution.py:298
  23.6 11.1 %collective-permute-start.1 = (bf16[4,128,256]{2,1,0:T(8,128)(2,1)S(1)}, bf16[4,128,256]{2,1,0:T(8,128)(2,1)S(1)}, u32[]{:S(2)}, u32[]{:S(2)}) collective-permute-start(bf16[4,128,256]{2,1,0:T(8,128)(2,1)S(1)} %all-to-all-done.ring0), channel_id=1, source_target_pairs={{4,0},{8,4},{12,8},{16,12},{20,16},{24,20},{28,24},{32,28},{36,32}... | collective-permute-start | bytes 786440 | tf_op jit(solution)/shard_map/ppermute | solution.py:294
  34.7 3.1 %collective-permute-start = (bf16[3,128,256]{2,1,0:T(8,128)(2,1)S(1)}, bf16[3,128,256]{2,1,0:T(8,128)(2,1)S(1)}, u32[]{:S(2)}, u32[]{:S(2)}) collective-permute-start(bf16[3,128,256]{2,1,0:T(8,128)(2,1)S(1)} %slice.4), channel_id=1, source_target_pairs={{8,0},{12,4},{16,8},{20,12},{24,16},{28,20},{32,24},{36,28},{40,32... | collective-permute-start | bytes 589832 | tf_op jit(solution)/shard_map/ppermute | solution.py:294
  38.2 1.7 %shard_map.105.before = f32[4,128,256]{2,1,0:T(8,128)S(1)} custom-call(bf16[4,128,256]{2,1,0:T(8,128)(2,1)S(1)} %all-to-all-done.ring0, bf16[4,128,256]{2,1,0:T(8,128)(2,1)S(1)} %collective-permute-done.1.ring1, bf16[4,400,256]{2,1,0:T(8,128)(2,1)S(1)} %all-to-all-done.1.bundle), custom_call_target="tpu_custom_call" | custom-call | tf_op jit(solution)/shard_map/pallas_call | solution.py:22
  39.9 5.6 %collective-permute-done.ring2 = bf16[3,128,256]{2,1,0:T(8,128)(2,1)S(1)} collective-permute-done((bf16[3,128,256]{2,1,0:T(8,128)(2,1)S(1)}, bf16[3,128,256]{2,1,0:T(8,128)(2,1)S(1)}, u32[]{:S(2)}, u32[]{:S(2)}) %collective-permute-start) | collective-permute-done | bytes 196640 | tf_op jit(solution)/shard_map/ppermute | solution.py:294
  46.3 8.4 %all_to_all.30.stats = f32[4,16,256]{2,1,0:T(8,128)S(1)} all-to-all(f32[4,16,256]{2,1,0:T(8,128)S(1)} %broadcast_in_dim.2), channel_id=1, replica_groups=mesh['y'=4,'core'=2,'zh'=4,'zl'=4,'x'=4] {'x'}, dimensions={0} | all-to-all | bytes 131072 | tf_op jit(solution)/shard_map/all_to_all | solution.py:298
  55.7 2.7 %shard_map.108 = bf16[2,4,32,512]{3,2,1,0:T(8,128)(2,1)} custom-call(bf16[4,128,256]{2,1,0:T(8,128)(2,1)} %copy-done.2, bf16[4,224,1024]{2,1,0:T(8,128)(2,1)} %bitcast.10), custom_call_target="tpu_custom_call" | custom-call | tf_op jit(solution)/shard_map/pallas_call | solution.py:45
  58.4 9.0 %all-to-all-start.3 = ((bf16[8,32,512]{2,1,0:T(8,128)(2,1)}), bf16[8,32,512]{2,1,0:T(8,128)(2,1)S(1)}, u32[]{:S(2)}, u32[]{:S(2)}) async-start(bf16[8,32,512]{2,1,0:T(8,128)(2,1)} %bitcast.11), calls=%async_computation.3 | async-start | bytes 524288 | tf_op jit(solution)/shard_map/all_to_all | solution.py:298
  68.2 3.4 %collective-permute-start.2 = (bf16[3,128,256]{2,1,0:T(8,128)(2,1)S(1)}, bf16[3,128,256]{2,1,0:T(8,128)(2,1)S(1)}, u32[]{:S(2)}, u32[]{:S(2)}) collective-permute-start(bf16[3,128,256]{2,1,0:T(8,128)(2,1)S(1)} %shard_map.110), channel_id=1, source_target_pairs={{60,0},{0,4},{4,8},{8,12},{12,16},{16,20},{20,24},{24,28},{28,32},... | collective-permute-start | bytes 589832 | tf_op jit(solution)/shard_map/ppermute | solution.py:294
  71.6 8.9 %collective-permute-done.2.arrived = bf16[3,128,256]{2,1,0:T(8,128)(2,1)S(1)} collective-permute-done((bf16[3,128,256]{2,1,0:T(8,128)(2,1)S(1)}, bf16[3,128,256]{2,1,0:T(8,128)(2,1)S(1)}, u32[]{:S(2)}, u32[]{:S(2)}) %collective-permute-start.2) | collective-permute-done | bytes 196640 | tf_op jit(solution)/shard_map/ppermute | solution.py:294
  80.6 1.7 %shard_map.111 = bf16[4,128,256]{2,1,0:T(8,128)(2,1)S(1)} custom-call(bf16[4,128,256]{2,1,0:T(8,128)(2,1)S(1)} %collective-permute-done.1.ring1, bf16[4,400,256]{2,1,0:T(8,128)(2,1)S(1)} %all-to-all-done.1.bundle, bf16[4,128,256]{2,1,0:T(8,128)(2,1)S(1)} %get-tuple-element.21.grads, bf16[3,128,256]{2,1,0:T(8,128)(2,1)S(1)} %collective-permute-done.2.arrived), custom_call_target="tpu_custom_call" | custom-call | tf_op jit(solution)/shard_map/pallas_call | solution.py:366
  83.7 7.0 %all-to-all-start.4 = ((bf16[16,8,512]{2,1,0:T(8,128)(2,1)}), bf16[16,8,512]{2,1,0:T(8,128)(2,1)S(1)}, u32[]{:S(2)}, u32[]{:S(2)}) async-start(bf16[16,8,512]{2,1,0:T(8,128)(2,1)} %bitcast.5), calls=%async_computation.4 | async-start | bytes 262144 | tf_op jit(solution)/shard_map/all_to_all | solution.py:298
  90.7 3.0 %collective-permute-start.3 = (bf16[4,128,256]{2,1,0:T(8,128)(2,1)}, bf16[4,128,256]{2,1,0:T(8,128)(2,1)S(1)}, u32[]{:S(2)}, u32[]{:S(2)}) collective-permute-start(bf16[4,128,256]{2,1,0:T(8,128)(2,1)} %copy-done.4), channel_id=1, source_target_pairs={{60,0},{0,4},{4,8},{8,12},{12,16},{16,20},{20,24},{24,28},{28,32},... | collective-permute-start | bytes 786440 | tf_op jit(solution)/shard_map/ppermute | solution.py:294
  93.8 1.3 shard_map.109.back0
  95.0 12.9 %collective-permute-done.3.back1 = bf16[4,128,256]{2,1,0:T(8,128)(2,1)S(1)} collective-permute-done((bf16[4,128,256]{2,1,0:T(8,128)(2,1)}, bf16[4,128,256]{2,1,0:T(8,128)(2,1)S(1)}, u32[]{:S(2)}, u32[]{:S(2)}) %collective-permute-start.3) | collective-permute-done | bytes 262176 | tf_op jit(solution)/shard_map/ppermute | solution.py:294
  108.0 3.1 %collective-permute-start.4 = (bf16[256,256]{1,0:T(8,128)(2,1)S(1)}, bf16[256,256]{1,0:T(8,128)(2,1)S(1)}, u32[]{:S(2)}, u32[]{:S(2)}) collective-permute-start(bf16[256,256]{1,0:T(8,128)(2,1)S(1)} %get-tuple-element.25), channel_id=1, source_target_pairs={{0,1},{1,2},{2,3},{3,0},{4,5},{5,6},{6,7},{7,4},{8,9},{9,10},{10,1... | collective-permute-start | bytes 393224 | tf_op jit(solution)/shard_map/ppermute | solution.py:387
  111.1 4.3 %collective-permute-start.5 = (bf16[256,256]{1,0:T(8,128)(2,1)S(1)}, bf16[256,256]{1,0:T(8,128)(2,1)S(1)}, u32[]{:S(2)}, u32[]{:S(2)}) collective-permute-start(bf16[256,256]{1,0:T(8,128)(2,1)S(1)} %get-tuple-element.26), channel_id=1, source_target_pairs={{0,2},{1,3},{2,0},{3,1},{4,6},{5,7},{6,4},{7,5},{8,10},{9,11},{10,... | collective-permute-start | bytes 393224 | tf_op jit(solution)/shard_map/ppermute | solution.py:387
  115.4 3.1 %collective-permute-start.6 = (bf16[256,256]{1,0:T(8,128)(2,1)S(1)}, bf16[256,256]{1,0:T(8,128)(2,1)S(1)}, u32[]{:S(2)}, u32[]{:S(2)}) collective-permute-start(bf16[256,256]{1,0:T(8,128)(2,1)S(1)} %get-tuple-element.27), channel_id=1, source_target_pairs={{0,3},{1,0},{2,1},{3,2},{4,7},{5,4},{6,5},{7,6},{8,11},{9,8},{10,9... | collective-permute-start | bytes 393224 | tf_op jit(solution)/shard_map/ppermute | solution.py:387
  119.2 6.0 %all-to-all-start.5 = ((f32[8,8,512]{2,1,0:T(8,128)}), f32[8,8,512]{2,1,0:T(8,128)S(1)}, u32[]{:S(2)}, u32[]{:S(2)}) async-start(f32[8,8,512]{2,1,0:T(8,128)} %shard_map.115), calls=%async_computation.5 | async-start | bytes 262144 | tf_op jit(solution)/shard_map/all_to_all | solution.py:298
  125.3 1.5 %shard_map.113 = (bf16[224,1024]{1,0:T(8,128)(2,1)}, bf16[128,1024]{1,0:T(8,128)(2,1)}) custom-call(s32[1]{0:T(128)} %bitcast.place_ref, bf16[224,1024]{1,0:T(8,128)(2,1)S(1)} %copy-done.1, bf16[512,1024]{1,0:T(8,128)(2,1)S(1)} %copy-done, bf16[256,256]{1,0:T(8,128)(2,1)S(1)} %get-tuple-element.24.refs_0_, ...), custom_call_target="tpu_custom_call" | custom-call | tf_op jit(solution)/shard_map/pallas_call | solution.py:22
  126.8 3.7 %all-to-all-done.5 = f32[8,8,512]{2,1,0:T(8,128)S(1)} async-done(((f32[8,8,512]{2,1,0:T(8,128)}), f32[8,8,512]{2,1,0:T(8,128)S(1)}, u32[]{:S(2)}, u32[]{:S(2)}) %all-to-all-start.5) | async-done | bytes 131104 | tf_op jit(solution)/shard_map/all_to_all | solution.py:298
  (32 shorter events, 7.9 us)
Async XLA Ops:
  7.2 48.5 %all-gather.3.cloned.1.call-start = ((), (), s32[]{:S(2)}) async-start(), calls=%async_computation.6 | async-start | bytes 2293760 | tf_op jit(solution)/shard_map/all_gather | solution.py:329
  7.9 1.0 copy-start.5
  9.6 10.4 %all-to-all-start = ((bf16[4,128,256]{2,1,0:T(8,128)(2,1)}), bf16[4,128,256]{2,1,0:T(8,128)(2,1)S(1)}, u32[]{:S(2)}, u32[]{:S(2)}) async-start(bf16[4,128,256]{2,1,0:T(8,128)(2,1)} %shard_map.103), calls=%async_computation | async-start | bytes 524288 | tf_op jit(solution)/shard_map/all_to_all | solution.py:298
  20.0 18.3 %all-to-all-start.1 = ((bf16[4,400,256]{2,1,0:T(8,128)(2,1)}), bf16[4,400,256]{2,1,0:T(8,128)(2,1)S(1)}, u32[]{:S(2)}, u32[]{:S(2)}) async-start(bf16[4,400,256]{2,1,0:T(8,128)(2,1)} %shard_map.104), calls=%async_computation.1 | async-start | bytes 1638400 | tf_op jit(solution)/shard_map/all_to_all | solution.py:298
  23.6 14.7 %collective-permute-start.1 = (bf16[4,128,256]{2,1,0:T(8,128)(2,1)S(1)}, bf16[4,128,256]{2,1,0:T(8,128)(2,1)S(1)}, u32[]{:S(2)}, u32[]{:S(2)}) collective-permute-start(bf16[4,128,256]{2,1,0:T(8,128)(2,1)S(1)} %all-to-all-done.ring0), channel_id=1, source_target_pairs={{4,0},{8,4},{12,8},{16,12},{20,16},{24,20},{28,24},{32,28},{36,32}... | collective-permute-start | bytes 786440 | tf_op jit(solution)/shard_map/ppermute | solution.py:294
  34.7 10.8 %collective-permute-start = (bf16[3,128,256]{2,1,0:T(8,128)(2,1)S(1)}, bf16[3,128,256]{2,1,0:T(8,128)(2,1)S(1)}, u32[]{:S(2)}, u32[]{:S(2)}) collective-permute-start(bf16[3,128,256]{2,1,0:T(8,128)(2,1)S(1)} %slice.4), channel_id=1, source_target_pairs={{8,0},{12,4},{16,8},{20,12},{24,16},{28,20},{32,24},{36,28},{40,32... | collective-permute-start | bytes 589832 | tf_op jit(solution)/shard_map/ppermute | solution.py:294
  55.0 0.7 copy-start.2
  58.4 24.6 %all-to-all-start.3 = ((bf16[8,32,512]{2,1,0:T(8,128)(2,1)}), bf16[8,32,512]{2,1,0:T(8,128)(2,1)S(1)}, u32[]{:S(2)}, u32[]{:S(2)}) async-start(bf16[8,32,512]{2,1,0:T(8,128)(2,1)} %bitcast.11), calls=%async_computation.3 | async-start | bytes 524288 | tf_op jit(solution)/shard_map/all_to_all | solution.py:298
  68.2 39.7 %copy-start.3 = (bf16[4,128,256]{2,1,0:T(8,128)(2,1)S(1)}, bf16[4,128,256]{2,1,0:T(8,128)(2,1)}, u32[]{:S(2)}) copy-start(bf16[4,128,256]{2,1,0:T(8,128)(2,1)} %copy-done.2) | copy-start | bytes 786436
  68.2 12.4 %collective-permute-start.2 = (bf16[3,128,256]{2,1,0:T(8,128)(2,1)S(1)}, bf16[3,128,256]{2,1,0:T(8,128)(2,1)S(1)}, u32[]{:S(2)}, u32[]{:S(2)}) collective-permute-start(bf16[3,128,256]{2,1,0:T(8,128)(2,1)S(1)} %shard_map.110), channel_id=1, source_target_pairs={{60,0},{0,4},{4,8},{8,12},{12,16},{16,20},{20,24},{24,28},{28,32},... | collective-permute-start | bytes 589832 | tf_op jit(solution)/shard_map/ppermute | solution.py:294
  82.3 0.7 copy-start.4
  83.0 42.3 %copy-start = (bf16[512,1024]{1,0:T(8,128)(2,1)S(1)}, bf16[512,1024]{1,0:T(8,128)(2,1)}, u32[]{:S(2)}) copy-start(bf16[512,1024]{1,0:T(8,128)(2,1)} %out_ref.1) | copy-start | bytes 3145732
  83.0 42.3 %copy-start.1 = (bf16[224,1024]{1,0:T(8,128)(2,1)S(1)}, bf16[224,1024]{1,0:T(8,128)(2,1)}, u32[]{:S(2)}) copy-start(bf16[224,1024]{1,0:T(8,128)(2,1)} %cand_ref.1) | copy-start | bytes 1376260
  83.7 34.8 %all-to-all-start.4 = ((bf16[16,8,512]{2,1,0:T(8,128)(2,1)}), bf16[16,8,512]{2,1,0:T(8,128)(2,1)S(1)}, u32[]{:S(2)}, u32[]{:S(2)}) async-start(bf16[16,8,512]{2,1,0:T(8,128)(2,1)} %bitcast.5), calls=%async_computation.4 | async-start | bytes 262144 | tf_op jit(solution)/shard_map/all_to_all | solution.py:298
  90.7 17.2 %collective-permute-start.3 = (bf16[4,128,256]{2,1,0:T(8,128)(2,1)}, bf16[4,128,256]{2,1,0:T(8,128)(2,1)S(1)}, u32[]{:S(2)}, u32[]{:S(2)}) collective-permute-start(bf16[4,128,256]{2,1,0:T(8,128)(2,1)} %copy-done.4), channel_id=1, source_target_pairs={{60,0},{0,4},{4,8},{8,12},{12,16},{16,20},{20,24},{24,28},{28,32},... | collective-permute-start | bytes 786440 | tf_op jit(solution)/shard_map/ppermute | solution.py:294
  108.0 17.2 %collective-permute-start.4 = (bf16[256,256]{1,0:T(8,128)(2,1)S(1)}, bf16[256,256]{1,0:T(8,128)(2,1)S(1)}, u32[]{:S(2)}, u32[]{:S(2)}) collective-permute-start(bf16[256,256]{1,0:T(8,128)(2,1)S(1)} %get-tuple-element.25), channel_id=1, source_target_pairs={{0,1},{1,2},{2,3},{3,0},{4,5},{5,6},{6,7},{7,4},{8,9},{9,10},{10,1... | collective-permute-start | bytes 393224 | tf_op jit(solution)/shard_map/ppermute | solution.py:387
  111.1 14.1 %collective-permute-start.5 = (bf16[256,256]{1,0:T(8,128)(2,1)S(1)}, bf16[256,256]{1,0:T(8,128)(2,1)S(1)}, u32[]{:S(2)}, u32[]{:S(2)}) collective-permute-start(bf16[256,256]{1,0:T(8,128)(2,1)S(1)} %get-tuple-element.26), channel_id=1, source_target_pairs={{0,2},{1,3},{2,0},{3,1},{4,6},{5,7},{6,4},{7,5},{8,10},{9,11},{10,... | collective-permute-start | bytes 393224 | tf_op jit(solution)/shard_map/ppermute | solution.py:387
  115.4 9.8 %collective-permute-start.6 = (bf16[256,256]{1,0:T(8,128)(2,1)S(1)}, bf16[256,256]{1,0:T(8,128)(2,1)S(1)}, u32[]{:S(2)}, u32[]{:S(2)}) collective-permute-start(bf16[256,256]{1,0:T(8,128)(2,1)S(1)} %get-tuple-element.27), channel_id=1, source_target_pairs={{0,3},{1,0},{2,1},{3,2},{4,7},{5,4},{6,5},{7,6},{8,11},{9,8},{10,9... | collective-permute-start | bytes 393224 | tf_op jit(solution)/shard_map/ppermute | solution.py:387
  119.2 11.3 %all-to-all-start.5 = ((f32[8,8,512]{2,1,0:T(8,128)}), f32[8,8,512]{2,1,0:T(8,128)S(1)}, u32[]{:S(2)}, u32[]{:S(2)}) async-start(f32[8,8,512]{2,1,0:T(8,128)} %shard_map.115), calls=%async_computation.5 | async-start | bytes 262144 | tf_op jit(solution)/shard_map/all_to_all | solution.py:298
Sparse Core Ops, SparseCore 0:
  10.1 43.9 all-gather.2

commit v6 on v5

--- a/solution.py
+++ b/solution.py
@@ -28,30 +28,37 @@
     )(*scalars, *operands)
 
 
-def on_fetched(kernel, outs, *operands, scalars=()):
-    many = len(scalars) + len(operands)
-    first = len(jax.tree.leaves(outs)) + many
+def on_fetched(kernel, outs, *operands, scalars=(), local=()):
+    fetched = list(scalars) + list(operands)
+    many = len(fetched)
+    first = many + len(local) + len(jax.tree.leaves(outs))
+    pieces = [4 if one.size >= 1 << 19 else 1 for one in fetched]
 
     def body(*refs):
         places, arrivals = refs[first : first + many], refs[first + many]
-        copies = [
-            pltpu.make_async_copy(source, place, arrivals.at[i])
-            for i, (source, place) in enumerate(zip(refs[:many], places))
-        ]
-        for copy in copies:
-            copy.start()
-        kernel(*zip(places, [copy.wait for copy in copies]), *refs[many:first])
+        waits = []
+        for i, (source, place) in enumerate(zip(refs[:many], places)):
+            step = place.shape[0] // pieces[i]
+            copies = []
+            for part in range(pieces[i]):
+                rows = (slice(None),) if pieces[i] == 1 else (pl.ds(part * step, step),)
+                copy = pltpu.make_async_copy(source.at[rows], place.at[rows], arrivals.at[i, part])
+                copy.start()
+                copies.append(copy)
+            waits.append(lambda copies=copies: [copy.wait() for copy in copies])
+        kernel(*zip(places, waits), *refs[many:first])
 
     return pl.pallas_call(
         body,
         out_shape=outs,
-        in_specs=[pl.BlockSpec(memory_space=pl.ANY)] * many,
+        in_specs=[pl.BlockSpec(memory_space=pl.ANY)] * many
+        + [pl.BlockSpec(memory_space=pltpu.VMEM)] * len(local),
         out_specs=jax.tree.map(lambda _: pl.BlockSpec(memory_space=pltpu.VMEM), outs),
         scratch_shapes=[pltpu.SMEM(one.shape, one.dtype) for one in scalars]
         + [pltpu.VMEM(one.shape, one.dtype) for one in operands]
-        + [pltpu.SemaphoreType.DMA((many,))],
+        + [pltpu.SemaphoreType.DMA((many, 4))],
         compiler_params=pltpu.CompilerParams(vmem_limit_bytes=56 * 1024 * 1024),
-    )(*scalars, *operands)
+    )(*fetched, *local)
 
 
 def shaped(shape, kind):
@@ -66,12 +73,24 @@
     return {0: range(group, HEADS), 1: range(0, HEADS), 2: range(0, group)}[ring]
 
 
-def split_kernel(history_ref, chunks_ref):
+def split_kernel(history_ref, chunks_ref, arrivals):
     heads, _, both = chunks_ref.shape
     size = both // 2
+    copies = []
     for head in range(heads):
-        chunks_ref[head, :, :size] = history_ref[:, head * size : (head + 1) * size]
-        chunks_ref[head, :, size:] = history_ref[:, (heads + head) * size : (heads + head + 1) * size]
+        for kind in range(2):
+            columns = pl.ds((kind * heads + head) * size, size)
+            copies.append(
+                pltpu.make_async_copy(
+                    history_ref.at[:, columns],
+                    chunks_ref.at[head, :, pl.ds(kind * size, size)],
+                    arrivals.at[head, kind],
+                )
+            )
+    for copy in copies:
+        copy.start()
+    for copy in copies:
+        copy.wait()
 
 
 def used_blocks(blocks_ref, length_ref, owner_ref):
@@ -180,11 +199,10 @@
         grad_ref[group] = (inv_scale * (dy - mean_dy - normed * mean_mixed)).astype(BF16)
 
 
-def out_grad_kernel(total_cands, gates, cot_rows, out_grad_ref):
-    (gated, gated_here), (cots, cots_here) = gates, cot_rows
+def out_grad_kernel(total_cands, cot_rows, gated, out_grad_ref):
+    cots, cots_here = cot_rows
     count = cots.shape[1]
     total = None
-    gated_here()
     cots_here()
     for group in range(HEADS):
         part = jnp.dot(gated[group, :, :count], cots[group], preferred_element_type=F32)
@@ -328,7 +346,15 @@
 
     cots = lax.all_gather(cotangent, "x")
     ring_shape = shaped((HEADS, tall, 2 * size), BF16)
-    ring0 = exchanged(on_core(split_kernel, ring_shape, history), "x")
+    by_head = pl.pallas_call(
+        split_kernel,
+        out_shape=ring_shape,
+        in_specs=[pl.BlockSpec(memory_space=pl.ANY)],
+        out_specs=pl.BlockSpec(memory_space=pltpu.VMEM),
+        scratch_shapes=[pltpu.SemaphoreType.DMA((HEADS, 2))],
+        compiler_params=pltpu.CompilerParams(vmem_limit_bytes=56 * 1024 * 1024),
+    )(history)
+    ring0 = exchanged(by_head, "x")
 
     ring2 = moved(ring0[: HEADS - 1], 2)
     ring1 = moved(ring0, 1)
@@ -354,12 +380,14 @@
     cores, zh, zl, xs = (lax.axis_size(name) for name in ("core", "zh", "zl", "x"))
     own, half = size // (zl * xs), out_weight.shape[1] // cores
     gated, grads = on_core(norm_kernel, (head_shape, head_shape), attended, bundle, stats)
-    back2 = moved(on_core(back2_kernel, shaped(ring2.shape, BF16), ring2, bundle, grads), -1)
+    back2 = on_core(back2_kernel, shaped(ring2.shape, BF16), ring2, bundle, grads)
+    gated, back2 = barrier((gated, back2))
+    back2 = moved(back2, -1)
     out_grad = on_fetched(
         lambda *refs: out_grad_kernel(total_cands, *refs),
         shaped((cores, zl, size // zl, half), BF16),
-        gated,
         cots,
+        local=(gated,),
     )
     out_grad, late_grads = barrier((out_grad, grads))
     part = exchanged(out_grad.reshape(cores * zl, size // zl, half), ("core", "zl"))
@@ -371,9 +399,8 @@
         scratch_shapes=[pltpu.VMEM(ring1.shape, F32)],
         compiler_params=pltpu.CompilerParams(vmem_limit_bytes=12 * 1024 * 1024),
     )(ring1, bundle, late_grads, back2)
-    part, back1 = barrier((part, back1))
-    back1 = moved(back1, -1)
-    part = on_core(fold_kernel, shaped((zh, xs, own, half), BF16), part)
+    part, back1 = barrier((part, moved(back1, -1)))
+    part, back1 = barrier((on_core(fold_kernel, shaped((zh, xs, own, half), BF16), part), back1))
     back0 = on_core(back0_kernel, shaped(ring0.shape, F32), ring0, bundle, late_grads)
     part = exchanged(part.reshape(zh * xs, own, half), ("zh", "x")).reshape(zh, xs, own, half)
     depth = lax.axis_index("zh").reshape(1).astype(jnp.int32)

time: 139 us -> 139 us (level)
  Pallas kernels: 18.4 us -> 20.2 us
  waiting for transfers between devices: 32.9 us -> 31.1 us
  local copies, waits for them, and re-layouts: 2.38 us -> 0.75 us
    ppermute x4, waiting for transfers between devices: 27.9 us -> 23.4 us  [moved(): lax.ppermute(block, DEPTH, [((i + distance) % size, i) for i in range(siz...]
    all_to_all x5, waiting for transfers between devices: 4.39 us -> 6.95 us  [exchanged(): return lax.all_to_all(chunks, axis, 0, 0, tiled=True)]
    all_to_all x5, starting transfers between devices: 30.5 us -> 32.6 us  [exchanged(): return lax.all_to_all(chunks, axis, 0, 0, tiled=True)]
    pallas_call x0 -> x1, Pallas kernels: none -> 1.65 us  [on_device(): pl.pallas_call(split_kernel, out_shape=ring_shape, in_specs=[pl.BlockSpec...]
    unnamed x12, local copies, waits for them, and re-layouts: 2.35 us -> 0.73 us
    pallas_call x11 -> x10, Pallas kernels: 9.03 us -> 8.29 us  [on_core(): pl.pallas_call(kernel, out_shape=outs, in_specs=[pl.BlockSpec(memory_spac...]
  transfers between devices with their start and end apart: 13 -> 13, of which waited for: 6 -> 7; matrix products, arithmetic and copies ran while one was open for 0% -> 0% of each run, Pallas kernels for 10% -> 11%
where the time goes in v6:
time: 139 us; the launch traced here: 138 us
  starting transfers between devices  63 us (45%)
  waiting for transfers between devices  31.1 us (22%)
  Pallas kernels  20.2 us (15%)
  between operations  14.3 us (10%)
  blocking collectives  8.47 us (6%)
    all_to_all x5, starting transfers between devices, exchanged(): return lax.all_to_all(chunks, axis, 0, 0, tiled=True)  32.6 us
    ppermute x4, waiting for transfers between devices, moved(): lax.ppermute(block, DEPTH, [((i + distance) % size, i) for i in range(siz...  23.4 us
    ppermute x4, starting transfers between devices, moved(): lax.ppermute(block, DEPTH, [((i + distance) % size, i) for i in range(siz...  19.6 us
    ppermute x3, starting transfers between devices, on_device(): lax.ppermute(parcel, 'x', [(i, (i + step) % HEADS) for i in range(HEADS)])  10.7 us
    pallas_call x2, Pallas kernels, on_fetched(): pl.pallas_call(body, out_shape=outs, in_specs=[pl.BlockSpec(memory_space=...  8.56 us
    all_to_all x1, blocking collectives, exchanged(): return lax.all_to_all(chunks, axis, 0, 0, tiled=True)  8.47 us
    pallas_call x10, Pallas kernels, on_core(): pl.pallas_call(kernel, out_shape=outs, in_specs=[pl.BlockSpec(memory_spac...  8.29 us
    all_to_all x5, waiting for transfers between devices, exchanged(): return lax.all_to_all(chunks, axis, 0, 0, tiled=True)  6.95 us
  transfers between devices with their start and end apart: 13, of which 7 were waited for; matrix products, arithmetic and copies ran while one was open for 0% of the time, Pallas kernels for 11%

profile of v6, /device:TPU:1, one launch (start us, length us, event | category | flops | bytes accessed | tf_op | source)
XLA Modules:
  0.0 137.8 jit_solution(7431975436791585516)
XLA Ops:
  7.9 1.6 %shard_map.103 = bf16[4,128,256]{2,1,0:T(8,128)(2,1)} custom-call(bf16[128,1024]{1,0:T(8,128)(2,1)} %history_ref.1), custom_call_target="tpu_custom_call" | custom-call | tf_op jit(solution)/shard_map/pallas_call | solution.py:349
  9.6 4.9 %all-to-all-start = ((bf16[4,128,256]{2,1,0:T(8,128)(2,1)}), bf16[4,128,256]{2,1,0:T(8,128)(2,1)S(1)}, u32[]{:S(2)}, u32[]{:S(2)}) async-start(bf16[4,128,256]{2,1,0:T(8,128)(2,1)} %shard_map.103), calls=%async_computation | async-start | bytes 524288 | tf_op jit(solution)/shard_map/all_to_all | solution.py:316
  14.4 5.0 %shard_map.104 = bf16[4,400,256]{2,1,0:T(8,128)(2,1)} custom-call(s32[2,8]{1,0:T(2,128)} %refs_0_.1, s32[2]{0:T(128)} %refs_1_.1, s32[1,224]{1,0:T(1,128)} %bitcast.12, bf16[224,1024]{1,0:T(8,128)(2,1)} %cand_ref.1, bf16[224,1024]{1,0:T(8,128)(2,1)} %refs_4_.1, bf16[1024,1024]{1,0:T(8,128)(2,1)} %refs_5_.1, bf16[512,1024]{1,0:T(8,128)(2,1)} %out_ref.1), custom_call_target="tpu_custom_call" | custom-call | tf_op jit(solution)/shard_map/pallas_call | solution.py:51
  19.9 3.7 %all-to-all-start.1 = ((bf16[4,400,256]{2,1,0:T(8,128)(2,1)}), bf16[4,400,256]{2,1,0:T(8,128)(2,1)S(1)}, u32[]{:S(2)}, u32[]{:S(2)}) async-start(bf16[4,400,256]{2,1,0:T(8,128)(2,1)} %shard_map.104), calls=%async_computation.1 | async-start | bytes 1638400 | tf_op jit(solution)/shard_map/all_to_all | solution.py:316
  23.7 11.1 %collective-permute-start.1 = (bf16[4,128,256]{2,1,0:T(8,128)(2,1)S(1)}, bf16[4,128,256]{2,1,0:T(8,128)(2,1)S(1)}, u32[]{:S(2)}, u32[]{:S(2)}) collective-permute-start(bf16[4,128,256]{2,1,0:T(8,128)(2,1)S(1)} %all-to-all-done.ring0), channel_id=1, source_target_pairs={{4,0},{8,4},{12,8},{16,12},{20,16},{24,20},{28,24},{32,28},{36,32}... | collective-permute-start | bytes 786440 | tf_op jit(solution)/shard_map/ppermute | solution.py:312
  34.8 3.1 %collective-permute-start = (bf16[3,128,256]{2,1,0:T(8,128)(2,1)S(1)}, bf16[3,128,256]{2,1,0:T(8,128)(2,1)S(1)}, u32[]{:S(2)}, u32[]{:S(2)}) collective-permute-start(bf16[3,128,256]{2,1,0:T(8,128)(2,1)S(1)} %slice.4), channel_id=1, source_target_pairs={{8,0},{12,4},{16,8},{20,12},{24,16},{28,20},{32,24},{36,28},{40,32... | collective-permute-start | bytes 589832 | tf_op jit(solution)/shard_map/ppermute | solution.py:312
  38.5 1.7 %shard_map.105.before = f32[4,128,256]{2,1,0:T(8,128)S(1)} custom-call(bf16[4,128,256]{2,1,0:T(8,128)(2,1)S(1)} %all-to-all-done.ring0, bf16[4,128,256]{2,1,0:T(8,128)(2,1)S(1)} %collective-permute-done.1.ring1, bf16[4,400,256]{2,1,0:T(8,128)(2,1)S(1)} %all-to-all-done.1.bundle), custom_call_target="tpu_custom_call" | custom-call | tf_op jit(solution)/shard_map/pallas_call | solution.py:22
  40.2 5.4 %collective-permute-done.ring2 = bf16[3,128,256]{2,1,0:T(8,128)(2,1)S(1)} collective-permute-done((bf16[3,128,256]{2,1,0:T(8,128)(2,1)S(1)}, bf16[3,128,256]{2,1,0:T(8,128)(2,1)S(1)}, u32[]{:S(2)}, u32[]{:S(2)}) %collective-permute-start) | collective-permute-done | bytes 196640 | tf_op jit(solution)/shard_map/ppermute | solution.py:312
  46.4 8.5 %all_to_all.30.stats = f32[4,16,256]{2,1,0:T(8,128)S(1)} all-to-all(f32[4,16,256]{2,1,0:T(8,128)S(1)} %broadcast_in_dim.2), channel_id=1, replica_groups=mesh['y'=4,'core'=2,'zh'=4,'zl'=4,'x'=4] {'x'}, dimensions={0} | all-to-all | bytes 131072 | tf_op jit(solution)/shard_map/all_to_all | solution.py:316
  55.9 3.6 %shard_map.109 = bf16[2,4,32,512]{3,2,1,0:T(8,128)(2,1)} custom-call(bf16[4,224,1024]{2,1,0:T(8,128)(2,1)} %bitcast.10, bf16[4,128,256]{2,1,0:T(8,128)(2,1)} %copy-done.2), custom_call_target="tpu_custom_call" | custom-call | tf_op jit(solution)/shard_map/pallas_call | solution.py:51
  59.5 9.0 %all-to-all-start.3 = ((bf16[8,32,512]{2,1,0:T(8,128)(2,1)}), bf16[8,32,512]{2,1,0:T(8,128)(2,1)S(1)}, u32[]{:S(2)}, u32[]{:S(2)}) async-start(bf16[8,32,512]{2,1,0:T(8,128)(2,1)} %bitcast.11), calls=%async_computation.3 | async-start | bytes 524288 | tf_op jit(solution)/shard_map/all_to_all | solution.py:316
  68.5 3.4 %collective-permute-start.2 = (bf16[3,128,256]{2,1,0:T(8,128)(2,1)S(1)}, bf16[3,128,256]{2,1,0:T(8,128)(2,1)S(1)}, u32[]{:S(2)}, u32[]{:S(2)}) collective-permute-start(bf16[3,128,256]{2,1,0:T(8,128)(2,1)S(1)} %shard_map.108), channel_id=1, source_target_pairs={{60,0},{0,4},{4,8},{8,12},{12,16},{16,20},{20,24},{24,28},{28,32},... | collective-permute-start | bytes 589832 | tf_op jit(solution)/shard_map/ppermute | solution.py:312
  71.9 8.9 %collective-permute-done.2.arrived = bf16[3,128,256]{2,1,0:T(8,128)(2,1)S(1)} collective-permute-done((bf16[3,128,256]{2,1,0:T(8,128)(2,1)S(1)}, bf16[3,128,256]{2,1,0:T(8,128)(2,1)S(1)}, u32[]{:S(2)}, u32[]{:S(2)}) %collective-permute-start.2) | collective-permute-done | bytes 196640 | tf_op jit(solution)/shard_map/ppermute | solution.py:312
  80.8 1.7 %shard_map.111 = bf16[4,128,256]{2,1,0:T(8,128)(2,1)S(1)} custom-call(bf16[4,128,256]{2,1,0:T(8,128)(2,1)S(1)} %collective-permute-done.1.ring1, bf16[4,400,256]{2,1,0:T(8,128)(2,1)S(1)} %all-to-all-done.1.bundle, bf16[4,128,256]{2,1,0:T(8,128)(2,1)S(1)} %get-tuple-element.26.grads, bf16[3,128,256]{2,1,0:T(8,128)(2,1)S(1)} %collective-permute-done.2.arrived), custom_call_target="tpu_custom_call" | custom-call | tf_op jit(solution)/shard_map/pallas_call | solution.py:394
  82.5 2.1 %collective-permute-start.3 = (bf16[4,128,256]{2,1,0:T(8,128)(2,1)S(1)}, bf16[4,128,256]{2,1,0:T(8,128)(2,1)S(1)}, u32[]{:S(2)}, u32[]{:S(2)}) collective-permute-start(bf16[4,128,256]{2,1,0:T(8,128)(2,1)S(1)} %shard_map.111), channel_id=1, source_target_pairs={{60,0},{0,4},{4,8},{8,12},{12,16},{16,20},{20,24},{24,28},{28,32},... | collective-permute-start | bytes 786440 | tf_op jit(solution)/shard_map/ppermute | solution.py:312
  84.6 8.5 %collective-permute-done.3.back1 = bf16[4,128,256]{2,1,0:T(8,128)(2,1)S(1)} collective-permute-done((bf16[4,128,256]{2,1,0:T(8,128)(2,1)S(1)}, bf16[4,128,256]{2,1,0:T(8,128)(2,1)S(1)}, u32[]{:S(2)}, u32[]{:S(2)}) %collective-permute-start.3) | collective-permute-done | bytes 262176 | tf_op jit(solution)/shard_map/ppermute | solution.py:312
  94.6 6.8 %all-to-all-start.4 = ((bf16[16,8,512]{2,1,0:T(8,128)(2,1)}), bf16[16,8,512]{2,1,0:T(8,128)(2,1)S(1)}, u32[]{:S(2)}, u32[]{:S(2)}) async-start(bf16[16,8,512]{2,1,0:T(8,128)(2,1)} %bitcast.5), calls=%async_computation.4 | async-start | bytes 262144 | tf_op jit(solution)/shard_map/all_to_all | solution.py:316
  102.7 3.3 %collective-permute-start.4 = (bf16[256,256]{1,0:T(8,128)(2,1)S(1)}, bf16[256,256]{1,0:T(8,128)(2,1)S(1)}, u32[]{:S(2)}, u32[]{:S(2)}) collective-permute-start(bf16[256,256]{1,0:T(8,128)(2,1)S(1)} %get-tuple-element.33), channel_id=1, source_target_pairs={{0,1},{1,2},{2,3},{3,0},{4,5},{5,6},{6,7},{7,4},{8,9},{9,10},{10,1... | collective-permute-start | bytes 393224 | tf_op jit(solution)/shard_map/ppermute | solution.py:414
  106.0 4.3 %collective-permute-start.5 = (bf16[256,256]{1,0:T(8,128)(2,1)S(1)}, bf16[256,256]{1,0:T(8,128)(2,1)S(1)}, u32[]{:S(2)}, u32[]{:S(2)}) collective-permute-start(bf16[256,256]{1,0:T(8,128)(2,1)S(1)} %get-tuple-element.34), channel_id=1, source_target_pairs={{0,2},{1,3},{2,0},{3,1},{4,6},{5,7},{6,4},{7,5},{8,10},{9,11},{10,... | collective-permute-start | bytes 393224 | tf_op jit(solution)/shard_map/ppermute | solution.py:414
  110.3 3.1 %collective-permute-start.6 = (bf16[256,256]{1,0:T(8,128)(2,1)S(1)}, bf16[256,256]{1,0:T(8,128)(2,1)S(1)}, u32[]{:S(2)}, u32[]{:S(2)}) collective-permute-start(bf16[256,256]{1,0:T(8,128)(2,1)S(1)} %get-tuple-element.35), channel_id=1, source_target_pairs={{0,3},{1,0},{2,1},{3,2},{4,7},{5,4},{6,5},{7,6},{8,11},{9,8},{10,9... | collective-permute-start | bytes 393224 | tf_op jit(solution)/shard_map/ppermute | solution.py:414
  113.4 2.7 %all-to-all-done.4 = bf16[16,8,512]{2,1,0:T(8,128)(2,1)S(1)} async-done(((bf16[16,8,512]{2,1,0:T(8,128)(2,1)}), bf16[16,8,512]{2,1,0:T(8,128)(2,1)S(1)}, u32[]{:S(2)}, u32[]{:S(2)}) %all-to-all-start.4) | async-done | bytes 131104 | tf_op jit(solution)/shard_map/all_to_all | solution.py:316
  116.8 8.3 %all-to-all-start.5 = ((f32[8,8,512]{2,1,0:T(8,128)}), f32[8,8,512]{2,1,0:T(8,128)S(1)}, u32[]{:S(2)}, u32[]{:S(2)}) async-start(f32[8,8,512]{2,1,0:T(8,128)} %shard_map.115), calls=%async_computation.5 | async-start | bytes 262144 | tf_op jit(solution)/shard_map/all_to_all | solution.py:316
  125.1 1.5 %shard_map.114 = (bf16[224,1024]{1,0:T(8,128)(2,1)}, bf16[128,1024]{1,0:T(8,128)(2,1)}) custom-call(s32[1]{0:T(128)} %bitcast.place_ref, bf16[224,1024]{1,0:T(8,128)(2,1)S(1)} %copy-done.1, bf16[512,1024]{1,0:T(8,128)(2,1)S(1)} %copy-done, bf16[256,256]{1,0:T(8,128)(2,1)S(1)} %get-tuple-element.32.refs_0_, ...), custom_call_target="tpu_custom_call" | custom-call | tf_op jit(solution)/shard_map/pallas_call | solution.py:22
  126.6 3.7 %all-to-all-done.5 = f32[8,8,512]{2,1,0:T(8,128)S(1)} async-done(((f32[8,8,512]{2,1,0:T(8,128)}), f32[8,8,512]{2,1,0:T(8,128)S(1)}, u32[]{:S(2)}, u32[]{:S(2)}) %all-to-all-start.5) | async-done | bytes 131104 | tf_op jit(solution)/shard_map/all_to_all | solution.py:316
  (32 shorter events, 7.7 us)
Async XLA Ops:
  7.2 48.8 %all-gather.3.cloned.1.call-start = ((), (), s32[]{:S(2)}) async-start(), calls=%async_computation.6 | async-start | bytes 2293760 | tf_op jit(solution)/shard_map/all_gather | solution.py:347
  9.6 10.4 %all-to-all-start = ((bf16[4,128,256]{2,1,0:T(8,128)(2,1)}), bf16[4,128,256]{2,1,0:T(8,128)(2,1)S(1)}, u32[]{:S(2)}, u32[]{:S(2)}) async-start(bf16[4,128,256]{2,1,0:T(8,128)(2,1)} %shard_map.103), calls=%async_computation | async-start | bytes 524288 | tf_op jit(solution)/shard_map/all_to_all | solution.py:316
  19.9 18.6 %all-to-all-start.1 = ((bf16[4,400,256]{2,1,0:T(8,128)(2,1)}), bf16[4,400,256]{2,1,0:T(8,128)(2,1)S(1)}, u32[]{:S(2)}, u32[]{:S(2)}) async-start(bf16[4,400,256]{2,1,0:T(8,128)(2,1)} %shard_map.104), calls=%async_computation.1 | async-start | bytes 1638400 | tf_op jit(solution)/shard_map/all_to_all | solution.py:316
  23.7 14.8 %collective-permute-start.1 = (bf16[4,128,256]{2,1,0:T(8,128)(2,1)S(1)}, bf16[4,128,256]{2,1,0:T(8,128)(2,1)S(1)}, u32[]{:S(2)}, u32[]{:S(2)}) collective-permute-start(bf16[4,128,256]{2,1,0:T(8,128)(2,1)S(1)} %all-to-all-done.ring0), channel_id=1, source_target_pairs={{4,0},{8,4},{12,8},{16,12},{20,16},{24,20},{28,24},{32,28},{36,32}... | collective-permute-start | bytes 786440 | tf_op jit(solution)/shard_map/ppermute | solution.py:312
  34.8 10.7 %collective-permute-start = (bf16[3,128,256]{2,1,0:T(8,128)(2,1)S(1)}, bf16[3,128,256]{2,1,0:T(8,128)(2,1)S(1)}, u32[]{:S(2)}, u32[]{:S(2)}) collective-permute-start(bf16[3,128,256]{2,1,0:T(8,128)(2,1)S(1)} %slice.4), channel_id=1, source_target_pairs={{8,0},{12,4},{16,8},{20,12},{24,16},{28,20},{32,24},{36,28},{40,32... | collective-permute-start | bytes 589832 | tf_op jit(solution)/shard_map/ppermute | solution.py:312
  55.1 0.8 copy-start.2
  59.5 34.4 %all-to-all-start.3 = ((bf16[8,32,512]{2,1,0:T(8,128)(2,1)}), bf16[8,32,512]{2,1,0:T(8,128)(2,1)S(1)}, u32[]{:S(2)}, u32[]{:S(2)}) async-start(bf16[8,32,512]{2,1,0:T(8,128)(2,1)} %bitcast.11), calls=%async_computation.3 | async-start | bytes 524288 | tf_op jit(solution)/shard_map/all_to_all | solution.py:316
  68.5 34.2 %copy-start.3 = (bf16[4,128,256]{2,1,0:T(8,128)(2,1)S(1)}, bf16[4,128,256]{2,1,0:T(8,128)(2,1)}, u32[]{:S(2)}) copy-start(bf16[4,128,256]{2,1,0:T(8,128)(2,1)} %copy-done.2) | copy-start | bytes 786436
  68.5 12.3 %collective-permute-start.2 = (bf16[3,128,256]{2,1,0:T(8,128)(2,1)S(1)}, bf16[3,128,256]{2,1,0:T(8,128)(2,1)S(1)}, u32[]{:S(2)}, u32[]{:S(2)}) collective-permute-start(bf16[3,128,256]{2,1,0:T(8,128)(2,1)S(1)} %shard_map.108), channel_id=1, source_target_pairs={{60,0},{0,4},{4,8},{8,12},{12,16},{16,20},{20,24},{24,28},{28,32},... | collective-permute-start | bytes 589832 | tf_op jit(solution)/shard_map/ppermute | solution.py:312
  82.5 42.6 %copy-start = (bf16[512,1024]{1,0:T(8,128)(2,1)S(1)}, bf16[512,1024]{1,0:T(8,128)(2,1)}, u32[]{:S(2)}) copy-start(bf16[512,1024]{1,0:T(8,128)(2,1)} %out_ref.1) | copy-start | bytes 3145732
  82.5 42.6 %copy-start.1 = (bf16[224,1024]{1,0:T(8,128)(2,1)S(1)}, bf16[224,1024]{1,0:T(8,128)(2,1)}, u32[]{:S(2)}) copy-start(bf16[224,1024]{1,0:T(8,128)(2,1)} %cand_ref.1) | copy-start | bytes 1376260
  82.5 10.6 %collective-permute-start.3 = (bf16[4,128,256]{2,1,0:T(8,128)(2,1)S(1)}, bf16[4,128,256]{2,1,0:T(8,128)(2,1)S(1)}, u32[]{:S(2)}, u32[]{:S(2)}) collective-permute-start(bf16[4,128,256]{2,1,0:T(8,128)(2,1)S(1)} %shard_map.111), channel_id=1, source_target_pairs={{60,0},{0,4},{4,8},{8,12},{12,16},{16,20},{20,24},{24,28},{28,32},... | collective-permute-start | bytes 786440 | tf_op jit(solution)/shard_map/ppermute | solution.py:312
  93.2 0.7 copy-start.4
  94.6 8.1 %copy-start.5 = (bf16[4,128,256]{2,1,0:T(8,128)(2,1)S(1)}, bf16[4,128,256]{2,1,0:T(8,128)(2,1)}, u32[]{:S(2)}) copy-start(bf16[4,128,256]{2,1,0:T(8,128)(2,1)} %copy-done.4) | copy-start | bytes 786436
  94.6 21.6 %all-to-all-start.4 = ((bf16[16,8,512]{2,1,0:T(8,128)(2,1)}), bf16[16,8,512]{2,1,0:T(8,128)(2,1)S(1)}, u32[]{:S(2)}, u32[]{:S(2)}) async-start(bf16[16,8,512]{2,1,0:T(8,128)(2,1)} %bitcast.5), calls=%async_computation.4 | async-start | bytes 262144 | tf_op jit(solution)/shard_map/all_to_all | solution.py:316
  102.7 22.3 %collective-permute-start.4 = (bf16[256,256]{1,0:T(8,128)(2,1)S(1)}, bf16[256,256]{1,0:T(8,128)(2,1)S(1)}, u32[]{:S(2)}, u32[]{:S(2)}) collective-permute-start(bf16[256,256]{1,0:T(8,128)(2,1)S(1)} %get-tuple-element.33), channel_id=1, source_target_pairs={{0,1},{1,2},{2,3},{3,0},{4,5},{5,6},{6,7},{7,4},{8,9},{9,10},{10,1... | collective-permute-start | bytes 393224 | tf_op jit(solution)/shard_map/ppermute | solution.py:414
  106.0 19.1 %collective-permute-start.5 = (bf16[256,256]{1,0:T(8,128)(2,1)S(1)}, bf16[256,256]{1,0:T(8,128)(2,1)S(1)}, u32[]{:S(2)}, u32[]{:S(2)}) collective-permute-start(bf16[256,256]{1,0:T(8,128)(2,1)S(1)} %get-tuple-element.34), channel_id=1, source_target_pairs={{0,2},{1,3},{2,0},{3,1},{4,6},{5,7},{6,4},{7,5},{8,10},{9,11},{10,... | collective-permute-start | bytes 393224 | tf_op jit(solution)/shard_map/ppermute | solution.py:414
  110.3 14.8 %collective-permute-start.6 = (bf16[256,256]{1,0:T(8,128)(2,1)S(1)}, bf16[256,256]{1,0:T(8,128)(2,1)S(1)}, u32[]{:S(2)}, u32[]{:S(2)}) collective-permute-start(bf16[256,256]{1,0:T(8,128)(2,1)S(1)} %get-tuple-element.35), channel_id=1, source_target_pairs={{0,3},{1,0},{2,1},{3,2},{4,7},{5,4},{6,5},{7,6},{8,11},{9,8},{10,9... | collective-permute-start | bytes 393224 | tf_op jit(solution)/shard_map/ppermute | solution.py:414
  116.8 13.5 %all-to-all-start.5 = ((f32[8,8,512]{2,1,0:T(8,128)}), f32[8,8,512]{2,1,0:T(8,128)S(1)}, u32[]{:S(2)}, u32[]{:S(2)}) async-start(f32[8,8,512]{2,1,0:T(8,128)} %shard_map.115), calls=%async_computation.5 | async-start | bytes 262144 | tf_op jit(solution)/shard_map/all_to_all | solution.py:316
Sparse Core Ops, SparseCore 0:
  10.1 43.9 all-gather.2

commit v7 on v6

--- a/solution.py
+++ b/solution.py
@@ -389,7 +389,7 @@
         cots,
         local=(gated,),
     )
-    out_grad, late_grads = barrier((out_grad, grads))
+    out_grad, back2, late_grads = barrier((out_grad, back2, grads))
     part = exchanged(out_grad.reshape(cores * zl, size // zl, half), ("core", "zl"))
     back1 = pl.pallas_call(
         back1_kernel,
@@ -399,9 +399,10 @@
         scratch_shapes=[pltpu.VMEM(ring1.shape, F32)],
         compiler_params=pltpu.CompilerParams(vmem_limit_bytes=12 * 1024 * 1024),
     )(ring1, bundle, late_grads, back2)
-    part, back1 = barrier((part, moved(back1, -1)))
-    part, back1 = barrier((on_core(fold_kernel, shaped((zh, xs, own, half), BF16), part), back1))
     back0 = on_core(back0_kernel, shaped(ring0.shape, F32), ring0, bundle, late_grads)
+    part, back0, back1 = barrier((part, back0, moved(back1, -1)))
+    part = on_core(fold_kernel, shaped((zh, xs, own, half), BF16), part)
+    part, back0, back1 = barrier((part, back0, back1))
     part = exchanged(part.reshape(zh * xs, own, half), ("zh", "x")).reshape(zh, xs, own, half)
     depth = lax.axis_index("zh").reshape(1).astype(jnp.int32)
     peers = lax.axis_size("y") * cores

time: 139 us -> 135 us (0.971)
  waiting for transfers between devices: 31.1 us -> 21.8 us
  starting transfers between devices: 63 us -> 65.8 us
  local copies, waits for them, and re-layouts: 0.75 us -> 2.64 us
    ppermute x4, waiting for transfers between devices: 23.4 us -> 15.2 us  [moved(): lax.ppermute(block, DEPTH, [((i + distance) % size, i) for i in range(siz...]
    all_to_all x5, starting transfers between devices: 32.6 us -> 35.6 us  [exchanged(): return lax.all_to_all(chunks, axis, 0, 0, tiled=True)]
    unnamed x12, local copies, waits for them, and re-layouts: 0.73 us -> 2.62 us
  transfers between devices with their start and end apart: 13 -> 13, of which waited for: 7 -> 7; matrix products, arithmetic and copies ran while one was open for 0% -> 0% of each run, Pallas kernels for 11% -> 14%
where the time goes in v7:
time: 135 us; the launch traced here: 134 us
  starting transfers between devices  65.8 us (49%)
  waiting for transfers between devices  21.8 us (16%)
  Pallas kernels  21.1 us (16%)
  between operations  14.3 us (11%)
  blocking collectives  8.47 us (6%)
  local copies, waits for them, and re-layouts  2.64 us (2%)
    all_to_all x5, starting transfers between devices, exchanged(): return lax.all_to_all(chunks, axis, 0, 0, tiled=True)  35.6 us
    ppermute x4, starting transfers between devices, moved(): lax.ppermute(block, DEPTH, [((i + distance) % size, i) for i in range(siz...  19.5 us
    ppermute x4, waiting for transfers between devices, moved(): lax.ppermute(block, DEPTH, [((i + distance) % size, i) for i in range(siz...  15.2 us
    ppermute x3, starting transfers between devices, on_device(): lax.ppermute(parcel, 'x', [(i, (i + step) % HEADS) for i in range(HEADS)])  10.7 us
    pallas_call x10, Pallas kernels, on_core(): pl.pallas_call(kernel, out_shape=outs, in_specs=[pl.BlockSpec(memory_spac...  9.21 us
    pallas_call x2, Pallas kernels, on_fetched(): pl.pallas_call(body, out_shape=outs, in_specs=[pl.BlockSpec(memory_space=...  8.56 us
    all_to_all x1, blocking collectives, exchanged(): return lax.all_to_all(chunks, axis, 0, 0, tiled=True)  8.47 us
    all_to_all x5, waiting for transfers between devices, exchanged(): return lax.all_to_all(chunks, axis, 0, 0, tiled=True)  5.86 us
  transfers between devices with their start and end apart: 13, of which 7 were waited for; matrix products, arithmetic and copies ran while one was open for 0% of the time, Pallas kernels for 14%

profile of v7, /device:TPU:1, one launch (start us, length us, event | category | flops | bytes accessed | tf_op | source)
XLA Modules:
  0.0 134.1 jit_solution(17679183581711176720)
XLA Ops:
  7.9 1.6 %shard_map.103 = bf16[4,128,256]{2,1,0:T(8,128)(2,1)} custom-call(bf16[128,1024]{1,0:T(8,128)(2,1)} %history_ref.1), custom_call_target="tpu_custom_call" | custom-call | tf_op jit(solution)/shard_map/pallas_call | solution.py:349
  9.6 4.9 %all-to-all-start = ((bf16[4,128,256]{2,1,0:T(8,128)(2,1)}), bf16[4,128,256]{2,1,0:T(8,128)(2,1)S(1)}, u32[]{:S(2)}, u32[]{:S(2)}) async-start(bf16[4,128,256]{2,1,0:T(8,128)(2,1)} %shard_map.103), calls=%async_computation | async-start | bytes 524288 | tf_op jit(solution)/shard_map/all_to_all | solution.py:316
  14.4 5.0 %shard_map.104 = bf16[4,400,256]{2,1,0:T(8,128)(2,1)} custom-call(s32[2,8]{1,0:T(2,128)} %refs_0_.1, s32[2]{0:T(128)} %refs_1_.1, s32[1,224]{1,0:T(1,128)} %bitcast.12, bf16[224,1024]{1,0:T(8,128)(2,1)} %cand_ref.1, bf16[224,1024]{1,0:T(8,128)(2,1)} %refs_4_.1, bf16[1024,1024]{1,0:T(8,128)(2,1)} %refs_5_.1, bf16[512,1024]{1,0:T(8,128)(2,1)} %out_ref.1), custom_call_target="tpu_custom_call" | custom-call | tf_op jit(solution)/shard_map/pallas_call | solution.py:51
  19.9 3.7 %all-to-all-start.1 = ((bf16[4,400,256]{2,1,0:T(8,128)(2,1)}), bf16[4,400,256]{2,1,0:T(8,128)(2,1)S(1)}, u32[]{:S(2)}, u32[]{:S(2)}) async-start(bf16[4,400,256]{2,1,0:T(8,128)(2,1)} %shard_map.104), calls=%async_computation.1 | async-start | bytes 1638400 | tf_op jit(solution)/shard_map/all_to_all | solution.py:316
  23.7 11.1 %collective-permute-start.1 = (bf16[4,128,256]{2,1,0:T(8,128)(2,1)S(1)}, bf16[4,128,256]{2,1,0:T(8,128)(2,1)S(1)}, u32[]{:S(2)}, u32[]{:S(2)}) collective-permute-start(bf16[4,128,256]{2,1,0:T(8,128)(2,1)S(1)} %all-to-all-done.ring0), channel_id=1, source_target_pairs={{4,0},{8,4},{12,8},{16,12},{20,16},{24,20},{28,24},{32,28},{36,32}... | collective-permute-start | bytes 786440 | tf_op jit(solution)/shard_map/ppermute | solution.py:312
  34.8 3.1 %collective-permute-start = (bf16[3,128,256]{2,1,0:T(8,128)(2,1)S(1)}, bf16[3,128,256]{2,1,0:T(8,128)(2,1)S(1)}, u32[]{:S(2)}, u32[]{:S(2)}) collective-permute-start(bf16[3,128,256]{2,1,0:T(8,128)(2,1)S(1)} %slice.4), channel_id=1, source_target_pairs={{8,0},{12,4},{16,8},{20,12},{24,16},{28,20},{32,24},{36,28},{40,32... | collective-permute-start | bytes 589832 | tf_op jit(solution)/shard_map/ppermute | solution.py:312
  38.5 1.7 %shard_map.105.before = f32[4,128,256]{2,1,0:T(8,128)S(1)} custom-call(bf16[4,128,256]{2,1,0:T(8,128)(2,1)S(1)} %all-to-all-done.ring0, bf16[4,128,256]{2,1,0:T(8,128)(2,1)S(1)} %collective-permute-done.1.ring1, bf16[4,400,256]{2,1,0:T(8,128)(2,1)S(1)} %all-to-all-done.1.bundle), custom_call_target="tpu_custom_call" | custom-call | tf_op jit(solution)/shard_map/pallas_call | solution.py:22
  40.2 5.4 %collective-permute-done.ring2 = bf16[3,128,256]{2,1,0:T(8,128)(2,1)S(1)} collective-permute-done((bf16[3,128,256]{2,1,0:T(8,128)(2,1)S(1)}, bf16[3,128,256]{2,1,0:T(8,128)(2,1)S(1)}, u32[]{:S(2)}, u32[]{:S(2)}) %collective-permute-start) | collective-permute-done | bytes 196640 | tf_op jit(solution)/shard_map/ppermute | solution.py:312
  46.4 8.5 %all_to_all.30.stats = f32[4,16,256]{2,1,0:T(8,128)S(1)} all-to-all(f32[4,16,256]{2,1,0:T(8,128)S(1)} %broadcast_in_dim.2), channel_id=1, replica_groups=mesh['y'=4,'core'=2,'zh'=4,'zl'=4,'x'=4] {'x'}, dimensions={0} | all-to-all | bytes 131072 | tf_op jit(solution)/shard_map/all_to_all | solution.py:316
  55.9 1.9 %collective-permute-start.2 = (bf16[3,128,256]{2,1,0:T(8,128)(2,1)S(1)}, bf16[3,128,256]{2,1,0:T(8,128)(2,1)S(1)}, u32[]{:S(2)}, u32[]{:S(2)}) collective-permute-start(bf16[3,128,256]{2,1,0:T(8,128)(2,1)S(1)} %shard_map.108), channel_id=1, source_target_pairs={{60,0},{0,4},{4,8},{8,12},{12,16},{16,20},{20,24},{24,28},{28,32},... | collective-permute-start | bytes 589832 | tf_op jit(solution)/shard_map/ppermute | solution.py:312
  57.9 3.6 %shard_map.109 = bf16[2,4,32,512]{3,2,1,0:T(8,128)(2,1)} custom-call(bf16[4,224,1024]{2,1,0:T(8,128)(2,1)} %bitcast.10, bf16[4,128,256]{2,1,0:T(8,128)(2,1)} %copy-done.2), custom_call_target="tpu_custom_call" | custom-call | tf_op jit(solution)/shard_map/pallas_call | solution.py:51
  61.4 2.1 %collective-permute-done.2.arrived = bf16[3,128,256]{2,1,0:T(8,128)(2,1)S(1)} collective-permute-done((bf16[3,128,256]{2,1,0:T(8,128)(2,1)S(1)}, bf16[3,128,256]{2,1,0:T(8,128)(2,1)S(1)}, u32[]{:S(2)}, u32[]{:S(2)}) %collective-permute-start.2) | collective-permute-done | bytes 196640 | tf_op jit(solution)/shard_map/ppermute | solution.py:312
  63.5 11.7 %all-to-all-start.3 = ((bf16[8,32,512]{2,1,0:T(8,128)(2,1)}), bf16[8,32,512]{2,1,0:T(8,128)(2,1)}, u32[]{:S(2)}, u32[]{:S(2)}) async-start(bf16[8,32,512]{2,1,0:T(8,128)(2,1)} %bitcast.11), calls=%async_computation.3 | async-start | bytes 524288 | tf_op jit(solution)/shard_map/all_to_all | solution.py:316
  75.2 1.7 %shard_map.111 = bf16[4,128,256]{2,1,0:T(8,128)(2,1)S(1)} custom-call(bf16[4,128,256]{2,1,0:T(8,128)(2,1)S(1)} %collective-permute-done.1.ring1, bf16[4,400,256]{2,1,0:T(8,128)(2,1)S(1)} %all-to-all-done.1.bundle, bf16[4,128,256]{2,1,0:T(8,128)(2,1)S(1)} %get-tuple-element.31.grads, bf16[3,128,256]{2,1,0:T(8,128)(2,1)S(1)} %collective-permute-done.2.arrived), custom_call_target="tpu_custom_call" | custom-call | tf_op jit(solution)/shard_map/pallas_call | solution.py:394
  76.9 3.4 %collective-permute-start.3 = (bf16[4,128,256]{2,1,0:T(8,128)(2,1)S(1)}, bf16[4,128,256]{2,1,0:T(8,128)(2,1)S(1)}, u32[]{:S(2)}, u32[]{:S(2)}) collective-permute-start(bf16[4,128,256]{2,1,0:T(8,128)(2,1)S(1)} %shard_map.111), channel_id=1, source_target_pairs={{60,0},{0,4},{4,8},{8,12},{12,16},{16,20},{20,24},{24,28},{28,32},... | collective-permute-start | bytes 786440 | tf_op jit(solution)/shard_map/ppermute | solution.py:312
  81.6 7.1 %collective-permute-done.3.back1 = bf16[4,128,256]{2,1,0:T(8,128)(2,1)S(1)} collective-permute-done((bf16[4,128,256]{2,1,0:T(8,128)(2,1)S(1)}, bf16[4,128,256]{2,1,0:T(8,128)(2,1)S(1)}, u32[]{:S(2)}, u32[]{:S(2)}) %collective-permute-start.3) | collective-permute-done | bytes 262176 | tf_op jit(solution)/shard_map/ppermute | solution.py:312
  89.4 1.6 %shard_map.112 = bf16[4,4,8,512]{3,2,1,0:T(8,128)(2,1)} custom-call(bf16[8,32,512]{2,1,0:T(8,128)(2,1)} %all-to-all-done.3.parts), custom_call_target="tpu_custom_call" | custom-call | tf_op jit(solution)/shard_map/pallas_call | solution.py:22
  91.1 7.3 %all-to-all-start.4 = ((bf16[16,8,512]{2,1,0:T(8,128)(2,1)}), bf16[16,8,512]{2,1,0:T(8,128)(2,1)S(1)}, u32[]{:S(2)}, u32[]{:S(2)}) async-start(bf16[16,8,512]{2,1,0:T(8,128)(2,1)} %bitcast.5), calls=%async_computation.4 | async-start | bytes 262144 | tf_op jit(solution)/shard_map/all_to_all | solution.py:316
  100.3 3.3 %collective-permute-start.4 = (bf16[256,256]{1,0:T(8,128)(2,1)S(1)}, bf16[256,256]{1,0:T(8,128)(2,1)S(1)}, u32[]{:S(2)}, u32[]{:S(2)}) collective-permute-start(bf16[256,256]{1,0:T(8,128)(2,1)S(1)} %get-tuple-element.39), channel_id=1, source_target_pairs={{0,1},{1,2},{2,3},{3,0},{4,5},{5,6},{6,7},{7,4},{8,9},{9,10},{10,1... | collective-permute-start | bytes 393224 | tf_op jit(solution)/shard_map/ppermute | solution.py:415
  103.6 4.3 %collective-permute-start.5 = (bf16[256,256]{1,0:T(8,128)(2,1)S(1)}, bf16[256,256]{1,0:T(8,128)(2,1)S(1)}, u32[]{:S(2)}, u32[]{:S(2)}) collective-permute-start(bf16[256,256]{1,0:T(8,128)(2,1)S(1)} %get-tuple-element.40), channel_id=1, source_target_pairs={{0,2},{1,3},{2,0},{3,1},{4,6},{5,7},{6,4},{7,5},{8,10},{9,11},{10,... | collective-permute-start | bytes 393224 | tf_op jit(solution)/shard_map/ppermute | solution.py:415
  107.9 3.1 %collective-permute-start.6 = (bf16[256,256]{1,0:T(8,128)(2,1)S(1)}, bf16[256,256]{1,0:T(8,128)(2,1)S(1)}, u32[]{:S(2)}, u32[]{:S(2)}) collective-permute-start(bf16[256,256]{1,0:T(8,128)(2,1)S(1)} %get-tuple-element.41), channel_id=1, source_target_pairs={{0,3},{1,0},{2,1},{3,2},{4,7},{5,4},{6,5},{7,6},{8,11},{9,8},{10,9... | collective-permute-start | bytes 393224 | tf_op jit(solution)/shard_map/ppermute | solution.py:415
  111.0 1.6 %all-to-all-done.4 = bf16[16,8,512]{2,1,0:T(8,128)(2,1)S(1)} async-done(((bf16[16,8,512]{2,1,0:T(8,128)(2,1)}), bf16[16,8,512]{2,1,0:T(8,128)(2,1)S(1)}, u32[]{:S(2)}, u32[]{:S(2)}) %all-to-all-start.4) | async-done | bytes 131104 | tf_op jit(solution)/shard_map/all_to_all | solution.py:316
  113.3 8.1 %all-to-all-start.5 = ((f32[8,8,512]{2,1,0:T(8,128)}), f32[8,8,512]{2,1,0:T(8,128)S(1)}, u32[]{:S(2)}, u32[]{:S(2)}) async-start(f32[8,8,512]{2,1,0:T(8,128)} %shard_map.115), calls=%async_computation.5 | async-start | bytes 262144 | tf_op jit(solution)/shard_map/all_to_all | solution.py:316
  122.9 3.7 %all-to-all-done.5 = f32[8,8,512]{2,1,0:T(8,128)S(1)} async-done(((f32[8,8,512]{2,1,0:T(8,128)}), f32[8,8,512]{2,1,0:T(8,128)S(1)}, u32[]{:S(2)}, u32[]{:S(2)}) %all-to-all-start.5) | async-done | bytes 131104 | tf_op jit(solution)/shard_map/all_to_all | solution.py:316
  (32 shorter events, 10.4 us)
Async XLA Ops:
  7.2 50.7 %all-gather.3.cloned.1.call-start = ((), (), s32[]{:S(2)}) async-start(), calls=%async_computation.6 | async-start | bytes 2293760 | tf_op jit(solution)/shard_map/all_gather | solution.py:347
  9.6 10.4 %all-to-all-start = ((bf16[4,128,256]{2,1,0:T(8,128)(2,1)}), bf16[4,128,256]{2,1,0:T(8,128)(2,1)S(1)}, u32[]{:S(2)}, u32[]{:S(2)}) async-start(bf16[4,128,256]{2,1,0:T(8,128)(2,1)} %shard_map.103), calls=%async_computation | async-start | bytes 524288 | tf_op jit(solution)/shard_map/all_to_all | solution.py:316
  19.9 18.6 %all-to-all-start.1 = ((bf16[4,400,256]{2,1,0:T(8,128)(2,1)}), bf16[4,400,256]{2,1,0:T(8,128)(2,1)S(1)}, u32[]{:S(2)}, u32[]{:S(2)}) async-start(bf16[4,400,256]{2,1,0:T(8,128)(2,1)} %shard_map.104), calls=%async_computation.1 | async-start | bytes 1638400 | tf_op jit(solution)/shard_map/all_to_all | solution.py:316
  23.7 14.8 %collective-permute-start.1 = (bf16[4,128,256]{2,1,0:T(8,128)(2,1)S(1)}, bf16[4,128,256]{2,1,0:T(8,128)(2,1)S(1)}, u32[]{:S(2)}, u32[]{:S(2)}) collective-permute-start(bf16[4,128,256]{2,1,0:T(8,128)(2,1)S(1)} %all-to-all-done.ring0), channel_id=1, source_target_pairs={{4,0},{8,4},{12,8},{16,12},{20,16},{24,20},{28,24},{32,28},{36,32}... | collective-permute-start | bytes 786440 | tf_op jit(solution)/shard_map/ppermute | solution.py:312
  34.8 10.7 %collective-permute-start = (bf16[3,128,256]{2,1,0:T(8,128)(2,1)S(1)}, bf16[3,128,256]{2,1,0:T(8,128)(2,1)S(1)}, u32[]{:S(2)}, u32[]{:S(2)}) collective-permute-start(bf16[3,128,256]{2,1,0:T(8,128)(2,1)S(1)} %slice.4), channel_id=1, source_target_pairs={{8,0},{12,4},{16,8},{20,12},{24,16},{28,20},{32,24},{36,28},{40,32... | collective-permute-start | bytes 589832 | tf_op jit(solution)/shard_map/ppermute | solution.py:312
  55.1 2.8 %copy-start.2 = (bf16[4,128,256]{2,1,0:T(8,128)(2,1)}, bf16[4,128,256]{2,1,0:T(8,128)(2,1)S(1)}, u32[]{:S(2)}) copy-start(bf16[4,128,256]{2,1,0:T(8,128)(2,1)S(1)} %get-tuple-element.28.refs_1_.gated_ref) | copy-start | bytes 786436
  55.9 7.6 %collective-permute-start.2 = (bf16[3,128,256]{2,1,0:T(8,128)(2,1)S(1)}, bf16[3,128,256]{2,1,0:T(8,128)(2,1)S(1)}, u32[]{:S(2)}, u32[]{:S(2)}) collective-permute-start(bf16[3,128,256]{2,1,0:T(8,128)(2,1)S(1)} %shard_map.108), channel_id=1, source_target_pairs={{60,0},{0,4},{4,8},{8,12},{12,16},{16,20},{20,24},{24,28},{28,32},... | collective-permute-start | bytes 589832 | tf_op jit(solution)/shard_map/ppermute | solution.py:312
  63.5 25.9 %all-to-all-start.3 = ((bf16[8,32,512]{2,1,0:T(8,128)(2,1)}), bf16[8,32,512]{2,1,0:T(8,128)(2,1)}, u32[]{:S(2)}, u32[]{:S(2)}) async-start(bf16[8,32,512]{2,1,0:T(8,128)(2,1)} %bitcast.11), calls=%async_computation.3 | async-start | bytes 524288 | tf_op jit(solution)/shard_map/all_to_all | solution.py:316
  76.9 44.4 %copy-start = (bf16[512,1024]{1,0:T(8,128)(2,1)S(1)}, bf16[512,1024]{1,0:T(8,128)(2,1)}, u32[]{:S(2)}) copy-start(bf16[512,1024]{1,0:T(8,128)(2,1)} %out_ref.1) | copy-start | bytes 3145732
  76.9 44.4 %copy-start.1 = (bf16[224,1024]{1,0:T(8,128)(2,1)S(1)}, bf16[224,1024]{1,0:T(8,128)(2,1)}, u32[]{:S(2)}) copy-start(bf16[224,1024]{1,0:T(8,128)(2,1)} %cand_ref.1) | copy-start | bytes 1376260
  76.9 11.8 %collective-permute-start.3 = (bf16[4,128,256]{2,1,0:T(8,128)(2,1)S(1)}, bf16[4,128,256]{2,1,0:T(8,128)(2,1)S(1)}, u32[]{:S(2)}, u32[]{:S(2)}) collective-permute-start(bf16[4,128,256]{2,1,0:T(8,128)(2,1)S(1)} %shard_map.111), channel_id=1, source_target_pairs={{60,0},{0,4},{4,8},{8,12},{12,16},{16,20},{20,24},{24,28},{28,32},... | collective-permute-start | bytes 786440 | tf_op jit(solution)/shard_map/ppermute | solution.py:312
  88.7 0.7 copy-start.4
  91.1 21.5 %all-to-all-start.4 = ((bf16[16,8,512]{2,1,0:T(8,128)(2,1)}), bf16[16,8,512]{2,1,0:T(8,128)(2,1)S(1)}, u32[]{:S(2)}, u32[]{:S(2)}) async-start(bf16[16,8,512]{2,1,0:T(8,128)(2,1)} %bitcast.5), calls=%async_computation.4 | async-start | bytes 262144 | tf_op jit(solution)/shard_map/all_to_all | solution.py:316
  98.3 1.0 copy-start.3
  99.3 0.9 copy-start.5
  100.3 21.0 %collective-permute-start.4 = (bf16[256,256]{1,0:T(8,128)(2,1)S(1)}, bf16[256,256]{1,0:T(8,128)(2,1)S(1)}, u32[]{:S(2)}, u32[]{:S(2)}) collective-permute-start(bf16[256,256]{1,0:T(8,128)(2,1)S(1)} %get-tuple-element.39), channel_id=1, source_target_pairs={{0,1},{1,2},{2,3},{3,0},{4,5},{5,6},{6,7},{7,4},{8,9},{9,10},{10,1... | collective-permute-start | bytes 393224 | tf_op jit(solution)/shard_map/ppermute | solution.py:415
  103.6 17.8 %collective-permute-start.5 = (bf16[256,256]{1,0:T(8,128)(2,1)S(1)}, bf16[256,256]{1,0:T(8,128)(2,1)S(1)}, u32[]{:S(2)}, u32[]{:S(2)}) collective-permute-start(bf16[256,256]{1,0:T(8,128)(2,1)S(1)} %get-tuple-element.40), channel_id=1, source_target_pairs={{0,2},{1,3},{2,0},{3,1},{4,6},{5,7},{6,4},{7,5},{8,10},{9,11},{10,... | collective-permute-start | bytes 393224 | tf_op jit(solution)/shard_map/ppermute | solution.py:415
  107.9 13.4 %collective-permute-start.6 = (bf16[256,256]{1,0:T(8,128)(2,1)S(1)}, bf16[256,256]{1,0:T(8,128)(2,1)S(1)}, u32[]{:S(2)}, u32[]{:S(2)}) collective-permute-start(bf16[256,256]{1,0:T(8,128)(2,1)S(1)} %get-tuple-element.41), channel_id=1, source_target_pairs={{0,3},{1,0},{2,1},{3,2},{4,7},{5,4},{6,5},{7,6},{8,11},{9,8},{10,9... | collective-permute-start | bytes 393224 | tf_op jit(solution)/shard_map/ppermute | solution.py:415
  113.3 13.3 %all-to-all-start.5 = ((f32[8,8,512]{2,1,0:T(8,128)}), f32[8,8,512]{2,1,0:T(8,128)S(1)}, u32[]{:S(2)}, u32[]{:S(2)}) async-start(f32[8,8,512]{2,1,0:T(8,128)} %shard_map.115), calls=%async_computation.5 | async-start | bytes 262144 | tf_op jit(solution)/shard_map/all_to_all | solution.py:316
Sparse Core Ops, SparseCore 0:
  10.1 43.9 all-gather.2

commit v8 on v7

--- a/solution.py
+++ b/solution.py
@@ -28,10 +28,10 @@
     )(*scalars, *operands)
 
 
-def on_fetched(kernel, outs, *operands, scalars=(), local=()):
+def on_fetched(kernel, outs, *operands, scalars=()):
     fetched = list(scalars) + list(operands)
     many = len(fetched)
-    first = many + len(local) + len(jax.tree.leaves(outs))
+    first = many + len(jax.tree.leaves(outs))
     pieces = [4 if one.size >= 1 << 19 else 1 for one in fetched]
 
     def body(*refs):
@@ -51,14 +51,13 @@
     return pl.pallas_call(
         body,
         out_shape=outs,
-        in_specs=[pl.BlockSpec(memory_space=pl.ANY)] * many
-        + [pl.BlockSpec(memory_space=pltpu.VMEM)] * len(local),
+        in_specs=[pl.BlockSpec(memory_space=pl.ANY)] * many,
         out_specs=jax.tree.map(lambda _: pl.BlockSpec(memory_space=pltpu.VMEM), outs),
         scratch_shapes=[pltpu.SMEM(one.shape, one.dtype) for one in scalars]
         + [pltpu.VMEM(one.shape, one.dtype) for one in operands]
         + [pltpu.SemaphoreType.DMA((many, 4))],
         compiler_params=pltpu.CompilerParams(vmem_limit_bytes=56 * 1024 * 1024),
-    )(*fetched, *local)
+    )(*fetched)
 
 
 def shaped(shape, kind):
@@ -199,11 +198,9 @@
         grad_ref[group] = (inv_scale * (dy - mean_dy - normed * mean_mixed)).astype(BF16)
 
 
-def out_grad_kernel(total_cands, cot_rows, gated, out_grad_ref):
-    cots, cots_here = cot_rows
+def out_grad_kernel(total_cands, cots, gated, out_grad_ref):
     count = cots.shape[1]
     total = None
-    cots_here()
     for group in range(HEADS):
         part = jnp.dot(gated[group, :, :count], cots[group], preferred_element_type=F32)
         total = part if total is None else total + part
@@ -250,11 +247,14 @@
     back(2, ring2, bundle, grads, sum_ref)
 
 
-def back1_kernel(ring1, bundle, grads, arrived, sum_ref, total):
-    back(1, ring1, bundle, grads, total)
+def back1_kernel(ring1, bundle, grads, sum_ref):
+    back(1, ring1, bundle, grads, sum_ref)
+
+
+def add_kernel(own, arrived, sum_ref):
     count = arrived.shape[0]
-    sum_ref[:count] = (total[:count] + arrived[...].astype(F32)).astype(BF16)
-    sum_ref[count:] = total[count:].astype(BF16)
+    sum_ref[:count] = (own[:count] + arrived[...].astype(F32)).astype(BF16)
+    sum_ref[count:] = own[count:].astype(BF16)
 
 
 def back0_kernel(ring0, bundle, grads, sum_ref):
@@ -383,22 +383,16 @@
     back2 = on_core(back2_kernel, shaped(ring2.shape, BF16), ring2, bundle, grads)
     gated, back2 = barrier((gated, back2))
     back2 = moved(back2, -1)
-    out_grad = on_fetched(
+    out_grad = on_core(
         lambda *refs: out_grad_kernel(total_cands, *refs),
         shaped((cores, zl, size // zl, half), BF16),
         cots,
-        local=(gated,),
-    )
-    out_grad, back2, late_grads = barrier((out_grad, back2, grads))
+        gated,
+    )
+    back1 = on_core(back1_kernel, shaped(ring1.shape, F32), ring1, bundle, grads)
+    back1 = on_core(add_kernel, shaped(ring1.shape, BF16), back1, back2)
+    out_grad, back1, late_grads = barrier((out_grad, back1, grads))
     part = exchanged(out_grad.reshape(cores * zl, size // zl, half), ("core", "zl"))
-    back1 = pl.pallas_call(
-        back1_kernel,
-        out_shape=shaped(ring1.shape, BF16),
-        in_specs=[pl.BlockSpec(memory_space=pltpu.VMEM)] * 4,
-        out_specs=pl.BlockSpec(memory_space=pltpu.VMEM),
-        scratch_shapes=[pltpu.VMEM(ring1.shape, F32)],
-        compiler_params=pltpu.CompilerParams(vmem_limit_bytes=12 * 1024 * 1024),
-    )(ring1, bundle, late_grads, back2)
     back0 = on_core(back0_kernel, shaped(ring0.shape, F32), ring0, bundle, late_grads)
     part, back0, back1 = barrier((part, back0, moved(back1, -1)))
     part = on_core(fold_kernel, shaped((zh, xs, own, half), BF16), part)

time: 135 us -> 138 us (1.022)
  waiting for transfers between devices: 21.8 us -> 23.7 us
  Pallas kernels: 21.1 us -> 19.5 us
  local copies, waits for them, and re-layouts: 2.64 us -> 4.13 us
    pallas_call x10 -> x13, Pallas kernels: 9.21 us -> 12.9 us  [on_core(): pl.pallas_call(kernel, out_shape=outs, in_specs=[pl.BlockSpec(memory_spac...]
    pallas_call x2 -> x1, Pallas kernels: 8.56 us -> 5.02 us  [on_fetched(): pl.pallas_call(body, out_shape=outs, in_specs=[pl.BlockSpec(memory_space=...]
    ppermute x4, waiting for transfers between devices: 15.2 us -> 17.3 us  [moved(): lax.ppermute(block, DEPTH, [((i + distance) % size, i) for i in range(siz...]
    pallas_call x1 -> x0, Pallas kernels: 1.73 us -> none  [on_device(): pl.pallas_call(back1_kernel, out_shape=shaped(ring1.shape, BF16), in_spec...]
    unnamed x12 -> x14, local copies, waits for them, and re-layouts: 2.62 us -> 4.11 us
  transfers between devices with their start and end apart: 13 -> 13, of which waited for: 7 -> 7; matrix products, arithmetic and copies ran while one was open for 0% -> 0% of each run, Pallas kernels for 14% -> 12%
where the time goes in v8:
time: 138 us; the launch traced here: 137 us
  starting transfers between devices  66.6 us (48%)
  waiting for transfers between devices  23.7 us (17%)
  Pallas kernels  19.5 us (14%)
  between operations  14.2 us (10%)
  blocking collectives  8.48 us (6%)
  local copies, waits for them, and re-layouts  4.13 us (3%)
    all_to_all x5, starting transfers between devices, exchanged(): return lax.all_to_all(chunks, axis, 0, 0, tiled=True)  36.4 us
    ppermute x4, starting transfers between devices, moved(): lax.ppermute(block, DEPTH, [((i + distance) % size, i) for i in range(siz...  19.5 us
    ppermute x4, waiting for transfers between devices, moved(): lax.ppermute(block, DEPTH, [((i + distance) % size, i) for i in range(siz...  17.3 us
    pallas_call x13, Pallas kernels, on_core(): pl.pallas_call(kernel, out_shape=outs, in_specs=[pl.BlockSpec(memory_spac...  12.9 us
    ppermute x3, starting transfers between devices, on_device(): lax.ppermute(parcel, 'x', [(i, (i + step) % HEADS) for i in range(HEADS)])  10.7 us
    all_to_all x1, blocking collectives, exchanged(): return lax.all_to_all(chunks, axis, 0, 0, tiled=True)  8.48 us
    all_to_all x5, waiting for transfers between devices, exchanged(): return lax.all_to_all(chunks, axis, 0, 0, tiled=True)  5.75 us
    pallas_call x1, Pallas kernels, on_fetched(): pl.pallas_call(body, out_shape=outs, in_specs=[pl.BlockSpec(memory_space=...  5.02 us
  transfers between devices with their start and end apart: 13, of which 7 were waited for; matrix products, arithmetic and copies ran while one was open for 0% of the time, Pallas kernels for 12%

profile of v8, /device:TPU:1, one launch (start us, length us, event | category | flops | bytes accessed | tf_op | source)
XLA Modules:
  0.0 136.6 jit_solution(91996252344083940)
XLA Ops:
  7.9 1.6 %shard_map.103 = bf16[4,128,256]{2,1,0:T(8,128)(2,1)} custom-call(bf16[128,1024]{1,0:T(8,128)(2,1)} %history_ref.1), custom_call_target="tpu_custom_call" | custom-call | tf_op jit(solution)/shard_map/pallas_call | solution.py:349
  9.6 4.9 %all-to-all-start = ((bf16[4,128,256]{2,1,0:T(8,128)(2,1)}), bf16[4,128,256]{2,1,0:T(8,128)(2,1)S(1)}, u32[]{:S(2)}, u32[]{:S(2)}) async-start(bf16[4,128,256]{2,1,0:T(8,128)(2,1)} %shard_map.103), calls=%async_computation | async-start | bytes 524288 | tf_op jit(solution)/shard_map/all_to_all | solution.py:316
  14.4 5.0 %shard_map.104 = bf16[4,400,256]{2,1,0:T(8,128)(2,1)} custom-call(s32[2,8]{1,0:T(2,128)} %refs_0_.1, s32[2]{0:T(128)} %refs_1_.1, s32[1,224]{1,0:T(1,128)} %bitcast.11, bf16[224,1024]{1,0:T(8,128)(2,1)} %cand_ref.1, bf16[224,1024]{1,0:T(8,128)(2,1)} %refs_4_.1, bf16[1024,1024]{1,0:T(8,128)(2,1)} %refs_5_.1, bf16[512,1024]{1,0:T(8,128)(2,1)} %out_ref.1), custom_call_target="tpu_custom_call" | custom-call | tf_op jit(solution)/shard_map/pallas_call | solution.py:51
  19.9 3.8 %all-to-all-start.1 = ((bf16[4,400,256]{2,1,0:T(8,128)(2,1)}), bf16[4,400,256]{2,1,0:T(8,128)(2,1)S(1)}, u32[]{:S(2)}, u32[]{:S(2)}) async-start(bf16[4,400,256]{2,1,0:T(8,128)(2,1)} %shard_map.104), calls=%async_computation.1 | async-start | bytes 1638400 | tf_op jit(solution)/shard_map/all_to_all | solution.py:316
  23.7 11.1 %collective-permute-start.1 = (bf16[4,128,256]{2,1,0:T(8,128)(2,1)S(1)}, bf16[4,128,256]{2,1,0:T(8,128)(2,1)S(1)}, u32[]{:S(2)}, u32[]{:S(2)}) collective-permute-start(bf16[4,128,256]{2,1,0:T(8,128)(2,1)S(1)} %all-to-all-done.ring0), channel_id=1, source_target_pairs={{4,0},{8,4},{12,8},{16,12},{20,16},{24,20},{28,24},{32,28},{36,32}... | collective-permute-start | bytes 786440 | tf_op jit(solution)/shard_map/ppermute | solution.py:312
  34.8 3.1 %collective-permute-start = (bf16[3,128,256]{2,1,0:T(8,128)(2,1)S(1)}, bf16[3,128,256]{2,1,0:T(8,128)(2,1)S(1)}, u32[]{:S(2)}, u32[]{:S(2)}) collective-permute-start(bf16[3,128,256]{2,1,0:T(8,128)(2,1)S(1)} %slice.4), channel_id=1, source_target_pairs={{8,0},{12,4},{16,8},{20,12},{24,16},{28,20},{32,24},{36,28},{40,32... | collective-permute-start | bytes 589832 | tf_op jit(solution)/shard_map/ppermute | solution.py:312
  38.5 1.7 %shard_map.105.before = f32[4,128,256]{2,1,0:T(8,128)S(1)} custom-call(bf16[4,128,256]{2,1,0:T(8,128)(2,1)S(1)} %all-to-all-done.ring0, bf16[4,128,256]{2,1,0:T(8,128)(2,1)S(1)} %collective-permute-done.1.ring1, bf16[4,400,256]{2,1,0:T(8,128)(2,1)S(1)} %all-to-all-done.1.bundle), custom_call_target="tpu_custom_call" | custom-call | tf_op jit(solution)/shard_map/pallas_call | solution.py:22
  40.2 5.4 %collective-permute-done.ring2 = bf16[3,128,256]{2,1,0:T(8,128)(2,1)S(1)} collective-permute-done((bf16[3,128,256]{2,1,0:T(8,128)(2,1)S(1)}, bf16[3,128,256]{2,1,0:T(8,128)(2,1)S(1)}, u32[]{:S(2)}, u32[]{:S(2)}) %collective-permute-start) | collective-permute-done | bytes 196640 | tf_op jit(solution)/shard_map/ppermute | solution.py:312
  46.4 8.5 %all_to_all.30.stats = f32[4,16,256]{2,1,0:T(8,128)S(1)} all-to-all(f32[4,16,256]{2,1,0:T(8,128)S(1)} %broadcast_in_dim.2), channel_id=1, replica_groups=mesh['y'=4,'core'=2,'zh'=4,'zl'=4,'x'=4] {'x'}, dimensions={0} | all-to-all | bytes 131072 | tf_op jit(solution)/shard_map/all_to_all | solution.py:316
  55.9 1.9 %collective-permute-start.2 = (bf16[3,128,256]{2,1,0:T(8,128)(2,1)S(1)}, bf16[3,128,256]{2,1,0:T(8,128)(2,1)S(1)}, u32[]{:S(2)}, u32[]{:S(2)}) collective-permute-start(bf16[3,128,256]{2,1,0:T(8,128)(2,1)S(1)} %shard_map.108), channel_id=1, source_target_pairs={{60,0},{0,4},{4,8},{8,12},{12,16},{16,20},{20,24},{24,28},{28,32},... | collective-permute-start | bytes 589832 | tf_op jit(solution)/shard_map/ppermute | solution.py:312
  57.8 1.7 %shard_map.110.own = f32[4,128,256]{2,1,0:T(8,128)S(1)} custom-call(bf16[4,128,256]{2,1,0:T(8,128)(2,1)S(1)} %collective-permute-done.1.ring1, bf16[4,400,256]{2,1,0:T(8,128)(2,1)S(1)} %all-to-all-done.1.bundle, bf16[4,128,256]{2,1,0:T(8,128)(2,1)S(1)} %get-tuple-element.31.grads), custom_call_target="tpu_custom_call" | custom-call | tf_op jit(solution)/shard_map/pallas_call | solution.py:22
  59.6 4.0 %collective-permute-done.2.arrived = bf16[3,128,256]{2,1,0:T(8,128)(2,1)S(1)} collective-permute-done((bf16[3,128,256]{2,1,0:T(8,128)(2,1)S(1)}, bf16[3,128,256]{2,1,0:T(8,128)(2,1)S(1)}, u32[]{:S(2)}, u32[]{:S(2)}) %collective-permute-start.2) | collective-permute-done | bytes 196640 | tf_op jit(solution)/shard_map/ppermute | solution.py:312
  67.0 11.6 %all-to-all-start.3 = ((bf16[8,32,512]{2,1,0:T(8,128)(2,1)}), bf16[8,32,512]{2,1,0:T(8,128)(2,1)}, u32[]{:S(2)}, u32[]{:S(2)}) async-start(bf16[8,32,512]{2,1,0:T(8,128)(2,1)} %bitcast.3), calls=%async_computation.3 | async-start | bytes 524288 | tf_op jit(solution)/shard_map/all_to_all | solution.py:316
  78.6 3.4 %collective-permute-start.3 = (bf16[4,128,256]{2,1,0:T(8,128)(2,1)}, bf16[4,128,256]{2,1,0:T(8,128)(2,1)S(1)}, u32[]{:S(2)}, u32[]{:S(2)}) collective-permute-start(bf16[4,128,256]{2,1,0:T(8,128)(2,1)} %shard_map.111), channel_id=1, source_target_pairs={{60,0},{0,4},{4,8},{8,12},{12,16},{16,20},{20,24},{24,28},{28,32},... | collective-permute-start | bytes 786440 | tf_op jit(solution)/shard_map/ppermute | solution.py:312
  83.3 7.3 %collective-permute-done.3.back1 = bf16[4,128,256]{2,1,0:T(8,128)(2,1)S(1)} collective-permute-done((bf16[4,128,256]{2,1,0:T(8,128)(2,1)}, bf16[4,128,256]{2,1,0:T(8,128)(2,1)S(1)}, u32[]{:S(2)}, u32[]{:S(2)}) %collective-permute-start.3) | collective-permute-done | bytes 262176 | tf_op jit(solution)/shard_map/ppermute | solution.py:312
  91.3 1.6 %shard_map.113 = bf16[4,4,8,512]{3,2,1,0:T(8,128)(2,1)} custom-call(bf16[8,32,512]{2,1,0:T(8,128)(2,1)} %all-to-all-done.3.parts), custom_call_target="tpu_custom_call" | custom-call | tf_op jit(solution)/shard_map/pallas_call | solution.py:22
  92.9 7.2 %all-to-all-start.4 = ((bf16[16,8,512]{2,1,0:T(8,128)(2,1)}), bf16[16,8,512]{2,1,0:T(8,128)(2,1)S(1)}, u32[]{:S(2)}, u32[]{:S(2)}) async-start(bf16[16,8,512]{2,1,0:T(8,128)(2,1)} %bitcast.5), calls=%async_computation.4 | async-start | bytes 262144 | tf_op jit(solution)/shard_map/all_to_all | solution.py:316
  102.1 3.3 %collective-permute-start.4 = (bf16[256,256]{1,0:T(8,128)(2,1)S(1)}, bf16[256,256]{1,0:T(8,128)(2,1)S(1)}, u32[]{:S(2)}, u32[]{:S(2)}) collective-permute-start(bf16[256,256]{1,0:T(8,128)(2,1)S(1)} %get-tuple-element.39), channel_id=1, source_target_pairs={{0,1},{1,2},{2,3},{3,0},{4,5},{5,6},{6,7},{7,4},{8,9},{9,10},{10,1... | collective-permute-start | bytes 393224 | tf_op jit(solution)/shard_map/ppermute | solution.py:409
  105.4 4.3 %collective-permute-start.5 = (bf16[256,256]{1,0:T(8,128)(2,1)S(1)}, bf16[256,256]{1,0:T(8,128)(2,1)S(1)}, u32[]{:S(2)}, u32[]{:S(2)}) collective-permute-start(bf16[256,256]{1,0:T(8,128)(2,1)S(1)} %get-tuple-element.40), channel_id=1, source_target_pairs={{0,2},{1,3},{2,0},{3,1},{4,6},{5,7},{6,4},{7,5},{8,10},{9,11},{10,... | collective-permute-start | bytes 393224 | tf_op jit(solution)/shard_map/ppermute | solution.py:409
  109.7 3.1 %collective-permute-start.6 = (bf16[256,256]{1,0:T(8,128)(2,1)S(1)}, bf16[256,256]{1,0:T(8,128)(2,1)S(1)}, u32[]{:S(2)}, u32[]{:S(2)}) collective-permute-start(bf16[256,256]{1,0:T(8,128)(2,1)S(1)} %get-tuple-element.41), channel_id=1, source_target_pairs={{0,3},{1,0},{2,1},{3,2},{4,7},{5,4},{6,5},{7,6},{8,11},{9,8},{10,9... | collective-permute-start | bytes 393224 | tf_op jit(solution)/shard_map/ppermute | solution.py:409
  112.8 1.5 %all-to-all-done.4 = bf16[16,8,512]{2,1,0:T(8,128)(2,1)S(1)} async-done(((bf16[16,8,512]{2,1,0:T(8,128)(2,1)}), bf16[16,8,512]{2,1,0:T(8,128)(2,1)S(1)}, u32[]{:S(2)}, u32[]{:S(2)}) %all-to-all-start.4) | async-done | bytes 131104 | tf_op jit(solution)/shard_map/all_to_all | solution.py:316
  115.0 8.9 %all-to-all-start.5 = ((f32[8,8,512]{2,1,0:T(8,128)}), f32[8,8,512]{2,1,0:T(8,128)S(1)}, u32[]{:S(2)}, u32[]{:S(2)}) async-start(f32[8,8,512]{2,1,0:T(8,128)} %shard_map.116), calls=%async_computation.5 | async-start | bytes 262144 | tf_op jit(solution)/shard_map/all_to_all | solution.py:316
  123.9 1.5 %shard_map.115 = (bf16[224,1024]{1,0:T(8,128)(2,1)}, bf16[128,1024]{1,0:T(8,128)(2,1)}) custom-call(s32[1]{0:T(128)} %bitcast.place_ref, bf16[224,1024]{1,0:T(8,128)(2,1)S(1)} %copy-done.1, bf16[512,1024]{1,0:T(8,128)(2,1)S(1)} %copy-done, bf16[256,256]{1,0:T(8,128)(2,1)S(1)} %get-tuple-element.38.refs_0_, ...), custom_call_target="tpu_custom_call" | custom-call | tf_op jit(solution)/shard_map/pallas_call | solution.py:22
  125.5 3.7 %all-to-all-done.5 = f32[8,8,512]{2,1,0:T(8,128)S(1)} async-done(((f32[8,8,512]{2,1,0:T(8,128)}), f32[8,8,512]{2,1,0:T(8,128)S(1)}, u32[]{:S(2)}, u32[]{:S(2)}) %all-to-all-start.5) | async-done | bytes 131104 | tf_op jit(solution)/shard_map/all_to_all | solution.py:316
  (35 shorter events, 12.3 us)
Async XLA Ops:
  7.2 57.1 %all-gather.3.cloned.1.call-start = ((), (), s32[]{:S(2)}) async-start(), calls=%async_computation.6 | async-start | bytes 2293760 | tf_op jit(solution)/shard_map/all_gather | solution.py:347
  9.6 10.4 %all-to-all-start = ((bf16[4,128,256]{2,1,0:T(8,128)(2,1)}), bf16[4,128,256]{2,1,0:T(8,128)(2,1)S(1)}, u32[]{:S(2)}, u32[]{:S(2)}) async-start(bf16[4,128,256]{2,1,0:T(8,128)(2,1)} %shard_map.103), calls=%async_computation | async-start | bytes 524288 | tf_op jit(solution)/shard_map/all_to_all | solution.py:316
  19.9 18.6 %all-to-all-start.1 = ((bf16[4,400,256]{2,1,0:T(8,128)(2,1)}), bf16[4,400,256]{2,1,0:T(8,128)(2,1)S(1)}, u32[]{:S(2)}, u32[]{:S(2)}) async-start(bf16[4,400,256]{2,1,0:T(8,128)(2,1)} %shard_map.104), calls=%async_computation.1 | async-start | bytes 1638400 | tf_op jit(solution)/shard_map/all_to_all | solution.py:316
  23.7 14.8 %collective-permute-start.1 = (bf16[4,128,256]{2,1,0:T(8,128)(2,1)S(1)}, bf16[4,128,256]{2,1,0:T(8,128)(2,1)S(1)}, u32[]{:S(2)}, u32[]{:S(2)}) collective-permute-start(bf16[4,128,256]{2,1,0:T(8,128)(2,1)S(1)} %all-to-all-done.ring0), channel_id=1, source_target_pairs={{4,0},{8,4},{12,8},{16,12},{20,16},{24,20},{28,24},{32,28},{36,32}... | collective-permute-start | bytes 786440 | tf_op jit(solution)/shard_map/ppermute | solution.py:312
  34.8 10.7 %collective-permute-start = (bf16[3,128,256]{2,1,0:T(8,128)(2,1)S(1)}, bf16[3,128,256]{2,1,0:T(8,128)(2,1)S(1)}, u32[]{:S(2)}, u32[]{:S(2)}) collective-permute-start(bf16[3,128,256]{2,1,0:T(8,128)(2,1)S(1)} %slice.4), channel_id=1, source_target_pairs={{8,0},{12,4},{16,8},{20,12},{24,16},{28,20},{32,24},{36,28},{40,32... | collective-permute-start | bytes 589832 | tf_op jit(solution)/shard_map/ppermute | solution.py:312
  55.1 9.2 %copy-start.3 = (bf16[4,128,256]{2,1,0:T(8,128)(2,1)}, bf16[4,128,256]{2,1,0:T(8,128)(2,1)S(1)}, u32[]{:S(2)}) copy-start(bf16[4,128,256]{2,1,0:T(8,128)(2,1)S(1)} %get-tuple-element.28.refs_1_.gated_ref) | copy-start | bytes 786436
  55.9 7.6 %collective-permute-start.2 = (bf16[3,128,256]{2,1,0:T(8,128)(2,1)S(1)}, bf16[3,128,256]{2,1,0:T(8,128)(2,1)S(1)}, u32[]{:S(2)}, u32[]{:S(2)}) collective-permute-start(bf16[3,128,256]{2,1,0:T(8,128)(2,1)S(1)} %shard_map.108), channel_id=1, source_target_pairs={{60,0},{0,4},{4,8},{8,12},{12,16},{16,20},{20,24},{24,28},{28,32},... | collective-permute-start | bytes 589832 | tf_op jit(solution)/shard_map/ppermute | solution.py:312
  64.3 1.5 %copy-start.2 = (bf16[896,1024]{1,0:T(8,128)(2,1)S(1)}, bf16[896,1024]{1,0:T(8,128)(2,1)}, u32[]{:S(2)}) copy-start(bf16[896,1024]{1,0:T(8,128)(2,1)} %all-gather.3.cloned.1.call-done) | copy-start | bytes 5505028
  67.0 24.3 %all-to-all-start.3 = ((bf16[8,32,512]{2,1,0:T(8,128)(2,1)}), bf16[8,32,512]{2,1,0:T(8,128)(2,1)}, u32[]{:S(2)}, u32[]{:S(2)}) async-start(bf16[8,32,512]{2,1,0:T(8,128)(2,1)} %bitcast.3), calls=%async_computation.3 | async-start | bytes 524288 | tf_op jit(solution)/shard_map/all_to_all | solution.py:316
  78.6 45.3 %copy-start = (bf16[512,1024]{1,0:T(8,128)(2,1)S(1)}, bf16[512,1024]{1,0:T(8,128)(2,1)}, u32[]{:S(2)}) copy-start(bf16[512,1024]{1,0:T(8,128)(2,1)} %out_ref.1) | copy-start | bytes 3145732
  78.6 45.3 %copy-start.1 = (bf16[224,1024]{1,0:T(8,128)(2,1)S(1)}, bf16[224,1024]{1,0:T(8,128)(2,1)}, u32[]{:S(2)}) copy-start(bf16[224,1024]{1,0:T(8,128)(2,1)} %cand_ref.1) | copy-start | bytes 1376260
  78.6 12.0 %collective-permute-start.3 = (bf16[4,128,256]{2,1,0:T(8,128)(2,1)}, bf16[4,128,256]{2,1,0:T(8,128)(2,1)S(1)}, u32[]{:S(2)}, u32[]{:S(2)}) collective-permute-start(bf16[4,128,256]{2,1,0:T(8,128)(2,1)} %shard_map.111), channel_id=1, source_target_pairs={{60,0},{0,4},{4,8},{8,12},{12,16},{16,20},{20,24},{24,28},{28,32},... | collective-permute-start | bytes 786440 | tf_op jit(solution)/shard_map/ppermute | solution.py:312
  90.6 0.7 copy-start.5
  92.9 21.4 %all-to-all-start.4 = ((bf16[16,8,512]{2,1,0:T(8,128)(2,1)}), bf16[16,8,512]{2,1,0:T(8,128)(2,1)S(1)}, u32[]{:S(2)}, u32[]{:S(2)}) async-start(bf16[16,8,512]{2,1,0:T(8,128)(2,1)} %bitcast.5), calls=%async_computation.4 | async-start | bytes 262144 | tf_op jit(solution)/shard_map/all_to_all | solution.py:316
  100.2 1.0 copy-start.4
  101.1 0.9 copy-start.6
  102.1 21.8 %collective-permute-start.4 = (bf16[256,256]{1,0:T(8,128)(2,1)S(1)}, bf16[256,256]{1,0:T(8,128)(2,1)S(1)}, u32[]{:S(2)}, u32[]{:S(2)}) collective-permute-start(bf16[256,256]{1,0:T(8,128)(2,1)S(1)} %get-tuple-element.39), channel_id=1, source_target_pairs={{0,1},{1,2},{2,3},{3,0},{4,5},{5,6},{6,7},{7,4},{8,9},{9,10},{10,1... | collective-permute-start | bytes 393224 | tf_op jit(solution)/shard_map/ppermute | solution.py:409
  105.4 18.5 %collective-permute-start.5 = (bf16[256,256]{1,0:T(8,128)(2,1)S(1)}, bf16[256,256]{1,0:T(8,128)(2,1)S(1)}, u32[]{:S(2)}, u32[]{:S(2)}) collective-permute-start(bf16[256,256]{1,0:T(8,128)(2,1)S(1)} %get-tuple-element.40), channel_id=1, source_target_pairs={{0,2},{1,3},{2,0},{3,1},{4,6},{5,7},{6,4},{7,5},{8,10},{9,11},{10,... | collective-permute-start | bytes 393224 | tf_op jit(solution)/shard_map/ppermute | solution.py:409
  109.7 14.2 %collective-permute-start.6 = (bf16[256,256]{1,0:T(8,128)(2,1)S(1)}, bf16[256,256]{1,0:T(8,128)(2,1)S(1)}, u32[]{:S(2)}, u32[]{:S(2)}) collective-permute-start(bf16[256,256]{1,0:T(8,128)(2,1)S(1)} %get-tuple-element.41), channel_id=1, source_target_pairs={{0,3},{1,0},{2,1},{3,2},{4,7},{5,4},{6,5},{7,6},{8,11},{9,8},{10,9... | collective-permute-start | bytes 393224 | tf_op jit(solution)/shard_map/ppermute | solution.py:409
  115.0 14.2 %all-to-all-start.5 = ((f32[8,8,512]{2,1,0:T(8,128)}), f32[8,8,512]{2,1,0:T(8,128)S(1)}, u32[]{:S(2)}, u32[]{:S(2)}) async-start(f32[8,8,512]{2,1,0:T(8,128)} %shard_map.116), calls=%async_computation.5 | async-start | bytes 262144 | tf_op jit(solution)/shard_map/all_to_all | solution.py:316
Sparse Core Ops, SparseCore 0:
  10.1 43.9 all-gather.2

commit v9 on v8

--- a/solution.py
+++ b/solution.py
@@ -389,22 +389,22 @@
         cots,
         gated,
     )
-    back1 = on_core(back1_kernel, shaped(ring1.shape, F32), ring1, bundle, grads)
+    out_grad, late_grads = barrier((out_grad, grads))
+    back1 = on_core(back1_kernel, shaped(ring1.shape, F32), ring1, bundle, late_grads)
+    out_grad, back2, back1, late_grads = barrier((out_grad, back2, back1, late_grads))
+    part = exchanged(out_grad.reshape(cores * zl, size // zl, half), ("core", "zl"))
     back1 = on_core(add_kernel, shaped(ring1.shape, BF16), back1, back2)
-    out_grad, back1, late_grads = barrier((out_grad, back1, grads))
-    part = exchanged(out_grad.reshape(cores * zl, size // zl, half), ("core", "zl"))
     back0 = on_core(back0_kernel, shaped(ring0.shape, F32), ring0, bundle, late_grads)
-    part, back0, back1 = barrier((part, back0, moved(back1, -1)))
-    part = on_core(fold_kernel, shaped((zh, xs, own, half), BF16), part)
-    part, back0, back1 = barrier((part, back0, back1))
+    parcels = on_core(
+        parcel_kernel, [shaped((2 * size, lanes), BF16)] * HEADS, gated, back0, moved(back1, -1), scalars=(place,)
+    )
+    part, *parcels = barrier((part, *parcels))
+    part, *parcels = barrier((on_core(fold_kernel, shaped((zh, xs, own, half), BF16), part), *parcels))
     part = exchanged(part.reshape(zh * xs, own, half), ("zh", "x")).reshape(zh, xs, own, half)
     depth = lax.axis_index("zh").reshape(1).astype(jnp.int32)
     peers = lax.axis_size("y") * cores
     part = on_core(pick_kernel, shaped((peers, own, half), F32), part, scalars=(depth,))
 
-    parcels = on_core(
-        parcel_kernel, [shaped((2 * size, lanes), BF16)] * HEADS, gated, back0, back1, scalars=(place,)
-    )
     arrived = [
         lax.ppermute(parcel, "x", [(i, (i + step) % HEADS) for i in range(HEADS)]) if step else parcel
         for step, parcel in enumerate(parcels)

time: 138 us -> 133 us (0.964)
  local copies, waits for them, and re-layouts: 4.13 us -> 1.52 us
    unnamed x14 -> x6, local copies, waits for them, and re-layouts: 4.11 us -> 1.5 us
    ppermute x4, waiting for transfers between devices: 17.3 us -> 14.7 us  [moved(): lax.ppermute(block, DEPTH, [((i + distance) % size, i) for i in range(siz...]
    all_to_all x5, waiting for transfers between devices: 5.75 us -> 7.73 us  [exchanged(): return lax.all_to_all(chunks, axis, 0, 0, tiled=True)]
  transfers between devices with their start and end apart: 13 -> 13, of which waited for: 7 -> 7; matrix products, arithmetic and copies ran while one was open for 0% -> 0% of each run, Pallas kernels for 12% -> 14%
where the time goes in v9:
time: 133 us; the launch traced here: 132 us
  starting transfers between devices  65.6 us (49%)
  waiting for transfers between devices  23.2 us (17%)
  Pallas kernels  19.5 us (15%)
  between operations  14.2 us (11%)
  blocking collectives  8.47 us (6%)
  local copies, waits for them, and re-layouts  1.52 us (1%)
    all_to_all x5, starting transfers between devices, exchanged(): return lax.all_to_all(chunks, axis, 0, 0, tiled=True)  35.4 us
    ppermute x4, starting transfers between devices, moved(): lax.ppermute(block, DEPTH, [((i + distance) % size, i) for i in range(siz...  19.5 us
    ppermute x4, waiting for transfers between devices, moved(): lax.ppermute(block, DEPTH, [((i + distance) % size, i) for i in range(siz...  14.7 us
    pallas_call x13, Pallas kernels, on_core(): pl.pallas_call(kernel, out_shape=outs, in_specs=[pl.BlockSpec(memory_spac...  12.8 us
    ppermute x3, starting transfers between devices, on_device(): lax.ppermute(parcel, 'x', [(i, (i + step) % HEADS) for i in range(HEADS)])  10.7 us
    all_to_all x1, blocking collectives, exchanged(): return lax.all_to_all(chunks, axis, 0, 0, tiled=True)  8.47 us
    all_to_all x5, waiting for transfers between devices, exchanged(): return lax.all_to_all(chunks, axis, 0, 0, tiled=True)  7.73 us
    pallas_call x1, Pallas kernels, on_fetched(): pl.pallas_call(body, out_shape=outs, in_specs=[pl.BlockSpec(memory_space=...  5 us
  transfers between devices with their start and end apart: 13, of which 7 were waited for; matrix products, arithmetic and copies ran while one was open for 0% of the time, Pallas kernels for 14%

profile of v9, /device:TPU:1, one launch (start us, length us, event | category | flops | bytes accessed | tf_op | source)
XLA Modules:
  0.0 132.4 jit_solution(6198952646369091545)
XLA Ops:
  7.9 1.6 %shard_map.103 = bf16[4,128,256]{2,1,0:T(8,128)(2,1)} custom-call(bf16[128,1024]{1,0:T(8,128)(2,1)} %history_ref.1), custom_call_target="tpu_custom_call" | custom-call | tf_op jit(solution)/shard_map/pallas_call | solution.py:349
  9.6 4.9 %all-to-all-start = ((bf16[4,128,256]{2,1,0:T(8,128)(2,1)}), bf16[4,128,256]{2,1,0:T(8,128)(2,1)S(1)}, u32[]{:S(2)}, u32[]{:S(2)}) async-start(bf16[4,128,256]{2,1,0:T(8,128)(2,1)} %shard_map.103), calls=%async_computation | async-start | bytes 524288 | tf_op jit(solution)/shard_map/all_to_all | solution.py:316
  14.4 5.0 %shard_map.104 = bf16[4,400,256]{2,1,0:T(8,128)(2,1)} custom-call(s32[2,8]{1,0:T(2,128)} %refs_0_.1, s32[2]{0:T(128)} %refs_1_.1, s32[1,224]{1,0:T(1,128)} %bitcast.11, bf16[224,1024]{1,0:T(8,128)(2,1)} %cand_ref.1, bf16[224,1024]{1,0:T(8,128)(2,1)} %refs_4_.1, bf16[1024,1024]{1,0:T(8,128)(2,1)} %refs_5_.1, bf16[512,1024]{1,0:T(8,128)(2,1)} %out_ref.1), custom_call_target="tpu_custom_call" | custom-call | tf_op jit(solution)/shard_map/pallas_call | solution.py:51
  19.9 3.7 %all-to-all-start.1 = ((bf16[4,400,256]{2,1,0:T(8,128)(2,1)}), bf16[4,400,256]{2,1,0:T(8,128)(2,1)S(1)}, u32[]{:S(2)}, u32[]{:S(2)}) async-start(bf16[4,400,256]{2,1,0:T(8,128)(2,1)} %shard_map.104), calls=%async_computation.1 | async-start | bytes 1638400 | tf_op jit(solution)/shard_map/all_to_all | solution.py:316
  23.7 11.1 %collective-permute-start.1 = (bf16[4,128,256]{2,1,0:T(8,128)(2,1)S(1)}, bf16[4,128,256]{2,1,0:T(8,128)(2,1)S(1)}, u32[]{:S(2)}, u32[]{:S(2)}) collective-permute-start(bf16[4,128,256]{2,1,0:T(8,128)(2,1)S(1)} %all-to-all-done.ring0), channel_id=1, source_target_pairs={{4,0},{8,4},{12,8},{16,12},{20,16},{24,20},{28,24},{32,28},{36,32}... | collective-permute-start | bytes 786440 | tf_op jit(solution)/shard_map/ppermute | solution.py:312
  34.8 3.1 %collective-permute-start = (bf16[3,128,256]{2,1,0:T(8,128)(2,1)S(1)}, bf16[3,128,256]{2,1,0:T(8,128)(2,1)S(1)}, u32[]{:S(2)}, u32[]{:S(2)}) collective-permute-start(bf16[3,128,256]{2,1,0:T(8,128)(2,1)S(1)} %slice.4), channel_id=1, source_target_pairs={{8,0},{12,4},{16,8},{20,12},{24,16},{28,20},{32,24},{36,28},{40,32... | collective-permute-start | bytes 589832 | tf_op jit(solution)/shard_map/ppermute | solution.py:312
  38.5 1.7 %shard_map.105.before = f32[4,128,256]{2,1,0:T(8,128)S(1)} custom-call(bf16[4,128,256]{2,1,0:T(8,128)(2,1)S(1)} %all-to-all-done.ring0, bf16[4,128,256]{2,1,0:T(8,128)(2,1)S(1)} %collective-permute-done.1.ring1, bf16[4,400,256]{2,1,0:T(8,128)(2,1)S(1)} %all-to-all-done.1.bundle), custom_call_target="tpu_custom_call" | custom-call | tf_op jit(solution)/shard_map/pallas_call | solution.py:22
  40.2 5.4 %collective-permute-done.ring2 = bf16[3,128,256]{2,1,0:T(8,128)(2,1)S(1)} collective-permute-done((bf16[3,128,256]{2,1,0:T(8,128)(2,1)S(1)}, bf16[3,128,256]{2,1,0:T(8,128)(2,1)S(1)}, u32[]{:S(2)}, u32[]{:S(2)}) %collective-permute-start) | collective-permute-done | bytes 196640 | tf_op jit(solution)/shard_map/ppermute | solution.py:312
  46.4 8.5 %all_to_all.30.stats = f32[4,16,256]{2,1,0:T(8,128)S(1)} all-to-all(f32[4,16,256]{2,1,0:T(8,128)S(1)} %broadcast_in_dim.2), channel_id=1, replica_groups=mesh['y'=4,'core'=2,'zh'=4,'zl'=4,'x'=4] {'x'}, dimensions={0} | all-to-all | bytes 131072 | tf_op jit(solution)/shard_map/all_to_all | solution.py:316
  55.9 1.9 %collective-permute-start.2 = (bf16[3,128,256]{2,1,0:T(8,128)(2,1)S(1)}, bf16[3,128,256]{2,1,0:T(8,128)(2,1)S(1)}, u32[]{:S(2)}, u32[]{:S(2)}) collective-permute-start(bf16[3,128,256]{2,1,0:T(8,128)(2,1)S(1)} %shard_map.108), channel_id=1, source_target_pairs={{60,0},{0,4},{4,8},{8,12},{12,16},{16,20},{20,24},{24,28},{28,32},... | collective-permute-start | bytes 589832 | tf_op jit(solution)/shard_map/ppermute | solution.py:312
  57.9 1.5 %copy-done.2 = bf16[896,1024]{1,0:T(8,128)(2,1)S(1)} copy-done((bf16[896,1024]{1,0:T(8,128)(2,1)S(1)}, bf16[896,1024]{1,0:T(8,128)(2,1)}, u32[]{:S(2)}) %copy-start.2) | copy-done | bytes 1835032
  60.5 1.7 %shard_map.110.own = f32[4,128,256]{2,1,0:T(8,128)S(1)} custom-call(bf16[4,128,256]{2,1,0:T(8,128)(2,1)S(1)} %collective-permute-done.1.ring1, bf16[4,400,256]{2,1,0:T(8,128)(2,1)S(1)} %all-to-all-done.1.bundle, bf16[4,128,256]{2,1,0:T(8,128)(2,1)S(1)} %get-tuple-element.40.grads), custom_call_target="tpu_custom_call" | custom-call | tf_op jit(solution)/shard_map/pallas_call | solution.py:22
  62.2 1.3 collective-permute-done.2.arrived
  63.5 11.0 %all-to-all-start.3 = ((bf16[8,32,512]{2,1,0:T(8,128)(2,1)}), bf16[8,32,512]{2,1,0:T(8,128)(2,1)S(1)}, u32[]{:S(2)}, u32[]{:S(2)}) async-start(bf16[8,32,512]{2,1,0:T(8,128)(2,1)} %bitcast.3), calls=%async_computation.3 | async-start | bytes 524288 | tf_op jit(solution)/shard_map/all_to_all | solution.py:316
  75.3 3.4 %collective-permute-start.3 = (bf16[4,128,256]{2,1,0:T(8,128)(2,1)}, bf16[4,128,256]{2,1,0:T(8,128)(2,1)}, u32[]{:S(2)}, u32[]{:S(2)}) collective-permute-start(bf16[4,128,256]{2,1,0:T(8,128)(2,1)} %shard_map.112), channel_id=1, source_target_pairs={{60,0},{0,4},{4,8},{8,12},{12,16},{16,20},{20,24},{24,28},{28,32},... | collective-permute-start | bytes 786440 | tf_op jit(solution)/shard_map/ppermute | solution.py:312
  80.0 7.4 %collective-permute-done.3.back1 = bf16[4,128,256]{2,1,0:T(8,128)(2,1)} collective-permute-done((bf16[4,128,256]{2,1,0:T(8,128)(2,1)}, bf16[4,128,256]{2,1,0:T(8,128)(2,1)}, u32[]{:S(2)}, u32[]{:S(2)}) %collective-permute-start.3) | collective-permute-done | bytes 262176 | tf_op jit(solution)/shard_map/ppermute | solution.py:312
  89.1 7.3 %all-to-all-start.4 = ((bf16[16,8,512]{2,1,0:T(8,128)(2,1)}), bf16[16,8,512]{2,1,0:T(8,128)(2,1)S(1)}, u32[]{:S(2)}, u32[]{:S(2)}) async-start(bf16[16,8,512]{2,1,0:T(8,128)(2,1)} %bitcast.5), calls=%async_computation.4 | async-start | bytes 262144 | tf_op jit(solution)/shard_map/all_to_all | solution.py:316
  96.5 3.3 %collective-permute-start.4 = (bf16[256,256]{1,0:T(8,128)(2,1)S(1)}, bf16[256,256]{1,0:T(8,128)(2,1)S(1)}, u32[]{:S(2)}, u32[]{:S(2)}) collective-permute-start(bf16[256,256]{1,0:T(8,128)(2,1)S(1)} %get-tuple-element.53), channel_id=1, source_target_pairs={{0,1},{1,2},{2,3},{3,0},{4,5},{5,6},{6,7},{7,4},{8,9},{9,10},{10,1... | collective-permute-start | bytes 393224 | tf_op jit(solution)/shard_map/ppermute | solution.py:409
  99.7 4.3 %collective-permute-start.5 = (bf16[256,256]{1,0:T(8,128)(2,1)S(1)}, bf16[256,256]{1,0:T(8,128)(2,1)S(1)}, u32[]{:S(2)}, u32[]{:S(2)}) collective-permute-start(bf16[256,256]{1,0:T(8,128)(2,1)S(1)} %get-tuple-element.54), channel_id=1, source_target_pairs={{0,2},{1,3},{2,0},{3,1},{4,6},{5,7},{6,4},{7,5},{8,10},{9,11},{10,... | collective-permute-start | bytes 393224 | tf_op jit(solution)/shard_map/ppermute | solution.py:409
  104.0 3.1 %collective-permute-start.6 = (bf16[256,256]{1,0:T(8,128)(2,1)S(1)}, bf16[256,256]{1,0:T(8,128)(2,1)S(1)}, u32[]{:S(2)}, u32[]{:S(2)}) collective-permute-start(bf16[256,256]{1,0:T(8,128)(2,1)S(1)} %get-tuple-element.55), channel_id=1, source_target_pairs={{0,3},{1,0},{2,1},{3,2},{4,7},{5,4},{6,5},{7,6},{8,11},{9,8},{10,9... | collective-permute-start | bytes 393224 | tf_op jit(solution)/shard_map/ppermute | solution.py:409
  107.1 3.5 %all-to-all-done.4 = bf16[16,8,512]{2,1,0:T(8,128)(2,1)S(1)} async-done(((bf16[16,8,512]{2,1,0:T(8,128)(2,1)}), bf16[16,8,512]{2,1,0:T(8,128)(2,1)S(1)}, u32[]{:S(2)}, u32[]{:S(2)}) %all-to-all-start.4) | async-done | bytes 131104 | tf_op jit(solution)/shard_map/all_to_all | solution.py:316
  111.3 8.4 %all-to-all-start.5 = ((f32[8,8,512]{2,1,0:T(8,128)}), f32[8,8,512]{2,1,0:T(8,128)S(1)}, u32[]{:S(2)}, u32[]{:S(2)}) async-start(f32[8,8,512]{2,1,0:T(8,128)} %shard_map.116), calls=%async_computation.5 | async-start | bytes 262144 | tf_op jit(solution)/shard_map/all_to_all | solution.py:316
  119.7 1.5 %shard_map.115 = (bf16[224,1024]{1,0:T(8,128)(2,1)}, bf16[128,1024]{1,0:T(8,128)(2,1)}) custom-call(s32[1]{0:T(128)} %bitcast.place_ref, bf16[224,1024]{1,0:T(8,128)(2,1)S(1)} %copy-done.1, bf16[512,1024]{1,0:T(8,128)(2,1)S(1)} %copy-done, bf16[256,256]{1,0:T(8,128)(2,1)S(1)} %get-tuple-element.52.refs_0_, ...), custom_call_target="tpu_custom_call" | custom-call | tf_op jit(solution)/shard_map/pallas_call | solution.py:22
  121.3 3.7 %all-to-all-done.5 = f32[8,8,512]{2,1,0:T(8,128)S(1)} async-done(((f32[8,8,512]{2,1,0:T(8,128)}), f32[8,8,512]{2,1,0:T(8,128)S(1)}, u32[]{:S(2)}, u32[]{:S(2)}) %all-to-all-start.5) | async-done | bytes 131104 | tf_op jit(solution)/shard_map/all_to_all | solution.py:316
  (27 shorter events, 9.8 us)
Async XLA Ops:
  7.2 50.7 %all-gather.3.cloned.1.call-start = ((), (), s32[]{:S(2)}) async-start(), calls=%async_computation.6 | async-start | bytes 2293760 | tf_op jit(solution)/shard_map/all_gather | solution.py:347
  9.6 10.4 %all-to-all-start = ((bf16[4,128,256]{2,1,0:T(8,128)(2,1)}), bf16[4,128,256]{2,1,0:T(8,128)(2,1)S(1)}, u32[]{:S(2)}, u32[]{:S(2)}) async-start(bf16[4,128,256]{2,1,0:T(8,128)(2,1)} %shard_map.103), calls=%async_computation | async-start | bytes 524288 | tf_op jit(solution)/shard_map/all_to_all | solution.py:316
  19.9 18.5 %all-to-all-start.1 = ((bf16[4,400,256]{2,1,0:T(8,128)(2,1)}), bf16[4,400,256]{2,1,0:T(8,128)(2,1)S(1)}, u32[]{:S(2)}, u32[]{:S(2)}) async-start(bf16[4,400,256]{2,1,0:T(8,128)(2,1)} %shard_map.104), calls=%async_computation.1 | async-start | bytes 1638400 | tf_op jit(solution)/shard_map/all_to_all | solution.py:316
  23.7 14.8 %collective-permute-start.1 = (bf16[4,128,256]{2,1,0:T(8,128)(2,1)S(1)}, bf16[4,128,256]{2,1,0:T(8,128)(2,1)S(1)}, u32[]{:S(2)}, u32[]{:S(2)}) collective-permute-start(bf16[4,128,256]{2,1,0:T(8,128)(2,1)S(1)} %all-to-all-done.ring0), channel_id=1, source_target_pairs={{4,0},{8,4},{12,8},{16,12},{20,16},{24,20},{28,24},{32,28},{36,32}... | collective-permute-start | bytes 786440 | tf_op jit(solution)/shard_map/ppermute | solution.py:312
  34.8 10.7 %collective-permute-start = (bf16[3,128,256]{2,1,0:T(8,128)(2,1)S(1)}, bf16[3,128,256]{2,1,0:T(8,128)(2,1)S(1)}, u32[]{:S(2)}, u32[]{:S(2)}) collective-permute-start(bf16[3,128,256]{2,1,0:T(8,128)(2,1)S(1)} %slice.4), channel_id=1, source_target_pairs={{8,0},{12,4},{16,8},{20,12},{24,16},{28,20},{32,24},{36,28},{40,32... | collective-permute-start | bytes 589832 | tf_op jit(solution)/shard_map/ppermute | solution.py:312
  55.9 7.6 %collective-permute-start.2 = (bf16[3,128,256]{2,1,0:T(8,128)(2,1)S(1)}, bf16[3,128,256]{2,1,0:T(8,128)(2,1)S(1)}, u32[]{:S(2)}, u32[]{:S(2)}) collective-permute-start(bf16[3,128,256]{2,1,0:T(8,128)(2,1)S(1)} %shard_map.108), channel_id=1, source_target_pairs={{60,0},{0,4},{4,8},{8,12},{12,16},{16,20},{20,24},{24,28},{28,32},... | collective-permute-start | bytes 589832 | tf_op jit(solution)/shard_map/ppermute | solution.py:312
  57.8 1.5 %copy-start.2 = (bf16[896,1024]{1,0:T(8,128)(2,1)S(1)}, bf16[896,1024]{1,0:T(8,128)(2,1)}, u32[]{:S(2)}) copy-start(bf16[896,1024]{1,0:T(8,128)(2,1)} %all-gather.3.cloned.1.call-done) | copy-start | bytes 5505028
  63.5 24.9 %all-to-all-start.3 = ((bf16[8,32,512]{2,1,0:T(8,128)(2,1)}), bf16[8,32,512]{2,1,0:T(8,128)(2,1)S(1)}, u32[]{:S(2)}, u32[]{:S(2)}) async-start(bf16[8,32,512]{2,1,0:T(8,128)(2,1)} %bitcast.3), calls=%async_computation.3 | async-start | bytes 524288 | tf_op jit(solution)/shard_map/all_to_all | solution.py:316
  75.3 44.4 %copy-start = (bf16[512,1024]{1,0:T(8,128)(2,1)S(1)}, bf16[512,1024]{1,0:T(8,128)(2,1)}, u32[]{:S(2)}) copy-start(bf16[512,1024]{1,0:T(8,128)(2,1)} %out_ref.1) | copy-start | bytes 3145732
  75.3 44.4 %copy-start.1 = (bf16[224,1024]{1,0:T(8,128)(2,1)S(1)}, bf16[224,1024]{1,0:T(8,128)(2,1)}, u32[]{:S(2)}) copy-start(bf16[224,1024]{1,0:T(8,128)(2,1)} %cand_ref.1) | copy-start | bytes 1376260
  75.3 12.1 %collective-permute-start.3 = (bf16[4,128,256]{2,1,0:T(8,128)(2,1)}, bf16[4,128,256]{2,1,0:T(8,128)(2,1)}, u32[]{:S(2)}, u32[]{:S(2)}) collective-permute-start(bf16[4,128,256]{2,1,0:T(8,128)(2,1)} %shard_map.112), channel_id=1, source_target_pairs={{60,0},{0,4},{4,8},{8,12},{12,16},{16,20},{20,24},{24,28},{28,32},... | collective-permute-start | bytes 786440 | tf_op jit(solution)/shard_map/ppermute | solution.py:312
  89.1 21.5 %all-to-all-start.4 = ((bf16[16,8,512]{2,1,0:T(8,128)(2,1)}), bf16[16,8,512]{2,1,0:T(8,128)(2,1)S(1)}, u32[]{:S(2)}, u32[]{:S(2)}) async-start(bf16[16,8,512]{2,1,0:T(8,128)(2,1)} %bitcast.5), calls=%async_computation.4 | async-start | bytes 262144 | tf_op jit(solution)/shard_map/all_to_all | solution.py:316
  96.5 23.2 %collective-permute-start.4 = (bf16[256,256]{1,0:T(8,128)(2,1)S(1)}, bf16[256,256]{1,0:T(8,128)(2,1)S(1)}, u32[]{:S(2)}, u32[]{:S(2)}) collective-permute-start(bf16[256,256]{1,0:T(8,128)(2,1)S(1)} %get-tuple-element.53), channel_id=1, source_target_pairs={{0,1},{1,2},{2,3},{3,0},{4,5},{5,6},{6,7},{7,4},{8,9},{9,10},{10,1... | collective-permute-start | bytes 393224 | tf_op jit(solution)/shard_map/ppermute | solution.py:409
  99.7 20.0 %collective-permute-start.5 = (bf16[256,256]{1,0:T(8,128)(2,1)S(1)}, bf16[256,256]{1,0:T(8,128)(2,1)S(1)}, u32[]{:S(2)}, u32[]{:S(2)}) collective-permute-start(bf16[256,256]{1,0:T(8,128)(2,1)S(1)} %get-tuple-element.54), channel_id=1, source_target_pairs={{0,2},{1,3},{2,0},{3,1},{4,6},{5,7},{6,4},{7,5},{8,10},{9,11},{10,... | collective-permute-start | bytes 393224 | tf_op jit(solution)/shard_map/ppermute | solution.py:409
  104.0 15.7 %collective-permute-start.6 = (bf16[256,256]{1,0:T(8,128)(2,1)S(1)}, bf16[256,256]{1,0:T(8,128)(2,1)S(1)}, u32[]{:S(2)}, u32[]{:S(2)}) collective-permute-start(bf16[256,256]{1,0:T(8,128)(2,1)S(1)} %get-tuple-element.55), channel_id=1, source_target_pairs={{0,3},{1,0},{2,1},{3,2},{4,7},{5,4},{6,5},{7,6},{8,11},{9,8},{10,9... | collective-permute-start | bytes 393224 | tf_op jit(solution)/shard_map/ppermute | solution.py:409
  111.3 13.7 %all-to-all-start.5 = ((f32[8,8,512]{2,1,0:T(8,128)}), f32[8,8,512]{2,1,0:T(8,128)S(1)}, u32[]{:S(2)}, u32[]{:S(2)}) async-start(f32[8,8,512]{2,1,0:T(8,128)} %shard_map.116), calls=%async_computation.5 | async-start | bytes 262144 | tf_op jit(solution)/shard_map/all_to_all | solution.py:316
Sparse Core Ops, SparseCore 0:
  10.1 43.9 all-gather.2

commit v10 on v9

--- a/solution.py
+++ b/solution.py
@@ -344,7 +344,6 @@
     barrier = lax.optimization_barrier
     place = lax.axis_index("x").reshape(1).astype(jnp.int32)
 
-    cots = lax.all_gather(cotangent, "x")
     ring_shape = shaped((HEADS, tall, 2 * size), BF16)
     by_head = pl.pallas_call(
         split_kernel,
@@ -368,6 +367,8 @@
         out_weight,
         scalars=(request_blocks, request_length),
     )
+    bundle, cots = barrier((bundle, cotangent))
+    cots = lax.all_gather(cots, "x")
     bundle = exchanged(bundle, "x")
 
     attended_shape = shaped((HEADS, size, lanes), F32)

time: 133 us -> 138 us (1.038)
  blocking collectives: 8.47 us -> 18.7 us
  starting transfers between devices: 65.6 us -> 59 us
  waiting for transfers between devices: 23.2 us -> 24.6 us
    all_to_all x1 -> x2, blocking collectives: 8.47 us -> 18.7 us  [exchanged(): return lax.all_to_all(chunks, axis, 0, 0, tiled=True)]
    all_to_all x5 -> x4, starting transfers between devices: 35.4 us -> 28.7 us  [exchanged(): return lax.all_to_all(chunks, axis, 0, 0, tiled=True)]
    ppermute x4, waiting for transfers between devices: 14.7 us -> 17.3 us  [moved(): lax.ppermute(block, DEPTH, [((i + distance) % size, i) for i in range(siz...]
    all_to_all x5 -> x4, waiting for transfers between devices: 7.73 us -> 7.22 us  [exchanged(): return lax.all_to_all(chunks, axis, 0, 0, tiled=True)]
  transfers between devices with their start and end apart: 13 -> 12, of which waited for: 7 -> 6; matrix products, arithmetic and copies ran while one was open for 0% -> 0% of each run, Pallas kernels for 14% -> 10%
where the time goes in v10:
time: 138 us; the launch traced here: 137 us
  starting transfers between devices  59 us (43%)
  waiting for transfers between devices  24.6 us (18%)
  Pallas kernels  19.5 us (14%)
  blocking collectives  18.7 us (14%)
  between operations  14.2 us (10%)
  local copies, waits for them, and re-layouts  1.52 us (1%)
    all_to_all x4, starting transfers between devices, exchanged(): return lax.all_to_all(chunks, axis, 0, 0, tiled=True)  28.7 us
    ppermute x4, starting transfers between devices, moved(): lax.ppermute(block, DEPTH, [((i + distance) % size, i) for i in range(siz...  19.6 us
    all_to_all x2, blocking collectives, exchanged(): return lax.all_to_all(chunks, axis, 0, 0, tiled=True)  18.7 us
    ppermute x4, waiting for transfers between devices, moved(): lax.ppermute(block, DEPTH, [((i + distance) % size, i) for i in range(siz...  17.3 us
    pallas_call x13, Pallas kernels, on_core(): pl.pallas_call(kernel, out_shape=outs, in_specs=[pl.BlockSpec(memory_spac...  12.8 us
    ppermute x3, starting transfers between devices, on_device(): lax.ppermute(parcel, 'x', [(i, (i + step) % HEADS) for i in range(HEADS)])  10.7 us
    all_to_all x4, waiting for transfers between devices, exchanged(): return lax.all_to_all(chunks, axis, 0, 0, tiled=True)  7.22 us
    pallas_call x1, Pallas kernels, on_fetched(): pl.pallas_call(body, out_shape=outs, in_specs=[pl.BlockSpec(memory_space=...  5 us
  transfers between devices with their start and end apart: 12, of which 6 were waited for; matrix products, arithmetic and copies ran while one was open for 0% of the time, Pallas kernels for 10%

profile of v10, /device:TPU:1, one launch (start us, length us, event | category | flops | bytes accessed | tf_op | source)
XLA Modules:
  0.0 137.5 jit_solution(3703520361843642640)
XLA Ops:
  7.2 5.0 %shard_map.103 = bf16[4,400,256]{2,1,0:T(8,128)(2,1)} custom-call(s32[2,8]{1,0:T(2,128)} %refs_0_.1, s32[2]{0:T(128)} %refs_1_.1, s32[1,224]{1,0:T(1,128)} %bitcast.11, bf16[224,1024]{1,0:T(8,128)(2,1)} %cand_ref.1, bf16[224,1024]{1,0:T(8,128)(2,1)} %refs_4_.1, bf16[1024,1024]{1,0:T(8,128)(2,1)} %refs_5_.1, bf16[512,1024]{1,0:T(8,128)(2,1)} %out_ref.1), custom_call_target="tpu_custom_call" | custom-call | tf_op jit(solution)/shard_map/pallas_call | solution.py:51
  12.2 1.6 %shard_map.104 = bf16[4,128,256]{2,1,0:T(8,128)(2,1)} custom-call(bf16[128,1024]{1,0:T(8,128)(2,1)} %history_ref.1), custom_call_target="tpu_custom_call" | custom-call | tf_op jit(solution)/shard_map/pallas_call | solution.py:348
  13.9 10.4 %all_to_all.30.ring0 = bf16[4,128,256]{2,1,0:T(8,128)(2,1)S(1)} all-to-all(bf16[4,128,256]{2,1,0:T(8,128)(2,1)} %shard_map.104), channel_id=1, replica_groups=mesh['y'=4,'core'=2,'zh'=4,'zl'=4,'x'=4] {'x'}, dimensions={0} | all-to-all | bytes 524288 | tf_op jit(solution)/shard_map/all_to_all | solution.py:316
  24.3 3.5 %all-to-all-start.1 = ((bf16[4,400,256]{2,1,0:T(8,128)(2,1)}), bf16[4,400,256]{2,1,0:T(8,128)(2,1)S(1)}, u32[]{:S(2)}, u32[]{:S(2)}) async-start(bf16[4,400,256]{2,1,0:T(8,128)(2,1)} %shard_map.103), calls=%async_computation.1 | async-start | bytes 1638400 | tf_op jit(solution)/shard_map/all_to_all | solution.py:316
  27.8 11.2 %collective-permute-start.1 = (bf16[4,128,256]{2,1,0:T(8,128)(2,1)S(1)}, bf16[4,128,256]{2,1,0:T(8,128)(2,1)S(1)}, u32[]{:S(2)}, u32[]{:S(2)}) collective-permute-start(bf16[4,128,256]{2,1,0:T(8,128)(2,1)S(1)} %all_to_all.30.ring0), channel_id=1, source_target_pairs={{4,0},{8,4},{12,8},{16,12},{20,16},{24,20},{28,24},{32,28},{36,32}... | collective-permute-start | bytes 786440 | tf_op jit(solution)/shard_map/ppermute | solution.py:312
  39.0 3.1 %collective-permute-start = (bf16[3,128,256]{2,1,0:T(8,128)(2,1)S(1)}, bf16[3,128,256]{2,1,0:T(8,128)(2,1)S(1)}, u32[]{:S(2)}, u32[]{:S(2)}) collective-permute-start(bf16[3,128,256]{2,1,0:T(8,128)(2,1)S(1)} %slice.4), channel_id=1, source_target_pairs={{8,0},{12,4},{16,8},{20,12},{24,16},{28,20},{32,24},{36,28},{40,32... | collective-permute-start | bytes 589832 | tf_op jit(solution)/shard_map/ppermute | solution.py:312
  42.2 1.7 %shard_map.105.before = f32[4,128,256]{2,1,0:T(8,128)S(1)} custom-call(bf16[4,128,256]{2,1,0:T(8,128)(2,1)S(1)} %all_to_all.30.ring0, bf16[4,128,256]{2,1,0:T(8,128)(2,1)S(1)} %collective-permute-done.1.ring1, bf16[4,400,256]{2,1,0:T(8,128)(2,1)S(1)} %all-to-all-done.1.bundle), custom_call_target="tpu_custom_call" | custom-call | tf_op jit(solution)/shard_map/pallas_call | solution.py:22
  43.9 5.9 %collective-permute-done.ring2 = bf16[3,128,256]{2,1,0:T(8,128)(2,1)S(1)} collective-permute-done((bf16[3,128,256]{2,1,0:T(8,128)(2,1)S(1)}, bf16[3,128,256]{2,1,0:T(8,128)(2,1)S(1)}, u32[]{:S(2)}, u32[]{:S(2)}) %collective-permute-start) | collective-permute-done | bytes 196640 | tf_op jit(solution)/shard_map/ppermute | solution.py:312
  50.6 8.3 %all_to_all.31.stats = f32[4,16,256]{2,1,0:T(8,128)S(1)} all-to-all(f32[4,16,256]{2,1,0:T(8,128)S(1)} %broadcast_in_dim.2), channel_id=1, replica_groups=mesh['y'=4,'core'=2,'zh'=4,'zl'=4,'x'=4] {'x'}, dimensions={0} | all-to-all | bytes 131072 | tf_op jit(solution)/shard_map/all_to_all | solution.py:316
  60.0 1.9 %collective-permute-start.2 = (bf16[3,128,256]{2,1,0:T(8,128)(2,1)S(1)}, bf16[3,128,256]{2,1,0:T(8,128)(2,1)S(1)}, u32[]{:S(2)}, u32[]{:S(2)}) collective-permute-start(bf16[3,128,256]{2,1,0:T(8,128)(2,1)S(1)} %shard_map.108), channel_id=1, source_target_pairs={{60,0},{0,4},{4,8},{8,12},{12,16},{16,20},{20,24},{24,28},{28,32},... | collective-permute-start | bytes 589832 | tf_op jit(solution)/shard_map/ppermute | solution.py:312
  61.9 1.5 %copy-done.2 = bf16[896,1024]{1,0:T(8,128)(2,1)S(1)} copy-done((bf16[896,1024]{1,0:T(8,128)(2,1)S(1)}, bf16[896,1024]{1,0:T(8,128)(2,1)}, u32[]{:S(2)}) %copy-start.2) | copy-done | bytes 1835032
  64.6 1.7 %shard_map.110.own = f32[4,128,256]{2,1,0:T(8,128)S(1)} custom-call(bf16[4,128,256]{2,1,0:T(8,128)(2,1)S(1)} %collective-permute-done.1.ring1, bf16[4,400,256]{2,1,0:T(8,128)(2,1)S(1)} %all-to-all-done.1.bundle, bf16[4,128,256]{2,1,0:T(8,128)(2,1)S(1)} %get-tuple-element.44.grads), custom_call_target="tpu_custom_call" | custom-call | tf_op jit(solution)/shard_map/pallas_call | solution.py:22
  66.3 3.1 %collective-permute-done.2.arrived = bf16[3,128,256]{2,1,0:T(8,128)(2,1)S(1)} collective-permute-done((bf16[3,128,256]{2,1,0:T(8,128)(2,1)S(1)}, bf16[3,128,256]{2,1,0:T(8,128)(2,1)S(1)}, u32[]{:S(2)}, u32[]{:S(2)}) %collective-permute-start.2) | collective-permute-done | bytes 196640 | tf_op jit(solution)/shard_map/ppermute | solution.py:312
  69.4 10.8 %all-to-all-start.3 = ((bf16[8,32,512]{2,1,0:T(8,128)(2,1)}), bf16[8,32,512]{2,1,0:T(8,128)(2,1)S(1)}, u32[]{:S(2)}, u32[]{:S(2)}) async-start(bf16[8,32,512]{2,1,0:T(8,128)(2,1)} %bitcast.3), calls=%async_computation.3 | async-start | bytes 524288 | tf_op jit(solution)/shard_map/all_to_all | solution.py:316
  80.9 3.4 %collective-permute-start.3 = (bf16[4,128,256]{2,1,0:T(8,128)(2,1)}, bf16[4,128,256]{2,1,0:T(8,128)(2,1)}, u32[]{:S(2)}, u32[]{:S(2)}) collective-permute-start(bf16[4,128,256]{2,1,0:T(8,128)(2,1)} %shard_map.112), channel_id=1, source_target_pairs={{60,0},{0,4},{4,8},{8,12},{12,16},{16,20},{20,24},{24,28},{28,32},... | collective-permute-start | bytes 786440 | tf_op jit(solution)/shard_map/ppermute | solution.py:312
  85.5 8.2 %collective-permute-done.3.back1 = bf16[4,128,256]{2,1,0:T(8,128)(2,1)} collective-permute-done((bf16[4,128,256]{2,1,0:T(8,128)(2,1)}, bf16[4,128,256]{2,1,0:T(8,128)(2,1)}, u32[]{:S(2)}, u32[]{:S(2)}) %collective-permute-start.3) | collective-permute-done | bytes 262176 | tf_op jit(solution)/shard_map/ppermute | solution.py:312
  95.4 5.9 %all-to-all-start.4 = ((bf16[16,8,512]{2,1,0:T(8,128)(2,1)}), bf16[16,8,512]{2,1,0:T(8,128)(2,1)S(1)}, u32[]{:S(2)}, u32[]{:S(2)}) async-start(bf16[16,8,512]{2,1,0:T(8,128)(2,1)} %bitcast.5), calls=%async_computation.4 | async-start | bytes 262144 | tf_op jit(solution)/shard_map/all_to_all | solution.py:316
  101.3 3.3 %collective-permute-start.4 = (bf16[256,256]{1,0:T(8,128)(2,1)S(1)}, bf16[256,256]{1,0:T(8,128)(2,1)S(1)}, u32[]{:S(2)}, u32[]{:S(2)}) collective-permute-start(bf16[256,256]{1,0:T(8,128)(2,1)S(1)} %get-tuple-element.57), channel_id=1, source_target_pairs={{0,1},{1,2},{2,3},{3,0},{4,5},{5,6},{6,7},{7,4},{8,9},{9,10},{10,1... | collective-permute-start | bytes 393224 | tf_op jit(solution)/shard_map/ppermute | solution.py:410
  104.6 4.3 %collective-permute-start.5 = (bf16[256,256]{1,0:T(8,128)(2,1)S(1)}, bf16[256,256]{1,0:T(8,128)(2,1)S(1)}, u32[]{:S(2)}, u32[]{:S(2)}) collective-permute-start(bf16[256,256]{1,0:T(8,128)(2,1)S(1)} %get-tuple-element.58), channel_id=1, source_target_pairs={{0,2},{1,3},{2,0},{3,1},{4,6},{5,7},{6,4},{7,5},{8,10},{9,11},{10,... | collective-permute-start | bytes 393224 | tf_op jit(solution)/shard_map/ppermute | solution.py:410
  108.9 3.1 %collective-permute-start.6 = (bf16[256,256]{1,0:T(8,128)(2,1)S(1)}, bf16[256,256]{1,0:T(8,128)(2,1)S(1)}, u32[]{:S(2)}, u32[]{:S(2)}) collective-permute-start(bf16[256,256]{1,0:T(8,128)(2,1)S(1)} %get-tuple-element.59), channel_id=1, source_target_pairs={{0,3},{1,0},{2,1},{3,2},{4,7},{5,4},{6,5},{7,6},{8,11},{9,8},{10,9... | collective-permute-start | bytes 393224 | tf_op jit(solution)/shard_map/ppermute | solution.py:410
  112.0 3.5 %all-to-all-done.4 = bf16[16,8,512]{2,1,0:T(8,128)(2,1)S(1)} async-done(((bf16[16,8,512]{2,1,0:T(8,128)(2,1)}), bf16[16,8,512]{2,1,0:T(8,128)(2,1)S(1)}, u32[]{:S(2)}, u32[]{:S(2)}) %all-to-all-start.4) | async-done | bytes 131104 | tf_op jit(solution)/shard_map/all_to_all | solution.py:316
  116.1 8.6 %all-to-all-start.5 = ((f32[8,8,512]{2,1,0:T(8,128)}), f32[8,8,512]{2,1,0:T(8,128)S(1)}, u32[]{:S(2)}, u32[]{:S(2)}) async-start(f32[8,8,512]{2,1,0:T(8,128)} %shard_map.116), calls=%async_computation.5 | async-start | bytes 262144 | tf_op jit(solution)/shard_map/all_to_all | solution.py:316
  124.8 1.5 %shard_map.115 = (bf16[224,1024]{1,0:T(8,128)(2,1)}, bf16[128,1024]{1,0:T(8,128)(2,1)}) custom-call(s32[1]{0:T(128)} %bitcast.place_ref, bf16[224,1024]{1,0:T(8,128)(2,1)S(1)} %copy-done.1, bf16[512,1024]{1,0:T(8,128)(2,1)S(1)} %copy-done, bf16[256,256]{1,0:T(8,128)(2,1)S(1)} %get-tuple-element.56.refs_0_, ...), custom_call_target="tpu_custom_call" | custom-call | tf_op jit(solution)/shard_map/pallas_call | solution.py:22
  126.3 3.7 %all-to-all-done.5 = f32[8,8,512]{2,1,0:T(8,128)S(1)} async-done(((f32[8,8,512]{2,1,0:T(8,128)}), f32[8,8,512]{2,1,0:T(8,128)S(1)}, u32[]{:S(2)}, u32[]{:S(2)}) %all-to-all-start.5) | async-done | bytes 131104 | tf_op jit(solution)/shard_map/all_to_all | solution.py:316
  (26 shorter events, 8.2 us)
Async XLA Ops:
  7.2 54.7 %all-gather.3.cloned.1.call-start = ((), (), s32[]{:S(2)}) async-start(), calls=%async_computation.6 | async-start | bytes 2293760 | tf_op jit(solution)/shard_map/all_gather | solution.py:371
  24.3 18.0 %all-to-all-start.1 = ((bf16[4,400,256]{2,1,0:T(8,128)(2,1)}), bf16[4,400,256]{2,1,0:T(8,128)(2,1)S(1)}, u32[]{:S(2)}, u32[]{:S(2)}) async-start(bf16[4,400,256]{2,1,0:T(8,128)(2,1)} %shard_map.103), calls=%async_computation.1 | async-start | bytes 1638400 | tf_op jit(solution)/shard_map/all_to_all | solution.py:316
  27.8 14.5 %collective-permute-start.1 = (bf16[4,128,256]{2,1,0:T(8,128)(2,1)S(1)}, bf16[4,128,256]{2,1,0:T(8,128)(2,1)S(1)}, u32[]{:S(2)}, u32[]{:S(2)}) collective-permute-start(bf16[4,128,256]{2,1,0:T(8,128)(2,1)S(1)} %all_to_all.30.ring0), channel_id=1, source_target_pairs={{4,0},{8,4},{12,8},{16,12},{20,16},{24,20},{28,24},{32,28},{36,32}... | collective-permute-start | bytes 786440 | tf_op jit(solution)/shard_map/ppermute | solution.py:312
  39.0 10.8 %collective-permute-start = (bf16[3,128,256]{2,1,0:T(8,128)(2,1)S(1)}, bf16[3,128,256]{2,1,0:T(8,128)(2,1)S(1)}, u32[]{:S(2)}, u32[]{:S(2)}) collective-permute-start(bf16[3,128,256]{2,1,0:T(8,128)(2,1)S(1)} %slice.4), channel_id=1, source_target_pairs={{8,0},{12,4},{16,8},{20,12},{24,16},{28,20},{32,24},{36,28},{40,32... | collective-permute-start | bytes 589832 | tf_op jit(solution)/shard_map/ppermute | solution.py:312
  60.0 9.4 %collective-permute-start.2 = (bf16[3,128,256]{2,1,0:T(8,128)(2,1)S(1)}, bf16[3,128,256]{2,1,0:T(8,128)(2,1)S(1)}, u32[]{:S(2)}, u32[]{:S(2)}) collective-permute-start(bf16[3,128,256]{2,1,0:T(8,128)(2,1)S(1)} %shard_map.108), channel_id=1, source_target_pairs={{60,0},{0,4},{4,8},{8,12},{12,16},{16,20},{20,24},{24,28},{28,32},... | collective-permute-start | bytes 589832 | tf_op jit(solution)/shard_map/ppermute | solution.py:312
  61.9 1.5 %copy-start.2 = (bf16[896,1024]{1,0:T(8,128)(2,1)S(1)}, bf16[896,1024]{1,0:T(8,128)(2,1)}, u32[]{:S(2)}) copy-start(bf16[896,1024]{1,0:T(8,128)(2,1)} %all-gather.3.cloned.1.call-done) | copy-start | bytes 5505028
  69.4 25.4 %all-to-all-start.3 = ((bf16[8,32,512]{2,1,0:T(8,128)(2,1)}), bf16[8,32,512]{2,1,0:T(8,128)(2,1)S(1)}, u32[]{:S(2)}, u32[]{:S(2)}) async-start(bf16[8,32,512]{2,1,0:T(8,128)(2,1)} %bitcast.3), calls=%async_computation.3 | async-start | bytes 524288 | tf_op jit(solution)/shard_map/all_to_all | solution.py:316
  80.8 43.9 %copy-start = (bf16[512,1024]{1,0:T(8,128)(2,1)S(1)}, bf16[512,1024]{1,0:T(8,128)(2,1)}, u32[]{:S(2)}) copy-start(bf16[512,1024]{1,0:T(8,128)(2,1)} %out_ref.1) | copy-start | bytes 3145732
  80.8 43.9 %copy-start.1 = (bf16[224,1024]{1,0:T(8,128)(2,1)S(1)}, bf16[224,1024]{1,0:T(8,128)(2,1)}, u32[]{:S(2)}) copy-start(bf16[224,1024]{1,0:T(8,128)(2,1)} %cand_ref.1) | copy-start | bytes 1376260
  80.9 12.8 %collective-permute-start.3 = (bf16[4,128,256]{2,1,0:T(8,128)(2,1)}, bf16[4,128,256]{2,1,0:T(8,128)(2,1)}, u32[]{:S(2)}, u32[]{:S(2)}) collective-permute-start(bf16[4,128,256]{2,1,0:T(8,128)(2,1)} %shard_map.112), channel_id=1, source_target_pairs={{60,0},{0,4},{4,8},{8,12},{12,16},{16,20},{20,24},{24,28},{28,32},... | collective-permute-start | bytes 786440 | tf_op jit(solution)/shard_map/ppermute | solution.py:312
  95.4 20.1 %all-to-all-start.4 = ((bf16[16,8,512]{2,1,0:T(8,128)(2,1)}), bf16[16,8,512]{2,1,0:T(8,128)(2,1)S(1)}, u32[]{:S(2)}, u32[]{:S(2)}) async-start(bf16[16,8,512]{2,1,0:T(8,128)(2,1)} %bitcast.5), calls=%async_computation.4 | async-start | bytes 262144 | tf_op jit(solution)/shard_map/all_to_all | solution.py:316
  101.3 23.4 %collective-permute-start.4 = (bf16[256,256]{1,0:T(8,128)(2,1)S(1)}, bf16[256,256]{1,0:T(8,128)(2,1)S(1)}, u32[]{:S(2)}, u32[]{:S(2)}) collective-permute-start(bf16[256,256]{1,0:T(8,128)(2,1)S(1)} %get-tuple-element.57), channel_id=1, source_target_pairs={{0,1},{1,2},{2,3},{3,0},{4,5},{5,6},{6,7},{7,4},{8,9},{9,10},{10,1... | collective-permute-start | bytes 393224 | tf_op jit(solution)/shard_map/ppermute | solution.py:410
  104.6 20.1 %collective-permute-start.5 = (bf16[256,256]{1,0:T(8,128)(2,1)S(1)}, bf16[256,256]{1,0:T(8,128)(2,1)S(1)}, u32[]{:S(2)}, u32[]{:S(2)}) collective-permute-start(bf16[256,256]{1,0:T(8,128)(2,1)S(1)} %get-tuple-element.58), channel_id=1, source_target_pairs={{0,2},{1,3},{2,0},{3,1},{4,6},{5,7},{6,4},{7,5},{8,10},{9,11},{10,... | collective-permute-start | bytes 393224 | tf_op jit(solution)/shard_map/ppermute | solution.py:410
  108.9 15.8 %collective-permute-start.6 = (bf16[256,256]{1,0:T(8,128)(2,1)S(1)}, bf16[256,256]{1,0:T(8,128)(2,1)S(1)}, u32[]{:S(2)}, u32[]{:S(2)}) collective-permute-start(bf16[256,256]{1,0:T(8,128)(2,1)S(1)} %get-tuple-element.59), channel_id=1, source_target_pairs={{0,3},{1,0},{2,1},{3,2},{4,7},{5,4},{6,5},{7,6},{8,11},{9,8},{10,9... | collective-permute-start | bytes 393224 | tf_op jit(solution)/shard_map/ppermute | solution.py:410
  116.1 13.8 %all-to-all-start.5 = ((f32[8,8,512]{2,1,0:T(8,128)}), f32[8,8,512]{2,1,0:T(8,128)S(1)}, u32[]{:S(2)}, u32[]{:S(2)}) async-start(f32[8,8,512]{2,1,0:T(8,128)} %shard_map.116), calls=%async_computation.5 | async-start | bytes 262144 | tf_op jit(solution)/shard_map/all_to_all | solution.py:316
Sparse Core Ops, SparseCore 0:
  12.4 45.9 all-gather.2

commit v11 on v9

--- a/solution.py
+++ b/solution.py
@@ -395,11 +395,11 @@
     part = exchanged(out_grad.reshape(cores * zl, size // zl, half), ("core", "zl"))
     back1 = on_core(add_kernel, shaped(ring1.shape, BF16), back1, back2)
     back0 = on_core(back0_kernel, shaped(ring0.shape, F32), ring0, bundle, late_grads)
+    part, back0, back1 = barrier((part, back0, back1))
+    part = on_core(fold_kernel, shaped((zh, xs, own, half), BF16), part)
     parcels = on_core(
         parcel_kernel, [shaped((2 * size, lanes), BF16)] * HEADS, gated, back0, moved(back1, -1), scalars=(place,)
     )
-    part, *parcels = barrier((part, *parcels))
-    part, *parcels = barrier((on_core(fold_kernel, shaped((zh, xs, own, half), BF16), part), *parcels))
     part = exchanged(part.reshape(zh * xs, own, half), ("zh", "x")).reshape(zh, xs, own, half)
     depth = lax.axis_index("zh").reshape(1).astype(jnp.int32)
     peers = lax.axis_size("y") * cores

time: 133 us -> 141 us (1.060)
  waiting for transfers between devices: 23.2 us -> 32.6 us
  starting transfers between devices: 65.6 us -> 62.8 us
  local copies, waits for them, and re-layouts: 1.52 us -> 3.18 us
    ppermute x4, waiting for transfers between devices: 14.7 us -> 20.5 us  [moved(): lax.ppermute(block, DEPTH, [((i + distance) % size, i) for i in range(siz...]
    all_to_all x5, waiting for transfers between devices: 7.73 us -> 11.4 us  [exchanged(): return lax.all_to_all(chunks, axis, 0, 0, tiled=True)]
    unnamed x6 -> x12, local copies, waits for them, and re-layouts: 1.5 us -> 3.15 us
    ppermute x4, starting transfers between devices: 19.5 us -> 18 us  [moved(): lax.ppermute(block, DEPTH, [((i + distance) % size, i) for i in range(siz...]
  transfers between devices with their start and end apart: 13 -> 13, of which waited for: 7 -> 7; matrix products, arithmetic and copies ran while one was open for 0% -> 0% of each run, Pallas kernels for 14% -> 12%
where the time goes in v11:
time: 141 us; the launch traced here: 140 us
  starting transfers between devices  62.8 us (45%)
  waiting for transfers between devices  32.6 us (23%)
  Pallas kernels  18.8 us (13%)
  between operations  14.3 us (10%)
  blocking collectives  8.47 us (6%)
  local copies, waits for them, and re-layouts  3.18 us (2%)
    all_to_all x5, starting transfers between devices, exchanged(): return lax.all_to_all(chunks, axis, 0, 0, tiled=True)  34.1 us
    ppermute x4, waiting for transfers between devices, moved(): lax.ppermute(block, DEPTH, [((i + distance) % size, i) for i in range(siz...  20.5 us
    ppermute x4, starting transfers between devices, moved(): lax.ppermute(block, DEPTH, [((i + distance) % size, i) for i in range(siz...  18 us
    pallas_call x13, Pallas kernels, on_core(): pl.pallas_call(kernel, out_shape=outs, in_specs=[pl.BlockSpec(memory_spac...  12.1 us
    all_to_all x5, waiting for transfers between devices, exchanged(): return lax.all_to_all(chunks, axis, 0, 0, tiled=True)  11.4 us
    ppermute x3, starting transfers between devices, on_device(): lax.ppermute(parcel, 'x', [(i, (i + step) % HEADS) for i in range(HEADS)])  10.7 us
    all_to_all x1, blocking collectives, exchanged(): return lax.all_to_all(chunks, axis, 0, 0, tiled=True)  8.47 us
    pallas_call x1, Pallas kernels, on_fetched(): pl.pallas_call(body, out_shape=outs, in_specs=[pl.BlockSpec(memory_space=...  5.01 us
  transfers between devices with their start and end apart: 13, of which 7 were waited for; matrix products, arithmetic and copies ran while one was open for 0% of the time, Pallas kernels for 12%

profile of v11, /device:TPU:1, one launch (start us, length us, event | category | flops | bytes accessed | tf_op | source)
XLA Modules:
  0.0 140.1 jit_solution(13027845328481244610)
XLA Ops:
  7.9 1.6 %shard_map.103 = bf16[4,128,256]{2,1,0:T(8,128)(2,1)} custom-call(bf16[128,1024]{1,0:T(8,128)(2,1)} %history_ref.1), custom_call_target="tpu_custom_call" | custom-call | tf_op jit(solution)/shard_map/pallas_call | solution.py:349
  9.6 4.9 %all-to-all-start = ((bf16[4,128,256]{2,1,0:T(8,128)(2,1)}), bf16[4,128,256]{2,1,0:T(8,128)(2,1)S(1)}, u32[]{:S(2)}, u32[]{:S(2)}) async-start(bf16[4,128,256]{2,1,0:T(8,128)(2,1)} %shard_map.103), calls=%async_computation | async-start | bytes 524288 | tf_op jit(solution)/shard_map/all_to_all | solution.py:316
  14.4 5.0 %shard_map.104 = bf16[4,400,256]{2,1,0:T(8,128)(2,1)} custom-call(s32[2,8]{1,0:T(2,128)} %refs_0_.1, s32[2]{0:T(128)} %refs_1_.1, s32[1,224]{1,0:T(1,128)} %bitcast.11, bf16[224,1024]{1,0:T(8,128)(2,1)} %cand_ref.1, bf16[224,1024]{1,0:T(8,128)(2,1)} %refs_4_.1, bf16[1024,1024]{1,0:T(8,128)(2,1)} %refs_5_.1, bf16[512,1024]{1,0:T(8,128)(2,1)} %out_ref.1), custom_call_target="tpu_custom_call" | custom-call | tf_op jit(solution)/shard_map/pallas_call | solution.py:51
  19.9 3.7 %all-to-all-start.1 = ((bf16[4,400,256]{2,1,0:T(8,128)(2,1)}), bf16[4,400,256]{2,1,0:T(8,128)(2,1)S(1)}, u32[]{:S(2)}, u32[]{:S(2)}) async-start(bf16[4,400,256]{2,1,0:T(8,128)(2,1)} %shard_map.104), calls=%async_computation.1 | async-start | bytes 1638400 | tf_op jit(solution)/shard_map/all_to_all | solution.py:316
  23.7 11.1 %collective-permute-start.1 = (bf16[4,128,256]{2,1,0:T(8,128)(2,1)S(1)}, bf16[4,128,256]{2,1,0:T(8,128)(2,1)S(1)}, u32[]{:S(2)}, u32[]{:S(2)}) collective-permute-start(bf16[4,128,256]{2,1,0:T(8,128)(2,1)S(1)} %all-to-all-done.ring0), channel_id=1, source_target_pairs={{4,0},{8,4},{12,8},{16,12},{20,16},{24,20},{28,24},{32,28},{36,32}... | collective-permute-start | bytes 786440 | tf_op jit(solution)/shard_map/ppermute | solution.py:312
  34.8 3.1 %collective-permute-start = (bf16[3,128,256]{2,1,0:T(8,128)(2,1)S(1)}, bf16[3,128,256]{2,1,0:T(8,128)(2,1)S(1)}, u32[]{:S(2)}, u32[]{:S(2)}) collective-permute-start(bf16[3,128,256]{2,1,0:T(8,128)(2,1)S(1)} %slice.4), channel_id=1, source_target_pairs={{8,0},{12,4},{16,8},{20,12},{24,16},{28,20},{32,24},{36,28},{40,32... | collective-permute-start | bytes 589832 | tf_op jit(solution)/shard_map/ppermute | solution.py:312
  38.5 1.7 %shard_map.105.before = f32[4,128,256]{2,1,0:T(8,128)S(1)} custom-call(bf16[4,128,256]{2,1,0:T(8,128)(2,1)S(1)} %all-to-all-done.ring0, bf16[4,128,256]{2,1,0:T(8,128)(2,1)S(1)} %collective-permute-done.1.ring1, bf16[4,400,256]{2,1,0:T(8,128)(2,1)S(1)} %all-to-all-done.1.bundle), custom_call_target="tpu_custom_call" | custom-call | tf_op jit(solution)/shard_map/pallas_call | solution.py:22
  40.2 5.4 %collective-permute-done.ring2 = bf16[3,128,256]{2,1,0:T(8,128)(2,1)S(1)} collective-permute-done((bf16[3,128,256]{2,1,0:T(8,128)(2,1)S(1)}, bf16[3,128,256]{2,1,0:T(8,128)(2,1)S(1)}, u32[]{:S(2)}, u32[]{:S(2)}) %collective-permute-start) | collective-permute-done | bytes 196640 | tf_op jit(solution)/shard_map/ppermute | solution.py:312
  46.4 8.5 %all_to_all.30.stats = f32[4,16,256]{2,1,0:T(8,128)S(1)} all-to-all(f32[4,16,256]{2,1,0:T(8,128)S(1)} %broadcast_in_dim.2), channel_id=1, replica_groups=mesh['y'=4,'core'=2,'zh'=4,'zl'=4,'x'=4] {'x'}, dimensions={0} | all-to-all | bytes 131072 | tf_op jit(solution)/shard_map/all_to_all | solution.py:316
  55.9 1.9 %collective-permute-start.2 = (bf16[3,128,256]{2,1,0:T(8,128)(2,1)S(1)}, bf16[3,128,256]{2,1,0:T(8,128)(2,1)S(1)}, u32[]{:S(2)}, u32[]{:S(2)}) collective-permute-start(bf16[3,128,256]{2,1,0:T(8,128)(2,1)S(1)} %shard_map.108), channel_id=1, source_target_pairs={{60,0},{0,4},{4,8},{8,12},{12,16},{16,20},{20,24},{24,28},{28,32},... | collective-permute-start | bytes 589832 | tf_op jit(solution)/shard_map/ppermute | solution.py:312
  57.9 1.5 %copy-done.2 = bf16[896,1024]{1,0:T(8,128)(2,1)S(1)} copy-done((bf16[896,1024]{1,0:T(8,128)(2,1)S(1)}, bf16[896,1024]{1,0:T(8,128)(2,1)}, u32[]{:S(2)}) %copy-start.2) | copy-done | bytes 1835032
  60.5 1.7 %shard_map.110.own = f32[4,128,256]{2,1,0:T(8,128)S(1)} custom-call(bf16[4,128,256]{2,1,0:T(8,128)(2,1)S(1)} %collective-permute-done.1.ring1, bf16[4,400,256]{2,1,0:T(8,128)(2,1)S(1)} %all-to-all-done.1.bundle, bf16[4,128,256]{2,1,0:T(8,128)(2,1)S(1)} %get-tuple-element.33.grads), custom_call_target="tpu_custom_call" | custom-call | tf_op jit(solution)/shard_map/pallas_call | solution.py:22
  63.5 11.7 %all-to-all-start.3 = ((bf16[8,32,512]{2,1,0:T(8,128)(2,1)}), bf16[8,32,512]{2,1,0:T(8,128)(2,1)}, u32[]{:S(2)}, u32[]{:S(2)}) async-start(bf16[8,32,512]{2,1,0:T(8,128)(2,1)} %bitcast.3), calls=%async_computation.3 | async-start | bytes 524288 | tf_op jit(solution)/shard_map/all_to_all | solution.py:316
  77.2 7.1 %all-to-all-done.3.parts = bf16[8,32,512]{2,1,0:T(8,128)(2,1)} async-done(((bf16[8,32,512]{2,1,0:T(8,128)(2,1)}), bf16[8,32,512]{2,1,0:T(8,128)(2,1)}, u32[]{:S(2)}, u32[]{:S(2)}) %all-to-all-start.3) | async-done | bytes 262176 | tf_op jit(solution)/shard_map/all_to_all | solution.py:316
  84.3 1.6 %shard_map.115 = bf16[4,4,8,512]{3,2,1,0:T(8,128)(2,1)} custom-call(bf16[8,32,512]{2,1,0:T(8,128)(2,1)} %all-to-all-done.3.parts), custom_call_target="tpu_custom_call" | custom-call | tf_op jit(solution)/shard_map/pallas_call | solution.py:22
  86.0 8.0 %all-to-all-start.4 = ((bf16[16,8,512]{2,1,0:T(8,128)(2,1)}), bf16[16,8,512]{2,1,0:T(8,128)(2,1)S(1)}, u32[]{:S(2)}, u32[]{:S(2)}) async-start(bf16[16,8,512]{2,1,0:T(8,128)(2,1)} %bitcast.5), calls=%async_computation.4 | async-start | bytes 262144 | tf_op jit(solution)/shard_map/all_to_all | solution.py:316
  94.0 1.9 %collective-permute-start.3 = (bf16[4,128,256]{2,1,0:T(8,128)(2,1)}, bf16[4,128,256]{2,1,0:T(8,128)(2,1)S(1)}, u32[]{:S(2)}, u32[]{:S(2)}) collective-permute-start(bf16[4,128,256]{2,1,0:T(8,128)(2,1)} %copy-done.5), channel_id=1, source_target_pairs={{60,0},{0,4},{4,8},{8,12},{12,16},{16,20},{20,24},{24,28},{28,32},... | collective-permute-start | bytes 786440 | tf_op jit(solution)/shard_map/ppermute | solution.py:312
  95.9 13.2 %collective-permute-done.3.back1 = bf16[4,128,256]{2,1,0:T(8,128)(2,1)S(1)} collective-permute-done((bf16[4,128,256]{2,1,0:T(8,128)(2,1)}, bf16[4,128,256]{2,1,0:T(8,128)(2,1)S(1)}, u32[]{:S(2)}, u32[]{:S(2)}) %collective-permute-start.3) | collective-permute-done | bytes 262176 | tf_op jit(solution)/shard_map/ppermute | solution.py:312
  110.2 3.3 %collective-permute-start.4 = (bf16[256,256]{1,0:T(8,128)(2,1)S(1)}, bf16[256,256]{1,0:T(8,128)(2,1)S(1)}, u32[]{:S(2)}, u32[]{:S(2)}) collective-permute-start(bf16[256,256]{1,0:T(8,128)(2,1)S(1)} %get-tuple-element.39), channel_id=1, source_target_pairs={{0,1},{1,2},{2,3},{3,0},{4,5},{5,6},{6,7},{7,4},{8,9},{9,10},{10,1... | collective-permute-start | bytes 393224 | tf_op jit(solution)/shard_map/ppermute | solution.py:409
  113.4 4.3 %collective-permute-start.5 = (bf16[256,256]{1,0:T(8,128)(2,1)S(1)}, bf16[256,256]{1,0:T(8,128)(2,1)S(1)}, u32[]{:S(2)}, u32[]{:S(2)}) collective-permute-start(bf16[256,256]{1,0:T(8,128)(2,1)S(1)} %get-tuple-element.40), channel_id=1, source_target_pairs={{0,2},{1,3},{2,0},{3,1},{4,6},{5,7},{6,4},{7,5},{8,10},{9,11},{10,... | collective-permute-start | bytes 393224 | tf_op jit(solution)/shard_map/ppermute | solution.py:409
  117.7 3.1 %collective-permute-start.6 = (bf16[256,256]{1,0:T(8,128)(2,1)S(1)}, bf16[256,256]{1,0:T(8,128)(2,1)S(1)}, u32[]{:S(2)}, u32[]{:S(2)}) collective-permute-start(bf16[256,256]{1,0:T(8,128)(2,1)S(1)} %get-tuple-element.41), channel_id=1, source_target_pairs={{0,3},{1,0},{2,1},{3,2},{4,7},{5,4},{6,5},{7,6},{8,11},{9,8},{10,9... | collective-permute-start | bytes 393224 | tf_op jit(solution)/shard_map/ppermute | solution.py:409
  121.5 5.8 %all-to-all-start.5 = ((f32[8,8,512]{2,1,0:T(8,128)}), f32[8,8,512]{2,1,0:T(8,128)S(1)}, u32[]{:S(2)}, u32[]{:S(2)}) async-start(f32[8,8,512]{2,1,0:T(8,128)} %shard_map.116), calls=%async_computation.5 | async-start | bytes 262144 | tf_op jit(solution)/shard_map/all_to_all | solution.py:316
  127.4 1.5 %shard_map.114 = (bf16[224,1024]{1,0:T(8,128)(2,1)}, bf16[128,1024]{1,0:T(8,128)(2,1)}) custom-call(s32[1]{0:T(128)} %bitcast.place_ref, bf16[224,1024]{1,0:T(8,128)(2,1)S(1)} %copy-done.1, bf16[512,1024]{1,0:T(8,128)(2,1)S(1)} %copy-done, bf16[256,256]{1,0:T(8,128)(2,1)S(1)} %get-tuple-element.38.refs_0_, ...), custom_call_target="tpu_custom_call" | custom-call | tf_op jit(solution)/shard_map/pallas_call | solution.py:22
  128.9 3.7 %all-to-all-done.5 = f32[8,8,512]{2,1,0:T(8,128)S(1)} async-done(((f32[8,8,512]{2,1,0:T(8,128)}), f32[8,8,512]{2,1,0:T(8,128)S(1)}, u32[]{:S(2)}, u32[]{:S(2)}) %all-to-all-start.5) | async-done | bytes 131104 | tf_op jit(solution)/shard_map/all_to_all | solution.py:316
  (33 shorter events, 10.4 us)
Async XLA Ops:
  7.2 50.7 %all-gather.3.cloned.1.call-start = ((), (), s32[]{:S(2)}) async-start(), calls=%async_computation.6 | async-start | bytes 2293760 | tf_op jit(solution)/shard_map/all_gather | solution.py:347
  9.6 10.4 %all-to-all-start = ((bf16[4,128,256]{2,1,0:T(8,128)(2,1)}), bf16[4,128,256]{2,1,0:T(8,128)(2,1)S(1)}, u32[]{:S(2)}, u32[]{:S(2)}) async-start(bf16[4,128,256]{2,1,0:T(8,128)(2,1)} %shard_map.103), calls=%async_computation | async-start | bytes 524288 | tf_op jit(solution)/shard_map/all_to_all | solution.py:316
  19.9 18.6 %all-to-all-start.1 = ((bf16[4,400,256]{2,1,0:T(8,128)(2,1)}), bf16[4,400,256]{2,1,0:T(8,128)(2,1)S(1)}, u32[]{:S(2)}, u32[]{:S(2)}) async-start(bf16[4,400,256]{2,1,0:T(8,128)(2,1)} %shard_map.104), calls=%async_computation.1 | async-start | bytes 1638400 | tf_op jit(solution)/shard_map/all_to_all | solution.py:316
  23.7 14.8 %collective-permute-start.1 = (bf16[4,128,256]{2,1,0:T(8,128)(2,1)S(1)}, bf16[4,128,256]{2,1,0:T(8,128)(2,1)S(1)}, u32[]{:S(2)}, u32[]{:S(2)}) collective-permute-start(bf16[4,128,256]{2,1,0:T(8,128)(2,1)S(1)} %all-to-all-done.ring0), channel_id=1, source_target_pairs={{4,0},{8,4},{12,8},{16,12},{20,16},{24,20},{28,24},{32,28},{36,32}... | collective-permute-start | bytes 786440 | tf_op jit(solution)/shard_map/ppermute | solution.py:312
  34.8 10.7 %collective-permute-start = (bf16[3,128,256]{2,1,0:T(8,128)(2,1)S(1)}, bf16[3,128,256]{2,1,0:T(8,128)(2,1)S(1)}, u32[]{:S(2)}, u32[]{:S(2)}) collective-permute-start(bf16[3,128,256]{2,1,0:T(8,128)(2,1)S(1)} %slice.4), channel_id=1, source_target_pairs={{8,0},{12,4},{16,8},{20,12},{24,16},{28,20},{32,24},{36,28},{40,32... | collective-permute-start | bytes 589832 | tf_op jit(solution)/shard_map/ppermute | solution.py:312
  55.1 7.1 %copy-start.3 = (bf16[4,128,256]{2,1,0:T(8,128)(2,1)}, bf16[4,128,256]{2,1,0:T(8,128)(2,1)S(1)}, u32[]{:S(2)}) copy-start(bf16[4,128,256]{2,1,0:T(8,128)(2,1)S(1)} %get-tuple-element.28.refs_1_.gated_ref) | copy-start | bytes 786436
  55.9 7.6 %collective-permute-start.2 = (bf16[3,128,256]{2,1,0:T(8,128)(2,1)S(1)}, bf16[3,128,256]{2,1,0:T(8,128)(2,1)S(1)}, u32[]{:S(2)}, u32[]{:S(2)}) collective-permute-start(bf16[3,128,256]{2,1,0:T(8,128)(2,1)S(1)} %shard_map.108), channel_id=1, source_target_pairs={{60,0},{0,4},{4,8},{8,12},{12,16},{16,20},{20,24},{24,28},{28,32},... | collective-permute-start | bytes 589832 | tf_op jit(solution)/shard_map/ppermute | solution.py:312
  57.9 1.5 %copy-start.2 = (bf16[896,1024]{1,0:T(8,128)(2,1)S(1)}, bf16[896,1024]{1,0:T(8,128)(2,1)}, u32[]{:S(2)}) copy-start(bf16[896,1024]{1,0:T(8,128)(2,1)} %all-gather.3.cloned.1.call-done) | copy-start | bytes 5505028
  63.5 20.8 %all-to-all-start.3 = ((bf16[8,32,512]{2,1,0:T(8,128)(2,1)}), bf16[8,32,512]{2,1,0:T(8,128)(2,1)}, u32[]{:S(2)}, u32[]{:S(2)}) async-start(bf16[8,32,512]{2,1,0:T(8,128)(2,1)} %bitcast.3), calls=%async_computation.3 | async-start | bytes 524288 | tf_op jit(solution)/shard_map/all_to_all | solution.py:316
  75.2 0.7 copy-start.5
  75.9 51.4 %copy-start = (bf16[512,1024]{1,0:T(8,128)(2,1)S(1)}, bf16[512,1024]{1,0:T(8,128)(2,1)}, u32[]{:S(2)}) copy-start(bf16[512,1024]{1,0:T(8,128)(2,1)} %out_ref.1) | copy-start | bytes 3145732
  75.9 51.4 %copy-start.1 = (bf16[224,1024]{1,0:T(8,128)(2,1)S(1)}, bf16[224,1024]{1,0:T(8,128)(2,1)}, u32[]{:S(2)}) copy-start(bf16[224,1024]{1,0:T(8,128)(2,1)} %cand_ref.1) | copy-start | bytes 1376260
  86.0 34.9 %all-to-all-start.4 = ((bf16[16,8,512]{2,1,0:T(8,128)(2,1)}), bf16[16,8,512]{2,1,0:T(8,128)(2,1)S(1)}, u32[]{:S(2)}, u32[]{:S(2)}) async-start(bf16[16,8,512]{2,1,0:T(8,128)(2,1)} %bitcast.5), calls=%async_computation.4 | async-start | bytes 262144 | tf_op jit(solution)/shard_map/all_to_all | solution.py:316
  94.0 15.2 %collective-permute-start.3 = (bf16[4,128,256]{2,1,0:T(8,128)(2,1)}, bf16[4,128,256]{2,1,0:T(8,128)(2,1)S(1)}, u32[]{:S(2)}, u32[]{:S(2)}) collective-permute-start(bf16[4,128,256]{2,1,0:T(8,128)(2,1)} %copy-done.5), channel_id=1, source_target_pairs={{60,0},{0,4},{4,8},{8,12},{12,16},{16,20},{20,24},{24,28},{28,32},... | collective-permute-start | bytes 786440 | tf_op jit(solution)/shard_map/ppermute | solution.py:312
  109.1 1.0 copy-start.4
  110.2 17.2 %collective-permute-start.4 = (bf16[256,256]{1,0:T(8,128)(2,1)S(1)}, bf16[256,256]{1,0:T(8,128)(2,1)S(1)}, u32[]{:S(2)}, u32[]{:S(2)}) collective-permute-start(bf16[256,256]{1,0:T(8,128)(2,1)S(1)} %get-tuple-element.39), channel_id=1, source_target_pairs={{0,1},{1,2},{2,3},{3,0},{4,5},{5,6},{6,7},{7,4},{8,9},{9,10},{10,1... | collective-permute-start | bytes 393224 | tf_op jit(solution)/shard_map/ppermute | solution.py:409
  113.4 13.9 %collective-permute-start.5 = (bf16[256,256]{1,0:T(8,128)(2,1)S(1)}, bf16[256,256]{1,0:T(8,128)(2,1)S(1)}, u32[]{:S(2)}, u32[]{:S(2)}) collective-permute-start(bf16[256,256]{1,0:T(8,128)(2,1)S(1)} %get-tuple-element.40), channel_id=1, source_target_pairs={{0,2},{1,3},{2,0},{3,1},{4,6},{5,7},{6,4},{7,5},{8,10},{9,11},{10,... | collective-permute-start | bytes 393224 | tf_op jit(solution)/shard_map/ppermute | solution.py:409
  117.7 9.6 %collective-permute-start.6 = (bf16[256,256]{1,0:T(8,128)(2,1)S(1)}, bf16[256,256]{1,0:T(8,128)(2,1)S(1)}, u32[]{:S(2)}, u32[]{:S(2)}) collective-permute-start(bf16[256,256]{1,0:T(8,128)(2,1)S(1)} %get-tuple-element.41), channel_id=1, source_target_pairs={{0,3},{1,0},{2,1},{3,2},{4,7},{5,4},{6,5},{7,6},{8,11},{9,8},{10,9... | collective-permute-start | bytes 393224 | tf_op jit(solution)/shard_map/ppermute | solution.py:409
  121.5 11.1 %all-to-all-start.5 = ((f32[8,8,512]{2,1,0:T(8,128)}), f32[8,8,512]{2,1,0:T(8,128)S(1)}, u32[]{:S(2)}, u32[]{:S(2)}) async-start(f32[8,8,512]{2,1,0:T(8,128)} %shard_map.116), calls=%async_computation.5 | async-start | bytes 262144 | tf_op jit(solution)/shard_map/all_to_all | solution.py:316
Sparse Core Ops, SparseCore 0:
  10.1 43.9 all-gather.2

commit v12 on v9

--- a/solution.py
+++ b/solution.py
@@ -198,19 +198,17 @@
         grad_ref[group] = (inv_scale * (dy - mean_dy - normed * mean_mixed)).astype(BF16)
 
 
-def out_grad_kernel(total_cands, cots, gated, out_grad_ref):
-    count = cots.shape[1]
-    total = None
-    for group in range(HEADS):
-        part = jnp.dot(gated[group, :, :count], cots[group], preferred_element_type=F32)
-        total = part if total is None else total + part
-    total = (total * (1.0 / math.sqrt(total_cands))).astype(BF16)
-    halves, rows_of, lines, columns = out_grad_ref.shape
-    for half in range(halves):
+def out_grad_kernel(total_cands, low, high, gated, out_grad_ref):
+    count = low.shape[1]
+    _, rows_of, lines, _ = out_grad_ref.shape
+    for half, cots in enumerate((low, high)):
+        total = None
+        for group in range(HEADS):
+            part = jnp.dot(gated[group, :, :count], cots[group], preferred_element_type=F32)
+            total = part if total is None else total + part
+        total = (total * (1.0 / math.sqrt(total_cands))).astype(BF16)
         for row in range(rows_of):
-            out_grad_ref[half, row] = total[
-                row * lines : (row + 1) * lines, half * columns : (half + 1) * columns
-            ]
+            out_grad_ref[half, row] = total[row * lines : (row + 1) * lines]
 
 
 def back(ring, blocks_ref, bundle, grads, sum_ref):
@@ -335,8 +333,8 @@
     in_weight,
     out_weight,
 ):
-    tall, wide = history.shape
-    inner = wide // 2
+    tall = history.shape[0]
+    inner = history.shape[1] // 2
     size = inner // HEADS
     count = candidates.shape[0]
     lanes = 2 * size
@@ -344,7 +342,6 @@
     barrier = lax.optimization_barrier
     place = lax.axis_index("x").reshape(1).astype(jnp.int32)
 
-    cots = lax.all_gather(cotangent, "x")
     ring_shape = shaped((HEADS, tall, 2 * size), BF16)
     by_head = pl.pallas_call(
         split_kernel,
@@ -369,31 +366,38 @@
         scalars=(request_blocks, request_length),
     )
     bundle = exchanged(bundle, "x")
+    cores = lax.axis_size("core")
+    half = out_weight.shape[1] // cores
+    wide = (lax.axis_size("x"), count, half)
+    bundle, low, high = barrier(
+        (bundle,) + tuple(jnp.broadcast_to(cotangent[None, :, i * half : (i + 1) * half], wide) for i in range(2))
+    )
+    low = exchanged(low, "x")
 
     attended_shape = shaped((HEADS, size, lanes), F32)
     before = on_core(early_kernel, attended_shape, ring0, ring1, bundle)
     attended, stats = on_core(
         late_kernel, (attended_shape, shaped((4 * HEADS, lanes), F32)), ring2, bundle, before
     )
-    stats = spread_over(stats, "x")
+    stats, high = barrier((spread_over(stats, "x"), high))
+    high = exchanged(high, "x")
     head_shape = shaped((HEADS, size, lanes), BF16)
-    cores, zh, zl, xs = (lax.axis_size(name) for name in ("core", "zh", "zl", "x"))
-    own, half = size // (zl * xs), out_weight.shape[1] // cores
+    zh, zl, xs = (lax.axis_size(name) for name in ("zh", "zl", "x"))
+    own = size // (zl * xs)
     gated, grads = on_core(norm_kernel, (head_shape, head_shape), attended, bundle, stats)
-    back2 = on_core(back2_kernel, shaped(ring2.shape, BF16), ring2, bundle, grads)
-    gated, back2 = barrier((gated, back2))
-    back2 = moved(back2, -1)
+    back2 = moved(on_core(back2_kernel, shaped(ring2.shape, BF16), ring2, bundle, grads), -1)
+    back1 = on_core(back1_kernel, shaped(ring1.shape, F32), ring1, bundle, grads)
+    back1 = on_core(add_kernel, shaped(ring1.shape, BF16), back1, back2)
+    high, back1 = barrier((high, back1))
     out_grad = on_core(
         lambda *refs: out_grad_kernel(total_cands, *refs),
         shaped((cores, zl, size // zl, half), BF16),
-        cots,
+        low,
+        high,
         gated,
     )
     out_grad, late_grads = barrier((out_grad, grads))
-    back1 = on_core(back1_kernel, shaped(ring1.shape, F32), ring1, bundle, late_grads)
-    out_grad, back2, back1, late_grads = barrier((out_grad, back2, back1, late_grads))
     part = exchanged(out_grad.reshape(cores * zl, size // zl, half), ("core", "zl"))
-    back1 = on_core(add_kernel, shaped(ring1.shape, BF16), back1, back2)
     back0 = on_core(back0_kernel, shaped(ring0.shape, F32), ring0, bundle, late_grads)
     parcels = on_core(
         parcel_kernel, [shaped((2 * size, lanes), BF16)] * HEADS, gated, back0, moved(back1, -1), scalars=(place,)

time: 133 us -> 144 us (1.083)
  between operations: 14.2 us -> 0.94 us
  blocking collectives: 8.47 us -> 20 us
  local copies, waits for them, and re-layouts: 1.52 us -> 6.05 us
  waiting for transfers between devices: 23.2 us -> 27.5 us
  starting transfers between devices: 65.6 us -> 69.5 us
    all_to_all x1 -> x2, blocking collectives: 8.47 us -> 20 us  [exchanged(): return lax.all_to_all(chunks, axis, 0, 0, tiled=True)]
    ppermute x4, waiting for transfers between devices: 14.7 us -> 19.8 us  [moved(): lax.ppermute(block, DEPTH, [((i + distance) % size, i) for i in range(siz...]
    all_to_all x5 -> x6, starting transfers between devices: 35.4 us -> 39.4 us  [exchanged(): return lax.all_to_all(chunks, axis, 0, 0, tiled=True)]
    unnamed x6 -> x24, local copies, waits for them, and re-layouts: 1.5 us -> 4.25 us
    all_to_all x5 -> x6, waiting for transfers between devices: 7.73 us -> 7.65 us  [exchanged(): return lax.all_to_all(chunks, axis, 0, 0, tiled=True)]
  transfers between devices with their start and end apart: 13 -> 13, of which waited for: 7 -> 6; matrix products, arithmetic and copies ran while one was open for 0% -> 1% of each run, Pallas kernels for 14% -> 10%
where the time goes in v12:
time: 144 us; the launch traced here: 143 us
  starting transfers between devices  69.5 us (48%)
  waiting for transfers between devices  27.5 us (19%)
  blocking collectives  20 us (14%)
  Pallas kernels  19 us (13%)
  local copies, waits for them, and re-layouts  6.05 us (4%)
    all_to_all x6, starting transfers between devices, exchanged(): return lax.all_to_all(chunks, axis, 0, 0, tiled=True)  39.4 us
    all_to_all x2, blocking collectives, exchanged(): return lax.all_to_all(chunks, axis, 0, 0, tiled=True)  20 us
    ppermute x4, waiting for transfers between devices, moved(): lax.ppermute(block, DEPTH, [((i + distance) % size, i) for i in range(siz...  19.8 us
    ppermute x4, starting transfers between devices, moved(): lax.ppermute(block, DEPTH, [((i + distance) % size, i) for i in range(siz...  19.5 us
    pallas_call x13, Pallas kernels, on_core(): pl.pallas_call(kernel, out_shape=outs, in_specs=[pl.BlockSpec(memory_spac...  12.3 us
    ppermute x3, starting transfers between devices, on_device(): lax.ppermute(parcel, 'x', [(i, (i + step) % HEADS) for i in range(HEADS)])  10.7 us
    all_to_all x6, waiting for transfers between devices, exchanged(): return lax.all_to_all(chunks, axis, 0, 0, tiled=True)  7.65 us
    pallas_call x1, Pallas kernels, on_fetched(): pl.pallas_call(body, out_shape=outs, in_specs=[pl.BlockSpec(memory_space=...  5 us
  transfers between devices with their start and end apart: 13, of which 6 were waited for; matrix products, arithmetic and copies ran while one was open for 1% of the time, Pallas kernels for 10%

profile of v12, /device:TPU:1, one launch (start us, length us, event | category | flops | bytes accessed | tf_op | source)
XLA Modules:
  0.0 143.0 jit_solution(5479665997228936431)
XLA Ops:
  0.6 1.6 %shard_map.104 = bf16[4,128,256]{2,1,0:T(8,128)(2,1)} custom-call(bf16[128,1024]{1,0:T(8,128)(2,1)} %history_ref.1), custom_call_target="tpu_custom_call" | custom-call | tf_op jit(solution)/shard_map/pallas_call | solution.py:346
  2.3 4.9 %all-to-all-start.2 = ((bf16[4,128,256]{2,1,0:T(8,128)(2,1)}), bf16[4,128,256]{2,1,0:T(8,128)(2,1)S(1)}, u32[]{:S(2)}, u32[]{:S(2)}) async-start(bf16[4,128,256]{2,1,0:T(8,128)(2,1)} %shard_map.104), calls=%async_computation.2 | async-start | bytes 524288 | tf_op jit(solution)/shard_map/all_to_all | solution.py:314
  7.1 5.0 %shard_map.103 = bf16[4,400,256]{2,1,0:T(8,128)(2,1)} custom-call(s32[2,8]{1,0:T(2,128)} %refs_0_.1, s32[2]{0:T(128)} %refs_1_.1, s32[1,224]{1,0:T(1,128)} %bitcast.10, bf16[224,1024]{1,0:T(8,128)(2,1)} %cand_ref.1, bf16[224,1024]{1,0:T(8,128)(2,1)} %refs_4_.1, bf16[1024,1024]{1,0:T(8,128)(2,1)} %refs_5_.1, bf16[512,1024]{1,0:T(8,128)(2,1)} %out_ref.1), custom_call_target="tpu_custom_call" | custom-call | tf_op jit(solution)/shard_map/pallas_call | solution.py:51
  12.7 3.9 %all-to-all-start = ((bf16[4,400,256]{2,1,0:T(8,128)(2,1)}), bf16[4,400,256]{2,1,0:T(8,128)(2,1)S(1)}, u32[]{:S(2)}, u32[]{:S(2)}) async-start(bf16[4,400,256]{2,1,0:T(8,128)(2,1)} %shard_map.103), calls=%async_computation | async-start | bytes 1638400 | tf_op jit(solution)/shard_map/all_to_all | solution.py:314
  16.5 11.1 %collective-permute-start.1 = (bf16[4,128,256]{2,1,0:T(8,128)(2,1)S(1)}, bf16[4,128,256]{2,1,0:T(8,128)(2,1)S(1)}, u32[]{:S(2)}, u32[]{:S(2)}) collective-permute-start(bf16[4,128,256]{2,1,0:T(8,128)(2,1)S(1)} %all-to-all-done.2.ring0), channel_id=1, source_target_pairs={{4,0},{8,4},{12,8},{16,12},{20,16},{24,20},{28,24},{32,28},{36,32}... | collective-permute-start | bytes 786440 | tf_op jit(solution)/shard_map/ppermute | solution.py:310
  28.4 3.1 %collective-permute-start = (bf16[3,128,256]{2,1,0:T(8,128)(2,1)}, bf16[3,128,256]{2,1,0:T(8,128)(2,1)S(1)}, u32[]{:S(2)}, u32[]{:S(2)}) collective-permute-start(bf16[3,128,256]{2,1,0:T(8,128)(2,1)} %slice.12), channel_id=1, source_target_pairs={{8,0},{12,4},{16,8},{20,12},{24,16},{28,20},{32,24},{36,28},{40,32... | collective-permute-start | bytes 589832 | tf_op jit(solution)/shard_map/ppermute | solution.py:310
  32.6 1.7 %shard_map.105.before = f32[4,128,256]{2,1,0:T(8,128)S(1)} custom-call(bf16[4,128,256]{2,1,0:T(8,128)(2,1)S(1)} %all-to-all-done.2.ring0, bf16[4,128,256]{2,1,0:T(8,128)(2,1)S(1)} %collective-permute-done.1.ring1, bf16[4,400,256]{2,1,0:T(8,128)(2,1)S(1)} %all-to-all-done.bundle), custom_call_target="tpu_custom_call" | custom-call | tf_op jit(solution)/shard_map/pallas_call | solution.py:22
  34.3 4.3 %collective-permute-done.ring2 = bf16[3,128,256]{2,1,0:T(8,128)(2,1)S(1)} collective-permute-done((bf16[3,128,256]{2,1,0:T(8,128)(2,1)}, bf16[3,128,256]{2,1,0:T(8,128)(2,1)S(1)}, u32[]{:S(2)}, u32[]{:S(2)}) %collective-permute-start) | collective-permute-done | bytes 196640 | tf_op jit(solution)/shard_map/ppermute | solution.py:310
  40.2 8.6 %all_to_all.40.stats = f32[4,16,256]{2,1,0:T(8,128)S(1)} all-to-all(f32[4,16,256]{2,1,0:T(8,128)S(1)} %broadcast_in_dim.8), channel_id=1, replica_groups=mesh['y'=4,'core'=2,'zh'=4,'zl'=4,'x'=4] {'x'}, dimensions={0} | all-to-all | bytes 131072 | tf_op jit(solution)/shard_map/all_to_all | solution.py:314
  48.7 11.4 %all_to_all.41.refs_1_ = bf16[4,224,512]{2,1,0:T(8,128)(2,1)S(1)} all-to-all(bf16[4,224,512]{2,1,0:T(8,128)(2,1)S(1)} %broadcast_in_dim.7), channel_id=1, replica_groups=mesh['y'=4,'core'=2,'zh'=4,'zl'=4,'x'=4] {'x'}, dimensions={0} | all-to-all | bytes 1835008 | tf_op jit(solution)/shard_map/all_to_all | solution.py:314
  60.2 3.5 %all-to-all-start.1 = ((bf16[4,224,512]{2,1,0:T(8,128)(2,1)}), bf16[4,224,512]{2,1,0:T(8,128)(2,1)S(1)}, u32[]{:S(2)}, u32[]{:S(2)}) async-start(bf16[4,224,512]{2,1,0:T(8,128)(2,1)} %broadcast_in_dim.6), calls=%async_computation.1 | async-start | bytes 1835008 | tf_op jit(solution)/shard_map/all_to_all | solution.py:314
  65.8 1.9 %collective-permute-start.2 = (bf16[3,128,256]{2,1,0:T(8,128)(2,1)S(1)}, bf16[3,128,256]{2,1,0:T(8,128)(2,1)S(1)}, u32[]{:S(2)}, u32[]{:S(2)}) collective-permute-start(bf16[3,128,256]{2,1,0:T(8,128)(2,1)S(1)} %shard_map.109), channel_id=1, source_target_pairs={{60,0},{0,4},{4,8},{8,12},{12,16},{16,20},{20,24},{24,28},{28,32},... | collective-permute-start | bytes 589832 | tf_op jit(solution)/shard_map/ppermute | solution.py:310
  67.8 1.7 %shard_map.108.own = f32[4,128,256]{2,1,0:T(8,128)S(1)} custom-call(bf16[4,128,256]{2,1,0:T(8,128)(2,1)S(1)} %copy-done.3, bf16[4,400,256]{2,1,0:T(8,128)(2,1)S(1)} %all-to-all-done.bundle, bf16[4,128,256]{2,1,0:T(8,128)(2,1)S(1)} %get-tuple-element.43.grads), custom_call_target="tpu_custom_call" | custom-call | tf_op jit(solution)/shard_map/pallas_call | solution.py:22
  69.5 6.0 %collective-permute-done.2.arrived = bf16[3,128,256]{2,1,0:T(8,128)(2,1)S(1)} collective-permute-done((bf16[3,128,256]{2,1,0:T(8,128)(2,1)S(1)}, bf16[3,128,256]{2,1,0:T(8,128)(2,1)S(1)}, u32[]{:S(2)}, u32[]{:S(2)}) %collective-permute-start.2) | collective-permute-done | bytes 196640 | tf_op jit(solution)/shard_map/ppermute | solution.py:310
  78.3 9.9 %all-to-all-start.5 = ((bf16[8,32,512]{2,1,0:T(8,128)(2,1)}), bf16[8,32,512]{2,1,0:T(8,128)(2,1)}, u32[]{:S(2)}, u32[]{:S(2)}) async-start(bf16[8,32,512]{2,1,0:T(8,128)(2,1)} %bitcast.7), calls=%async_computation.5 | async-start | bytes 524288 | tf_op jit(solution)/shard_map/all_to_all | solution.py:314
  88.2 3.4 %collective-permute-start.3 = (bf16[4,128,256]{2,1,0:T(8,128)(2,1)}, bf16[4,128,256]{2,1,0:T(8,128)(2,1)}, u32[]{:S(2)}, u32[]{:S(2)}) collective-permute-start(bf16[4,128,256]{2,1,0:T(8,128)(2,1)} %copy-done.10), channel_id=1, source_target_pairs={{60,0},{0,4},{4,8},{8,12},{12,16},{16,20},{20,24},{24,28},{28,32},... | collective-permute-start | bytes 786440 | tf_op jit(solution)/shard_map/ppermute | solution.py:310
  92.9 9.5 %collective-permute-done.3.back1 = bf16[4,128,256]{2,1,0:T(8,128)(2,1)} collective-permute-done((bf16[4,128,256]{2,1,0:T(8,128)(2,1)}, bf16[4,128,256]{2,1,0:T(8,128)(2,1)}, u32[]{:S(2)}, u32[]{:S(2)}) %collective-permute-start.3) | collective-permute-done | bytes 262176 | tf_op jit(solution)/shard_map/ppermute | solution.py:310
  105.1 8.3 %all-to-all-start.6 = ((bf16[16,8,512]{2,1,0:T(8,128)(2,1)}), bf16[16,8,512]{2,1,0:T(8,128)(2,1)S(1)}, u32[]{:S(2)}, u32[]{:S(2)}) async-start(bf16[16,8,512]{2,1,0:T(8,128)(2,1)} %bitcast.4), calls=%async_computation.6 | async-start | bytes 262144 | tf_op jit(solution)/shard_map/all_to_all | solution.py:314
  113.3 3.3 %collective-permute-start.4 = (bf16[256,256]{1,0:T(8,128)(2,1)S(1)}, bf16[256,256]{1,0:T(8,128)(2,1)S(1)}, u32[]{:S(2)}, u32[]{:S(2)}) collective-permute-start(bf16[256,256]{1,0:T(8,128)(2,1)S(1)} %get-tuple-element.55), channel_id=1, source_target_pairs={{0,1},{1,2},{2,3},{3,0},{4,5},{5,6},{6,7},{7,4},{8,9},{9,10},{10,1... | collective-permute-start | bytes 393224 | tf_op jit(solution)/shard_map/ppermute | solution.py:413
  116.6 4.3 %collective-permute-start.5 = (bf16[256,256]{1,0:T(8,128)(2,1)S(1)}, bf16[256,256]{1,0:T(8,128)(2,1)S(1)}, u32[]{:S(2)}, u32[]{:S(2)}) collective-permute-start(bf16[256,256]{1,0:T(8,128)(2,1)S(1)} %get-tuple-element.56), channel_id=1, source_target_pairs={{0,2},{1,3},{2,0},{3,1},{4,6},{5,7},{6,4},{7,5},{8,10},{9,11},{10,... | collective-permute-start | bytes 393224 | tf_op jit(solution)/shard_map/ppermute | solution.py:413
  120.9 3.1 %collective-permute-start.6 = (bf16[256,256]{1,0:T(8,128)(2,1)S(1)}, bf16[256,256]{1,0:T(8,128)(2,1)S(1)}, u32[]{:S(2)}, u32[]{:S(2)}) collective-permute-start(bf16[256,256]{1,0:T(8,128)(2,1)S(1)} %get-tuple-element.57), channel_id=1, source_target_pairs={{0,3},{1,0},{2,1},{3,2},{4,7},{5,4},{6,5},{7,6},{8,11},{9,8},{10,9... | collective-permute-start | bytes 393224 | tf_op jit(solution)/shard_map/ppermute | solution.py:413
  124.0 3.4 %all-to-all-done.6 = bf16[16,8,512]{2,1,0:T(8,128)(2,1)S(1)} async-done(((bf16[16,8,512]{2,1,0:T(8,128)(2,1)}), bf16[16,8,512]{2,1,0:T(8,128)(2,1)S(1)}, u32[]{:S(2)}, u32[]{:S(2)}) %all-to-all-start.6) | async-done | bytes 131104 | tf_op jit(solution)/shard_map/all_to_all | solution.py:314
  128.1 9.0 %all-to-all-start.7 = ((f32[8,8,512]{2,1,0:T(8,128)}), f32[8,8,512]{2,1,0:T(8,128)S(1)}, u32[]{:S(2)}, u32[]{:S(2)}) async-start(f32[8,8,512]{2,1,0:T(8,128)} %shard_map.116), calls=%async_computation.7 | async-start | bytes 262144 | tf_op jit(solution)/shard_map/all_to_all | solution.py:314
  138.6 3.7 %all-to-all-done.7 = f32[8,8,512]{2,1,0:T(8,128)S(1)} async-done(((f32[8,8,512]{2,1,0:T(8,128)}), f32[8,8,512]{2,1,0:T(8,128)S(1)}, u32[]{:S(2)}, u32[]{:S(2)}) %all-to-all-start.7) | async-done | bytes 131104 | tf_op jit(solution)/shard_map/all_to_all | solution.py:314
  (48 shorter events, 15.6 us)
Async XLA Ops:
  2.3 10.4 %all-to-all-start.2 = ((bf16[4,128,256]{2,1,0:T(8,128)(2,1)}), bf16[4,128,256]{2,1,0:T(8,128)(2,1)S(1)}, u32[]{:S(2)}, u32[]{:S(2)}) async-start(bf16[4,128,256]{2,1,0:T(8,128)(2,1)} %shard_map.104), calls=%async_computation.2 | async-start | bytes 524288 | tf_op jit(solution)/shard_map/all_to_all | solution.py:314
  12.1 19.3 %copy-start.11 = (bf16[224,1024]{1,0:T(8,128)(2,1)S(1)}, bf16[224,1024]{1,0:T(8,128)(2,1)}, u32[]{:S(2)}) copy-start(bf16[224,1024]{1,0:T(8,128)(2,1)} %refs_4_.1) | copy-start | bytes 1376260
  12.7 18.8 %all-to-all-start = ((bf16[4,400,256]{2,1,0:T(8,128)(2,1)}), bf16[4,400,256]{2,1,0:T(8,128)(2,1)S(1)}, u32[]{:S(2)}, u32[]{:S(2)}) async-start(bf16[4,400,256]{2,1,0:T(8,128)(2,1)} %shard_map.103), calls=%async_computation | async-start | bytes 1638400 | tf_op jit(solution)/shard_map/all_to_all | solution.py:314
  16.5 16.0 %collective-permute-start.1 = (bf16[4,128,256]{2,1,0:T(8,128)(2,1)S(1)}, bf16[4,128,256]{2,1,0:T(8,128)(2,1)S(1)}, u32[]{:S(2)}, u32[]{:S(2)}) collective-permute-start(bf16[4,128,256]{2,1,0:T(8,128)(2,1)S(1)} %all-to-all-done.2.ring0), channel_id=1, source_target_pairs={{4,0},{8,4},{12,8},{16,12},{20,16},{24,20},{28,24},{32,28},{36,32}... | collective-permute-start | bytes 786440 | tf_op jit(solution)/shard_map/ppermute | solution.py:310
  28.4 10.2 %collective-permute-start = (bf16[3,128,256]{2,1,0:T(8,128)(2,1)}, bf16[3,128,256]{2,1,0:T(8,128)(2,1)S(1)}, u32[]{:S(2)}, u32[]{:S(2)}) collective-permute-start(bf16[3,128,256]{2,1,0:T(8,128)(2,1)} %slice.12), channel_id=1, source_target_pairs={{8,0},{12,4},{16,8},{20,12},{24,16},{28,20},{32,24},{36,28},{40,32... | collective-permute-start | bytes 589832 | tf_op jit(solution)/shard_map/ppermute | solution.py:310
  32.6 7.6 %copy-start.2 = (bf16[4,128,256]{2,1,0:T(8,128)(2,1)}, bf16[4,128,256]{2,1,0:T(8,128)(2,1)S(1)}, u32[]{:S(2)}) copy-start(bf16[4,128,256]{2,1,0:T(8,128)(2,1)S(1)} %collective-permute-done.1.ring1) | copy-start | bytes 786436
  39.3 0.8 copy-start.8
  60.2 16.1 %all-to-all-start.1 = ((bf16[4,224,512]{2,1,0:T(8,128)(2,1)}), bf16[4,224,512]{2,1,0:T(8,128)(2,1)S(1)}, u32[]{:S(2)}, u32[]{:S(2)}) async-start(bf16[4,224,512]{2,1,0:T(8,128)(2,1)} %broadcast_in_dim.6), calls=%async_computation.1 | async-start | bytes 1835008 | tf_op jit(solution)/shard_map/all_to_all | solution.py:314
  63.7 4.1 %copy-start.3 = (bf16[4,128,256]{2,1,0:T(8,128)(2,1)S(1)}, bf16[4,128,256]{2,1,0:T(8,128)(2,1)}, u32[]{:S(2)}) copy-start(bf16[4,128,256]{2,1,0:T(8,128)(2,1)} %copy-done.2) | copy-start | bytes 786436
  63.7 1.1 copy-start.9
  65.0 10.5 %copy-start.5 = (bf16[4,128,256]{2,1,0:T(8,128)(2,1)}, bf16[4,128,256]{2,1,0:T(8,128)(2,1)S(1)}, u32[]{:S(2)}) copy-start(bf16[4,128,256]{2,1,0:T(8,128)(2,1)S(1)} %get-tuple-element.41.refs_2_.gated_ref) | copy-start | bytes 786436
  65.8 9.6 %collective-permute-start.2 = (bf16[3,128,256]{2,1,0:T(8,128)(2,1)S(1)}, bf16[3,128,256]{2,1,0:T(8,128)(2,1)S(1)}, u32[]{:S(2)}, u32[]{:S(2)}) collective-permute-start(bf16[3,128,256]{2,1,0:T(8,128)(2,1)S(1)} %shard_map.109), channel_id=1, source_target_pairs={{60,0},{0,4},{4,8},{8,12},{12,16},{16,20},{20,24},{24,28},{28,32},... | collective-permute-start | bytes 589832 | tf_op jit(solution)/shard_map/ppermute | solution.py:310
  75.5 0.7 copy-start.10
  76.2 1.0 copy-start.6
  78.3 24.1 %copy-start.7 = (bf16[4,128,256]{2,1,0:T(8,128)(2,1)S(1)}, bf16[4,128,256]{2,1,0:T(8,128)(2,1)}, u32[]{:S(2)}) copy-start(bf16[4,128,256]{2,1,0:T(8,128)(2,1)} %copy-done.5) | copy-start | bytes 786436
  78.3 25.1 %all-to-all-start.5 = ((bf16[8,32,512]{2,1,0:T(8,128)(2,1)}), bf16[8,32,512]{2,1,0:T(8,128)(2,1)}, u32[]{:S(2)}, u32[]{:S(2)}) async-start(bf16[8,32,512]{2,1,0:T(8,128)(2,1)} %bitcast.7), calls=%async_computation.5 | async-start | bytes 524288 | tf_op jit(solution)/shard_map/all_to_all | solution.py:314
  88.2 48.9 %copy-start = (bf16[512,1024]{1,0:T(8,128)(2,1)S(1)}, bf16[512,1024]{1,0:T(8,128)(2,1)}, u32[]{:S(2)}) copy-start(bf16[512,1024]{1,0:T(8,128)(2,1)} %out_ref.1) | copy-start | bytes 3145732
  88.2 48.9 %copy-start.1 = (bf16[224,1024]{1,0:T(8,128)(2,1)S(1)}, bf16[224,1024]{1,0:T(8,128)(2,1)}, u32[]{:S(2)}) copy-start(bf16[224,1024]{1,0:T(8,128)(2,1)} %cand_ref.1) | copy-start | bytes 1376260
  88.2 14.2 %collective-permute-start.3 = (bf16[4,128,256]{2,1,0:T(8,128)(2,1)}, bf16[4,128,256]{2,1,0:T(8,128)(2,1)}, u32[]{:S(2)}, u32[]{:S(2)}) collective-permute-start(bf16[4,128,256]{2,1,0:T(8,128)(2,1)} %copy-done.10), channel_id=1, source_target_pairs={{60,0},{0,4},{4,8},{8,12},{12,16},{16,20},{20,24},{24,28},{28,32},... | collective-permute-start | bytes 786440 | tf_op jit(solution)/shard_map/ppermute | solution.py:310
  105.1 22.4 %all-to-all-start.6 = ((bf16[16,8,512]{2,1,0:T(8,128)(2,1)}), bf16[16,8,512]{2,1,0:T(8,128)(2,1)S(1)}, u32[]{:S(2)}, u32[]{:S(2)}) async-start(bf16[16,8,512]{2,1,0:T(8,128)(2,1)} %bitcast.4), calls=%async_computation.6 | async-start | bytes 262144 | tf_op jit(solution)/shard_map/all_to_all | solution.py:314
  113.3 23.7 %collective-permute-start.4 = (bf16[256,256]{1,0:T(8,128)(2,1)S(1)}, bf16[256,256]{1,0:T(8,128)(2,1)S(1)}, u32[]{:S(2)}, u32[]{:S(2)}) collective-permute-start(bf16[256,256]{1,0:T(8,128)(2,1)S(1)} %get-tuple-element.55), channel_id=1, source_target_pairs={{0,1},{1,2},{2,3},{3,0},{4,5},{5,6},{6,7},{7,4},{8,9},{9,10},{10,1... | collective-permute-start | bytes 393224 | tf_op jit(solution)/shard_map/ppermute | solution.py:413
  116.6 20.5 %collective-permute-start.5 = (bf16[256,256]{1,0:T(8,128)(2,1)S(1)}, bf16[256,256]{1,0:T(8,128)(2,1)S(1)}, u32[]{:S(2)}, u32[]{:S(2)}) collective-permute-start(bf16[256,256]{1,0:T(8,128)(2,1)S(1)} %get-tuple-element.56), channel_id=1, source_target_pairs={{0,2},{1,3},{2,0},{3,1},{4,6},{5,7},{6,4},{7,5},{8,10},{9,11},{10,... | collective-permute-start | bytes 393224 | tf_op jit(solution)/shard_map/ppermute | solution.py:413
  120.9 16.2 %collective-permute-start.6 = (bf16[256,256]{1,0:T(8,128)(2,1)S(1)}, bf16[256,256]{1,0:T(8,128)(2,1)S(1)}, u32[]{:S(2)}, u32[]{:S(2)}) collective-permute-start(bf16[256,256]{1,0:T(8,128)(2,1)S(1)} %get-tuple-element.57), channel_id=1, source_target_pairs={{0,3},{1,0},{2,1},{3,2},{4,7},{5,4},{6,5},{7,6},{8,11},{9,8},{10,9... | collective-permute-start | bytes 393224 | tf_op jit(solution)/shard_map/ppermute | solution.py:413
  128.1 14.3 %all-to-all-start.7 = ((f32[8,8,512]{2,1,0:T(8,128)}), f32[8,8,512]{2,1,0:T(8,128)S(1)}, u32[]{:S(2)}, u32[]{:S(2)}) async-start(f32[8,8,512]{2,1,0:T(8,128)} %shard_map.116), calls=%async_computation.7 | async-start | bytes 262144 | tf_op jit(solution)/shard_map/all_to_all | solution.py:314
  (1 other events, 0.7 us)

commit v13 on v9

--- a/solution.py
+++ b/solution.py
@@ -198,11 +198,13 @@
         grad_ref[group] = (inv_scale * (dy - mean_dy - normed * mean_mixed)).astype(BF16)
 
 
-def out_grad_kernel(total_cands, cots, gated, out_grad_ref):
-    count = cots.shape[1]
+def out_grad_kernel(total_cands, place_ref, gated, *refs):
+    *cots, out_grad_ref = refs
+    count = cots[0].shape[0]
     total = None
-    for group in range(HEADS):
-        part = jnp.dot(gated[group, :, :count], cots[group], preferred_element_type=F32)
+    for step, rows in enumerate(cots):
+        group = lax.rem(place_ref[0] + HEADS - step, HEADS)
+        part = jnp.dot(gated[group, :, :count], rows[...], preferred_element_type=F32)
         total = part if total is None else total + part
     total = (total * (1.0 / math.sqrt(total_cands))).astype(BF16)
     halves, rows_of, lines, columns = out_grad_ref.shape
@@ -344,7 +346,9 @@
     barrier = lax.optimization_barrier
     place = lax.axis_index("x").reshape(1).astype(jnp.int32)
 
-    cots = lax.all_gather(cotangent, "x")
+    cots = [cotangent] + [
+        lax.ppermute(cotangent, "x", [(i, (i + step) % HEADS) for i in range(HEADS)]) for step in range(1, HEADS)
+    ]
     ring_shape = shaped((HEADS, tall, 2 * size), BF16)
     by_head = pl.pallas_call(
         split_kernel,
@@ -386,8 +390,9 @@
     out_grad = on_core(
         lambda *refs: out_grad_kernel(total_cands, *refs),
         shaped((cores, zl, size // zl, half), BF16),
-        cots,
         gated,
+        *cots,
+        scalars=(place,),
     )
     out_grad, late_grads = barrier((out_grad, grads))
     back1 = on_core(back1_kernel, shaped(ring1.shape, F32), ring1, bundle, late_grads)

time: 133 us -> 124 us (0.932)
  between operations: 14.2 us -> 0.91 us
  starting transfers between devices: 65.6 us -> 74.5 us
  blocking collectives: 8.47 us -> 6.84 us
  local copies, waits for them, and re-layouts: 1.52 us -> 0.04 us
    ppermute x0 -> x3, starting transfers between devices: none -> 10.8 us  [on_device(): lax.ppermute(cotangent, 'x', [(i, (i + step) % HEADS) for i in range(HEAD...]
    all_to_all x5, starting transfers between devices: 35.4 us -> 33.5 us  [exchanged(): return lax.all_to_all(chunks, axis, 0, 0, tiled=True)]
    all_to_all x1, blocking collectives: 8.47 us -> 6.84 us  [exchanged(): return lax.all_to_all(chunks, axis, 0, 0, tiled=True)]
    unnamed x6, local copies, waits for them, and re-layouts: 1.5 us -> 0.02 us
  transfers between devices with their start and end apart: 13 -> 15, of which waited for: 7 -> 6; matrix products, arithmetic and copies ran while one was open for 0% -> 0% of each run, Pallas kernels for 14% -> 13%
where the time goes in v13:
time: 124 us; the launch traced here: 123 us
  starting transfers between devices  74.5 us (60%)
  waiting for transfers between devices  21.9 us (18%)
  Pallas kernels  19.1 us (15%)
  blocking collectives  6.84 us (6%)
    all_to_all x5, starting transfers between devices, exchanged(): return lax.all_to_all(chunks, axis, 0, 0, tiled=True)  33.5 us
    ppermute x4, starting transfers between devices, moved(): lax.ppermute(block, DEPTH, [((i + distance) % size, i) for i in range(siz...  19.5 us
    ppermute x4, waiting for transfers between devices, moved(): lax.ppermute(block, DEPTH, [((i + distance) % size, i) for i in range(siz...  14.3 us
    pallas_call x13, Pallas kernels, on_core(): pl.pallas_call(kernel, out_shape=outs, in_specs=[pl.BlockSpec(memory_spac...  12.4 us
    ppermute x3, starting transfers between devices, on_device(): lax.ppermute(cotangent, 'x', [(i, (i + step) % HEADS) for i in range(HEAD...  10.8 us
    ppermute x3, starting transfers between devices, on_device(): lax.ppermute(parcel, 'x', [(i, (i + step) % HEADS) for i in range(HEADS)])  10.7 us
    all_to_all x5, waiting for transfers between devices, exchanged(): return lax.all_to_all(chunks, axis, 0, 0, tiled=True)  7.6 us
    all_to_all x1, blocking collectives, exchanged(): return lax.all_to_all(chunks, axis, 0, 0, tiled=True)  6.84 us
  transfers between devices with their start and end apart: 15, of which 6 were waited for; matrix products, arithmetic and copies ran while one was open for 0% of the time, Pallas kernels for 13%

profile of v13, /device:TPU:1, one launch (start us, length us, event | category | flops | bytes accessed | tf_op | source)
XLA Modules:
  0.0 123.2 jit_solution(8703734573909664934)
XLA Ops:
  2.3 4.9 %all-to-all-start = ((bf16[4,128,256]{2,1,0:T(8,128)(2,1)}), bf16[4,128,256]{2,1,0:T(8,128)(2,1)S(1)}, u32[]{:S(2)}, u32[]{:S(2)}) async-start(bf16[4,128,256]{2,1,0:T(8,128)(2,1)} %shard_map.103), calls=%async_computation | async-start | bytes 524288 | tf_op jit(solution)/shard_map/all_to_all | solution.py:318
  7.1 5.1 %shard_map.104 = bf16[4,400,256]{2,1,0:T(8,128)(2,1)} custom-call(s32[2,8]{1,0:T(2,128)} %refs_0_.1, s32[2]{0:T(128)} %refs_1_.1, s32[1,224]{1,0:T(1,128)} %bitcast.9, bf16[224,1024]{1,0:T(8,128)(2,1)} %cand_ref.1, bf16[224,1024]{1,0:T(8,128)(2,1)} %refs_2_.1, bf16[1024,1024]{1,0:T(8,128)(2,1)} %refs_5_.1, bf16[512,1024]{1,0:T(8,128)(2,1)} %out_ref.1), custom_call_target="tpu_custom_call" | custom-call | tf_op jit(solution)/shard_map/pallas_call | solution.py:51
  12.7 3.8 %all-to-all-start.1 = ((bf16[4,400,256]{2,1,0:T(8,128)(2,1)}), bf16[4,400,256]{2,1,0:T(8,128)(2,1)S(1)}, u32[]{:S(2)}, u32[]{:S(2)}) async-start(bf16[4,400,256]{2,1,0:T(8,128)(2,1)} %shard_map.104), calls=%async_computation.1 | async-start | bytes 1638400 | tf_op jit(solution)/shard_map/all_to_all | solution.py:318
  16.5 11.1 %collective-permute-start.1 = (bf16[4,128,256]{2,1,0:T(8,128)(2,1)S(1)}, bf16[4,128,256]{2,1,0:T(8,128)(2,1)S(1)}, u32[]{:S(2)}, u32[]{:S(2)}) collective-permute-start(bf16[4,128,256]{2,1,0:T(8,128)(2,1)S(1)} %all-to-all-done.ring0), channel_id=1, source_target_pairs={{4,0},{8,4},{12,8},{16,12},{20,16},{24,20},{28,24},{32,28},{36,32}... | collective-permute-start | bytes 786440 | tf_op jit(solution)/shard_map/ppermute | solution.py:314
  27.6 3.4 %collective-permute-start.2 = (bf16[224,1024]{1,0:T(8,128)(2,1)S(1)}, bf16[224,1024]{1,0:T(8,128)(2,1)S(1)}, u32[]{:S(2)}, u32[]{:S(2)}) collective-permute-start(bf16[224,1024]{1,0:T(8,128)(2,1)S(1)} %copy-done.1), channel_id=1, source_target_pairs={{0,1},{1,2},{2,3},{3,0},{4,5},{5,6},{6,7},{7,4},{8,9},{9,10},{10,1... | collective-permute-start | bytes 1376264 | tf_op jit(solution)/shard_map/ppermute | solution.py:350
  31.0 4.3 %collective-permute-start.3 = (bf16[224,1024]{1,0:T(8,128)(2,1)S(1)}, bf16[224,1024]{1,0:T(8,128)(2,1)}, u32[]{:S(2)}, u32[]{:S(2)}) collective-permute-start(bf16[224,1024]{1,0:T(8,128)(2,1)S(1)} %copy-done.1), channel_id=1, source_target_pairs={{0,2},{1,3},{2,0},{3,1},{4,6},{5,7},{6,4},{7,5},{8,10},{9,11},{10,... | collective-permute-start | bytes 1376264 | tf_op jit(solution)/shard_map/ppermute | solution.py:350
  35.3 3.1 %collective-permute-start.4 = (bf16[224,1024]{1,0:T(8,128)(2,1)S(1)}, bf16[224,1024]{1,0:T(8,128)(2,1)}, u32[]{:S(2)}, u32[]{:S(2)}) collective-permute-start(bf16[224,1024]{1,0:T(8,128)(2,1)S(1)} %copy-done.1), channel_id=1, source_target_pairs={{0,3},{1,0},{2,1},{3,2},{4,7},{5,4},{6,5},{7,6},{8,11},{9,8},{10,9... | collective-permute-start | bytes 1376264 | tf_op jit(solution)/shard_map/ppermute | solution.py:350
  38.4 3.1 %collective-permute-start = (bf16[3,128,256]{2,1,0:T(8,128)(2,1)S(1)}, bf16[3,128,256]{2,1,0:T(8,128)(2,1)S(1)}, u32[]{:S(2)}, u32[]{:S(2)}) collective-permute-start(bf16[3,128,256]{2,1,0:T(8,128)(2,1)S(1)} %slice.4), channel_id=1, source_target_pairs={{8,0},{12,4},{16,8},{20,12},{24,16},{28,20},{32,24},{36,28},{40,32... | collective-permute-start | bytes 589832 | tf_op jit(solution)/shard_map/ppermute | solution.py:314
  41.5 1.7 %shard_map.105.before = f32[4,128,256]{2,1,0:T(8,128)S(1)} custom-call(bf16[4,128,256]{2,1,0:T(8,128)(2,1)S(1)} %all-to-all-done.ring0, bf16[4,128,256]{2,1,0:T(8,128)(2,1)S(1)} %collective-permute-done.1.ring1, bf16[4,400,256]{2,1,0:T(8,128)(2,1)S(1)} %all-to-all-done.1.bundle), custom_call_target="tpu_custom_call" | custom-call | tf_op jit(solution)/shard_map/pallas_call | solution.py:22
  43.2 5.6 %collective-permute-done.ring2 = bf16[3,128,256]{2,1,0:T(8,128)(2,1)S(1)} collective-permute-done((bf16[3,128,256]{2,1,0:T(8,128)(2,1)S(1)}, bf16[3,128,256]{2,1,0:T(8,128)(2,1)S(1)}, u32[]{:S(2)}, u32[]{:S(2)}) %collective-permute-start) | collective-permute-done | bytes 196640 | tf_op jit(solution)/shard_map/ppermute | solution.py:314
  49.5 6.8 %all_to_all.30.stats = f32[4,16,256]{2,1,0:T(8,128)S(1)} all-to-all(f32[4,16,256]{2,1,0:T(8,128)S(1)} %broadcast_in_dim.2), channel_id=1, replica_groups=mesh['y'=4,'core'=2,'zh'=4,'zl'=4,'x'=4] {'x'}, dimensions={0} | all-to-all | bytes 131072 | tf_op jit(solution)/shard_map/all_to_all | solution.py:318
  57.4 1.9 %collective-permute-start.5 = (bf16[3,128,256]{2,1,0:T(8,128)(2,1)S(1)}, bf16[3,128,256]{2,1,0:T(8,128)(2,1)S(1)}, u32[]{:S(2)}, u32[]{:S(2)}) collective-permute-start(bf16[3,128,256]{2,1,0:T(8,128)(2,1)S(1)} %shard_map.108), channel_id=1, source_target_pairs={{60,0},{0,4},{4,8},{8,12},{12,16},{16,20},{20,24},{24,28},{28,32},... | collective-permute-start | bytes 589832 | tf_op jit(solution)/shard_map/ppermute | solution.py:314
  59.4 2.3 %shard_map.109 = bf16[2,4,32,512]{3,2,1,0:T(8,128)(2,1)} custom-call(s32[1]{0:T(128)} %bitcast.refs_0_.place_ref, bf16[4,128,256]{2,1,0:T(8,128)(2,1)S(1)} %get-tuple-element.35.refs_1_.gated_ref, bf16[224,1024]{1,0:T(8,128)(2,1)S(1)} %copy-done.1, bf16[224,1024]{1,0:T(8,128)(2,1)S(1)} %collective-permute-done.2.refs_3_, ...), custom_call_target="tpu_custom_call" | custom-call | tf_op jit(solution)/shard_map/pallas_call | solution.py:22
  61.7 1.7 %shard_map.110.own = f32[4,128,256]{2,1,0:T(8,128)S(1)} custom-call(bf16[4,128,256]{2,1,0:T(8,128)(2,1)S(1)} %collective-permute-done.1.ring1, bf16[4,400,256]{2,1,0:T(8,128)(2,1)S(1)} %all-to-all-done.1.bundle, bf16[4,128,256]{2,1,0:T(8,128)(2,1)S(1)} %get-tuple-element.40.grads), custom_call_target="tpu_custom_call" | custom-call | tf_op jit(solution)/shard_map/pallas_call | solution.py:22
  65.1 8.7 %all-to-all-start.3 = ((bf16[8,32,512]{2,1,0:T(8,128)(2,1)}), bf16[8,32,512]{2,1,0:T(8,128)(2,1)S(1)}, u32[]{:S(2)}, u32[]{:S(2)}) async-start(bf16[8,32,512]{2,1,0:T(8,128)(2,1)} %bitcast.2), calls=%async_computation.3 | async-start | bytes 524288 | tf_op jit(solution)/shard_map/all_to_all | solution.py:318
  73.9 3.4 %collective-permute-start.6 = (bf16[4,128,256]{2,1,0:T(8,128)(2,1)S(1)}, bf16[4,128,256]{2,1,0:T(8,128)(2,1)S(1)}, u32[]{:S(2)}, u32[]{:S(2)}) collective-permute-start(bf16[4,128,256]{2,1,0:T(8,128)(2,1)S(1)} %shard_map.112), channel_id=1, source_target_pairs={{60,0},{0,4},{4,8},{8,12},{12,16},{16,20},{20,24},{24,28},{28,32},... | collective-permute-start | bytes 786440 | tf_op jit(solution)/shard_map/ppermute | solution.py:314
  78.6 7.1 %collective-permute-done.6.back1 = bf16[4,128,256]{2,1,0:T(8,128)(2,1)S(1)} collective-permute-done((bf16[4,128,256]{2,1,0:T(8,128)(2,1)S(1)}, bf16[4,128,256]{2,1,0:T(8,128)(2,1)S(1)}, u32[]{:S(2)}, u32[]{:S(2)}) %collective-permute-start.6) | collective-permute-done | bytes 262176 | tf_op jit(solution)/shard_map/ppermute | solution.py:314
  86.4 7.2 %all-to-all-start.4 = ((bf16[16,8,512]{2,1,0:T(8,128)(2,1)}), bf16[16,8,512]{2,1,0:T(8,128)(2,1)S(1)}, u32[]{:S(2)}, u32[]{:S(2)}) async-start(bf16[16,8,512]{2,1,0:T(8,128)(2,1)} %bitcast.4), calls=%async_computation.4 | async-start | bytes 262144 | tf_op jit(solution)/shard_map/all_to_all | solution.py:318
  93.6 3.3 %collective-permute-start.7 = (bf16[256,256]{1,0:T(8,128)(2,1)S(1)}, bf16[256,256]{1,0:T(8,128)(2,1)S(1)}, u32[]{:S(2)}, u32[]{:S(2)}) collective-permute-start(bf16[256,256]{1,0:T(8,128)(2,1)S(1)} %get-tuple-element.53), channel_id=1, source_target_pairs={{0,1},{1,2},{2,3},{3,0},{4,5},{5,6},{6,7},{7,4},{8,9},{9,10},{10,1... | collective-permute-start | bytes 393224 | tf_op jit(solution)/shard_map/ppermute | solution.py:414
  96.9 4.3 %collective-permute-start.8 = (bf16[256,256]{1,0:T(8,128)(2,1)S(1)}, bf16[256,256]{1,0:T(8,128)(2,1)S(1)}, u32[]{:S(2)}, u32[]{:S(2)}) collective-permute-start(bf16[256,256]{1,0:T(8,128)(2,1)S(1)} %get-tuple-element.54), channel_id=1, source_target_pairs={{0,2},{1,3},{2,0},{3,1},{4,6},{5,7},{6,4},{7,5},{8,10},{9,11},{10,... | collective-permute-start | bytes 393224 | tf_op jit(solution)/shard_map/ppermute | solution.py:414
  101.2 3.1 %collective-permute-start.9 = (bf16[256,256]{1,0:T(8,128)(2,1)S(1)}, bf16[256,256]{1,0:T(8,128)(2,1)S(1)}, u32[]{:S(2)}, u32[]{:S(2)}) collective-permute-start(bf16[256,256]{1,0:T(8,128)(2,1)S(1)} %get-tuple-element.55), channel_id=1, source_target_pairs={{0,3},{1,0},{2,1},{3,2},{4,7},{5,4},{6,5},{7,6},{8,11},{9,8},{10,9... | collective-permute-start | bytes 393224 | tf_op jit(solution)/shard_map/ppermute | solution.py:414
  104.3 3.4 %all-to-all-done.4 = bf16[16,8,512]{2,1,0:T(8,128)(2,1)S(1)} async-done(((bf16[16,8,512]{2,1,0:T(8,128)(2,1)}), bf16[16,8,512]{2,1,0:T(8,128)(2,1)S(1)}, u32[]{:S(2)}, u32[]{:S(2)}) %all-to-all-start.4) | async-done | bytes 131104 | tf_op jit(solution)/shard_map/all_to_all | solution.py:318
  108.4 9.0 %all-to-all-start.5 = ((f32[8,8,512]{2,1,0:T(8,128)}), f32[8,8,512]{2,1,0:T(8,128)S(1)}, u32[]{:S(2)}, u32[]{:S(2)}) async-start(f32[8,8,512]{2,1,0:T(8,128)} %shard_map.116), calls=%async_computation.5 | async-start | bytes 262144 | tf_op jit(solution)/shard_map/all_to_all | solution.py:318
  118.9 3.7 %all-to-all-done.5 = f32[8,8,512]{2,1,0:T(8,128)S(1)} async-done(((f32[8,8,512]{2,1,0:T(8,128)}), f32[8,8,512]{2,1,0:T(8,128)S(1)}, u32[]{:S(2)}, u32[]{:S(2)}) %all-to-all-start.5) | async-done | bytes 131104 | tf_op jit(solution)/shard_map/all_to_all | solution.py:318
  (30 shorter events, 10.5 us)
Async XLA Ops:
  2.3 10.4 %all-to-all-start = ((bf16[4,128,256]{2,1,0:T(8,128)(2,1)}), bf16[4,128,256]{2,1,0:T(8,128)(2,1)S(1)}, u32[]{:S(2)}, u32[]{:S(2)}) async-start(bf16[4,128,256]{2,1,0:T(8,128)(2,1)} %shard_map.103), calls=%async_computation | async-start | bytes 524288 | tf_op jit(solution)/shard_map/all_to_all | solution.py:318
  7.1 20.5 %copy-start.1 = (bf16[224,1024]{1,0:T(8,128)(2,1)S(1)}, bf16[224,1024]{1,0:T(8,128)(2,1)}, u32[]{:S(2)}) copy-start(bf16[224,1024]{1,0:T(8,128)(2,1)} %refs_2_.1) | copy-start | bytes 1376260
  12.7 28.8 %all-to-all-start.1 = ((bf16[4,400,256]{2,1,0:T(8,128)(2,1)}), bf16[4,400,256]{2,1,0:T(8,128)(2,1)S(1)}, u32[]{:S(2)}, u32[]{:S(2)}) async-start(bf16[4,400,256]{2,1,0:T(8,128)(2,1)} %shard_map.104), calls=%async_computation.1 | async-start | bytes 1638400 | tf_op jit(solution)/shard_map/all_to_all | solution.py:318
  16.5 25.0 %collective-permute-start.1 = (bf16[4,128,256]{2,1,0:T(8,128)(2,1)S(1)}, bf16[4,128,256]{2,1,0:T(8,128)(2,1)S(1)}, u32[]{:S(2)}, u32[]{:S(2)}) collective-permute-start(bf16[4,128,256]{2,1,0:T(8,128)(2,1)S(1)} %all-to-all-done.ring0), channel_id=1, source_target_pairs={{4,0},{8,4},{12,8},{16,12},{20,16},{24,20},{28,24},{32,28},{36,32}... | collective-permute-start | bytes 786440 | tf_op jit(solution)/shard_map/ppermute | solution.py:314
  27.6 31.8 %collective-permute-start.2 = (bf16[224,1024]{1,0:T(8,128)(2,1)S(1)}, bf16[224,1024]{1,0:T(8,128)(2,1)S(1)}, u32[]{:S(2)}, u32[]{:S(2)}) collective-permute-start(bf16[224,1024]{1,0:T(8,128)(2,1)S(1)} %copy-done.1), channel_id=1, source_target_pairs={{0,1},{1,2},{2,3},{3,0},{4,5},{5,6},{6,7},{7,4},{8,9},{9,10},{10,1... | collective-permute-start | bytes 1376264 | tf_op jit(solution)/shard_map/ppermute | solution.py:350
  31.0 28.4 %collective-permute-start.3 = (bf16[224,1024]{1,0:T(8,128)(2,1)S(1)}, bf16[224,1024]{1,0:T(8,128)(2,1)}, u32[]{:S(2)}, u32[]{:S(2)}) collective-permute-start(bf16[224,1024]{1,0:T(8,128)(2,1)S(1)} %copy-done.1), channel_id=1, source_target_pairs={{0,2},{1,3},{2,0},{3,1},{4,6},{5,7},{6,4},{7,5},{8,10},{9,11},{10,... | collective-permute-start | bytes 1376264 | tf_op jit(solution)/shard_map/ppermute | solution.py:350
  35.3 24.1 %collective-permute-start.4 = (bf16[224,1024]{1,0:T(8,128)(2,1)S(1)}, bf16[224,1024]{1,0:T(8,128)(2,1)}, u32[]{:S(2)}, u32[]{:S(2)}) collective-permute-start(bf16[224,1024]{1,0:T(8,128)(2,1)S(1)} %copy-done.1), channel_id=1, source_target_pairs={{0,3},{1,0},{2,1},{3,2},{4,7},{5,4},{6,5},{7,6},{8,11},{9,8},{10,9... | collective-permute-start | bytes 1376264 | tf_op jit(solution)/shard_map/ppermute | solution.py:350
  38.4 10.3 %collective-permute-start = (bf16[3,128,256]{2,1,0:T(8,128)(2,1)S(1)}, bf16[3,128,256]{2,1,0:T(8,128)(2,1)S(1)}, u32[]{:S(2)}, u32[]{:S(2)}) collective-permute-start(bf16[3,128,256]{2,1,0:T(8,128)(2,1)S(1)} %slice.4), channel_id=1, source_target_pairs={{8,0},{12,4},{16,8},{20,12},{24,16},{28,20},{32,24},{36,28},{40,32... | collective-permute-start | bytes 589832 | tf_op jit(solution)/shard_map/ppermute | solution.py:314
  57.4 7.6 %collective-permute-start.5 = (bf16[3,128,256]{2,1,0:T(8,128)(2,1)S(1)}, bf16[3,128,256]{2,1,0:T(8,128)(2,1)S(1)}, u32[]{:S(2)}, u32[]{:S(2)}) collective-permute-start(bf16[3,128,256]{2,1,0:T(8,128)(2,1)S(1)} %shard_map.108), channel_id=1, source_target_pairs={{60,0},{0,4},{4,8},{8,12},{12,16},{16,20},{20,24},{24,28},{28,32},... | collective-permute-start | bytes 589832 | tf_op jit(solution)/shard_map/ppermute | solution.py:314
  65.1 20.7 %all-to-all-start.3 = ((bf16[8,32,512]{2,1,0:T(8,128)(2,1)}), bf16[8,32,512]{2,1,0:T(8,128)(2,1)S(1)}, u32[]{:S(2)}, u32[]{:S(2)}) async-start(bf16[8,32,512]{2,1,0:T(8,128)(2,1)} %bitcast.2), calls=%async_computation.3 | async-start | bytes 524288 | tf_op jit(solution)/shard_map/all_to_all | solution.py:318
  73.8 43.5 %copy-start = (bf16[512,1024]{1,0:T(8,128)(2,1)S(1)}, bf16[512,1024]{1,0:T(8,128)(2,1)}, u32[]{:S(2)}) copy-start(bf16[512,1024]{1,0:T(8,128)(2,1)} %out_ref.1) | copy-start | bytes 3145732
  73.9 43.5 %copy-start.2 = (bf16[224,1024]{1,0:T(8,128)(2,1)S(1)}, bf16[224,1024]{1,0:T(8,128)(2,1)}, u32[]{:S(2)}) copy-start(bf16[224,1024]{1,0:T(8,128)(2,1)} %cand_ref.1) | copy-start | bytes 1376260
  73.9 11.8 %collective-permute-start.6 = (bf16[4,128,256]{2,1,0:T(8,128)(2,1)S(1)}, bf16[4,128,256]{2,1,0:T(8,128)(2,1)S(1)}, u32[]{:S(2)}, u32[]{:S(2)}) collective-permute-start(bf16[4,128,256]{2,1,0:T(8,128)(2,1)S(1)} %shard_map.112), channel_id=1, source_target_pairs={{60,0},{0,4},{4,8},{8,12},{12,16},{16,20},{20,24},{24,28},{28,32},... | collective-permute-start | bytes 786440 | tf_op jit(solution)/shard_map/ppermute | solution.py:314
  86.4 21.3 %all-to-all-start.4 = ((bf16[16,8,512]{2,1,0:T(8,128)(2,1)}), bf16[16,8,512]{2,1,0:T(8,128)(2,1)S(1)}, u32[]{:S(2)}, u32[]{:S(2)}) async-start(bf16[16,8,512]{2,1,0:T(8,128)(2,1)} %bitcast.4), calls=%async_computation.4 | async-start | bytes 262144 | tf_op jit(solution)/shard_map/all_to_all | solution.py:318
  93.6 23.7 %collective-permute-start.7 = (bf16[256,256]{1,0:T(8,128)(2,1)S(1)}, bf16[256,256]{1,0:T(8,128)(2,1)S(1)}, u32[]{:S(2)}, u32[]{:S(2)}) collective-permute-start(bf16[256,256]{1,0:T(8,128)(2,1)S(1)} %get-tuple-element.53), channel_id=1, source_target_pairs={{0,1},{1,2},{2,3},{3,0},{4,5},{5,6},{6,7},{7,4},{8,9},{9,10},{10,1... | collective-permute-start | bytes 393224 | tf_op jit(solution)/shard_map/ppermute | solution.py:414
  96.9 20.5 %collective-permute-start.8 = (bf16[256,256]{1,0:T(8,128)(2,1)S(1)}, bf16[256,256]{1,0:T(8,128)(2,1)S(1)}, u32[]{:S(2)}, u32[]{:S(2)}) collective-permute-start(bf16[256,256]{1,0:T(8,128)(2,1)S(1)} %get-tuple-element.54), channel_id=1, source_target_pairs={{0,2},{1,3},{2,0},{3,1},{4,6},{5,7},{6,4},{7,5},{8,10},{9,11},{10,... | collective-permute-start | bytes 393224 | tf_op jit(solution)/shard_map/ppermute | solution.py:414
  101.2 16.2 %collective-permute-start.9 = (bf16[256,256]{1,0:T(8,128)(2,1)S(1)}, bf16[256,256]{1,0:T(8,128)(2,1)S(1)}, u32[]{:S(2)}, u32[]{:S(2)}) collective-permute-start(bf16[256,256]{1,0:T(8,128)(2,1)S(1)} %get-tuple-element.55), channel_id=1, source_target_pairs={{0,3},{1,0},{2,1},{3,2},{4,7},{5,4},{6,5},{7,6},{8,11},{9,8},{10,9... | collective-permute-start | bytes 393224 | tf_op jit(solution)/shard_map/ppermute | solution.py:414
  108.4 14.2 %all-to-all-start.5 = ((f32[8,8,512]{2,1,0:T(8,128)}), f32[8,8,512]{2,1,0:T(8,128)S(1)}, u32[]{:S(2)}, u32[]{:S(2)}) async-start(f32[8,8,512]{2,1,0:T(8,128)} %shard_map.116), calls=%async_computation.5 | async-start | bytes 262144 | tf_op jit(solution)/shard_map/all_to_all | solution.py:318
